TPU v7x, 32 devices: a whole 2x2x4 slice. The times are simulated.
32 devices in a mesh: row: 16 (over z, y, core), col: 2 (over x).
Axes of the slice: x: 2, y: 2, z: 4, core: 2. Of those that a mesh axis runs over, the one named last changes fastest.
Arguments:
- object_field: float32 [2, 4096, 512], P(None, 'row', 'col'), may hold values from -6 to 6
- probe_field: float32 [2, 256, 256], replicated, may hold values from -6 to 6
- intensity: float32 [16, 2, 4, 256, 256], P('row', 'col'), may hold values from 0.25 to 16
- view_offsets: int32 [16, 2, 4, 2], P('row', 'col'), may hold values from 0 to 128
- view_counts: int32 [16, 2], P('row', 'col'), may hold values from 1 to 4, as said below
Outputs:
- updated_object: float32 [2, 4096, 512], P(None, 'row', 'col')
Inputs may be any that keep to these rules, and one draw needn't show every extreme that they name: `view_counts`: every draw has some tile with 4 valid views. `view_offsets`: each view lies inside its tile's padded window.
All inputs are finite; a program needn't handle non-finite values.
Results may differ from a plain program's by a relative error of at most 0.0003.
Values sent between devices are 32-bit elements; how exact they have to be, the bound alone decides.
No kernel may reach another device: no remote copies, remote signals or barrier semaphores. Data moves between devices by JAX's collectives and lax.ppermute only.
A program may use at most 64 MiB of HBM per device.

v0:
```python
import functools
import math

import jax
import jax.numpy as jnp
import ml_dtypes
import numpy as np
from jax import lax
from jax.experimental import pallas as pl
from jax.experimental.pallas import tpu as pltpu
from jax.sharding import PartitionSpec as P

MARGIN = 64
LANES = 128
CHUNK = 64

smooth_eps = 0.1
step_size = 0.2

F32 = jnp.float32
BF16 = jnp.bfloat16


def dft_tables(length):
    half = length // 2
    counter = np.arange(half)
    factor = 1.0 / math.sqrt(length)
    product = np.outer(counter, counter)
    even = np.exp(-2j * np.pi * (product % half) / half) * factor
    odd = np.exp(-2j * np.pi * ((2 * product + counter[:, None]) % length) / length) * factor

    def as_real(table):
        return np.block([[table.real, table.imag], [-table.imag, table.real]])

    def parts(table):
        high = table.astype(ml_dtypes.bfloat16)
        low = (table - high.astype(np.float64)).astype(ml_dtypes.bfloat16)
        return high, low

    even, odd = as_real(even), as_real(odd)
    by_right = [np.concatenate(parts(t), 0) for t in (even, odd, even.T, odd.T)]
    by_left = [np.concatenate(parts(t), 1) for t in (even.T, odd.T, even, odd)]
    order = np.zeros((length, length))
    order[np.arange(length), (np.arange(length) % 2) * half + np.arange(length) // 2] = 1.0
    return np.stack(by_right), np.stack(by_left), order.astype(ml_dtypes.bfloat16)


def channels(mesh_cols):
    if mesh_cols == 1:
        return []
    if mesh_cols == 2:
        return [([(0, 1), (1, 0)], None, None)]
    forward = [(i, i + 1) for i in range(mesh_cols - 1)]
    return [(forward, True, False), ([(j, i) for i, j in forward], False, True)]


def row_pairs(count, first):
    pairs = [(i, i + 1) for i in range(first, count - 1, 2)]
    return pairs + [(j, i) for i, j in pairs]


def sends_right(channel):
    return lax.axis_index("col") == 0 if channel[1] is None else channel[1]


def takes_right(channel):
    return lax.axis_index("col") == 0 if channel[2] is None else channel[2]


def lower_partner():
    return lax.rem(lax.axis_index("row"), 2) == 0


def lane_ids():
    return lax.broadcasted_iota(jnp.int32, (1, LANES), 1)


def half_lanes(right):
    low = lane_ids() < LANES // 2
    if isinstance(right, bool):
        return low if right else ~low
    return lane_ids() // (LANES // 2) == jnp.where(right, 0, 1)


def split(value):
    high = value.astype(BF16)
    return high, (value - high.astype(F32)).astype(BF16)


def dot(first, second):
    return jnp.dot(first, second, preferred_element_type=F32)


def swap_halves(block):
    return pltpu.roll(block, LANES // 2, 1)


def pack_kernel(chans, object_ref, a_ref, b_ref, *edge_refs):
    size = object_ref.shape[1]
    top, bottom = pl.ds(0, MARGIN), pl.ds(size - MARGIN, MARGIN)
    lower = lower_partner()
    for part in range(2):
        head, tail = object_ref[part, top, :], object_ref[part, bottom, :]
        a_ref[part] = jnp.where(lower, tail, head)
        b_ref[part] = jnp.where(lower, head, tail)
    for number, channel in enumerate(chans):
        right = sends_right(channel)
        x_ref, k_ref = edge_refs[2 * number : 2 * number + 2]
        low = lane_ids() < LANES // 2
        for start in range(0, size, CHUNK):
            rows = slice(start, start + CHUNK)
            left_edge = jnp.where(
                low, object_ref[0, rows, :LANES], swap_halves(object_ref[1, rows, :LANES])
            )
            right_edge = jnp.where(
                low,
                swap_halves(object_ref[1, rows, size - LANES :]),
                object_ref[0, rows, size - LANES :],
            )
            x_ref[rows] = jnp.where(right, right_edge, left_edge)
        k_ref[...] = jnp.where(lower, x_ref[:MARGIN], x_ref[size - MARGIN :])


def pack_call(object_field, chans):
    size = object_field.shape[1]
    shapes = [(2, MARGIN, size)] * 2 + [(size, LANES), (MARGIN, LANES)] * len(chans)
    vmem = pl.BlockSpec(memory_space=pltpu.VMEM)
    return pl.pallas_call(
        functools.partial(pack_kernel, chans),
        out_shape=[jax.ShapeDtypeStruct(shape, F32) for shape in shapes],
        in_specs=[vmem],
        out_specs=[vmem] * len(shapes),
    )(object_field)


def prepare_kernel(offsets, counts, probe, intensity, order, placed, amplitude, doubled):
    views, size = intensity.shape[2], probe.shape[1]
    half = size // 2
    for part in range(2):
        doubled[part, :size] = probe[part]
        doubled[part, size : 2 * size] = probe[part]
    sublane = lax.broadcasted_iota(jnp.int32, (1, 8, 1), 1)
    for view in range(views):
        valid = (view < counts[0, 0]).astype(F32)
        high, low = split(jnp.sqrt(intensity[0, 0, view] + smooth_eps) * valid)
        ordered = dot(high, order[...]) + dot(low, order[...])
        amplitude[view, 0] = ordered[:, :half]
        amplitude[view, 1] = ordered[:, half:]
        shift_row = lax.rem(offsets[0, 0, view, 0] - MARGIN + size, size)
        shift_col = lax.rem(offsets[0, 0, view, 1] - MARGIN + size, size)
        start = lax.rem(size - shift_row, size)
        whole = pl.multiple_of((start // 8) * 8, 8)
        rest = start - whole
        for part in range(2):
            for row in range(0, size, CHUNK):
                block = doubled[part, pl.ds(whole + row, CHUNK + 8), :]
                block = pltpu.roll(block, shift_col, 1).reshape(CHUNK // 8 + 1, 8, size)
                block = pltpu.roll(block, lax.rem(8 - rest, 8), 1)
                block = jnp.where(sublane < 8 - rest, block[:-1], block[1:])
                placed[view, part, row : row + CHUNK] = block.reshape(CHUNK, size)


def prepare_call(offsets, counts, probe, intensity, order):
    views, size = intensity.shape[2], probe.shape[1]
    vmem = pl.BlockSpec(memory_space=pltpu.VMEM)
    smem = pl.BlockSpec(memory_space=pltpu.SMEM)
    return pl.pallas_call(
        prepare_kernel,
        out_shape=[
            jax.ShapeDtypeStruct((views, 2, size, size), F32),
            jax.ShapeDtypeStruct((views, 2, size, size // 2), F32),
        ],
        in_specs=[smem, smem, vmem, vmem, vmem],
        out_specs=[vmem] * 2,
        scratch_shapes=[pltpu.VMEM((2, 2 * size + 8, size), F32)],
        compiler_params=pltpu.CompilerParams(vmem_limit_bytes=20 * 1024 * 1024),
        cost_estimate=pl.CostEstimate(flops=2 * 10**9, bytes_accessed=6 * 10**6, transcendentals=0),
    )(offsets, counts, probe, intensity, order)


def views_kernel(chans, offsets, counts, core, placed, amplitude, right, left, a_in, b_in, *rest):
    count = len(chans)
    x_in, ka_in, kb_in = rest[:count], rest[count : 2 * count], rest[2 * count : 3 * count]
    rest = rest[3 * count :]
    g_core, g_a, g_b = rest[:3]
    g_x, g_kb = rest[3 : 3 + count], rest[3 + count : 3 + 2 * count]
    cols_m, rows_m, corner_m, s1, y, s2, z, s3, u, s4, g = rest[3 + 2 * count :]
    views, size = placed.shape[0], core.shape[1]
    half, m = size // 2, MARGIN
    lower = lower_partner()
    low_lanes = lane_ids() < LANES // 2
    zero = jnp.zeros((CHUNK, LANES), F32)

    def unpack(blocks):
        re = im = None
        for channel, block in zip(chans, blocks):
            mine = half_lanes(takes_right(channel))
            re = jnp.where(mine, block, 0.0 if re is None else re)
            im = jnp.where(mine, swap_halves(block), 0.0 if im is None else im)
        return (re, im) if blocks else (zero, zero)

    for row in range(0, size, CHUNK):
        rows = slice(row, row + CHUNK)
        cols_m[0, rows], cols_m[1, rows] = unpack([ref[rows] for ref in x_in])
    corner_a = unpack([ref[...] for ref in ka_in])
    corner_b = unpack([ref[...] for ref in kb_in])
    for part in range(2):
        a_rows, b_rows = a_in[part], b_in[part]
        rows_m[part, :m] = jnp.where(lower, a_rows, b_rows)
        rows_m[part, m:] = jnp.where(lower, b_rows, a_rows)
        corner_m[part, :m] = jnp.where(lower, corner_a[part], corner_b[part])
        corner_m[part, m:] = jnp.where(lower, corner_b[part], corner_a[part])

    def by_right(lhs, t):
        out = dot(lhs[:, :size], right[t, :size]) + dot(lhs[:, size:], right[t, :size])
        return out + dot(lhs[:, :size], right[t, size:])

    def by_left(t, rhs):
        out = dot(left[t, :, :size], rhs[:size]) + dot(left[t, :, :size], rhs[size:])
        return out + dot(left[t, :, size:], rhs[:size])

    def put_below(ref, row, col, value):
        high, low = split(value)
        rows, cols = value.shape
        ref[row : row + rows, col : col + cols] = high
        ref[size + row : size + row + rows, col : col + cols] = low

    def put_beside(ref, row, col, value):
        high, low = split(value)
        rows, cols = value.shape
        ref[row : row + rows, col : col + cols] = high
        ref[row : row + rows, size + col : size + col + cols] = low

    def row_mask(view, row):
        ids = row + lax.broadcasted_iota(jnp.int32, (CHUNK, LANES), 0)
        if row < m:
            return ids < offsets[0, 0, view, 0] - m, row
        if row >= size - m:
            return ids >= size - m + offsets[0, 0, view, 0], row - size + 2 * m
        return None, None

    def col_mask(view, block):
        if block == 0:
            return lane_ids() < offsets[0, 0, view, 1] - m
        return lane_ids() >= m + offsets[0, 0, view, 1]

    def patch(view, row, block):
        cols = slice(block * LANES, (block + 1) * LANES)
        rows = slice(row, row + CHUNK)
        beside = col_mask(view, block)
        beyond, place = row_mask(view, row)
        found = []
        for part in range(2):
            value = jnp.where(beside, cols_m[part, rows], core[part, rows, cols])
            if beyond is not None:
                there = slice(place, place + CHUNK)
                outer = jnp.where(beside, corner_m[part, there], rows_m[part, there, cols])
                value = jnp.where(beyond, outer, value)
            found.append(value)
        return found

    for view in range(views):
        for row in range(0, size, CHUNK):
            rows = slice(row, row + CHUNK)
            waves = []
            for block in range(2):
                cols = slice(block * LANES, (block + 1) * LANES)
                o_re, o_im = patch(view, row, block)
                p_re, p_im = placed[view, 0, rows, cols], placed[view, 1, rows, cols]
                waves.append((p_re * o_re - p_im * o_im, p_re * o_im + p_im * o_re))
            for part in range(2):
                put_beside(s1.at[view, 0], row, part * half, waves[0][part] + waves[1][part])
                put_beside(s1.at[view, 1], row, part * half, waves[0][part] - waves[1][part])
        for odd in range(2):
            y[view, odd] = by_right(s1.at[view, odd], odd)
        for odd in range(2):
            for part in range(2):
                cols = slice(part * half, (part + 1) * half)
                for row in range(0, half, CHUNK):
                    above = y[view, odd, row : row + CHUNK, cols]
                    below = y[view, odd, half + row : half + row + CHUNK, cols]
                    put_below(s2.at[view, 0], part * half + row, odd * half, above + below)
                    put_below(s2.at[view, 1], part * half + row, odd * half, above - below)
        for odd in range(2):
            z[view, odd] = by_left(odd, s2.at[view, odd])
        valid = (view < counts[0, 0]).astype(F32)
        for odd in range(2):
            for row in range(0, half, CHUNK):
                re, im = z[view, odd, row : row + CHUNK], z[view, odd, half + row : half + row + CHUNK]
                taken = pl.ds(2 * row + odd, CHUNK, stride=2)
                wanted = jnp.concatenate([amplitude[view, 0, taken], amplitude[view, 1, taken]], 1)
                scaling = valid - wanted * lax.rsqrt(re * re + im * im + smooth_eps)
                put_below(s3.at[view, odd], row, 0, re * scaling)
                put_below(s3.at[view, odd], half + row, 0, im * scaling)
        for odd in range(2):
            u[view, odd] = by_left(2 + odd, s3.at[view, odd])
        for part in range(2):
            for row in range(0, half, CHUNK):
                rows = slice(part * half + row, part * half + row + CHUNK)
                even_rows, odd_rows = u[view, 0, rows], u[view, 1, rows]
                for value, place in ((even_rows + odd_rows, row), (even_rows - odd_rows, half + row)):
                    put_beside(s4.at[view, 0], place, part * half, value[:, :half])
                    put_beside(s4.at[view, 1], place, part * half, value[:, half:])
        for odd in range(2):
            g[view, odd] = by_right(s4.at[view, odd], 2 + odd)

    for row in range(0, size, CHUNK):
        rows = slice(row, row + CHUNK)
        sums = {}

        def add(key, value):
            sums[key] = sums[key] + value if key in sums else value

        for view in range(views):
            beyond, place = row_mask(view, row)
            halves = []
            for part in range(2):
                cols = slice(part * half, (part + 1) * half)
                even_cols, odd_cols = g[view, 0, rows, cols], g[view, 1, rows, cols]
                halves.append((even_cols + odd_cols, even_cols - odd_cols))
            for block in range(2):
                cols = slice(block * LANES, (block + 1) * LANES)
                beside = col_mask(view, block)
                b_re, b_im = halves[0][block], halves[1][block]
                p_re, p_im = placed[view, 0, rows, cols], placed[view, 1, rows, cols]
                for part, value in enumerate((p_re * b_re + p_im * b_im, p_re * b_im - p_im * b_re)):
                    if beyond is not None:
                        outer, value = jnp.where(beyond, value, zero), jnp.where(beyond, zero, value)
                        add(("corner", part), jnp.where(beside, outer, zero))
                        add(("row", part, block), jnp.where(beside, zero, outer))
                    add(("col", part), jnp.where(beside, value, zero))
                    add(("core", part, block), jnp.where(beside, zero, value))
        for part in range(2):
            cols_m[part, rows] = sums["col", part]
            if place is not None:
                corner_m[part, place : place + CHUNK] = sums["corner", part]
            for block in range(2):
                cols = slice(block * LANES, (block + 1) * LANES)
                g_core[part, rows, cols] = sums["core", part, block]
                if place is not None:
                    rows_m[part, place : place + CHUNK, cols] = sums["row", part, block]

    def packed(channel, re, im):
        to_right = jnp.where(low_lanes, re, swap_halves(im))
        to_left = jnp.where(low_lanes, swap_halves(im), re)
        return jnp.where(sends_right(channel), to_right, to_left)

    for part in range(2):
        bottom, top = rows_m[part, :m], rows_m[part, m:]
        cols = slice(part * size, (part + 1) * size)
        g_a[:, cols] = jnp.where(lower, bottom, top)
        g_b[:, cols] = jnp.where(lower, top, bottom)
    bottom = (corner_m[0, :m], corner_m[1, :m])
    top = (corner_m[0, m:], corner_m[1, m:])
    for number, channel in enumerate(chans):
        for row in range(0, size, CHUNK):
            rows = slice(row, row + CHUNK)
            g_x[number][rows] = packed(channel, cols_m[0, rows], cols_m[1, rows])
        below, above = packed(channel, *bottom), packed(channel, *top)
        place = 2 * size + number * LANES
        g_a[:, place : place + LANES] = jnp.where(lower, below, above)
        g_kb[number][...] = jnp.where(lower, above, below)


def views_call(chans, offsets, counts, core, placed, amplitude, tables, a_in, b_in, x_in, ka_in, kb_in):
    views, size = placed.shape[0], core.shape[1]
    count = len(chans)
    vmem = pl.BlockSpec(memory_space=pltpu.VMEM)
    smem = pl.BlockSpec(memory_space=pltpu.SMEM)
    shapes = [(2, size, size), (MARGIN, 2 * size + count * LANES), (MARGIN, 2 * size)]
    shapes += [(size, LANES)] * count + [(MARGIN, LANES)] * count
    full = pltpu.VMEM((views, 2, size, size), F32)
    tall = pltpu.VMEM((views, 2, 2 * size, size), BF16)
    wide = pltpu.VMEM((views, 2, size, 2 * size), BF16)
    outs = pl.pallas_call(
        functools.partial(views_kernel, chans),
        out_shape=[jax.ShapeDtypeStruct(shape, F32) for shape in shapes],
        in_specs=[smem] * 2 + [vmem] * (7 + 3 * count),
        out_specs=[vmem] * len(shapes),
        scratch_shapes=[
            pltpu.VMEM((2, size, LANES), F32),
            pltpu.VMEM((2, 2 * MARGIN, size), F32),
            pltpu.VMEM((2, 2 * MARGIN, LANES), F32),
            wide, full, tall, full, tall, full, wide, full,
        ],
        compiler_params=pltpu.CompilerParams(vmem_limit_bytes=40 * 1024 * 1024),
    )(offsets, counts, core, placed, amplitude, *tables, a_in, b_in, *x_in, *ka_in, *kb_in)
    return outs[0], outs[1], outs[2], outs[3 : 3 + count], outs[3 + count :]


def finish_kernel(chans, object_ref, g_core, a_in, b_in, *rest):
    count = len(chans)
    x_in, kb_in, out = rest[:count], rest[count : 2 * count], rest[-1]
    size = object_ref.shape[1]
    lower = lower_partner()
    a_start = pl.multiple_of(jnp.where(lower, size - MARGIN, 0), MARGIN)
    b_start = pl.multiple_of(jnp.where(lower, 0, size - MARGIN), MARGIN)
    for part in range(2):
        out[part] = object_ref[part] - step_size * g_core[part]
        cols = slice(part * size, (part + 1) * size)
        out[part, pl.ds(a_start, MARGIN)] -= step_size * a_in[:, cols]
        out[part, pl.ds(b_start, MARGIN)] -= step_size * b_in[:, cols]
    for number, channel in enumerate(chans):
        right = takes_right(channel)
        block = pl.multiple_of(jnp.where(right, size - LANES, 0), LANES)
        mine = ~half_lanes(right) if isinstance(right, bool) else (
            lane_ids() // (LANES // 2) == jnp.where(right, 1, 0)
        )
        edge, corner = x_in[number][...], kb_in[number][...]
        for part in range(2):
            value = edge if part == 0 else swap_halves(edge)
            out[part, :, pl.ds(block, LANES)] -= step_size * jnp.where(mine, value, 0.0)
            value = corner if part == 0 else swap_halves(corner)
            out[part, pl.ds(b_start, MARGIN), pl.ds(block, LANES)] -= step_size * jnp.where(
                mine, value, 0.0
            )


def finish_call(chans, object_field, g_core, a_in, b_in, x_in, kb_in):
    vmem = pl.BlockSpec(memory_space=pltpu.VMEM)
    return pl.pallas_call(
        functools.partial(finish_kernel, chans),
        out_shape=jax.ShapeDtypeStruct(object_field.shape, F32),
        in_specs=[vmem] * (4 + 2 * len(chans)),
        out_specs=vmem,
    )(object_field, g_core, a_in, b_in, *x_in, *kb_in)


def per_device(object_field, probe_field, intensity, view_offsets, view_counts):
    size = object_field.shape[1]
    mesh_rows, mesh_cols = lax.axis_size("row"), lax.axis_size("col")
    chans = channels(mesh_cols)
    by_right, by_left, order = dft_tables(size)
    a_pairs, b_pairs = row_pairs(mesh_rows, 0), row_pairs(mesh_rows, 1)
    lower = lower_partner()

    def swap_a(block):
        return lax.ppermute(block, "row", a_pairs)

    def swap_b(block):
        return lax.ppermute(block, "row", b_pairs)

    def swap_x(block, channel):
        return lax.ppermute(block, "col", channel[0])

    def swap_diagonal(block, channel):
        route = [
            (i * mesh_cols + k, j * mesh_cols + l) for i, j in b_pairs for k, l in channel[0]
        ]
        return lax.ppermute(block, ("row", "col"), route)

    def edge(block):
        return jnp.where(lower, block[size - MARGIN :], block[:MARGIN])

    packs = pack_call(object_field, chans)
    a_send, b_send, x_send, k_send = packs[0], packs[1], packs[2::2], packs[3::2]
    x_in = [swap_x(block, channel) for block, channel in zip(x_send, chans)]
    b_in = swap_b(b_send)
    kb_in = [swap_diagonal(block, channel) for block, channel in zip(k_send, chans)]
    a_in = swap_a(a_send)
    placed, amplitude = prepare_call(view_offsets, view_counts, probe_field, intensity, order)
    ka_in = [swap_a(edge(block)) for block in x_in]
    g_core, g_a, g_b, g_x, g_kb = views_call(
        chans, view_offsets, view_counts, object_field, placed, amplitude,
        (by_right, by_left), a_in, b_in, x_in, ka_in, kb_in,
    )
    a_in = swap_a(g_a)
    b_in = swap_b(g_b)
    x_send = []
    for number, block in enumerate(g_x):
        start = 2 * size + number * LANES
        corner = a_in[:, start : start + LANES]
        none = jnp.zeros((size - MARGIN, LANES), F32)
        placed_corner = jnp.where(
            lower, jnp.concatenate([none, corner]), jnp.concatenate([corner, none])
        )
        x_send.append(block + placed_corner)
    x_in = [swap_x(block, channel) for block, channel in zip(x_send, chans)]
    kb_in = [swap_diagonal(block, channel) for block, channel in zip(g_kb, chans)]
    return finish_call(chans, object_field, g_core, a_in, b_in, x_in, kb_in)


def solution(mesh):
    in_specs = (
        P(None, "row", "col"),
        P(),
        P("row", "col", None, None, None),
        P("row", "col", None, None),
        P("row", "col"),
    )
    out_specs = P(None, "row", "col")
    return jax.shard_map(
        per_device, mesh=mesh, in_specs=in_specs, out_specs=out_specs, check_vma=False
    )
```

profile of v0, /device:TPU:13, one launch (start us, length us, event | category | flops | bytes accessed | tf_op | source)
XLA Modules:
  0.0 40.8 jit_solution(1616692474378696127)
XLA Ops:
  0.0 1.9 %shard_map.83 = (f32[2,64,256]{2,1,0:T(8,128)}, f32[2,64,256]{2,1,0:T(8,128)}, f32[256,128]{1,0:T(8,128)}, f32[64,128]{1,0:T(8,128)}) custom-call(f32[2,256,256]{2,1,0:T(8,128)} %object_ref.3), custom_call_target="tpu_custom_call" | custom-call | tf_op jit(solution)/shard_map/pallas_call | solution.py:128
  1.9 1.2 %collective-permute-start.2 = (f32[256,128]{1,0:T(8,128)}, f32[256,128]{1,0:T(8,128)S(1)}, u32[]{:S(2)}, u32[]{:S(2)}) collective-permute-start(f32[256,128]{1,0:T(8,128)} %get-tuple-element.20), channel_id=1, source_target_pairs={{0,1},{1,0},{2,3},{3,2},{4,5},{5,4},{6,7},{7,6},{8,9},{9,8},{10,11... | collective-permute-start | bytes 393224 | tf_op jit(solution)/shard_map/ppermute | solution.py:444
  3.1 3.9 %collective-permute-start.4 = (f32[64,128]{1,0:T(8,128)}, f32[64,128]{1,0:T(8,128)S(1)}, u32[]{:S(2)}, u32[]{:S(2)}) collective-permute-start(f32[64,128]{1,0:T(8,128)} %get-tuple-element.21), channel_id=1, source_target_pairs={{2,5},{3,4},{6,9},{7,8},{10,13},{11,12},{14,17},{15,16},{18,21},{1... | collective-permute-start | bytes 98312 | tf_op jit(solution)/shard_map/ppermute | solution.py:450
  7.0 0.1 collective-permute-start
  7.1 3.5 %collective-permute-start.1 = (f32[2,64,256]{2,1,0:T(8,128)}, f32[2,64,256]{2,1,0:T(8,128)S(1)}, u32[]{:S(2)}, u32[]{:S(2)}) collective-permute-start(f32[2,64,256]{2,1,0:T(8,128)} %get-tuple-element.19), channel_id=1, source_target_pairs={{2,4},{6,8},{10,12},{14,16},{18,20},{22,24},{26,28},{4,2},{8,6},{1... | collective-permute-start | bytes 393224 | tf_op jit(solution)/shard_map/ppermute | solution.py:441
  11.3 0.8 %copy.10.offsets = s32[1,1,4,2]{3,2,1,0:T(4,128)S(1)} copy(s32[1,1,4,2]{2,3,1,0:T(2,128)} %param.11) | data formatting | bytes 64 | tf_op args[3]
  12.1 0.0 collective-permute-done.2.rest_0_
  12.1 0.0 copy-start
  12.1 0.0 copy-start.1
  12.1 0.0 copy-start.2
  12.1 0.1 collective-permute-start.3
  12.2 0.0 copy-start.4
  12.2 1.4 %copy-done.4 = f32[1,1,4,256,256]{4,3,2,1,0:T(8,128)S(1)} copy-done((f32[1,1,4,256,256]{4,3,2,1,0:T(8,128)S(1)}, f32[1,1,4,256,256]{4,3,2,1,0:T(8,128)}, u32[]{:S(2)}) %copy-start.4) | copy-done | bytes 1048600
  13.6 0.0 copy-start.5
  13.6 1.0 %copy-done.5 = f32[2,256,256]{2,1,0:T(8,128)S(1)} copy-done((f32[2,256,256]{2,1,0:T(8,128)S(1)}, f32[2,256,256]{2,1,0:T(8,128)}, u32[]{:S(2)}) %copy-start.5) | copy-done | bytes 524312
  14.6 0.0 copy-start.6
  14.6 0.9 %copy-done.6 = bf16[256,256]{1,0:T(8,128)(2,1)S(1)} copy-done((bf16[256,256]{1,0:T(8,128)(2,1)S(1)}, bf16[256,256]{1,0:T(8,128)(2,1)}, u32[]{:S(2)}) %copy-start.6) | copy-done | bytes 131096
  15.5 1.7 %shard_map.82 = (f32[4,2,256,256]{3,2,1,0:T(8,128)S(1)}, f32[4,2,256,128]{3,2,1,0:T(8,128)S(1)}) custom-call(s32[1,1,4,2]{3,2,1,0:T(4,128)S(1)} %copy.10.offsets, s32[1,1]{1,0:T(1,128)S(6)} %copy.11.counts, f32[2,256,256]{2,1,0:T(8,128)S(1)} %copy-done.5, f32[1,1,4,256,256]{4,3,2,1,0:T(8,128)S(1)} %copy-done.4, bf16[256,256]{1,0:T(8,128)(2,1)S(1)} %copy-done.6), custom_call_target="tpu_custom_call" | custom-call | flops 2000000000 | bytes 6000000 | tf_op jit(solution)/shard_map/pallas_call | solution.py:167
  17.2 0.0 collective-permute-done.4.rest_2_
  17.2 0.0 collective-permute-done.a_in
  17.2 0.0 collective-permute-done.1.b_in
  17.2 0.0 collective-permute-done.3.rest_1_
  17.3 0.0 copy-done
  17.3 0.0 copy-done.1
  17.3 0.0 copy-done.2
  17.3 7.7 %shard_map.84 = (f32[2,256,256]{2,1,0:T(8,128)S(1)}, f32[64,640]{1,0:T(8,128)S(1)}, f32[64,512]{1,0:T(8,128)S(1)}, f32[256,128]{1,0:T(8,128)S(1)}, f32[64,128]{1,0:T(8,128)S(1)}) custom-call(s32[1,1,4,2]{3,2,1,0:T(4,128)S(1)} %copy.10.offsets, s32[1,1]{1,0:T(1,128)S(6)} %copy.11.counts, f32[2,256,256]{2,1,0:T(8,128)S(1)} %copy-done, ...), custom_call_target="tpu_custom_call" | custom-call | tf_op jit(solution)/shard_map/pallas_call | solution.py:375
  25.0 0.0 copy-start.3
  25.0 0.8 %copy-done.3 = f32[2,256,256]{2,1,0:T(8,128)} copy-done((f32[2,256,256]{2,1,0:T(8,128)}, f32[2,256,256]{2,1,0:T(8,128)S(1)}, u32[]{:S(2)}) %copy-start.3) | copy-done | bytes 524312
  25.8 0.4 collective-permute-start.5
  26.2 3.2 %collective-permute-start.6 = (f32[64,512]{1,0:T(8,128)S(1)}, f32[64,512]{1,0:T(8,128)S(1)}, u32[]{:S(2)}, u32[]{:S(2)}) collective-permute-start(f32[64,512]{1,0:T(8,128)S(1)} %get-tuple-element.24), channel_id=1, source_target_pairs={{2,4},{6,8},{10,12},{14,16},{18,20},{22,24},{26,28},{4,2},{8,6},{1... | collective-permute-start | bytes 393224 | tf_op jit(solution)/shard_map/ppermute | solution.py:441
  29.4 0.0 collective-permute-done.5.a_in
  29.4 0.0 copy-start.7
  29.4 1.3 %collective-permute-start.7 = (f32[256,128]{1,0:T(8,128)S(1)}, f32[256,128]{1,0:T(8,128)S(1)}, u32[]{:S(2)}, u32[]{:S(2)}) collective-permute-start(f32[256,128]{1,0:T(8,128)S(1)} %select_add_fusion), channel_id=1, source_target_pairs={{0,1},{1,0},{2,3},{3,2},{4,5},{5,4},{6,7},{7,6},{8,9},{9,8},{10,11... | collective-permute-start | bytes 393224 | tf_op jit(solution)/shard_map/ppermute | solution.py:444
  30.7 3.5 %collective-permute-start.8 = (f32[64,128]{1,0:T(8,128)S(1)}, f32[64,128]{1,0:T(8,128)S(1)}, u32[]{:S(2)}, u32[]{:S(2)}) collective-permute-start(f32[64,128]{1,0:T(8,128)S(1)} %get-tuple-element.26), channel_id=1, source_target_pairs={{2,5},{3,4},{6,9},{7,8},{10,13},{11,12},{14,17},{15,16},{18,21},{1... | collective-permute-start | bytes 98312 | tf_op jit(solution)/shard_map/ppermute | solution.py:450
  34.2 3.5 %collective-permute-done.8.rest_1_ = f32[64,128]{1,0:T(8,128)S(1)} collective-permute-done((f32[64,128]{1,0:T(8,128)S(1)}, f32[64,128]{1,0:T(8,128)S(1)}, u32[]{:S(2)}, u32[]{:S(2)}) %collective-permute-start.8) | collective-permute-done | bytes 32800 | tf_op jit(solution)/shard_map/ppermute | solution.py:450
  37.7 0.0 copy-start.10
  37.7 0.0 collective-permute-done.6.b_in
  37.7 0.0 copy-start.8
  37.7 0.0 collective-permute-done.7.rest_0_
  37.7 0.0 copy-start.9
  37.8 0.0 copy-done.7
  37.8 0.6 %copy-done.10 = f32[64,128]{1,0:T(8,128)} copy-done((f32[64,128]{1,0:T(8,128)}, f32[64,128]{1,0:T(8,128)S(1)}, u32[]{:S(2)}) %copy-start.10) | copy-done | bytes 32792
  38.3 0.1 copy-done.8
  38.4 0.1 copy-done.9
  38.5 2.4 %shard_map.85 = f32[2,256,256]{2,1,0:T(8,128)} custom-call(f32[2,256,256]{2,1,0:T(8,128)} %object_ref.3, f32[2,256,256]{2,1,0:T(8,128)} %copy-done.3, f32[64,640]{1,0:T(8,128)} %copy-done.7, f32[64,512]{1,0:T(8,128)} %copy-done.8, f32[256,128]{1,0:T(8,128)} %copy-done.9, f32[64,128]{1,0:T(8,128)} %copy-done.10), custom_call_target="tpu_custom_call" | custom-call | tf_op jit(solution)/shard_map/pallas_call | solution.py:421
  (3 shorter events, 0.0 us)
Async XLA Ops:
  1.9 10.2 %collective-permute-start.2 = (f32[256,128]{1,0:T(8,128)}, f32[256,128]{1,0:T(8,128)S(1)}, u32[]{:S(2)}, u32[]{:S(2)}) collective-permute-start(f32[256,128]{1,0:T(8,128)} %get-tuple-element.20), channel_id=1, source_target_pairs={{0,1},{1,0},{2,3},{3,2},{4,5},{5,4},{6,7},{7,6},{8,9},{9,8},{10,11... | collective-permute-start | bytes 393224 | tf_op jit(solution)/shard_map/ppermute | solution.py:444
  3.1 14.1 %collective-permute-start.4 = (f32[64,128]{1,0:T(8,128)}, f32[64,128]{1,0:T(8,128)S(1)}, u32[]{:S(2)}, u32[]{:S(2)}) collective-permute-start(f32[64,128]{1,0:T(8,128)} %get-tuple-element.21), channel_id=1, source_target_pairs={{2,5},{3,4},{6,9},{7,8},{10,13},{11,12},{14,17},{15,16},{18,21},{1... | collective-permute-start | bytes 98312 | tf_op jit(solution)/shard_map/ppermute | solution.py:450
  7.0 10.2 %collective-permute-start = (f32[2,64,256]{2,1,0:T(8,128)}, f32[2,64,256]{2,1,0:T(8,128)S(1)}, u32[]{:S(2)}, u32[]{:S(2)}) collective-permute-start(f32[2,64,256]{2,1,0:T(8,128)} %get-tuple-element.18), channel_id=1, source_target_pairs={{0,2},{4,6},{8,10},{12,14},{16,18},{20,22},{24,26},{28,30},{2,0},{... | collective-permute-start | bytes 393224 | tf_op jit(solution)/shard_map/ppermute | solution.py:438
  7.1 10.1 %collective-permute-start.1 = (f32[2,64,256]{2,1,0:T(8,128)}, f32[2,64,256]{2,1,0:T(8,128)S(1)}, u32[]{:S(2)}, u32[]{:S(2)}) collective-permute-start(f32[2,64,256]{2,1,0:T(8,128)} %get-tuple-element.19), channel_id=1, source_target_pairs={{2,4},{6,8},{10,12},{14,16},{18,20},{22,24},{26,28},{4,2},{8,6},{1... | collective-permute-start | bytes 393224 | tf_op jit(solution)/shard_map/ppermute | solution.py:441
  12.1 5.2 %copy-start = (f32[2,256,256]{2,1,0:T(8,128)S(1)}, f32[2,256,256]{2,1,0:T(8,128)}, u32[]{:S(2)}) copy-start(f32[2,256,256]{2,1,0:T(8,128)} %object_ref.3) | copy-start | bytes 1572868
  12.1 5.2 %copy-start.1 = (bf16[4,256,512]{2,1,0:T(8,128)(2,1)S(1)}, bf16[4,256,512]{2,1,0:T(8,128)(2,1)}, u32[]{:S(2)}) copy-start(bf16[4,256,512]{2,1,0:T(8,128)(2,1)} %constant.22.clone.left) | copy-start | bytes 3145732
  12.1 5.2 %copy-start.2 = (bf16[4,512,256]{2,1,0:T(8,128)(2,1)S(1)}, bf16[4,512,256]{2,1,0:T(8,128)(2,1)}, u32[]{:S(2)}) copy-start(bf16[4,512,256]{2,1,0:T(8,128)(2,1)} %constant.21.clone.right) | copy-start | bytes 3145732
  12.1 5.1 %collective-permute-start.3 = (f32[64,128]{1,0:T(8,128)S(1)}, f32[64,128]{1,0:T(8,128)S(1)}, u32[]{:S(2)}, u32[]{:S(2)}) collective-permute-start(f32[64,128]{1,0:T(8,128)S(1)} %slice_select_fusion), channel_id=1, source_target_pairs={{0,2},{4,6},{8,10},{12,14},{16,18},{20,22},{24,26},{28,30},{2,0},{... | collective-permute-start | bytes 98312 | tf_op jit(solution)/shard_map/ppermute | solution.py:438
  12.2 1.4 %copy-start.4 = (f32[1,1,4,256,256]{4,3,2,1,0:T(8,128)S(1)}, f32[1,1,4,256,256]{4,3,2,1,0:T(8,128)}, u32[]{:S(2)}) copy-start(f32[1,1,4,256,256]{4,3,2,1,0:T(8,128)} %intensity.1) | copy-start | bytes 3145732
  13.6 1.0 %copy-start.5 = (f32[2,256,256]{2,1,0:T(8,128)S(1)}, f32[2,256,256]{2,1,0:T(8,128)}, u32[]{:S(2)}) copy-start(f32[2,256,256]{2,1,0:T(8,128)} %probe.1) | copy-start | bytes 1572868
  14.6 0.9 %copy-start.6 = (bf16[256,256]{1,0:T(8,128)(2,1)S(1)}, bf16[256,256]{1,0:T(8,128)(2,1)}, u32[]{:S(2)}) copy-start(bf16[256,256]{1,0:T(8,128)(2,1)} %constant.20.clone.order) | copy-start | bytes 393220
  25.0 0.8 %copy-start.3 = (f32[2,256,256]{2,1,0:T(8,128)}, f32[2,256,256]{2,1,0:T(8,128)S(1)}, u32[]{:S(2)}) copy-start(f32[2,256,256]{2,1,0:T(8,128)S(1)} %get-tuple-element.22.g_core) | copy-start | bytes 1572868
  25.8 3.5 %collective-permute-start.5 = (f32[64,640]{1,0:T(8,128)S(1)}, f32[64,640]{1,0:T(8,128)S(1)}, u32[]{:S(2)}, u32[]{:S(2)}) collective-permute-start(f32[64,640]{1,0:T(8,128)S(1)} %get-tuple-element.23), channel_id=1, source_target_pairs={{0,2},{4,6},{8,10},{12,14},{16,18},{20,22},{24,26},{28,30},{2,0},{... | collective-permute-start | bytes 491528 | tf_op jit(solution)/shard_map/ppermute | solution.py:438
  26.2 11.5 %collective-permute-start.6 = (f32[64,512]{1,0:T(8,128)S(1)}, f32[64,512]{1,0:T(8,128)S(1)}, u32[]{:S(2)}, u32[]{:S(2)}) collective-permute-start(f32[64,512]{1,0:T(8,128)S(1)} %get-tuple-element.24), channel_id=1, source_target_pairs={{2,4},{6,8},{10,12},{14,16},{18,20},{22,24},{26,28},{4,2},{8,6},{1... | collective-permute-start | bytes 393224 | tf_op jit(solution)/shard_map/ppermute | solution.py:441
  29.4 8.4 %copy-start.7 = (f32[64,640]{1,0:T(8,128)}, f32[64,640]{1,0:T(8,128)S(1)}, u32[]{:S(2)}) copy-start(f32[64,640]{1,0:T(8,128)S(1)} %collective-permute-done.5.a_in) | copy-start | bytes 491524
  29.4 8.3 %collective-permute-start.7 = (f32[256,128]{1,0:T(8,128)S(1)}, f32[256,128]{1,0:T(8,128)S(1)}, u32[]{:S(2)}, u32[]{:S(2)}) collective-permute-start(f32[256,128]{1,0:T(8,128)S(1)} %select_add_fusion), channel_id=1, source_target_pairs={{0,1},{1,0},{2,3},{3,2},{4,5},{5,4},{6,7},{7,6},{8,9},{9,8},{10,11... | collective-permute-start | bytes 393224 | tf_op jit(solution)/shard_map/ppermute | solution.py:444
  30.7 7.0 %collective-permute-start.8 = (f32[64,128]{1,0:T(8,128)S(1)}, f32[64,128]{1,0:T(8,128)S(1)}, u32[]{:S(2)}, u32[]{:S(2)}) collective-permute-start(f32[64,128]{1,0:T(8,128)S(1)} %get-tuple-element.26), channel_id=1, source_target_pairs={{2,5},{3,4},{6,9},{7,8},{10,13},{11,12},{14,17},{15,16},{18,21},{1... | collective-permute-start | bytes 98312 | tf_op jit(solution)/shard_map/ppermute | solution.py:450
  37.7 0.6 %copy-start.10 = (f32[64,128]{1,0:T(8,128)}, f32[64,128]{1,0:T(8,128)S(1)}, u32[]{:S(2)}) copy-start(f32[64,128]{1,0:T(8,128)S(1)} %collective-permute-done.8.rest_1_) | copy-start | bytes 98308
  37.7 0.7 %copy-start.8 = (f32[64,512]{1,0:T(8,128)}, f32[64,512]{1,0:T(8,128)S(1)}, u32[]{:S(2)}) copy-start(f32[64,512]{1,0:T(8,128)S(1)} %collective-permute-done.6.b_in) | copy-start | bytes 393220
  37.7 0.7 %copy-start.9 = (f32[256,128]{1,0:T(8,128)}, f32[256,128]{1,0:T(8,128)S(1)}, u32[]{:S(2)}) copy-start(f32[256,128]{1,0:T(8,128)S(1)} %collective-permute-done.7.rest_0_) | copy-start | bytes 393220
where the time goes:
time: 41.2 us; the launch traced here: 40.8 us
  starting transfers between devices  17.1 us (42%)
  Pallas kernels  13.7 us (33%)
  local copies, waits for them, and re-layouts  5.6 us (14%)
  waiting for transfers between devices  3.52 us (9%)
  between operations  0.88 us (2%)
    pallas_call x1, Pallas kernels, views_call(): pl.pallas_call(functools.partial(views_kernel, chans), out_shape=[jax.Sha...  7.73 us
    ppermute x2, starting transfers between devices, swap_diagonal(): return lax.ppermute(block, ('row', 'col'), route)  7.46 us
    ppermute x2, starting transfers between devices, swap_b(): return lax.ppermute(block, 'row', b_pairs)  6.69 us
    unnamed x23, local copies, waits for them, and re-layouts  5.6 us
    ppermute x2, waiting for transfers between devices, swap_diagonal(): return lax.ppermute(block, ('row', 'col'), route)  3.5 us
    ppermute x2, starting transfers between devices, swap_x(): return lax.ppermute(block, 'col', channel[0])  2.49 us
    pallas_call x1, Pallas kernels, finish_call(): pl.pallas_call(functools.partial(finish_kernel, chans), out_shape=jax.Sha...  2.37 us
    pallas_call x1, Pallas kernels, pack_call(): pl.pallas_call(functools.partial(pack_kernel, chans), out_shape=[jax.Shap...  1.86 us
  transfers between devices with their start and end apart: 9, of which 1 were waited for; matrix products, arithmetic and copies ran while one was open for 2% of the time, Pallas kernels for 4%

commit v1 on v0

--- a/solution.py
+++ b/solution.py
@@ -40,9 +40,7 @@
     even, odd = as_real(even), as_real(odd)
     by_right = [np.concatenate(parts(t), 0) for t in (even, odd, even.T, odd.T)]
     by_left = [np.concatenate(parts(t), 1) for t in (even.T, odd.T, even, odd)]
-    order = np.zeros((length, length))
-    order[np.arange(length), (np.arange(length) % 2) * half + np.arange(length) // 2] = 1.0
-    return np.stack(by_right), np.stack(by_left), order.astype(ml_dtypes.bfloat16)
+    return np.stack(by_right), np.stack(by_left)
 
 
 def channels(mesh_cols):
@@ -57,6 +55,18 @@
 def row_pairs(count, first):
     pairs = [(i, i + 1) for i in range(first, count - 1, 2)]
     return pairs + [(j, i) for i, j in pairs]
+
+
+def spare_route(pairs, mesh_rows, mesh_cols):
+    rows = [i for i in range(mesh_rows) if i not in dict(pairs)]
+    if mesh_cols % 2:
+        return []
+    return [(i * mesh_cols + k, i * mesh_cols + (k ^ 1)) for i in rows for k in range(mesh_cols)]
+
+
+def b_partner():
+    row = lax.axis_index("row")
+    return jnp.where(lower_partner(), row > 0, row < lax.axis_size("row") - 1)
 
 
 def sends_right(channel):
@@ -105,7 +115,7 @@
         b_ref[part] = jnp.where(lower, head, tail)
     for number, channel in enumerate(chans):
         right = sends_right(channel)
-        x_ref, k_ref = edge_refs[2 * number : 2 * number + 2]
+        x_ref, ka_ref, kb_ref = edge_refs[3 * number : 3 * number + 3]
         low = lane_ids() < LANES // 2
         for start in range(0, size, CHUNK):
             rows = slice(start, start + CHUNK)
@@ -118,36 +128,44 @@
                 object_ref[0, rows, size - LANES :],
             )
             x_ref[rows] = jnp.where(right, right_edge, left_edge)
-        k_ref[...] = jnp.where(lower, x_ref[:MARGIN], x_ref[size - MARGIN :])
+        ka_ref[...] = jnp.where(lower, x_ref[size - MARGIN :], x_ref[:MARGIN])
+        kb_ref[...] = jnp.where(lower, x_ref[:MARGIN], x_ref[size - MARGIN :])
 
 
 def pack_call(object_field, chans):
     size = object_field.shape[1]
-    shapes = [(2, MARGIN, size)] * 2 + [(size, LANES), (MARGIN, LANES)] * len(chans)
+    shapes = [(2, MARGIN, size)] * 2 + [(size, LANES), (MARGIN, LANES), (MARGIN, LANES)] * len(chans)
     vmem = pl.BlockSpec(memory_space=pltpu.VMEM)
     return pl.pallas_call(
         functools.partial(pack_kernel, chans),
         out_shape=[jax.ShapeDtypeStruct(shape, F32) for shape in shapes],
         in_specs=[vmem],
         out_specs=[vmem] * len(shapes),
+        compiler_params=pltpu.CompilerParams(vmem_limit_bytes=4 * 1024 * 1024),
     )(object_field)
 
 
-def prepare_kernel(offsets, counts, probe, intensity, order, placed, amplitude, doubled):
-    views, size = intensity.shape[2], probe.shape[1]
+def prepare_kernel(offsets, counts, probe, intensity, placed, amplitude, doubled, measured, sems):
+    views, size = measured.shape[0], probe.shape[1]
     half = size // 2
-    for part in range(2):
-        doubled[part, :size] = probe[part]
-        doubled[part, size : 2 * size] = probe[part]
+    copies = [
+        pltpu.make_async_copy(probe, doubled.at[:, pl.ds(size * i, size)], sems.at[i]) for i in range(2)
+    ]
+    copies += [
+        pltpu.make_async_copy(intensity.at[0, 0, view], measured.at[view], sems.at[2 + view])
+        for view in range(views)
+    ]
+    for copy in copies:
+        copy.start()
+    source = lax.broadcasted_iota(jnp.int32, (size, size), 0)
+    target = lax.broadcasted_iota(jnp.int32, (size, size), 1)
+    order = (target == (source % 2) * half + source // 2).astype(F32).astype(BF16)
     sublane = lax.broadcasted_iota(jnp.int32, (1, 8, 1), 1)
+    copies[0].wait()
+    copies[1].wait()
     for view in range(views):
-        valid = (view < counts[0, 0]).astype(F32)
-        high, low = split(jnp.sqrt(intensity[0, 0, view] + smooth_eps) * valid)
-        ordered = dot(high, order[...]) + dot(low, order[...])
-        amplitude[view, 0] = ordered[:, :half]
-        amplitude[view, 1] = ordered[:, half:]
-        shift_row = lax.rem(offsets[0, 0, view, 0] - MARGIN + size, size)
-        shift_col = lax.rem(offsets[0, 0, view, 1] - MARGIN + size, size)
+        shift_row = lax.rem(offsets[0, 0, 0, view] - MARGIN + size, size)
+        shift_col = lax.rem(offsets[0, 0, 1, view] - MARGIN + size, size)
         start = lax.rem(size - shift_row, size)
         whole = pl.multiple_of((start // 8) * 8, 8)
         rest = start - whole
@@ -158,9 +176,17 @@
                 block = pltpu.roll(block, lax.rem(8 - rest, 8), 1)
                 block = jnp.where(sublane < 8 - rest, block[:-1], block[1:])
                 placed[view, part, row : row + CHUNK] = block.reshape(CHUNK, size)
-
-
-def prepare_call(offsets, counts, probe, intensity, order):
+    for view in range(views):
+        copies[2 + view].wait()
+        valid = (view < counts[0, 0]).astype(F32)
+        power = measured[view] + smooth_eps
+        high, low = split(power * lax.rsqrt(power) * valid)
+        ordered = dot(high, order) + dot(low, order)
+        amplitude[view, 0] = ordered[:, :half]
+        amplitude[view, 1] = ordered[:, half:]
+
+
+def prepare_call(offsets, counts, probe, intensity):
     views, size = intensity.shape[2], probe.shape[1]
     vmem = pl.BlockSpec(memory_space=pltpu.VMEM)
     smem = pl.BlockSpec(memory_space=pltpu.SMEM)
@@ -170,12 +196,16 @@
             jax.ShapeDtypeStruct((views, 2, size, size), F32),
             jax.ShapeDtypeStruct((views, 2, size, size // 2), F32),
         ],
-        in_specs=[smem, smem, vmem, vmem, vmem],
+        in_specs=[smem, smem] + [pl.BlockSpec(memory_space=pl.ANY)] * 2,
         out_specs=[vmem] * 2,
-        scratch_shapes=[pltpu.VMEM((2, 2 * size + 8, size), F32)],
-        compiler_params=pltpu.CompilerParams(vmem_limit_bytes=20 * 1024 * 1024),
+        scratch_shapes=[
+            pltpu.VMEM((2, 2 * size, size), F32),
+            pltpu.VMEM((views, size, size), F32),
+            pltpu.SemaphoreType.DMA((2 + views,)),
+        ],
+        compiler_params=pltpu.CompilerParams(vmem_limit_bytes=16 * 1024 * 1024),
         cost_estimate=pl.CostEstimate(flops=2 * 10**9, bytes_accessed=6 * 10**6, transcendentals=0),
-    )(offsets, counts, probe, intensity, order)
+    )(offsets, counts, probe, intensity)
 
 
 def views_kernel(chans, offsets, counts, core, placed, amplitude, right, left, a_in, b_in, *rest):
@@ -183,11 +213,12 @@
     x_in, ka_in, kb_in = rest[:count], rest[count : 2 * count], rest[2 * count : 3 * count]
     rest = rest[3 * count :]
     g_core, g_a, g_b = rest[:3]
-    g_x, g_kb = rest[3 : 3 + count], rest[3 + count : 3 + 2 * count]
-    cols_m, rows_m, corner_m, s1, y, s2, z, s3, u, s4, g = rest[3 + 2 * count :]
+    g_x, g_ka = rest[3 : 3 + count], rest[3 + count : 3 + 2 * count]
+    g_kb = rest[3 + 2 * count : 3 + 3 * count]
+    cols_m, rows_m, corner_m, s1, y, s2, z, s3, u, s4, g = rest[3 + 3 * count :]
     views, size = placed.shape[0], core.shape[1]
     half, m = size // 2, MARGIN
-    lower = lower_partner()
+    lower, partner = lower_partner(), b_partner()
     low_lanes = lane_ids() < LANES // 2
     zero = jnp.zeros((CHUNK, LANES), F32)
 
@@ -203,9 +234,9 @@
         rows = slice(row, row + CHUNK)
         cols_m[0, rows], cols_m[1, rows] = unpack([ref[rows] for ref in x_in])
     corner_a = unpack([ref[...] for ref in ka_in])
-    corner_b = unpack([ref[...] for ref in kb_in])
+    corner_b = [jnp.where(partner, part, 0.0) for part in unpack([ref[...] for ref in kb_in])]
     for part in range(2):
-        a_rows, b_rows = a_in[part], b_in[part]
+        a_rows, b_rows = a_in[part], jnp.where(partner, b_in[part], 0.0)
         rows_m[part, :m] = jnp.where(lower, a_rows, b_rows)
         rows_m[part, m:] = jnp.where(lower, b_rows, a_rows)
         corner_m[part, :m] = jnp.where(lower, corner_a[part], corner_b[part])
@@ -234,15 +265,15 @@
     def row_mask(view, row):
         ids = row + lax.broadcasted_iota(jnp.int32, (CHUNK, LANES), 0)
         if row < m:
-            return ids < offsets[0, 0, view, 0] - m, row
+            return ids < offsets[0, 0, 0, view] - m, row
         if row >= size - m:
-            return ids >= size - m + offsets[0, 0, view, 0], row - size + 2 * m
+            return ids >= size - m + offsets[0, 0, 0, view], row - size + 2 * m
         return None, None
 
     def col_mask(view, block):
         if block == 0:
-            return lane_ids() < offsets[0, 0, view, 1] - m
-        return lane_ids() >= m + offsets[0, 0, view, 1]
+            return lane_ids() < offsets[0, 0, 1, view] - m
+        return lane_ids() >= m + offsets[0, 0, 1, view]
 
     def patch(view, row, block):
         cols = slice(block * LANES, (block + 1) * LANES)
@@ -347,9 +378,8 @@
 
     for part in range(2):
         bottom, top = rows_m[part, :m], rows_m[part, m:]
-        cols = slice(part * size, (part + 1) * size)
-        g_a[:, cols] = jnp.where(lower, bottom, top)
-        g_b[:, cols] = jnp.where(lower, top, bottom)
+        g_a[part] = jnp.where(lower, bottom, top)
+        g_b[part] = jnp.where(lower, top, bottom)
     bottom = (corner_m[0, :m], corner_m[1, :m])
     top = (corner_m[0, m:], corner_m[1, m:])
     for number, channel in enumerate(chans):
@@ -357,8 +387,7 @@
             rows = slice(row, row + CHUNK)
             g_x[number][rows] = packed(channel, cols_m[0, rows], cols_m[1, rows])
         below, above = packed(channel, *bottom), packed(channel, *top)
-        place = 2 * size + number * LANES
-        g_a[:, place : place + LANES] = jnp.where(lower, below, above)
+        g_ka[number][...] = jnp.where(lower, below, above)
         g_kb[number][...] = jnp.where(lower, above, below)
 
 
@@ -367,8 +396,8 @@
     count = len(chans)
     vmem = pl.BlockSpec(memory_space=pltpu.VMEM)
     smem = pl.BlockSpec(memory_space=pltpu.SMEM)
-    shapes = [(2, size, size), (MARGIN, 2 * size + count * LANES), (MARGIN, 2 * size)]
-    shapes += [(size, LANES)] * count + [(MARGIN, LANES)] * count
+    shapes = [(2, size, size), (2, MARGIN, size), (2, MARGIN, size)]
+    shapes += [(size, LANES)] * count + [(MARGIN, LANES)] * (2 * count)
     full = pltpu.VMEM((views, 2, size, size), F32)
     tall = pltpu.VMEM((views, 2, 2 * size, size), BF16)
     wide = pltpu.VMEM((views, 2, size, 2 * size), BF16)
@@ -385,99 +414,90 @@
         ],
         compiler_params=pltpu.CompilerParams(vmem_limit_bytes=40 * 1024 * 1024),
     )(offsets, counts, core, placed, amplitude, *tables, a_in, b_in, *x_in, *ka_in, *kb_in)
-    return outs[0], outs[1], outs[2], outs[3 : 3 + count], outs[3 + count :]
+    return (*outs[:3], outs[3 : 3 + count], outs[3 + count : 3 + 2 * count], outs[3 + 2 * count :])
 
 
 def finish_kernel(chans, object_ref, g_core, a_in, b_in, *rest):
     count = len(chans)
-    x_in, kb_in, out = rest[:count], rest[count : 2 * count], rest[-1]
+    x_in, ka_in, kb_in = rest[:count], rest[count : 2 * count], rest[2 * count : 3 * count]
+    out = rest[-1]
     size = object_ref.shape[1]
     lower = lower_partner()
-    a_start = pl.multiple_of(jnp.where(lower, size - MARGIN, 0), MARGIN)
-    b_start = pl.multiple_of(jnp.where(lower, 0, size - MARGIN), MARGIN)
+    a_rows = pl.ds(pl.multiple_of(jnp.where(lower, size - MARGIN, 0), MARGIN), MARGIN)
+    b_rows = pl.ds(pl.multiple_of(jnp.where(lower, 0, size - MARGIN), MARGIN), MARGIN)
+    columns = []
+    for channel in chans:
+        right = takes_right(channel)
+        mine = lane_ids() // (LANES // 2) == jnp.where(right, 1, 0)
+        block = pl.multiple_of(jnp.where(right, size - LANES, 0), LANES)
+        columns.append((mine, pl.ds(block, LANES)))
+
+    def take(place, value):
+        out[place] -= step_size * value
+
+    def take_packed(rows, column, block):
+        mine, lanes = column
+        take((0, rows, lanes), jnp.where(mine, block, 0.0))
+        take((1, rows, lanes), jnp.where(mine, swap_halves(block), 0.0))
+
     for part in range(2):
         out[part] = object_ref[part] - step_size * g_core[part]
-        cols = slice(part * size, (part + 1) * size)
-        out[part, pl.ds(a_start, MARGIN)] -= step_size * a_in[:, cols]
-        out[part, pl.ds(b_start, MARGIN)] -= step_size * b_in[:, cols]
-    for number, channel in enumerate(chans):
-        right = takes_right(channel)
-        block = pl.multiple_of(jnp.where(right, size - LANES, 0), LANES)
-        mine = ~half_lanes(right) if isinstance(right, bool) else (
-            lane_ids() // (LANES // 2) == jnp.where(right, 1, 0)
-        )
-        edge, corner = x_in[number][...], kb_in[number][...]
+        take((part, a_rows), a_in[part])
+    for number, column in enumerate(columns):
+        take_packed(slice(None), column, x_in[number][...])
+        take_packed(a_rows, column, ka_in[number][...])
+
+    @pl.when(b_partner())
+    def _():
         for part in range(2):
-            value = edge if part == 0 else swap_halves(edge)
-            out[part, :, pl.ds(block, LANES)] -= step_size * jnp.where(mine, value, 0.0)
-            value = corner if part == 0 else swap_halves(corner)
-            out[part, pl.ds(b_start, MARGIN), pl.ds(block, LANES)] -= step_size * jnp.where(
-                mine, value, 0.0
-            )
-
-
-def finish_call(chans, object_field, g_core, a_in, b_in, x_in, kb_in):
+            take((part, b_rows), b_in[part])
+        for number, column in enumerate(columns):
+            take_packed(b_rows, column, kb_in[number][...])
+
+
+def finish_call(chans, object_field, g_core, a_in, b_in, x_in, ka_in, kb_in):
     vmem = pl.BlockSpec(memory_space=pltpu.VMEM)
     return pl.pallas_call(
         functools.partial(finish_kernel, chans),
         out_shape=jax.ShapeDtypeStruct(object_field.shape, F32),
-        in_specs=[vmem] * (4 + 2 * len(chans)),
+        in_specs=[vmem] * (4 + 3 * len(chans)),
         out_specs=vmem,
-    )(object_field, g_core, a_in, b_in, *x_in, *kb_in)
+        compiler_params=pltpu.CompilerParams(vmem_limit_bytes=6 * 1024 * 1024),
+    )(object_field, g_core, a_in, b_in, *x_in, *ka_in, *kb_in)
 
 
 def per_device(object_field, probe_field, intensity, view_offsets, view_counts):
     size = object_field.shape[1]
     mesh_rows, mesh_cols = lax.axis_size("row"), lax.axis_size("col")
     chans = channels(mesh_cols)
-    by_right, by_left, order = dft_tables(size)
+    tables = dft_tables(size)
     a_pairs, b_pairs = row_pairs(mesh_rows, 0), row_pairs(mesh_rows, 1)
-    lower = lower_partner()
-
-    def swap_a(block):
-        return lax.ppermute(block, "row", a_pairs)
-
-    def swap_b(block):
-        return lax.ppermute(block, "row", b_pairs)
-
-    def swap_x(block, channel):
-        return lax.ppermute(block, "col", channel[0])
-
-    def swap_diagonal(block, channel):
-        route = [
-            (i * mesh_cols + k, j * mesh_cols + l) for i, j in b_pairs for k, l in channel[0]
-        ]
-        return lax.ppermute(block, ("row", "col"), route)
-
-    def edge(block):
-        return jnp.where(lower, block[size - MARGIN :], block[:MARGIN])
+    spare = spare_route(b_pairs, mesh_rows, mesh_cols)
+
+    def over_rows(block, pairs, extra):
+        route = [(i * mesh_cols + k, j * mesh_cols + k) for i, j in pairs for k in range(mesh_cols)]
+        return lax.ppermute(block, ("row", "col"), route + extra)
+
+    def across(block, pairs, extra, channel):
+        route = [(i * mesh_cols + k, j * mesh_cols + l) for i, j in pairs for k, l in channel[0]]
+        return lax.ppermute(block, ("row", "col"), route + (extra if mesh_cols == 2 else []))
+
+    def exchange(a_send, b_send, x_send, ka_send, kb_send):
+        x_in = [lax.ppermute(block, "col", channel[0]) for block, channel in zip(x_send, chans)]
+        b_in = over_rows(b_send, b_pairs, spare)
+        kb_in = [across(block, b_pairs, spare, channel) for block, channel in zip(kb_send, chans)]
+        ka_in = [across(block, a_pairs, [], channel) for block, channel in zip(ka_send, chans)]
+        a_in = over_rows(a_send, a_pairs, [])
+        return a_in, b_in, x_in, ka_in, kb_in
 
     packs = pack_call(object_field, chans)
-    a_send, b_send, x_send, k_send = packs[0], packs[1], packs[2::2], packs[3::2]
-    x_in = [swap_x(block, channel) for block, channel in zip(x_send, chans)]
-    b_in = swap_b(b_send)
-    kb_in = [swap_diagonal(block, channel) for block, channel in zip(k_send, chans)]
-    a_in = swap_a(a_send)
-    placed, amplitude = prepare_call(view_offsets, view_counts, probe_field, intensity, order)
-    ka_in = [swap_a(edge(block)) for block in x_in]
-    g_core, g_a, g_b, g_x, g_kb = views_call(
-        chans, view_offsets, view_counts, object_field, placed, amplitude,
-        (by_right, by_left), a_in, b_in, x_in, ka_in, kb_in,
+    offsets = jnp.swapaxes(view_offsets, 2, 3)
+    margins = exchange(packs[0], packs[1], packs[2::3], packs[3::3], packs[4::3])
+    placed, amplitude = prepare_call(offsets, view_counts, probe_field, intensity)
+    g_core, *sends = views_call(
+        chans, offsets, view_counts, object_field, placed, amplitude, tables, *margins
     )
-    a_in = swap_a(g_a)
-    b_in = swap_b(g_b)
-    x_send = []
-    for number, block in enumerate(g_x):
-        start = 2 * size + number * LANES
-        corner = a_in[:, start : start + LANES]
-        none = jnp.zeros((size - MARGIN, LANES), F32)
-        placed_corner = jnp.where(
-            lower, jnp.concatenate([none, corner]), jnp.concatenate([corner, none])
-        )
-        x_send.append(block + placed_corner)
-    x_in = [swap_x(block, channel) for block, channel in zip(x_send, chans)]
-    kb_in = [swap_diagonal(block, channel) for block, channel in zip(g_kb, chans)]
-    return finish_call(chans, object_field, g_core, a_in, b_in, x_in, kb_in)
+    return finish_call(chans, object_field, g_core, *exchange(*sends))
 
 
 def solution(mesh):

time: 41.2 us -> 33 us (0.80)
  the two profiles are of different devices: /device:TPU:13 before, /device:TPU:0 now
where the time goes in v1:
time: 33 us; the launch traced here: 32.8 us
  Pallas kernels  11.5 us (35%)
  starting transfers between devices  10.6 us (32%)
  waiting for transfers between devices  5.93 us (18%)
  local copies, waits for them, and re-layouts  4 us (12%)
  between operations  0.77 us (2%)
    pallas_call x1, Pallas kernels, views_call(): pl.pallas_call(functools.partial(views_kernel, chans), out_shape=[jax.Sha...  7.7 us
    ppermute x4, waiting for transfers between devices, across(): lax.ppermute(block, ('row', 'col'), route + (extra if mesh_cols == 2 else...  5.92 us
    ppermute x4, starting transfers between devices, across(): lax.ppermute(block, ('row', 'col'), route + (extra if mesh_cols == 2 else...  4.67 us
    unnamed x16, local copies, waits for them, and re-layouts  4 us
    ppermute x4, starting transfers between devices, over_rows(): return lax.ppermute(block, ('row', 'col'), route + extra)  3.99 us
    pallas_call x1, Pallas kernels, prepare_call(): pl.pallas_call(prepare_kernel, out_shape=[jax.ShapeDtypeStruct((views, 2,...  2.62 us
    ppermute x2, starting transfers between devices, exchange(): lax.ppermute(block, 'col', channel[0])  1.92 us
    pallas_call x1, Pallas kernels, finish_call(): pl.pallas_call(functools.partial(finish_kernel, chans), out_shape=jax.Sha...  1.01 us
  transfers between devices with their start and end apart: 10, of which 2 were waited for; matrix products, arithmetic and copies ran while one was open for 0% of the time, Pallas kernels for 8%

profile of v1, /device:TPU:0, one launch (start us, length us, event | category | flops | bytes accessed | tf_op | source)
XLA Modules:
  0.0 32.8 jit_solution(7110587128603943835)
XLA Ops:
  0.0 0.0 copy-start
  0.0 1.0 %copy-done = f32[2,256,256]{2,1,0:T(8,128)S(1)} copy-done((f32[2,256,256]{2,1,0:T(8,128)S(1)}, f32[2,256,256]{2,1,0:T(8,128)}, u32[]{:S(2)}) %copy-start) | copy-done | bytes 524312
  1.0 0.1 shard_map.74
  1.2 2.4 %collective-permute-start.3 = (f32[64,128]{1,0:T(8,128)S(1)}, f32[64,128]{1,0:T(8,128)S(1)}, u32[]{:S(2)}, u32[]{:S(2)}) collective-permute-start(f32[64,128]{1,0:T(8,128)S(1)} %get-tuple-element.23), channel_id=1, source_target_pairs={{0,3},{1,2},{4,7},{5,6},{8,11},{9,10},{12,15},{13,14},{16,19},{17,... | collective-permute-start | bytes 98312 | tf_op jit(solution)/shard_map/ppermute | solution.py:483
  3.6 0.6 %collective-permute-start.4 = (f32[64,128]{1,0:T(8,128)S(1)}, f32[64,128]{1,0:T(8,128)S(1)}, u32[]{:S(2)}, u32[]{:S(2)}) collective-permute-start(f32[64,128]{1,0:T(8,128)S(1)} %get-tuple-element.24), channel_id=1, source_target_pairs={{2,5},{3,4},{6,9},{7,8},{10,13},{11,12},{14,17},{15,16},{18,21},{1... | collective-permute-start | bytes 98312 | tf_op jit(solution)/shard_map/ppermute | solution.py:483
  4.3 1.1 %collective-permute-start = (f32[2,64,256]{2,1,0:T(8,128)S(1)}, f32[2,64,256]{2,1,0:T(8,128)S(1)}, u32[]{:S(2)}, u32[]{:S(2)}) collective-permute-start(f32[2,64,256]{2,1,0:T(8,128)S(1)} %get-tuple-element.20), channel_id=1, source_target_pairs={{0,2},{1,3},{4,6},{5,7},{8,10},{9,11},{12,14},{13,15},{16,18},{17,... | collective-permute-start | bytes 393224 | tf_op jit(solution)/shard_map/ppermute | solution.py:479
  5.3 1.4 %collective-permute-start.1 = (f32[2,64,256]{2,1,0:T(8,128)S(1)}, f32[2,64,256]{2,1,0:T(8,128)S(1)}, u32[]{:S(2)}, u32[]{:S(2)}) collective-permute-start(f32[2,64,256]{2,1,0:T(8,128)S(1)} %get-tuple-element.21), channel_id=1, source_target_pairs={{2,4},{3,5},{6,8},{7,9},{10,12},{11,13},{14,16},{15,17},{18,20},{1... | collective-permute-start | bytes 393224 | tf_op jit(solution)/shard_map/ppermute | solution.py:479
  6.7 0.6 %collective-permute-start.2 = (f32[256,128]{1,0:T(8,128)S(1)}, f32[256,128]{1,0:T(8,128)S(1)}, u32[]{:S(2)}, u32[]{:S(2)}) collective-permute-start(f32[256,128]{1,0:T(8,128)S(1)} %get-tuple-element.22), channel_id=1, source_target_pairs={{0,1},{1,0},{2,3},{3,2},{4,5},{5,4},{6,7},{7,6},{8,9},{9,8},{10,11... | collective-permute-start | bytes 393224 | tf_op jit(solution)/shard_map/ppermute | solution.py:486
  8.0 0.0 copy-start.4
  8.0 0.7 %copy-done.4 = s32[1,1,4,2]{2,3,1,0:T(2,128)S(1)} copy-done((s32[1,1,4,2]{2,3,1,0:T(2,128)S(1)}, s32[1,1,4,2]{2,3,1,0:T(2,128)}, u32[]{:S(2)}) %copy-start.4) | copy-done | bytes 56
  8.7 0.0 copy-start.6
  8.7 1.2 %copy-done.6 = f32[1,1,4,256,256]{4,3,2,1,0:T(8,128)S(1)} copy-done((f32[1,1,4,256,256]{4,3,2,1,0:T(8,128)S(1)}, f32[1,1,4,256,256]{4,3,2,1,0:T(8,128)}, u32[]{:S(2)}) %copy-start.6) | copy-done | bytes 1048600
  9.9 0.0 copy-start.7
  9.9 1.0 %copy-done.7 = f32[2,256,256]{2,1,0:T(8,128)S(1)} copy-done((f32[2,256,256]{2,1,0:T(8,128)S(1)}, f32[2,256,256]{2,1,0:T(8,128)}, u32[]{:S(2)}) %copy-start.7) | copy-done | bytes 524312
  11.0 0.0 copy-start.1
  11.0 0.0 copy-start.2
  11.0 0.0 copy-start.3
  11.0 0.0 copy-start.5
  11.0 2.6 %shard_map.73 = (f32[4,2,256,256]{3,2,1,0:T(8,128)S(1)}, f32[4,2,256,128]{3,2,1,0:T(8,128)S(1)}) custom-call(s32[1,1,2,4]{3,2,1,0:T(2,128)S(1)} %bitcast.1, s32[1,1]{1,0:T(1,128)S(6)} %copy.8.counts, f32[2,256,256]{2,1,0:T(8,128)S(1)} %copy-done.7, f32[1,1,4,256,256]{4,3,2,1,0:T(8,128)S(1)} %copy-done.6), custom_call_target="tpu_custom_call" | custom-call | flops 2000000000 | bytes 6000000 | tf_op jit(solution)/shard_map/pallas_call | solution.py:193
  13.6 0.0 collective-permute-done.3.rest_1_
  13.6 0.0 collective-permute-done.4.rest_2_
  13.6 0.0 collective-permute-done.a_in
  13.6 0.0 collective-permute-done.1.b_in
  13.6 0.0 collective-permute-done.2.rest_0_
  13.7 0.0 copy-done.1
  13.7 0.0 copy-done.2
  13.7 0.0 copy-done.3
  13.7 0.0 copy-done.5
  13.7 7.7 %shard_map.75 = (f32[2,256,256]{2,1,0:T(8,128)S(1)}, f32[2,64,256]{2,1,0:T(8,128)S(1)}, f32[2,64,256]{2,1,0:T(8,128)S(1)}, f32[256,128]{1,0:T(8,128)S(1)}, f32[64,128]{1,0:T(8,128)S(1)}, /*index=5*/f32[64,128]{1,0:T(8,128)S(1)}) custom-call(s32[1,1,2,4]{3,2,1,0:T(2,128)S(1)} %bitcast.2, s32[1,1]{1,0:T(1,128)S(6)} %copy.8.counts, ...), custom_call_target="tpu_custom_call" | custom-call | tf_op jit(solution)/shard_map/pallas_call | solution.py:404
  21.4 0.8 %collective-permute-start.5 = (f32[2,64,256]{2,1,0:T(8,128)S(1)}, f32[2,64,256]{2,1,0:T(8,128)S(1)}, u32[]{:S(2)}, u32[]{:S(2)}) collective-permute-start(f32[2,64,256]{2,1,0:T(8,128)S(1)} %get-tuple-element.26), channel_id=1, source_target_pairs={{0,2},{1,3},{4,6},{5,7},{8,10},{9,11},{12,14},{13,15},{16,18},{17,... | collective-permute-start | bytes 393224 | tf_op jit(solution)/shard_map/ppermute | solution.py:479
  22.2 0.7 %collective-permute-start.6 = (f32[2,64,256]{2,1,0:T(8,128)S(1)}, f32[2,64,256]{2,1,0:T(8,128)S(1)}, u32[]{:S(2)}, u32[]{:S(2)}) collective-permute-start(f32[2,64,256]{2,1,0:T(8,128)S(1)} %get-tuple-element.27), channel_id=1, source_target_pairs={{2,4},{3,5},{6,8},{7,9},{10,12},{11,13},{14,16},{15,17},{18,20},{1... | collective-permute-start | bytes 393224 | tf_op jit(solution)/shard_map/ppermute | solution.py:479
  22.9 1.3 %collective-permute-start.7 = (f32[256,128]{1,0:T(8,128)S(1)}, f32[256,128]{1,0:T(8,128)S(1)}, u32[]{:S(2)}, u32[]{:S(2)}) collective-permute-start(f32[256,128]{1,0:T(8,128)S(1)} %get-tuple-element.28), channel_id=1, source_target_pairs={{0,1},{1,0},{2,3},{3,2},{4,5},{5,4},{6,7},{7,6},{8,9},{9,8},{10,11... | collective-permute-start | bytes 393224 | tf_op jit(solution)/shard_map/ppermute | solution.py:486
  24.2 1.0 %collective-permute-start.8 = (f32[64,128]{1,0:T(8,128)S(1)}, f32[64,128]{1,0:T(8,128)S(1)}, u32[]{:S(2)}, u32[]{:S(2)}) collective-permute-start(f32[64,128]{1,0:T(8,128)S(1)} %get-tuple-element.29), channel_id=1, source_target_pairs={{0,3},{1,2},{4,7},{5,6},{8,11},{9,10},{12,15},{13,14},{16,19},{17,... | collective-permute-start | bytes 98312 | tf_op jit(solution)/shard_map/ppermute | solution.py:483
  25.2 0.6 %collective-permute-start.9 = (f32[64,128]{1,0:T(8,128)S(1)}, f32[64,128]{1,0:T(8,128)S(1)}, u32[]{:S(2)}, u32[]{:S(2)}) collective-permute-start(f32[64,128]{1,0:T(8,128)S(1)} %get-tuple-element.30), channel_id=1, source_target_pairs={{2,5},{3,4},{6,9},{7,8},{10,13},{11,12},{14,17},{15,16},{18,21},{1... | collective-permute-start | bytes 98312 | tf_op jit(solution)/shard_map/ppermute | solution.py:483
  25.8 4.5 %collective-permute-done.8.rest_1_ = f32[64,128]{1,0:T(8,128)S(1)} collective-permute-done((f32[64,128]{1,0:T(8,128)S(1)}, f32[64,128]{1,0:T(8,128)S(1)}, u32[]{:S(2)}, u32[]{:S(2)}) %collective-permute-start.8) | collective-permute-done | bytes 32800 | tf_op jit(solution)/shard_map/ppermute | solution.py:483
  30.3 1.4 %collective-permute-done.9.rest_2_ = f32[64,128]{1,0:T(8,128)S(1)} collective-permute-done((f32[64,128]{1,0:T(8,128)S(1)}, f32[64,128]{1,0:T(8,128)S(1)}, u32[]{:S(2)}, u32[]{:S(2)}) %collective-permute-start.9) | collective-permute-done | bytes 32800 | tf_op jit(solution)/shard_map/ppermute | solution.py:483
  31.7 0.0 collective-permute-done.5.a_in
  31.7 0.0 collective-permute-done.6.b_in
  31.7 0.0 collective-permute-done.7.rest_0_
  31.7 1.0 %shard_map.76 = f32[2,256,256]{2,1,0:T(8,128)} custom-call(f32[2,256,256]{2,1,0:T(8,128)S(1)} %copy-done.1, f32[2,256,256]{2,1,0:T(8,128)S(1)} %get-tuple-element.25.g_core, f32[2,64,256]{2,1,0:T(8,128)S(1)} %collective-permute-done.5.a_in, f32[2,64,256]{2,1,0:T(8,128)S(1)} %collective-permute-done.6.b_in, f32[256,128]{1,0:T(8,128)S(1)} %collective-permute-done.7.rest_0_, ...), custom_call_target="tpu_custom_call" | custom-call | tf_op jit(solution)/shard_map/pallas_call | solution.py:460
Async XLA Ops:
  0.0 1.0 %copy-start = (f32[2,256,256]{2,1,0:T(8,128)S(1)}, f32[2,256,256]{2,1,0:T(8,128)}, u32[]{:S(2)}) copy-start(f32[2,256,256]{2,1,0:T(8,128)} %object_ref.3) | copy-start | bytes 1572868
  1.2 12.4 %collective-permute-start.3 = (f32[64,128]{1,0:T(8,128)S(1)}, f32[64,128]{1,0:T(8,128)S(1)}, u32[]{:S(2)}, u32[]{:S(2)}) collective-permute-start(f32[64,128]{1,0:T(8,128)S(1)} %get-tuple-element.23), channel_id=1, source_target_pairs={{0,3},{1,2},{4,7},{5,6},{8,11},{9,10},{12,15},{13,14},{16,19},{17,... | collective-permute-start | bytes 98312 | tf_op jit(solution)/shard_map/ppermute | solution.py:483
  3.6 10.0 %collective-permute-start.4 = (f32[64,128]{1,0:T(8,128)S(1)}, f32[64,128]{1,0:T(8,128)S(1)}, u32[]{:S(2)}, u32[]{:S(2)}) collective-permute-start(f32[64,128]{1,0:T(8,128)S(1)} %get-tuple-element.24), channel_id=1, source_target_pairs={{2,5},{3,4},{6,9},{7,8},{10,13},{11,12},{14,17},{15,16},{18,21},{1... | collective-permute-start | bytes 98312 | tf_op jit(solution)/shard_map/ppermute | solution.py:483
  4.3 9.4 %collective-permute-start = (f32[2,64,256]{2,1,0:T(8,128)S(1)}, f32[2,64,256]{2,1,0:T(8,128)S(1)}, u32[]{:S(2)}, u32[]{:S(2)}) collective-permute-start(f32[2,64,256]{2,1,0:T(8,128)S(1)} %get-tuple-element.20), channel_id=1, source_target_pairs={{0,2},{1,3},{4,6},{5,7},{8,10},{9,11},{12,14},{13,15},{16,18},{17,... | collective-permute-start | bytes 393224 | tf_op jit(solution)/shard_map/ppermute | solution.py:479
  5.3 8.3 %collective-permute-start.1 = (f32[2,64,256]{2,1,0:T(8,128)S(1)}, f32[2,64,256]{2,1,0:T(8,128)S(1)}, u32[]{:S(2)}, u32[]{:S(2)}) collective-permute-start(f32[2,64,256]{2,1,0:T(8,128)S(1)} %get-tuple-element.21), channel_id=1, source_target_pairs={{2,4},{3,5},{6,8},{7,9},{10,12},{11,13},{14,16},{15,17},{18,20},{1... | collective-permute-start | bytes 393224 | tf_op jit(solution)/shard_map/ppermute | solution.py:479
  6.7 6.9 %collective-permute-start.2 = (f32[256,128]{1,0:T(8,128)S(1)}, f32[256,128]{1,0:T(8,128)S(1)}, u32[]{:S(2)}, u32[]{:S(2)}) collective-permute-start(f32[256,128]{1,0:T(8,128)S(1)} %get-tuple-element.22), channel_id=1, source_target_pairs={{0,1},{1,0},{2,3},{3,2},{4,5},{5,4},{6,7},{7,6},{8,9},{9,8},{10,11... | collective-permute-start | bytes 393224 | tf_op jit(solution)/shard_map/ppermute | solution.py:486
  8.0 0.7 %copy-start.4 = (s32[1,1,4,2]{2,3,1,0:T(2,128)S(1)}, s32[1,1,4,2]{2,3,1,0:T(2,128)}, u32[]{:S(2)}) copy-start(s32[1,1,4,2]{2,3,1,0:T(2,128)} %param.10) | copy-start | bytes 100
  8.7 1.2 %copy-start.6 = (f32[1,1,4,256,256]{4,3,2,1,0:T(8,128)S(1)}, f32[1,1,4,256,256]{4,3,2,1,0:T(8,128)}, u32[]{:S(2)}) copy-start(f32[1,1,4,256,256]{4,3,2,1,0:T(8,128)} %intensity.1) | copy-start | bytes 3145732
  9.9 1.0 %copy-start.7 = (f32[2,256,256]{2,1,0:T(8,128)S(1)}, f32[2,256,256]{2,1,0:T(8,128)}, u32[]{:S(2)}) copy-start(f32[2,256,256]{2,1,0:T(8,128)} %probe.1) | copy-start | bytes 1572868
  11.0 2.7 %copy-start.1 = (f32[2,256,256]{2,1,0:T(8,128)S(1)}, f32[2,256,256]{2,1,0:T(8,128)}, u32[]{:S(2)}) copy-start(f32[2,256,256]{2,1,0:T(8,128)} %object_ref.3) | copy-start | bytes 1572868
  11.0 2.7 %copy-start.2 = (bf16[4,256,512]{2,1,0:T(8,128)(2,1)S(1)}, bf16[4,256,512]{2,1,0:T(8,128)(2,1)}, u32[]{:S(2)}) copy-start(bf16[4,256,512]{2,1,0:T(8,128)(2,1)} %constant.5.clone.left) | copy-start | bytes 3145732
  11.0 2.7 %copy-start.3 = (bf16[4,512,256]{2,1,0:T(8,128)(2,1)S(1)}, bf16[4,512,256]{2,1,0:T(8,128)(2,1)}, u32[]{:S(2)}) copy-start(bf16[4,512,256]{2,1,0:T(8,128)(2,1)} %constant.4.clone.right) | copy-start | bytes 3145732
  11.0 2.7 %copy-start.5 = (s32[1,1,4,2]{2,3,1,0:T(2,128)S(1)}, s32[1,1,4,2]{2,3,1,0:T(2,128)}, u32[]{:S(2)}) copy-start(s32[1,1,4,2]{2,3,1,0:T(2,128)} %param.10) | copy-start | bytes 100
  21.4 10.3 %collective-permute-start.5 = (f32[2,64,256]{2,1,0:T(8,128)S(1)}, f32[2,64,256]{2,1,0:T(8,128)S(1)}, u32[]{:S(2)}, u32[]{:S(2)}) collective-permute-start(f32[2,64,256]{2,1,0:T(8,128)S(1)} %get-tuple-element.26), channel_id=1, source_target_pairs={{0,2},{1,3},{4,6},{5,7},{8,10},{9,11},{12,14},{13,15},{16,18},{17,... | collective-permute-start | bytes 393224 | tf_op jit(solution)/shard_map/ppermute | solution.py:479
  22.2 9.5 %collective-permute-start.6 = (f32[2,64,256]{2,1,0:T(8,128)S(1)}, f32[2,64,256]{2,1,0:T(8,128)S(1)}, u32[]{:S(2)}, u32[]{:S(2)}) collective-permute-start(f32[2,64,256]{2,1,0:T(8,128)S(1)} %get-tuple-element.27), channel_id=1, source_target_pairs={{2,4},{3,5},{6,8},{7,9},{10,12},{11,13},{14,16},{15,17},{18,20},{1... | collective-permute-start | bytes 393224 | tf_op jit(solution)/shard_map/ppermute | solution.py:479
  22.9 8.8 %collective-permute-start.7 = (f32[256,128]{1,0:T(8,128)S(1)}, f32[256,128]{1,0:T(8,128)S(1)}, u32[]{:S(2)}, u32[]{:S(2)}) collective-permute-start(f32[256,128]{1,0:T(8,128)S(1)} %get-tuple-element.28), channel_id=1, source_target_pairs={{0,1},{1,0},{2,3},{3,2},{4,5},{5,4},{6,7},{7,6},{8,9},{9,8},{10,11... | collective-permute-start | bytes 393224 | tf_op jit(solution)/shard_map/ppermute | solution.py:486
  24.2 6.1 %collective-permute-start.8 = (f32[64,128]{1,0:T(8,128)S(1)}, f32[64,128]{1,0:T(8,128)S(1)}, u32[]{:S(2)}, u32[]{:S(2)}) collective-permute-start(f32[64,128]{1,0:T(8,128)S(1)} %get-tuple-element.29), channel_id=1, source_target_pairs={{0,3},{1,2},{4,7},{5,6},{8,11},{9,10},{12,15},{13,14},{16,19},{17,... | collective-permute-start | bytes 98312 | tf_op jit(solution)/shard_map/ppermute | solution.py:483
  25.2 6.5 %collective-permute-start.9 = (f32[64,128]{1,0:T(8,128)S(1)}, f32[64,128]{1,0:T(8,128)S(1)}, u32[]{:S(2)}, u32[]{:S(2)}) collective-permute-start(f32[64,128]{1,0:T(8,128)S(1)} %get-tuple-element.30), channel_id=1, source_target_pairs={{2,5},{3,4},{6,9},{7,8},{10,13},{11,12},{14,17},{15,16},{18,21},{1... | collective-permute-start | bytes 98312 | tf_op jit(solution)/shard_map/ppermute | solution.py:483

commit v2 on v1

--- a/solution.py
+++ b/solution.py
@@ -1,4 +1,5 @@
 import functools
+import itertools
 import math
 
 import jax
@@ -13,6 +14,7 @@
 MARGIN = 64
 LANES = 128
 CHUNK = 64
+STAGGER = 4
 
 smooth_eps = 0.1
 step_size = 0.2
@@ -103,6 +105,13 @@
 
 def swap_halves(block):
     return pltpu.roll(block, LANES // 2, 1)
+
+
+def fetch(pairs, sems):
+    copies = [pltpu.make_async_copy(source, target, sems.at[i]) for i, (source, target) in enumerate(pairs)]
+    for copy in copies:
+        copy.start()
+    return copies
 
 
 def pack_kernel(chans, object_ref, a_ref, b_ref, *edge_refs):
@@ -145,24 +154,23 @@
     )(object_field)
 
 
-def prepare_kernel(offsets, counts, probe, intensity, placed, amplitude, doubled, measured, sems):
+def prepare_kernel(
+    offsets_in, counts_in, probe, intensity, placed, amplitude, offsets, counts, doubled, measured, sems
+):
     views, size = measured.shape[0], probe.shape[1]
     half = size // 2
-    copies = [
-        pltpu.make_async_copy(probe, doubled.at[:, pl.ds(size * i, size)], sems.at[i]) for i in range(2)
-    ]
-    copies += [
-        pltpu.make_async_copy(intensity.at[0, 0, view], measured.at[view], sems.at[2 + view])
-        for view in range(views)
-    ]
-    for copy in copies:
-        copy.start()
+    copies = fetch(
+        [(offsets_in, offsets), (counts_in, counts)]
+        + [(probe, doubled.at[:, pl.ds(size * i, size)]) for i in range(2)]
+        + [(intensity.at[0, 0, view], measured.at[view]) for view in range(views)],
+        sems,
+    )
     source = lax.broadcasted_iota(jnp.int32, (size, size), 0)
     target = lax.broadcasted_iota(jnp.int32, (size, size), 1)
     order = (target == (source % 2) * half + source // 2).astype(F32).astype(BF16)
     sublane = lax.broadcasted_iota(jnp.int32, (1, 8, 1), 1)
-    copies[0].wait()
-    copies[1].wait()
+    for copy in copies[:4]:
+        copy.wait()
     for view in range(views):
         shift_row = lax.rem(offsets[0, 0, 0, view] - MARGIN + size, size)
         shift_col = lax.rem(offsets[0, 0, 1, view] - MARGIN + size, size)
@@ -177,7 +185,7 @@
                 block = jnp.where(sublane < 8 - rest, block[:-1], block[1:])
                 placed[view, part, row : row + CHUNK] = block.reshape(CHUNK, size)
     for view in range(views):
-        copies[2 + view].wait()
+        copies[4 + view].wait()
         valid = (view < counts[0, 0]).astype(F32)
         power = measured[view] + smooth_eps
         high, low = split(power * lax.rsqrt(power) * valid)
@@ -189,33 +197,35 @@
 def prepare_call(offsets, counts, probe, intensity):
     views, size = intensity.shape[2], probe.shape[1]
     vmem = pl.BlockSpec(memory_space=pltpu.VMEM)
-    smem = pl.BlockSpec(memory_space=pltpu.SMEM)
     return pl.pallas_call(
         prepare_kernel,
         out_shape=[
             jax.ShapeDtypeStruct((views, 2, size, size), F32),
             jax.ShapeDtypeStruct((views, 2, size, size // 2), F32),
         ],
-        in_specs=[smem, smem] + [pl.BlockSpec(memory_space=pl.ANY)] * 2,
+        in_specs=[pl.BlockSpec(memory_space=pltpu.HBM)] * 4,
         out_specs=[vmem] * 2,
         scratch_shapes=[
+            pltpu.SMEM(offsets.shape, jnp.int32),
+            pltpu.SMEM(counts.shape, jnp.int32),
             pltpu.VMEM((2, 2 * size, size), F32),
             pltpu.VMEM((views, size, size), F32),
-            pltpu.SemaphoreType.DMA((2 + views,)),
+            pltpu.SemaphoreType.DMA((4 + views,)),
         ],
         compiler_params=pltpu.CompilerParams(vmem_limit_bytes=16 * 1024 * 1024),
         cost_estimate=pl.CostEstimate(flops=2 * 10**9, bytes_accessed=6 * 10**6, transcendentals=0),
     )(offsets, counts, probe, intensity)
 
 
-def views_kernel(chans, offsets, counts, core, placed, amplitude, right, left, a_in, b_in, *rest):
+def views_kernel(chans, offsets_in, counts_in, core, placed, amplitude, right, left, a_in, b_in, *rest):
     count = len(chans)
     x_in, ka_in, kb_in = rest[:count], rest[count : 2 * count], rest[2 * count : 3 * count]
     rest = rest[3 * count :]
     g_core, g_a, g_b = rest[:3]
     g_x, g_ka = rest[3 : 3 + count], rest[3 + count : 3 + 2 * count]
     g_kb = rest[3 + 2 * count : 3 + 3 * count]
-    cols_m, rows_m, corner_m, s1, y, s2, z, s3, u, s4, g = rest[3 + 3 * count :]
+    offsets, counts, sems, cols_m, rows_m, corner_m, s1, y, s2, z, s3, u, s4, g = rest[3 + 3 * count :]
+    copies = fetch([(offsets_in, offsets), (counts_in, counts)], sems)
     views, size = placed.shape[0], core.shape[1]
     half, m = size // 2, MARGIN
     lower, partner = lower_partner(), b_partner()
@@ -228,11 +238,11 @@
             mine = half_lanes(takes_right(channel))
             re = jnp.where(mine, block, 0.0 if re is None else re)
             im = jnp.where(mine, swap_halves(block), 0.0 if im is None else im)
-        return (re, im) if blocks else (zero, zero)
+        return (re, im) if blocks else (jnp.zeros((MARGIN, LANES), F32),) * 2
 
     for row in range(0, size, CHUNK):
         rows = slice(row, row + CHUNK)
-        cols_m[0, rows], cols_m[1, rows] = unpack([ref[rows] for ref in x_in])
+        cols_m[0, rows], cols_m[1, rows] = unpack([ref[rows] for ref in x_in]) if chans else (zero, zero)
     corner_a = unpack([ref[...] for ref in ka_in])
     corner_b = [jnp.where(partner, part, 0.0) for part in unpack([ref[...] for ref in kb_in])]
     for part in range(2):
@@ -241,6 +251,9 @@
         rows_m[part, m:] = jnp.where(lower, b_rows, a_rows)
         corner_m[part, :m] = jnp.where(lower, corner_a[part], corner_b[part])
         corner_m[part, m:] = jnp.where(lower, corner_b[part], corner_a[part])
+
+    for copy in copies:
+        copy.wait()
 
     def by_right(lhs, t):
         out = dot(lhs[:, :size], right[t, :size]) + dot(lhs[:, size:], right[t, :size])
@@ -290,7 +303,7 @@
             found.append(value)
         return found
 
-    for view in range(views):
+    def steps(view):
         for row in range(0, size, CHUNK):
             rows = slice(row, row + CHUNK)
             waves = []
@@ -302,18 +315,22 @@
             for part in range(2):
                 put_beside(s1.at[view, 0], row, part * half, waves[0][part] + waves[1][part])
                 put_beside(s1.at[view, 1], row, part * half, waves[0][part] - waves[1][part])
+            yield
         for odd in range(2):
             y[view, odd] = by_right(s1.at[view, odd], odd)
+            yield
         for odd in range(2):
-            for part in range(2):
-                cols = slice(part * half, (part + 1) * half)
-                for row in range(0, half, CHUNK):
+            for row in range(0, half, CHUNK):
+                for part in range(2):
+                    cols = slice(part * half, (part + 1) * half)
                     above = y[view, odd, row : row + CHUNK, cols]
                     below = y[view, odd, half + row : half + row + CHUNK, cols]
                     put_below(s2.at[view, 0], part * half + row, odd * half, above + below)
                     put_below(s2.at[view, 1], part * half + row, odd * half, above - below)
+                yield
         for odd in range(2):
             z[view, odd] = by_left(odd, s2.at[view, odd])
+            yield
         valid = (view < counts[0, 0]).astype(F32)
         for odd in range(2):
             for row in range(0, half, CHUNK):
@@ -323,17 +340,28 @@
                 scaling = valid - wanted * lax.rsqrt(re * re + im * im + smooth_eps)
                 put_below(s3.at[view, odd], row, 0, re * scaling)
                 put_below(s3.at[view, odd], half + row, 0, im * scaling)
+                yield
         for odd in range(2):
             u[view, odd] = by_left(2 + odd, s3.at[view, odd])
-        for part in range(2):
-            for row in range(0, half, CHUNK):
+            yield
+        for row in range(0, half, CHUNK):
+            for part in range(2):
                 rows = slice(part * half + row, part * half + row + CHUNK)
                 even_rows, odd_rows = u[view, 0, rows], u[view, 1, rows]
                 for value, place in ((even_rows + odd_rows, row), (even_rows - odd_rows, half + row)):
                     put_beside(s4.at[view, 0], place, part * half, value[:, :half])
                     put_beside(s4.at[view, 1], place, part * half, value[:, half:])
+                yield
         for odd in range(2):
             g[view, odd] = by_right(s4.at[view, odd], 2 + odd)
+            yield
+
+    work = [steps(view) for view in range(views)]
+    for view in range(views):
+        for _ in range(view * STAGGER):
+            work[view] = itertools.chain([None], work[view])
+    for _ in itertools.zip_longest(*work):
+        pass
 
     for row in range(0, size, CHUNK):
         rows = slice(row, row + CHUNK)
@@ -395,7 +423,6 @@
     views, size = placed.shape[0], core.shape[1]
     count = len(chans)
     vmem = pl.BlockSpec(memory_space=pltpu.VMEM)
-    smem = pl.BlockSpec(memory_space=pltpu.SMEM)
     shapes = [(2, size, size), (2, MARGIN, size), (2, MARGIN, size)]
     shapes += [(size, LANES)] * count + [(MARGIN, LANES)] * (2 * count)
     full = pltpu.VMEM((views, 2, size, size), F32)
@@ -404,9 +431,12 @@
     outs = pl.pallas_call(
         functools.partial(views_kernel, chans),
         out_shape=[jax.ShapeDtypeStruct(shape, F32) for shape in shapes],
-        in_specs=[smem] * 2 + [vmem] * (7 + 3 * count),
+        in_specs=[pl.BlockSpec(memory_space=pltpu.HBM)] * 2 + [vmem] * (7 + 3 * count),
         out_specs=[vmem] * len(shapes),
         scratch_shapes=[
+            pltpu.SMEM(offsets.shape, jnp.int32),
+            pltpu.SMEM(counts.shape, jnp.int32),
+            pltpu.SemaphoreType.DMA((2,)),
             pltpu.VMEM((2, size, LANES), F32),
             pltpu.VMEM((2, 2 * MARGIN, size), F32),
             pltpu.VMEM((2, 2 * MARGIN, LANES), F32),

time: 33 us -> 30.7 us (0.930)
  Pallas kernels: 11.5 us -> 9.16 us
    pallas_call x1, Pallas kernels: 7.7 us -> 5.55 us  [views_call(): pl.pallas_call(functools.partial(views_kernel, chans), out_shape=[jax.Sha...]
where the time goes in v2:
time: 30.7 us; the launch traced here: 30.4 us
  starting transfers between devices  10.6 us (35%)
  Pallas kernels  9.16 us (30%)
  waiting for transfers between devices  5.93 us (19%)
  local copies, waits for them, and re-layouts  4 us (13%)
  between operations  0.77 us (3%)
    ppermute x4, waiting for transfers between devices, across(): lax.ppermute(block, ('row', 'col'), route + (extra if mesh_cols == 2 else...  5.91 us
    pallas_call x1, Pallas kernels, views_call(): pl.pallas_call(functools.partial(views_kernel, chans), out_shape=[jax.Sha...  5.55 us
    ppermute x4, starting transfers between devices, across(): lax.ppermute(block, ('row', 'col'), route + (extra if mesh_cols == 2 else...  4.68 us
    unnamed x16, local copies, waits for them, and re-layouts  4 us
    ppermute x4, starting transfers between devices, over_rows(): return lax.ppermute(block, ('row', 'col'), route + extra)  3.99 us
    pallas_call x1, Pallas kernels, prepare_call(): pl.pallas_call(prepare_kernel, out_shape=[jax.ShapeDtypeStruct((views, 2,...  2.46 us
    ppermute x2, starting transfers between devices, exchange(): lax.ppermute(block, 'col', channel[0])  1.91 us
    pallas_call x1, Pallas kernels, finish_call(): pl.pallas_call(functools.partial(finish_kernel, chans), out_shape=jax.Sha...  1.01 us
  transfers between devices with their start and end apart: 10, of which 2 were waited for; matrix products, arithmetic and copies ran while one was open for 0% of the time, Pallas kernels for 8%

profile of v2, /device:TPU:0, one launch (start us, length us, event | category | flops | bytes accessed | tf_op | source)
XLA Modules:
  0.0 30.4 jit_solution(6521139647918556880)
XLA Ops:
  0.0 0.0 copy-start
  0.0 1.0 %copy-done = f32[2,256,256]{2,1,0:T(8,128)S(1)} copy-done((f32[2,256,256]{2,1,0:T(8,128)S(1)}, f32[2,256,256]{2,1,0:T(8,128)}, u32[]{:S(2)}) %copy-start) | copy-done | bytes 524312
  1.0 0.1 shard_map.74
  1.2 2.4 %collective-permute-start.3 = (f32[64,128]{1,0:T(8,128)S(1)}, f32[64,128]{1,0:T(8,128)S(1)}, u32[]{:S(2)}, u32[]{:S(2)}) collective-permute-start(f32[64,128]{1,0:T(8,128)S(1)} %get-tuple-element.23), channel_id=1, source_target_pairs={{0,3},{1,2},{4,7},{5,6},{8,11},{9,10},{12,15},{13,14},{16,19},{17,... | collective-permute-start | bytes 98312 | tf_op jit(solution)/shard_map/ppermute | solution.py:513
  3.6 0.6 %collective-permute-start.4 = (f32[64,128]{1,0:T(8,128)S(1)}, f32[64,128]{1,0:T(8,128)S(1)}, u32[]{:S(2)}, u32[]{:S(2)}) collective-permute-start(f32[64,128]{1,0:T(8,128)S(1)} %get-tuple-element.24), channel_id=1, source_target_pairs={{2,5},{3,4},{6,9},{7,8},{10,13},{11,12},{14,17},{15,16},{18,21},{1... | collective-permute-start | bytes 98312 | tf_op jit(solution)/shard_map/ppermute | solution.py:513
  4.3 1.1 %collective-permute-start = (f32[2,64,256]{2,1,0:T(8,128)S(1)}, f32[2,64,256]{2,1,0:T(8,128)S(1)}, u32[]{:S(2)}, u32[]{:S(2)}) collective-permute-start(f32[2,64,256]{2,1,0:T(8,128)S(1)} %get-tuple-element.20), channel_id=1, source_target_pairs={{0,2},{1,3},{4,6},{5,7},{8,10},{9,11},{12,14},{13,15},{16,18},{17,... | collective-permute-start | bytes 393224 | tf_op jit(solution)/shard_map/ppermute | solution.py:509
  5.3 1.4 %collective-permute-start.1 = (f32[2,64,256]{2,1,0:T(8,128)S(1)}, f32[2,64,256]{2,1,0:T(8,128)S(1)}, u32[]{:S(2)}, u32[]{:S(2)}) collective-permute-start(f32[2,64,256]{2,1,0:T(8,128)S(1)} %get-tuple-element.21), channel_id=1, source_target_pairs={{2,4},{3,5},{6,8},{7,9},{10,12},{11,13},{14,16},{15,17},{18,20},{1... | collective-permute-start | bytes 393224 | tf_op jit(solution)/shard_map/ppermute | solution.py:509
  6.7 0.6 %collective-permute-start.2 = (f32[256,128]{1,0:T(8,128)S(1)}, f32[256,128]{1,0:T(8,128)S(1)}, u32[]{:S(2)}, u32[]{:S(2)}) collective-permute-start(f32[256,128]{1,0:T(8,128)S(1)} %get-tuple-element.22), channel_id=1, source_target_pairs={{0,1},{1,0},{2,3},{3,2},{4,5},{5,4},{6,7},{7,6},{8,9},{9,8},{10,11... | collective-permute-start | bytes 393224 | tf_op jit(solution)/shard_map/ppermute | solution.py:516
  8.0 0.0 copy-start.4
  8.0 0.7 %copy-done.4 = s32[1,1,4,2]{2,3,1,0:T(2,128)S(1)} copy-done((s32[1,1,4,2]{2,3,1,0:T(2,128)S(1)}, s32[1,1,4,2]{2,3,1,0:T(2,128)}, u32[]{:S(2)}) %copy-start.4) | copy-done | bytes 56
  8.7 0.0 copy-start.6
  8.7 1.2 %copy-done.6 = f32[1,1,4,256,256]{4,3,2,1,0:T(8,128)S(1)} copy-done((f32[1,1,4,256,256]{4,3,2,1,0:T(8,128)S(1)}, f32[1,1,4,256,256]{4,3,2,1,0:T(8,128)}, u32[]{:S(2)}) %copy-start.6) | copy-done | bytes 1048600
  9.9 0.0 copy-start.7
  9.9 1.0 %copy-done.7 = f32[2,256,256]{2,1,0:T(8,128)S(1)} copy-done((f32[2,256,256]{2,1,0:T(8,128)S(1)}, f32[2,256,256]{2,1,0:T(8,128)}, u32[]{:S(2)}) %copy-start.7) | copy-done | bytes 524312
  11.0 0.0 copy-start.1
  11.0 0.0 copy-start.2
  11.0 0.0 copy-start.3
  11.0 0.0 copy-start.5
  11.0 2.5 %shard_map.73 = (f32[4,2,256,256]{3,2,1,0:T(8,128)S(1)}, f32[4,2,256,128]{3,2,1,0:T(8,128)S(1)}) custom-call(s32[1,1,2,4]{3,2,1,0:T(2,128)S(1)} %bitcast.1, s32[1,1]{1,0:T(1,128)S(6)} %copy.8.counts_in, f32[2,256,256]{2,1,0:T(8,128)S(1)} %copy-done.7, f32[1,1,4,256,256]{4,3,2,1,0:T(8,128)S(1)} %copy-done.6), custom_call_target="tpu_custom_call" | custom-call | flops 2000000000 | bytes 6000000 | tf_op jit(solution)/shard_map/pallas_call | solution.py:200
  13.4 0.0 collective-permute-done.3.rest_1_
  13.5 0.0 collective-permute-done.4.rest_2_
  13.5 0.0 collective-permute-done.a_in
  13.5 0.0 collective-permute-done.1.b_in
  13.5 0.0 collective-permute-done.2.rest_0_
  13.5 0.0 copy-done.1
  13.5 0.0 copy-done.2
  13.5 0.0 copy-done.3
  13.5 0.0 copy-done.5
  13.5 5.6 %shard_map.75 = (f32[2,256,256]{2,1,0:T(8,128)S(1)}, f32[2,64,256]{2,1,0:T(8,128)S(1)}, f32[2,64,256]{2,1,0:T(8,128)S(1)}, f32[256,128]{1,0:T(8,128)S(1)}, f32[64,128]{1,0:T(8,128)S(1)}, /*index=5*/f32[64,128]{1,0:T(8,128)S(1)}) custom-call(s32[1,1,2,4]{3,2,1,0:T(2,128)S(1)} %bitcast.2, s32[1,1]{1,0:T(1,128)S(6)} %copy.8.counts_in, ...), custom_call_target="tpu_custom_call" | custom-call | tf_op jit(solution)/shard_map/pallas_call | solution.py:431
  19.1 0.8 %collective-permute-start.5 = (f32[2,64,256]{2,1,0:T(8,128)S(1)}, f32[2,64,256]{2,1,0:T(8,128)S(1)}, u32[]{:S(2)}, u32[]{:S(2)}) collective-permute-start(f32[2,64,256]{2,1,0:T(8,128)S(1)} %get-tuple-element.26), channel_id=1, source_target_pairs={{0,2},{1,3},{4,6},{5,7},{8,10},{9,11},{12,14},{13,15},{16,18},{17,... | collective-permute-start | bytes 393224 | tf_op jit(solution)/shard_map/ppermute | solution.py:509
  19.9 0.8 %collective-permute-start.6 = (f32[2,64,256]{2,1,0:T(8,128)S(1)}, f32[2,64,256]{2,1,0:T(8,128)S(1)}, u32[]{:S(2)}, u32[]{:S(2)}) collective-permute-start(f32[2,64,256]{2,1,0:T(8,128)S(1)} %get-tuple-element.27), channel_id=1, source_target_pairs={{2,4},{3,5},{6,8},{7,9},{10,12},{11,13},{14,16},{15,17},{18,20},{1... | collective-permute-start | bytes 393224 | tf_op jit(solution)/shard_map/ppermute | solution.py:509
  20.6 1.3 %collective-permute-start.7 = (f32[256,128]{1,0:T(8,128)S(1)}, f32[256,128]{1,0:T(8,128)S(1)}, u32[]{:S(2)}, u32[]{:S(2)}) collective-permute-start(f32[256,128]{1,0:T(8,128)S(1)} %get-tuple-element.28), channel_id=1, source_target_pairs={{0,1},{1,0},{2,3},{3,2},{4,5},{5,4},{6,7},{7,6},{8,9},{9,8},{10,11... | collective-permute-start | bytes 393224 | tf_op jit(solution)/shard_map/ppermute | solution.py:516
  21.9 1.0 %collective-permute-start.8 = (f32[64,128]{1,0:T(8,128)S(1)}, f32[64,128]{1,0:T(8,128)S(1)}, u32[]{:S(2)}, u32[]{:S(2)}) collective-permute-start(f32[64,128]{1,0:T(8,128)S(1)} %get-tuple-element.29), channel_id=1, source_target_pairs={{0,3},{1,2},{4,7},{5,6},{8,11},{9,10},{12,15},{13,14},{16,19},{17,... | collective-permute-start | bytes 98312 | tf_op jit(solution)/shard_map/ppermute | solution.py:513
  22.9 0.6 %collective-permute-start.9 = (f32[64,128]{1,0:T(8,128)S(1)}, f32[64,128]{1,0:T(8,128)S(1)}, u32[]{:S(2)}, u32[]{:S(2)}) collective-permute-start(f32[64,128]{1,0:T(8,128)S(1)} %get-tuple-element.30), channel_id=1, source_target_pairs={{2,5},{3,4},{6,9},{7,8},{10,13},{11,12},{14,17},{15,16},{18,21},{1... | collective-permute-start | bytes 98312 | tf_op jit(solution)/shard_map/ppermute | solution.py:513
  23.5 4.5 %collective-permute-done.8.rest_1_ = f32[64,128]{1,0:T(8,128)S(1)} collective-permute-done((f32[64,128]{1,0:T(8,128)S(1)}, f32[64,128]{1,0:T(8,128)S(1)}, u32[]{:S(2)}, u32[]{:S(2)}) %collective-permute-start.8) | collective-permute-done | bytes 32800 | tf_op jit(solution)/shard_map/ppermute | solution.py:513
  28.0 1.4 %collective-permute-done.9.rest_2_ = f32[64,128]{1,0:T(8,128)S(1)} collective-permute-done((f32[64,128]{1,0:T(8,128)S(1)}, f32[64,128]{1,0:T(8,128)S(1)}, u32[]{:S(2)}, u32[]{:S(2)}) %collective-permute-start.9) | collective-permute-done | bytes 32800 | tf_op jit(solution)/shard_map/ppermute | solution.py:513
  29.4 0.0 collective-permute-done.5.a_in
  29.4 0.0 collective-permute-done.6.b_in
  29.4 0.0 collective-permute-done.7.rest_0_
  29.4 1.0 %shard_map.76 = f32[2,256,256]{2,1,0:T(8,128)} custom-call(f32[2,256,256]{2,1,0:T(8,128)S(1)} %copy-done.1, f32[2,256,256]{2,1,0:T(8,128)S(1)} %get-tuple-element.25.g_core, f32[2,64,256]{2,1,0:T(8,128)S(1)} %collective-permute-done.5.a_in, f32[2,64,256]{2,1,0:T(8,128)S(1)} %collective-permute-done.6.b_in, f32[256,128]{1,0:T(8,128)S(1)} %collective-permute-done.7.rest_0_, ...), custom_call_target="tpu_custom_call" | custom-call | tf_op jit(solution)/shard_map/pallas_call | solution.py:490
Async XLA Ops:
  0.0 1.0 %copy-start = (f32[2,256,256]{2,1,0:T(8,128)S(1)}, f32[2,256,256]{2,1,0:T(8,128)}, u32[]{:S(2)}) copy-start(f32[2,256,256]{2,1,0:T(8,128)} %object_ref.3) | copy-start | bytes 1572868
  1.2 12.3 %collective-permute-start.3 = (f32[64,128]{1,0:T(8,128)S(1)}, f32[64,128]{1,0:T(8,128)S(1)}, u32[]{:S(2)}, u32[]{:S(2)}) collective-permute-start(f32[64,128]{1,0:T(8,128)S(1)} %get-tuple-element.23), channel_id=1, source_target_pairs={{0,3},{1,2},{4,7},{5,6},{8,11},{9,10},{12,15},{13,14},{16,19},{17,... | collective-permute-start | bytes 98312 | tf_op jit(solution)/shard_map/ppermute | solution.py:513
  3.6 9.8 %collective-permute-start.4 = (f32[64,128]{1,0:T(8,128)S(1)}, f32[64,128]{1,0:T(8,128)S(1)}, u32[]{:S(2)}, u32[]{:S(2)}) collective-permute-start(f32[64,128]{1,0:T(8,128)S(1)} %get-tuple-element.24), channel_id=1, source_target_pairs={{2,5},{3,4},{6,9},{7,8},{10,13},{11,12},{14,17},{15,16},{18,21},{1... | collective-permute-start | bytes 98312 | tf_op jit(solution)/shard_map/ppermute | solution.py:513
  4.3 9.2 %collective-permute-start = (f32[2,64,256]{2,1,0:T(8,128)S(1)}, f32[2,64,256]{2,1,0:T(8,128)S(1)}, u32[]{:S(2)}, u32[]{:S(2)}) collective-permute-start(f32[2,64,256]{2,1,0:T(8,128)S(1)} %get-tuple-element.20), channel_id=1, source_target_pairs={{0,2},{1,3},{4,6},{5,7},{8,10},{9,11},{12,14},{13,15},{16,18},{17,... | collective-permute-start | bytes 393224 | tf_op jit(solution)/shard_map/ppermute | solution.py:509
  5.3 8.1 %collective-permute-start.1 = (f32[2,64,256]{2,1,0:T(8,128)S(1)}, f32[2,64,256]{2,1,0:T(8,128)S(1)}, u32[]{:S(2)}, u32[]{:S(2)}) collective-permute-start(f32[2,64,256]{2,1,0:T(8,128)S(1)} %get-tuple-element.21), channel_id=1, source_target_pairs={{2,4},{3,5},{6,8},{7,9},{10,12},{11,13},{14,16},{15,17},{18,20},{1... | collective-permute-start | bytes 393224 | tf_op jit(solution)/shard_map/ppermute | solution.py:509
  6.7 6.8 %collective-permute-start.2 = (f32[256,128]{1,0:T(8,128)S(1)}, f32[256,128]{1,0:T(8,128)S(1)}, u32[]{:S(2)}, u32[]{:S(2)}) collective-permute-start(f32[256,128]{1,0:T(8,128)S(1)} %get-tuple-element.22), channel_id=1, source_target_pairs={{0,1},{1,0},{2,3},{3,2},{4,5},{5,4},{6,7},{7,6},{8,9},{9,8},{10,11... | collective-permute-start | bytes 393224 | tf_op jit(solution)/shard_map/ppermute | solution.py:516
  8.0 0.7 %copy-start.4 = (s32[1,1,4,2]{2,3,1,0:T(2,128)S(1)}, s32[1,1,4,2]{2,3,1,0:T(2,128)}, u32[]{:S(2)}) copy-start(s32[1,1,4,2]{2,3,1,0:T(2,128)} %param.10) | copy-start | bytes 100
  8.7 1.2 %copy-start.6 = (f32[1,1,4,256,256]{4,3,2,1,0:T(8,128)S(1)}, f32[1,1,4,256,256]{4,3,2,1,0:T(8,128)}, u32[]{:S(2)}) copy-start(f32[1,1,4,256,256]{4,3,2,1,0:T(8,128)} %intensity.1) | copy-start | bytes 3145732
  9.9 1.0 %copy-start.7 = (f32[2,256,256]{2,1,0:T(8,128)S(1)}, f32[2,256,256]{2,1,0:T(8,128)}, u32[]{:S(2)}) copy-start(f32[2,256,256]{2,1,0:T(8,128)} %probe.1) | copy-start | bytes 1572868
  11.0 2.5 %copy-start.1 = (f32[2,256,256]{2,1,0:T(8,128)S(1)}, f32[2,256,256]{2,1,0:T(8,128)}, u32[]{:S(2)}) copy-start(f32[2,256,256]{2,1,0:T(8,128)} %object_ref.3) | copy-start | bytes 1572868
  11.0 2.5 %copy-start.2 = (bf16[4,256,512]{2,1,0:T(8,128)(2,1)S(1)}, bf16[4,256,512]{2,1,0:T(8,128)(2,1)}, u32[]{:S(2)}) copy-start(bf16[4,256,512]{2,1,0:T(8,128)(2,1)} %constant.5.clone.left) | copy-start | bytes 3145732
  11.0 2.6 %copy-start.3 = (bf16[4,512,256]{2,1,0:T(8,128)(2,1)S(1)}, bf16[4,512,256]{2,1,0:T(8,128)(2,1)}, u32[]{:S(2)}) copy-start(bf16[4,512,256]{2,1,0:T(8,128)(2,1)} %constant.4.clone.right) | copy-start | bytes 3145732
  11.0 2.6 %copy-start.5 = (s32[1,1,4,2]{2,3,1,0:T(2,128)S(1)}, s32[1,1,4,2]{2,3,1,0:T(2,128)}, u32[]{:S(2)}) copy-start(s32[1,1,4,2]{2,3,1,0:T(2,128)} %param.10) | copy-start | bytes 100
  19.1 10.3 %collective-permute-start.5 = (f32[2,64,256]{2,1,0:T(8,128)S(1)}, f32[2,64,256]{2,1,0:T(8,128)S(1)}, u32[]{:S(2)}, u32[]{:S(2)}) collective-permute-start(f32[2,64,256]{2,1,0:T(8,128)S(1)} %get-tuple-element.26), channel_id=1, source_target_pairs={{0,2},{1,3},{4,6},{5,7},{8,10},{9,11},{12,14},{13,15},{16,18},{17,... | collective-permute-start | bytes 393224 | tf_op jit(solution)/shard_map/ppermute | solution.py:509
  19.9 9.5 %collective-permute-start.6 = (f32[2,64,256]{2,1,0:T(8,128)S(1)}, f32[2,64,256]{2,1,0:T(8,128)S(1)}, u32[]{:S(2)}, u32[]{:S(2)}) collective-permute-start(f32[2,64,256]{2,1,0:T(8,128)S(1)} %get-tuple-element.27), channel_id=1, source_target_pairs={{2,4},{3,5},{6,8},{7,9},{10,12},{11,13},{14,16},{15,17},{18,20},{1... | collective-permute-start | bytes 393224 | tf_op jit(solution)/shard_map/ppermute | solution.py:509
  20.6 8.8 %collective-permute-start.7 = (f32[256,128]{1,0:T(8,128)S(1)}, f32[256,128]{1,0:T(8,128)S(1)}, u32[]{:S(2)}, u32[]{:S(2)}) collective-permute-start(f32[256,128]{1,0:T(8,128)S(1)} %get-tuple-element.28), channel_id=1, source_target_pairs={{0,1},{1,0},{2,3},{3,2},{4,5},{5,4},{6,7},{7,6},{8,9},{9,8},{10,11... | collective-permute-start | bytes 393224 | tf_op jit(solution)/shard_map/ppermute | solution.py:516
  21.9 6.1 %collective-permute-start.8 = (f32[64,128]{1,0:T(8,128)S(1)}, f32[64,128]{1,0:T(8,128)S(1)}, u32[]{:S(2)}, u32[]{:S(2)}) collective-permute-start(f32[64,128]{1,0:T(8,128)S(1)} %get-tuple-element.29), channel_id=1, source_target_pairs={{0,3},{1,2},{4,7},{5,6},{8,11},{9,10},{12,15},{13,14},{16,19},{17,... | collective-permute-start | bytes 98312 | tf_op jit(solution)/shard_map/ppermute | solution.py:513
  22.9 6.5 %collective-permute-start.9 = (f32[64,128]{1,0:T(8,128)S(1)}, f32[64,128]{1,0:T(8,128)S(1)}, u32[]{:S(2)}, u32[]{:S(2)}) collective-permute-start(f32[64,128]{1,0:T(8,128)S(1)} %get-tuple-element.30), channel_id=1, source_target_pairs={{2,5},{3,4},{6,9},{7,8},{10,13},{11,12},{14,17},{15,16},{18,21},{1... | collective-permute-start | bytes 98312 | tf_op jit(solution)/shard_map/ppermute | solution.py:513

commit v3 on v2

--- a/solution.py
+++ b/solution.py
@@ -155,12 +155,12 @@
 
 
 def prepare_kernel(
-    offsets_in, counts_in, probe, intensity, placed, amplitude, offsets, counts, doubled, measured, sems
+    offsets_in, counts, probe, intensity, placed, amplitude, offsets, doubled, measured, sems
 ):
     views, size = measured.shape[0], probe.shape[1]
     half = size // 2
     copies = fetch(
-        [(offsets_in, offsets), (counts_in, counts)]
+        [(offsets_in, offsets)]
         + [(probe, doubled.at[:, pl.ds(size * i, size)]) for i in range(2)]
         + [(intensity.at[0, 0, view], measured.at[view]) for view in range(views)],
         sems,
@@ -169,7 +169,7 @@
     target = lax.broadcasted_iota(jnp.int32, (size, size), 1)
     order = (target == (source % 2) * half + source // 2).astype(F32).astype(BF16)
     sublane = lax.broadcasted_iota(jnp.int32, (1, 8, 1), 1)
-    for copy in copies[:4]:
+    for copy in copies[:3]:
         copy.wait()
     for view in range(views):
         shift_row = lax.rem(offsets[0, 0, 0, view] - MARGIN + size, size)
@@ -185,7 +185,7 @@
                 block = jnp.where(sublane < 8 - rest, block[:-1], block[1:])
                 placed[view, part, row : row + CHUNK] = block.reshape(CHUNK, size)
     for view in range(views):
-        copies[4 + view].wait()
+        copies[3 + view].wait()
         valid = (view < counts[0, 0]).astype(F32)
         power = measured[view] + smooth_eps
         high, low = split(power * lax.rsqrt(power) * valid)
@@ -196,36 +196,35 @@
 
 def prepare_call(offsets, counts, probe, intensity):
     views, size = intensity.shape[2], probe.shape[1]
-    vmem = pl.BlockSpec(memory_space=pltpu.VMEM)
+    vmem, hbm = pl.BlockSpec(memory_space=pltpu.VMEM), pl.BlockSpec(memory_space=pltpu.HBM)
     return pl.pallas_call(
         prepare_kernel,
         out_shape=[
             jax.ShapeDtypeStruct((views, 2, size, size), F32),
             jax.ShapeDtypeStruct((views, 2, size, size // 2), F32),
         ],
-        in_specs=[pl.BlockSpec(memory_space=pltpu.HBM)] * 4,
+        in_specs=[hbm, pl.BlockSpec(memory_space=pltpu.SMEM), hbm, hbm],
         out_specs=[vmem] * 2,
         scratch_shapes=[
             pltpu.SMEM(offsets.shape, jnp.int32),
-            pltpu.SMEM(counts.shape, jnp.int32),
             pltpu.VMEM((2, 2 * size, size), F32),
             pltpu.VMEM((views, size, size), F32),
-            pltpu.SemaphoreType.DMA((4 + views,)),
+            pltpu.SemaphoreType.DMA((3 + views,)),
         ],
         compiler_params=pltpu.CompilerParams(vmem_limit_bytes=16 * 1024 * 1024),
         cost_estimate=pl.CostEstimate(flops=2 * 10**9, bytes_accessed=6 * 10**6, transcendentals=0),
     )(offsets, counts, probe, intensity)
 
 
-def views_kernel(chans, offsets_in, counts_in, core, placed, amplitude, right, left, a_in, b_in, *rest):
+def views_kernel(chans, offsets_in, counts, core, placed, amplitude, right, left, a_in, b_in, *rest):
     count = len(chans)
     x_in, ka_in, kb_in = rest[:count], rest[count : 2 * count], rest[2 * count : 3 * count]
     rest = rest[3 * count :]
     g_core, g_a, g_b = rest[:3]
     g_x, g_ka = rest[3 : 3 + count], rest[3 + count : 3 + 2 * count]
     g_kb = rest[3 + 2 * count : 3 + 3 * count]
-    offsets, counts, sems, cols_m, rows_m, corner_m, s1, y, s2, z, s3, u, s4, g = rest[3 + 3 * count :]
-    copies = fetch([(offsets_in, offsets), (counts_in, counts)], sems)
+    offsets, sem, cols_m, rows_m, corner_m, s1, y, s2, z, s3, u, s4, g = rest[3 + 3 * count :]
+    (offsets_copy,) = fetch([(offsets_in, offsets)], sem)
     views, size = placed.shape[0], core.shape[1]
     half, m = size // 2, MARGIN
     lower, partner = lower_partner(), b_partner()
@@ -252,8 +251,7 @@
         corner_m[part, :m] = jnp.where(lower, corner_a[part], corner_b[part])
         corner_m[part, m:] = jnp.where(lower, corner_b[part], corner_a[part])
 
-    for copy in copies:
-        copy.wait()
+    offsets_copy.wait()
 
     def by_right(lhs, t):
         out = dot(lhs[:, :size], right[t, :size]) + dot(lhs[:, size:], right[t, :size])
@@ -431,12 +429,15 @@
     outs = pl.pallas_call(
         functools.partial(views_kernel, chans),
         out_shape=[jax.ShapeDtypeStruct(shape, F32) for shape in shapes],
-        in_specs=[pl.BlockSpec(memory_space=pltpu.HBM)] * 2 + [vmem] * (7 + 3 * count),
+        in_specs=[
+            pl.BlockSpec(memory_space=pltpu.HBM),
+            pl.BlockSpec(memory_space=pltpu.SMEM),
+            *[vmem] * (7 + 3 * count),
+        ],
         out_specs=[vmem] * len(shapes),
         scratch_shapes=[
             pltpu.SMEM(offsets.shape, jnp.int32),
-            pltpu.SMEM(counts.shape, jnp.int32),
-            pltpu.SemaphoreType.DMA((2,)),
+            pltpu.SemaphoreType.DMA((1,)),
             pltpu.VMEM((2, size, LANES), F32),
             pltpu.VMEM((2, 2 * MARGIN, size), F32),
             pltpu.VMEM((2, 2 * MARGIN, LANES), F32),
@@ -521,9 +522,12 @@
         return a_in, b_in, x_in, ka_in, kb_in
 
     packs = pack_call(object_field, chans)
-    offsets = jnp.swapaxes(view_offsets, 2, 3)
+    offsets, probe, measured = (
+        pltpu.with_memory_space_constraint(array, pltpu.HBM)
+        for array in (jnp.swapaxes(view_offsets, 2, 3), probe_field, intensity)
+    )
     margins = exchange(packs[0], packs[1], packs[2::3], packs[3::3], packs[4::3])
-    placed, amplitude = prepare_call(offsets, view_counts, probe_field, intensity)
+    placed, amplitude = prepare_call(offsets, view_counts, probe, measured)
     g_core, *sends = views_call(
         chans, offsets, view_counts, object_field, placed, amplitude, tables, *margins
     )

time: 30.7 us -> 29.1 us (0.948)
  local copies, waits for them, and re-layouts: 4 us -> 1.06 us
  waiting for transfers between devices: 5.93 us -> 8.03 us
  starting transfers between devices: 10.6 us -> 9.41 us
  Pallas kernels: 9.16 us -> 9.7 us
    unnamed x16 -> x8, local copies, waits for them, and re-layouts: 4 us -> 1.06 us
    ppermute x2, waiting for transfers between devices: 0.01 us -> 1.88 us  [exchange(): lax.ppermute(block, 'col', channel[0])]
    pallas_call x1, Pallas kernels: 2.46 us -> 3.25 us  [prepare_call(): pl.pallas_call(prepare_kernel, out_shape=[jax.ShapeDtypeStruct((views, 2,...]
    ppermute x4, starting transfers between devices: 4.68 us -> 4.15 us  [across(): lax.ppermute(block, ('row', 'col'), route + (extra if mesh_cols == 2 else...]
    ppermute x4, starting transfers between devices: 3.99 us -> 3.63 us  [over_rows(): return lax.ppermute(block, ('row', 'col'), route + extra)]
  transfers between devices with their start and end apart: 10 -> 10, of which waited for: 2 -> 4; matrix products, arithmetic and copies ran while one was open for 0% -> 0% of each run, Pallas kernels for 8% -> 11%
where the time goes in v3:
time: 29.1 us; the launch traced here: 28.9 us
  Pallas kernels  9.7 us (33%)
  starting transfers between devices  9.41 us (32%)
  waiting for transfers between devices  8.03 us (28%)
  local copies, waits for them, and re-layouts  1.06 us (4%)
  between operations  0.75 us (3%)
    ppermute x4, waiting for transfers between devices, across(): lax.ppermute(block, ('row', 'col'), route + (extra if mesh_cols == 2 else...  5.9 us
    pallas_call x1, Pallas kernels, views_call(): pl.pallas_call(functools.partial(views_kernel, chans), out_shape=[jax.Sha...  5.31 us
    ppermute x4, starting transfers between devices, across(): lax.ppermute(block, ('row', 'col'), route + (extra if mesh_cols == 2 else...  4.15 us
    ppermute x4, starting transfers between devices, over_rows(): return lax.ppermute(block, ('row', 'col'), route + extra)  3.63 us
    pallas_call x1, Pallas kernels, prepare_call(): pl.pallas_call(prepare_kernel, out_shape=[jax.ShapeDtypeStruct((views, 2,...  3.25 us
    ppermute x2, waiting for transfers between devices, exchange(): lax.ppermute(block, 'col', channel[0])  1.88 us
    ppermute x2, starting transfers between devices, exchange(): lax.ppermute(block, 'col', channel[0])  1.63 us
    unnamed x8, local copies, waits for them, and re-layouts  1.06 us
  transfers between devices with their start and end apart: 10, of which 4 were waited for; matrix products, arithmetic and copies ran while one was open for 0% of the time, Pallas kernels for 11%

profile of v3, /device:TPU:0, one launch (start us, length us, event | category | flops | bytes accessed | tf_op | source)
XLA Modules:
  0.0 28.9 jit_solution(12320896033677780251)
XLA Ops:
  0.0 0.0 copy-start
  0.0 1.0 %copy-done = f32[2,256,256]{2,1,0:T(8,128)S(1)} copy-done((f32[2,256,256]{2,1,0:T(8,128)S(1)}, f32[2,256,256]{2,1,0:T(8,128)}, u32[]{:S(2)}) %copy-start) | copy-done | bytes 524312
  1.0 0.1 shard_map.74
  1.2 2.4 %collective-permute-start.3 = (f32[64,128]{1,0:T(8,128)S(1)}, f32[64,128]{1,0:T(8,128)S(1)}, u32[]{:S(2)}, u32[]{:S(2)}) collective-permute-start(f32[64,128]{1,0:T(8,128)S(1)} %get-tuple-element.23), channel_id=1, source_target_pairs={{0,3},{1,2},{4,7},{5,6},{8,11},{9,10},{12,15},{13,14},{16,19},{17,... | collective-permute-start | bytes 98312 | tf_op jit(solution)/shard_map/ppermute | solution.py:514
  3.6 0.6 %collective-permute-start.4 = (f32[64,128]{1,0:T(8,128)S(1)}, f32[64,128]{1,0:T(8,128)S(1)}, u32[]{:S(2)}, u32[]{:S(2)}) collective-permute-start(f32[64,128]{1,0:T(8,128)S(1)} %get-tuple-element.24), channel_id=1, source_target_pairs={{2,5},{3,4},{6,9},{7,8},{10,13},{11,12},{14,17},{15,16},{18,21},{1... | collective-permute-start | bytes 98312 | tf_op jit(solution)/shard_map/ppermute | solution.py:514
  4.3 1.1 %collective-permute-start = (f32[2,64,256]{2,1,0:T(8,128)S(1)}, f32[2,64,256]{2,1,0:T(8,128)S(1)}, u32[]{:S(2)}, u32[]{:S(2)}) collective-permute-start(f32[2,64,256]{2,1,0:T(8,128)S(1)} %get-tuple-element.20), channel_id=1, source_target_pairs={{0,2},{1,3},{4,6},{5,7},{8,10},{9,11},{12,14},{13,15},{16,18},{17,... | collective-permute-start | bytes 393224 | tf_op jit(solution)/shard_map/ppermute | solution.py:510
  5.3 1.4 %collective-permute-start.1 = (f32[2,64,256]{2,1,0:T(8,128)S(1)}, f32[2,64,256]{2,1,0:T(8,128)S(1)}, u32[]{:S(2)}, u32[]{:S(2)}) collective-permute-start(f32[2,64,256]{2,1,0:T(8,128)S(1)} %get-tuple-element.21), channel_id=1, source_target_pairs={{2,4},{3,5},{6,8},{7,9},{10,12},{11,13},{14,16},{15,17},{18,20},{1... | collective-permute-start | bytes 393224 | tf_op jit(solution)/shard_map/ppermute | solution.py:510
  6.7 0.6 %collective-permute-start.2 = (f32[256,128]{1,0:T(8,128)S(1)}, f32[256,128]{1,0:T(8,128)S(1)}, u32[]{:S(2)}, u32[]{:S(2)}) collective-permute-start(f32[256,128]{1,0:T(8,128)S(1)} %get-tuple-element.22), channel_id=1, source_target_pairs={{0,1},{1,0},{2,3},{3,2},{4,5},{5,4},{6,7},{7,6},{8,9},{9,8},{10,11... | collective-permute-start | bytes 393224 | tf_op jit(solution)/shard_map/ppermute | solution.py:517
  8.0 0.0 copy-start.1
  8.0 0.0 copy-start.2
  8.0 0.0 copy-start.3
  8.1 3.3 %shard_map.73 = (f32[4,2,256,256]{3,2,1,0:T(8,128)S(1)}, f32[4,2,256,128]{3,2,1,0:T(8,128)S(1)}) custom-call(s32[1,1,2,4]{3,2,1,0:T(2,128)} %bitcast.1, s32[1,1]{1,0:T(1,128)S(6)} %copy.8.counts, f32[2,256,256]{2,1,0:T(8,128)} %probe.1, f32[1,1,4,256,256]{4,3,2,1,0:T(8,128)} %intensity.1), custom_call_target="tpu_custom_call" | custom-call | flops 2000000000 | bytes 6000000 | tf_op jit(solution)/shard_map/pallas_call | solution.py:200
  11.3 0.0 collective-permute-done.3.rest_1_
  11.3 0.0 collective-permute-done.4.rest_2_
  11.3 0.0 collective-permute-done.a_in
  11.3 0.2 collective-permute-done.1.b_in
  11.6 1.9 %collective-permute-done.2.rest_0_ = f32[256,128]{1,0:T(8,128)S(1)} collective-permute-done((f32[256,128]{1,0:T(8,128)S(1)}, f32[256,128]{1,0:T(8,128)S(1)}, u32[]{:S(2)}, u32[]{:S(2)}) %collective-permute-start.2) | collective-permute-done | bytes 131104 | tf_op jit(solution)/shard_map/ppermute | solution.py:517
  13.5 0.0 copy-done.1
  13.5 0.0 copy-done.2
  13.5 0.0 copy-done.3
  13.5 5.3 %shard_map.75 = (f32[2,256,256]{2,1,0:T(8,128)S(1)}, f32[2,64,256]{2,1,0:T(8,128)S(1)}, f32[2,64,256]{2,1,0:T(8,128)S(1)}, f32[256,128]{1,0:T(8,128)S(1)}, f32[64,128]{1,0:T(8,128)S(1)}, /*index=5*/f32[64,128]{1,0:T(8,128)S(1)}) custom-call(s32[1,1,2,4]{3,2,1,0:T(2,128)} %bitcast.2, s32[1,1]{1,0:T(1,128)S(6)} %copy.8.counts, f32[2,256,256]{2,1,0:T(8,128)S(1)} %copy-done.1, ...), custom_call_target="tpu_custom_call" | custom-call | tf_op jit(solution)/shard_map/pallas_call | solution.py:429
  18.8 0.1 collective-permute-start.5
  18.9 1.1 %collective-permute-start.6 = (f32[2,64,256]{2,1,0:T(8,128)S(1)}, f32[2,64,256]{2,1,0:T(8,128)S(1)}, u32[]{:S(2)}, u32[]{:S(2)}) collective-permute-start(f32[2,64,256]{2,1,0:T(8,128)S(1)} %get-tuple-element.27), channel_id=1, source_target_pairs={{2,4},{3,5},{6,8},{7,9},{10,12},{11,13},{14,16},{15,17},{18,20},{1... | collective-permute-start | bytes 393224 | tf_op jit(solution)/shard_map/ppermute | solution.py:510
  20.0 1.0 %collective-permute-start.7 = (f32[256,128]{1,0:T(8,128)S(1)}, f32[256,128]{1,0:T(8,128)S(1)}, u32[]{:S(2)}, u32[]{:S(2)}) collective-permute-start(f32[256,128]{1,0:T(8,128)S(1)} %get-tuple-element.28), channel_id=1, source_target_pairs={{0,1},{1,0},{2,3},{3,2},{4,5},{5,4},{6,7},{7,6},{8,9},{9,8},{10,11... | collective-permute-start | bytes 393224 | tf_op jit(solution)/shard_map/ppermute | solution.py:517
  21.0 0.0 collective-permute-start.8
  21.0 1.1 %collective-permute-start.9 = (f32[64,128]{1,0:T(8,128)S(1)}, f32[64,128]{1,0:T(8,128)S(1)}, u32[]{:S(2)}, u32[]{:S(2)}) collective-permute-start(f32[64,128]{1,0:T(8,128)S(1)} %get-tuple-element.30), channel_id=1, source_target_pairs={{2,5},{3,4},{6,9},{7,8},{10,13},{11,12},{14,17},{15,16},{18,21},{1... | collective-permute-start | bytes 98312 | tf_op jit(solution)/shard_map/ppermute | solution.py:514
  22.0 4.1 %collective-permute-done.8.rest_1_ = f32[64,128]{1,0:T(8,128)S(1)} collective-permute-done((f32[64,128]{1,0:T(8,128)S(1)}, f32[64,128]{1,0:T(8,128)S(1)}, u32[]{:S(2)}, u32[]{:S(2)}) %collective-permute-start.8) | collective-permute-done | bytes 32800 | tf_op jit(solution)/shard_map/ppermute | solution.py:514
  26.2 1.8 %collective-permute-done.9.rest_2_ = f32[64,128]{1,0:T(8,128)S(1)} collective-permute-done((f32[64,128]{1,0:T(8,128)S(1)}, f32[64,128]{1,0:T(8,128)S(1)}, u32[]{:S(2)}, u32[]{:S(2)}) %collective-permute-start.9) | collective-permute-done | bytes 32800 | tf_op jit(solution)/shard_map/ppermute | solution.py:514
  27.9 0.0 collective-permute-done.5.a_in
  27.9 0.0 collective-permute-done.6.b_in
  27.9 0.0 collective-permute-done.7.rest_0_
  27.9 1.0 %shard_map.76 = f32[2,256,256]{2,1,0:T(8,128)} custom-call(f32[2,256,256]{2,1,0:T(8,128)S(1)} %copy-done.1, f32[2,256,256]{2,1,0:T(8,128)S(1)} %get-tuple-element.25.g_core, f32[2,64,256]{2,1,0:T(8,128)S(1)} %collective-permute-done.5.a_in, f32[2,64,256]{2,1,0:T(8,128)S(1)} %collective-permute-done.6.b_in, f32[256,128]{1,0:T(8,128)S(1)} %collective-permute-done.7.rest_0_, ...), custom_call_target="tpu_custom_call" | custom-call | tf_op jit(solution)/shard_map/pallas_call | solution.py:491
Async XLA Ops:
  0.0 1.0 %copy-start = (f32[2,256,256]{2,1,0:T(8,128)S(1)}, f32[2,256,256]{2,1,0:T(8,128)}, u32[]{:S(2)}) copy-start(f32[2,256,256]{2,1,0:T(8,128)} %object_ref.3) | copy-start | bytes 1572868
  1.2 10.1 %collective-permute-start.3 = (f32[64,128]{1,0:T(8,128)S(1)}, f32[64,128]{1,0:T(8,128)S(1)}, u32[]{:S(2)}, u32[]{:S(2)}) collective-permute-start(f32[64,128]{1,0:T(8,128)S(1)} %get-tuple-element.23), channel_id=1, source_target_pairs={{0,3},{1,2},{4,7},{5,6},{8,11},{9,10},{12,15},{13,14},{16,19},{17,... | collective-permute-start | bytes 98312 | tf_op jit(solution)/shard_map/ppermute | solution.py:514
  3.6 7.7 %collective-permute-start.4 = (f32[64,128]{1,0:T(8,128)S(1)}, f32[64,128]{1,0:T(8,128)S(1)}, u32[]{:S(2)}, u32[]{:S(2)}) collective-permute-start(f32[64,128]{1,0:T(8,128)S(1)} %get-tuple-element.24), channel_id=1, source_target_pairs={{2,5},{3,4},{6,9},{7,8},{10,13},{11,12},{14,17},{15,16},{18,21},{1... | collective-permute-start | bytes 98312 | tf_op jit(solution)/shard_map/ppermute | solution.py:514
  4.3 7.1 %collective-permute-start = (f32[2,64,256]{2,1,0:T(8,128)S(1)}, f32[2,64,256]{2,1,0:T(8,128)S(1)}, u32[]{:S(2)}, u32[]{:S(2)}) collective-permute-start(f32[2,64,256]{2,1,0:T(8,128)S(1)} %get-tuple-element.20), channel_id=1, source_target_pairs={{0,2},{1,3},{4,6},{5,7},{8,10},{9,11},{12,14},{13,15},{16,18},{17,... | collective-permute-start | bytes 393224 | tf_op jit(solution)/shard_map/ppermute | solution.py:510
  5.3 6.2 %collective-permute-start.1 = (f32[2,64,256]{2,1,0:T(8,128)S(1)}, f32[2,64,256]{2,1,0:T(8,128)S(1)}, u32[]{:S(2)}, u32[]{:S(2)}) collective-permute-start(f32[2,64,256]{2,1,0:T(8,128)S(1)} %get-tuple-element.21), channel_id=1, source_target_pairs={{2,4},{3,5},{6,8},{7,9},{10,12},{11,13},{14,16},{15,17},{18,20},{1... | collective-permute-start | bytes 393224 | tf_op jit(solution)/shard_map/ppermute | solution.py:510
  6.7 6.7 %collective-permute-start.2 = (f32[256,128]{1,0:T(8,128)S(1)}, f32[256,128]{1,0:T(8,128)S(1)}, u32[]{:S(2)}, u32[]{:S(2)}) collective-permute-start(f32[256,128]{1,0:T(8,128)S(1)} %get-tuple-element.22), channel_id=1, source_target_pairs={{0,1},{1,0},{2,3},{3,2},{4,5},{5,4},{6,7},{7,6},{8,9},{9,8},{10,11... | collective-permute-start | bytes 393224 | tf_op jit(solution)/shard_map/ppermute | solution.py:517
  8.0 5.5 %copy-start.1 = (f32[2,256,256]{2,1,0:T(8,128)S(1)}, f32[2,256,256]{2,1,0:T(8,128)}, u32[]{:S(2)}) copy-start(f32[2,256,256]{2,1,0:T(8,128)} %object_ref.3) | copy-start | bytes 1572868
  8.0 5.4 %copy-start.2 = (bf16[4,256,512]{2,1,0:T(8,128)(2,1)S(1)}, bf16[4,256,512]{2,1,0:T(8,128)(2,1)}, u32[]{:S(2)}) copy-start(bf16[4,256,512]{2,1,0:T(8,128)(2,1)} %constant.5.clone.left) | copy-start | bytes 3145732
  8.0 5.4 %copy-start.3 = (bf16[4,512,256]{2,1,0:T(8,128)(2,1)S(1)}, bf16[4,512,256]{2,1,0:T(8,128)(2,1)}, u32[]{:S(2)}) copy-start(bf16[4,512,256]{2,1,0:T(8,128)(2,1)} %constant.4.clone.right) | copy-start | bytes 3145732
  18.8 9.1 %collective-permute-start.5 = (f32[2,64,256]{2,1,0:T(8,128)S(1)}, f32[2,64,256]{2,1,0:T(8,128)S(1)}, u32[]{:S(2)}, u32[]{:S(2)}) collective-permute-start(f32[2,64,256]{2,1,0:T(8,128)S(1)} %get-tuple-element.26), channel_id=1, source_target_pairs={{0,2},{1,3},{4,6},{5,7},{8,10},{9,11},{12,14},{13,15},{16,18},{17,... | collective-permute-start | bytes 393224 | tf_op jit(solution)/shard_map/ppermute | solution.py:510
  18.9 9.1 %collective-permute-start.6 = (f32[2,64,256]{2,1,0:T(8,128)S(1)}, f32[2,64,256]{2,1,0:T(8,128)S(1)}, u32[]{:S(2)}, u32[]{:S(2)}) collective-permute-start(f32[2,64,256]{2,1,0:T(8,128)S(1)} %get-tuple-element.27), channel_id=1, source_target_pairs={{2,4},{3,5},{6,8},{7,9},{10,12},{11,13},{14,16},{15,17},{18,20},{1... | collective-permute-start | bytes 393224 | tf_op jit(solution)/shard_map/ppermute | solution.py:510
  20.0 8.0 %collective-permute-start.7 = (f32[256,128]{1,0:T(8,128)S(1)}, f32[256,128]{1,0:T(8,128)S(1)}, u32[]{:S(2)}, u32[]{:S(2)}) collective-permute-start(f32[256,128]{1,0:T(8,128)S(1)} %get-tuple-element.28), channel_id=1, source_target_pairs={{0,1},{1,0},{2,3},{3,2},{4,5},{5,4},{6,7},{7,6},{8,9},{9,8},{10,11... | collective-permute-start | bytes 393224 | tf_op jit(solution)/shard_map/ppermute | solution.py:517
  21.0 5.2 %collective-permute-start.8 = (f32[64,128]{1,0:T(8,128)S(1)}, f32[64,128]{1,0:T(8,128)S(1)}, u32[]{:S(2)}, u32[]{:S(2)}) collective-permute-start(f32[64,128]{1,0:T(8,128)S(1)} %get-tuple-element.29), channel_id=1, source_target_pairs={{0,3},{1,2},{4,7},{5,6},{8,11},{9,10},{12,15},{13,14},{16,19},{17,... | collective-permute-start | bytes 98312 | tf_op jit(solution)/shard_map/ppermute | solution.py:514
  21.0 7.0 %collective-permute-start.9 = (f32[64,128]{1,0:T(8,128)S(1)}, f32[64,128]{1,0:T(8,128)S(1)}, u32[]{:S(2)}, u32[]{:S(2)}) collective-permute-start(f32[64,128]{1,0:T(8,128)S(1)} %get-tuple-element.30), channel_id=1, source_target_pairs={{2,5},{3,4},{6,9},{7,8},{10,13},{11,12},{14,17},{15,16},{18,21},{1... | collective-permute-start | bytes 98312 | tf_op jit(solution)/shard_map/ppermute | solution.py:514

commit v4 on v3

--- a/solution.py
+++ b/solution.py
@@ -216,10 +216,10 @@
     )(offsets, counts, probe, intensity)
 
 
-def views_kernel(chans, offsets_in, counts, core, placed, amplitude, right, left, a_in, b_in, *rest):
+def views_kernel(chans, offsets_in, counts, core, placed, amplitude, b_in, *rest):
     count = len(chans)
-    x_in, ka_in, kb_in = rest[:count], rest[count : 2 * count], rest[2 * count : 3 * count]
-    rest = rest[3 * count :]
+    x_in, kb_in, ka_in = rest[:count], rest[count : 2 * count], rest[2 * count : 3 * count]
+    a_in, right, left, *rest = rest[3 * count :]
     g_core, g_a, g_b = rest[:3]
     g_x, g_ka = rest[3 : 3 + count], rest[3 + count : 3 + 2 * count]
     g_kb = rest[3 + 2 * count : 3 + 3 * count]
@@ -444,14 +444,14 @@
             wide, full, tall, full, tall, full, wide, full,
         ],
         compiler_params=pltpu.CompilerParams(vmem_limit_bytes=40 * 1024 * 1024),
-    )(offsets, counts, core, placed, amplitude, *tables, a_in, b_in, *x_in, *ka_in, *kb_in)
+    )(offsets, counts, core, placed, amplitude, b_in, *x_in, *kb_in, *ka_in, a_in, *tables)
     return (*outs[:3], outs[3 : 3 + count], outs[3 + count : 3 + 2 * count], outs[3 + 2 * count :])
 
 
-def finish_kernel(chans, object_ref, g_core, a_in, b_in, *rest):
+def finish_kernel(chans, object_ref, g_core, b_in, *rest):
     count = len(chans)
-    x_in, ka_in, kb_in = rest[:count], rest[count : 2 * count], rest[2 * count : 3 * count]
-    out = rest[-1]
+    x_in, kb_in, ka_in = rest[:count], rest[count : 2 * count], rest[2 * count : 3 * count]
+    a_in, out = rest[3 * count :]
     size = object_ref.shape[1]
     lower = lower_partner()
     a_rows = pl.ds(pl.multiple_of(jnp.where(lower, size - MARGIN, 0), MARGIN), MARGIN)
@@ -494,7 +494,7 @@
         in_specs=[vmem] * (4 + 3 * len(chans)),
         out_specs=vmem,
         compiler_params=pltpu.CompilerParams(vmem_limit_bytes=6 * 1024 * 1024),
-    )(object_field, g_core, a_in, b_in, *x_in, *ka_in, *kb_in)
+    )(object_field, g_core, b_in, *x_in, *kb_in, *ka_in, a_in)
 
 
 def per_device(object_field, probe_field, intensity, view_offsets, view_counts):

time: 29.1 us -> 28.7 us (0.986)
  waiting for transfers between devices: 8.03 us -> 6.22 us
  starting transfers between devices: 9.41 us -> 10.8 us
    ppermute x4, starting transfers between devices: 4.15 us -> 5.86 us  [across(): lax.ppermute(block, ('row', 'col'), route + (extra if mesh_cols == 2 else...]
    ppermute x2, waiting for transfers between devices: 1.88 us -> 0.95 us  [exchange(): lax.ppermute(block, 'col', channel[0])]
    ppermute x4, waiting for transfers between devices: 5.9 us -> 5.26 us  [across(): lax.ppermute(block, ('row', 'col'), route + (extra if mesh_cols == 2 else...]
    ppermute x2, starting transfers between devices: 1.63 us -> 1.07 us  [exchange(): lax.ppermute(block, 'col', channel[0])]
  transfers between devices with their start and end apart: 10 -> 10, of which waited for: 4 -> 2; matrix products, arithmetic and copies ran while one was open for 0% -> 0% of each run, Pallas kernels for 11% -> 11%
where the time goes in v4:
time: 28.7 us; the launch traced here: 28.5 us
  starting transfers between devices  10.8 us (38%)
  Pallas kernels  9.7 us (34%)
  waiting for transfers between devices  6.22 us (22%)
  local copies, waits for them, and re-layouts  1.06 us (4%)
  between operations  0.76 us (3%)
    ppermute x4, starting transfers between devices, across(): lax.ppermute(block, ('row', 'col'), route + (extra if mesh_cols == 2 else...  5.86 us
    pallas_call x1, Pallas kernels, views_call(): pl.pallas_call(functools.partial(views_kernel, chans), out_shape=[jax.Sha...  5.31 us
    ppermute x4, waiting for transfers between devices, across(): lax.ppermute(block, ('row', 'col'), route + (extra if mesh_cols == 2 else...  5.26 us
    ppermute x4, starting transfers between devices, over_rows(): return lax.ppermute(block, ('row', 'col'), route + extra)  3.87 us
    pallas_call x1, Pallas kernels, prepare_call(): pl.pallas_call(prepare_kernel, out_shape=[jax.ShapeDtypeStruct((views, 2,...  3.25 us
    ppermute x2, starting transfers between devices, exchange(): lax.ppermute(block, 'col', channel[0])  1.07 us
    unnamed x8, local copies, waits for them, and re-layouts  1.06 us
    pallas_call x1, Pallas kernels, finish_call(): pl.pallas_call(functools.partial(finish_kernel, chans), out_shape=jax.Sha...  1 us
  transfers between devices with their start and end apart: 10, of which 2 were waited for; matrix products, arithmetic and copies ran while one was open for 0% of the time, Pallas kernels for 11%

profile of v4, /device:TPU:0, one launch (start us, length us, event | category | flops | bytes accessed | tf_op | source)
XLA Modules:
  0.0 28.5 jit_solution(5142533072728413231)
XLA Ops:
  0.0 0.0 copy-start
  0.0 1.0 %copy-done = f32[2,256,256]{2,1,0:T(8,128)S(1)} copy-done((f32[2,256,256]{2,1,0:T(8,128)S(1)}, f32[2,256,256]{2,1,0:T(8,128)}, u32[]{:S(2)}) %copy-start) | copy-done | bytes 524312
  1.0 0.1 shard_map.74
  1.2 3.0 %collective-permute-start.2 = (f32[64,128]{1,0:T(8,128)S(1)}, f32[64,128]{1,0:T(8,128)S(1)}, u32[]{:S(2)}, u32[]{:S(2)}) collective-permute-start(f32[64,128]{1,0:T(8,128)S(1)} %get-tuple-element.22), channel_id=1, source_target_pairs={{2,5},{3,4},{6,9},{7,8},{10,13},{11,12},{14,17},{15,16},{18,21},{1... | collective-permute-start | bytes 98312 | tf_op jit(solution)/shard_map/ppermute | solution.py:514
  4.2 1.2 %collective-permute-start.3 = (f32[64,128]{1,0:T(8,128)S(1)}, f32[64,128]{1,0:T(8,128)S(1)}, u32[]{:S(2)}, u32[]{:S(2)}) collective-permute-start(f32[64,128]{1,0:T(8,128)S(1)} %get-tuple-element.23), channel_id=1, source_target_pairs={{0,3},{1,2},{4,7},{5,6},{8,11},{9,10},{12,15},{13,14},{16,19},{17,... | collective-permute-start | bytes 98312 | tf_op jit(solution)/shard_map/ppermute | solution.py:514
  5.4 1.5 %collective-permute-start = (f32[2,64,256]{2,1,0:T(8,128)S(1)}, f32[2,64,256]{2,1,0:T(8,128)S(1)}, u32[]{:S(2)}, u32[]{:S(2)}) collective-permute-start(f32[2,64,256]{2,1,0:T(8,128)S(1)} %get-tuple-element.20), channel_id=1, source_target_pairs={{2,4},{3,5},{6,8},{7,9},{10,12},{11,13},{14,16},{15,17},{18,20},{1... | collective-permute-start | bytes 393224 | tf_op jit(solution)/shard_map/ppermute | solution.py:510
  6.9 0.5 %collective-permute-start.1 = (f32[256,128]{1,0:T(8,128)S(1)}, f32[256,128]{1,0:T(8,128)S(1)}, u32[]{:S(2)}, u32[]{:S(2)}) collective-permute-start(f32[256,128]{1,0:T(8,128)S(1)} %get-tuple-element.21), channel_id=1, source_target_pairs={{0,1},{1,0},{2,3},{3,2},{4,5},{5,4},{6,7},{7,6},{8,9},{9,8},{10,11... | collective-permute-start | bytes 393224 | tf_op jit(solution)/shard_map/ppermute | solution.py:517
  7.4 0.8 %collective-permute-start.4 = (f32[2,64,256]{2,1,0:T(8,128)S(1)}, f32[2,64,256]{2,1,0:T(8,128)S(1)}, u32[]{:S(2)}, u32[]{:S(2)}) collective-permute-start(f32[2,64,256]{2,1,0:T(8,128)S(1)} %get-tuple-element.24), channel_id=1, source_target_pairs={{0,2},{1,3},{4,6},{5,7},{8,10},{9,11},{12,14},{13,15},{16,18},{17,... | collective-permute-start | bytes 393224 | tf_op jit(solution)/shard_map/ppermute | solution.py:510
  8.9 0.0 copy-start.1
  8.9 0.0 copy-start.2
  8.9 0.0 copy-start.3
  8.9 3.3 %shard_map.73 = (f32[4,2,256,256]{3,2,1,0:T(8,128)S(1)}, f32[4,2,256,128]{3,2,1,0:T(8,128)S(1)}) custom-call(s32[1,1,2,4]{3,2,1,0:T(2,128)} %bitcast.1, s32[1,1]{1,0:T(1,128)S(6)} %copy.8.counts, f32[2,256,256]{2,1,0:T(8,128)} %probe.1, f32[1,1,4,256,256]{4,3,2,1,0:T(8,128)} %intensity.1), custom_call_target="tpu_custom_call" | custom-call | flops 2000000000 | bytes 6000000 | tf_op jit(solution)/shard_map/pallas_call | solution.py:200
  12.2 0.0 collective-permute-done.2.rest_1_
  12.2 0.0 collective-permute-done.3.rest_2_
  12.2 0.0 collective-permute-done.b_in
  12.2 0.9 %collective-permute-done.1.rest_0_ = f32[256,128]{1,0:T(8,128)S(1)} collective-permute-done((f32[256,128]{1,0:T(8,128)S(1)}, f32[256,128]{1,0:T(8,128)S(1)}, u32[]{:S(2)}, u32[]{:S(2)}) %collective-permute-start.1) | collective-permute-done | bytes 131104 | tf_op jit(solution)/shard_map/ppermute | solution.py:517
  13.2 0.0 collective-permute-done.4.rest_3_
  13.2 0.0 copy-done.1
  13.2 0.0 copy-done.2
  13.2 0.0 copy-done.3
  13.2 5.3 %shard_map.75 = (f32[2,256,256]{2,1,0:T(8,128)S(1)}, f32[2,64,256]{2,1,0:T(8,128)S(1)}, f32[2,64,256]{2,1,0:T(8,128)S(1)}, f32[256,128]{1,0:T(8,128)S(1)}, f32[64,128]{1,0:T(8,128)S(1)}, /*index=5*/f32[64,128]{1,0:T(8,128)S(1)}) custom-call(s32[1,1,2,4]{3,2,1,0:T(2,128)} %bitcast.2, s32[1,1]{1,0:T(1,128)S(6)} %copy.8.counts, f32[2,256,256]{2,1,0:T(8,128)S(1)} %copy-done.1, ...), custom_call_target="tpu_custom_call" | custom-call | tf_op jit(solution)/shard_map/pallas_call | solution.py:429
  18.5 1.6 %collective-permute-start.5 = (f32[2,64,256]{2,1,0:T(8,128)S(1)}, f32[2,64,256]{2,1,0:T(8,128)S(1)}, u32[]{:S(2)}, u32[]{:S(2)}) collective-permute-start(f32[2,64,256]{2,1,0:T(8,128)S(1)} %get-tuple-element.26), channel_id=1, source_target_pairs={{2,4},{3,5},{6,8},{7,9},{10,12},{11,13},{14,16},{15,17},{18,20},{1... | collective-permute-start | bytes 393224 | tf_op jit(solution)/shard_map/ppermute | solution.py:510
  20.1 0.5 %collective-permute-start.6 = (f32[256,128]{1,0:T(8,128)S(1)}, f32[256,128]{1,0:T(8,128)S(1)}, u32[]{:S(2)}, u32[]{:S(2)}) collective-permute-start(f32[256,128]{1,0:T(8,128)S(1)} %get-tuple-element.27), channel_id=1, source_target_pairs={{0,1},{1,0},{2,3},{3,2},{4,5},{5,4},{6,7},{7,6},{8,9},{9,8},{10,11... | collective-permute-start | bytes 393224 | tf_op jit(solution)/shard_map/ppermute | solution.py:517
  20.6 0.0 collective-permute-start.9
  20.6 1.5 %collective-permute-start.7 = (f32[64,128]{1,0:T(8,128)S(1)}, f32[64,128]{1,0:T(8,128)S(1)}, u32[]{:S(2)}, u32[]{:S(2)}) collective-permute-start(f32[64,128]{1,0:T(8,128)S(1)} %get-tuple-element.28), channel_id=1, source_target_pairs={{2,5},{3,4},{6,9},{7,8},{10,13},{11,12},{14,17},{15,16},{18,21},{1... | collective-permute-start | bytes 98312 | tf_op jit(solution)/shard_map/ppermute | solution.py:514
  22.1 0.2 collective-permute-start.8
  22.2 5.3 %collective-permute-done.7.rest_1_ = f32[64,128]{1,0:T(8,128)S(1)} collective-permute-done((f32[64,128]{1,0:T(8,128)S(1)}, f32[64,128]{1,0:T(8,128)S(1)}, u32[]{:S(2)}, u32[]{:S(2)}) %collective-permute-start.7) | collective-permute-done | bytes 32800 | tf_op jit(solution)/shard_map/ppermute | solution.py:514
  27.5 0.0 collective-permute-done.8.rest_2_
  27.5 0.0 collective-permute-done.5.b_in
  27.5 0.0 collective-permute-done.6.rest_0_
  27.5 0.0 collective-permute-done.9.rest_3_
  27.5 1.0 %shard_map.76 = f32[2,256,256]{2,1,0:T(8,128)} custom-call(f32[2,256,256]{2,1,0:T(8,128)S(1)} %copy-done.1, f32[2,256,256]{2,1,0:T(8,128)S(1)} %get-tuple-element.25.g_core, f32[2,64,256]{2,1,0:T(8,128)S(1)} %collective-permute-done.5.b_in, f32[256,128]{1,0:T(8,128)S(1)} %collective-permute-done.6.rest_0_, f32[64,128]{1,0:T(8,128)S(1)} %collective-permute-done.7.rest_1_, ...), custom_call_target="tpu_custom_call" | custom-call | tf_op jit(solution)/shard_map/pallas_call | solution.py:491
Async XLA Ops:
  0.0 1.0 %copy-start = (f32[2,256,256]{2,1,0:T(8,128)S(1)}, f32[2,256,256]{2,1,0:T(8,128)}, u32[]{:S(2)}) copy-start(f32[2,256,256]{2,1,0:T(8,128)} %object_ref.3) | copy-start | bytes 1572868
  1.2 11.0 %collective-permute-start.2 = (f32[64,128]{1,0:T(8,128)S(1)}, f32[64,128]{1,0:T(8,128)S(1)}, u32[]{:S(2)}, u32[]{:S(2)}) collective-permute-start(f32[64,128]{1,0:T(8,128)S(1)} %get-tuple-element.22), channel_id=1, source_target_pairs={{2,5},{3,4},{6,9},{7,8},{10,13},{11,12},{14,17},{15,16},{18,21},{1... | collective-permute-start | bytes 98312 | tf_op jit(solution)/shard_map/ppermute | solution.py:514
  4.2 8.0 %collective-permute-start.3 = (f32[64,128]{1,0:T(8,128)S(1)}, f32[64,128]{1,0:T(8,128)S(1)}, u32[]{:S(2)}, u32[]{:S(2)}) collective-permute-start(f32[64,128]{1,0:T(8,128)S(1)} %get-tuple-element.23), channel_id=1, source_target_pairs={{0,3},{1,2},{4,7},{5,6},{8,11},{9,10},{12,15},{13,14},{16,19},{17,... | collective-permute-start | bytes 98312 | tf_op jit(solution)/shard_map/ppermute | solution.py:514
  5.4 6.8 %collective-permute-start = (f32[2,64,256]{2,1,0:T(8,128)S(1)}, f32[2,64,256]{2,1,0:T(8,128)S(1)}, u32[]{:S(2)}, u32[]{:S(2)}) collective-permute-start(f32[2,64,256]{2,1,0:T(8,128)S(1)} %get-tuple-element.20), channel_id=1, source_target_pairs={{2,4},{3,5},{6,8},{7,9},{10,12},{11,13},{14,16},{15,17},{18,20},{1... | collective-permute-start | bytes 393224 | tf_op jit(solution)/shard_map/ppermute | solution.py:510
  6.9 6.3 %collective-permute-start.1 = (f32[256,128]{1,0:T(8,128)S(1)}, f32[256,128]{1,0:T(8,128)S(1)}, u32[]{:S(2)}, u32[]{:S(2)}) collective-permute-start(f32[256,128]{1,0:T(8,128)S(1)} %get-tuple-element.21), channel_id=1, source_target_pairs={{0,1},{1,0},{2,3},{3,2},{4,5},{5,4},{6,7},{7,6},{8,9},{9,8},{10,11... | collective-permute-start | bytes 393224 | tf_op jit(solution)/shard_map/ppermute | solution.py:517
  7.4 5.8 %collective-permute-start.4 = (f32[2,64,256]{2,1,0:T(8,128)S(1)}, f32[2,64,256]{2,1,0:T(8,128)S(1)}, u32[]{:S(2)}, u32[]{:S(2)}) collective-permute-start(f32[2,64,256]{2,1,0:T(8,128)S(1)} %get-tuple-element.24), channel_id=1, source_target_pairs={{0,2},{1,3},{4,6},{5,7},{8,10},{9,11},{12,14},{13,15},{16,18},{17,... | collective-permute-start | bytes 393224 | tf_op jit(solution)/shard_map/ppermute | solution.py:510
  8.9 4.3 %copy-start.1 = (f32[2,256,256]{2,1,0:T(8,128)S(1)}, f32[2,256,256]{2,1,0:T(8,128)}, u32[]{:S(2)}) copy-start(f32[2,256,256]{2,1,0:T(8,128)} %object_ref.3) | copy-start | bytes 1572868
  8.9 4.3 %copy-start.2 = (bf16[4,256,512]{2,1,0:T(8,128)(2,1)S(1)}, bf16[4,256,512]{2,1,0:T(8,128)(2,1)}, u32[]{:S(2)}) copy-start(bf16[4,256,512]{2,1,0:T(8,128)(2,1)} %constant.5.clone.rest_5_) | copy-start | bytes 3145732
  8.9 4.3 %copy-start.3 = (bf16[4,512,256]{2,1,0:T(8,128)(2,1)S(1)}, bf16[4,512,256]{2,1,0:T(8,128)(2,1)}, u32[]{:S(2)}) copy-start(bf16[4,512,256]{2,1,0:T(8,128)(2,1)} %constant.4.clone.rest_4_) | copy-start | bytes 3145732
  18.5 9.0 %collective-permute-start.5 = (f32[2,64,256]{2,1,0:T(8,128)S(1)}, f32[2,64,256]{2,1,0:T(8,128)S(1)}, u32[]{:S(2)}, u32[]{:S(2)}) collective-permute-start(f32[2,64,256]{2,1,0:T(8,128)S(1)} %get-tuple-element.26), channel_id=1, source_target_pairs={{2,4},{3,5},{6,8},{7,9},{10,12},{11,13},{14,16},{15,17},{18,20},{1... | collective-permute-start | bytes 393224 | tf_op jit(solution)/shard_map/ppermute | solution.py:510
  20.1 7.4 %collective-permute-start.6 = (f32[256,128]{1,0:T(8,128)S(1)}, f32[256,128]{1,0:T(8,128)S(1)}, u32[]{:S(2)}, u32[]{:S(2)}) collective-permute-start(f32[256,128]{1,0:T(8,128)S(1)} %get-tuple-element.27), channel_id=1, source_target_pairs={{0,1},{1,0},{2,3},{3,2},{4,5},{5,4},{6,7},{7,6},{8,9},{9,8},{10,11... | collective-permute-start | bytes 393224 | tf_op jit(solution)/shard_map/ppermute | solution.py:517
  20.6 6.9 %collective-permute-start.9 = (f32[2,64,256]{2,1,0:T(8,128)S(1)}, f32[2,64,256]{2,1,0:T(8,128)S(1)}, u32[]{:S(2)}, u32[]{:S(2)}) collective-permute-start(f32[2,64,256]{2,1,0:T(8,128)S(1)} %get-tuple-element.30), channel_id=1, source_target_pairs={{0,2},{1,3},{4,6},{5,7},{8,10},{9,11},{12,14},{13,15},{16,18},{17,... | collective-permute-start | bytes 393224 | tf_op jit(solution)/shard_map/ppermute | solution.py:510
  20.6 6.9 %collective-permute-start.7 = (f32[64,128]{1,0:T(8,128)S(1)}, f32[64,128]{1,0:T(8,128)S(1)}, u32[]{:S(2)}, u32[]{:S(2)}) collective-permute-start(f32[64,128]{1,0:T(8,128)S(1)} %get-tuple-element.28), channel_id=1, source_target_pairs={{2,5},{3,4},{6,9},{7,8},{10,13},{11,12},{14,17},{15,16},{18,21},{1... | collective-permute-start | bytes 98312 | tf_op jit(solution)/shard_map/ppermute | solution.py:514
  22.1 5.4 %collective-permute-start.8 = (f32[64,128]{1,0:T(8,128)S(1)}, f32[64,128]{1,0:T(8,128)S(1)}, u32[]{:S(2)}, u32[]{:S(2)}) collective-permute-start(f32[64,128]{1,0:T(8,128)S(1)} %get-tuple-element.29), channel_id=1, source_target_pairs={{0,3},{1,2},{4,7},{5,6},{8,11},{9,10},{12,15},{13,14},{16,19},{17,... | collective-permute-start | bytes 98312 | tf_op jit(solution)/shard_map/ppermute | solution.py:514

commit v5 on v4

--- a/solution.py
+++ b/solution.py
@@ -212,14 +212,15 @@
             pltpu.SemaphoreType.DMA((3 + views,)),
         ],
         compiler_params=pltpu.CompilerParams(vmem_limit_bytes=16 * 1024 * 1024),
-        cost_estimate=pl.CostEstimate(flops=2 * 10**9, bytes_accessed=6 * 10**6, transcendentals=0),
+        cost_estimate=pl.CostEstimate(flops=10**9, bytes_accessed=10**5, transcendentals=0),
     )(offsets, counts, probe, intensity)
 
 
-def views_kernel(chans, offsets_in, counts, core, placed, amplitude, b_in, *rest):
+def views_kernel(chans, offsets_in, counts, core, placed, amplitude, *rest):
     count = len(chans)
-    x_in, kb_in, ka_in = rest[:count], rest[count : 2 * count], rest[2 * count : 3 * count]
-    a_in, right, left, *rest = rest[3 * count :]
+    x_in, b_in, rest = rest[:count], rest[count], rest[count + 1 :]
+    kb_in, ka_in = rest[:count], rest[count : 2 * count]
+    a_in, right, left, *rest = rest[2 * count :]
     g_core, g_a, g_b = rest[:3]
     g_x, g_ka = rest[3 : 3 + count], rest[3 + count : 3 + 2 * count]
     g_kb = rest[3 + 2 * count : 3 + 3 * count]
@@ -444,14 +445,15 @@
             wide, full, tall, full, tall, full, wide, full,
         ],
         compiler_params=pltpu.CompilerParams(vmem_limit_bytes=40 * 1024 * 1024),
-    )(offsets, counts, core, placed, amplitude, b_in, *x_in, *kb_in, *ka_in, a_in, *tables)
+    )(offsets, counts, core, placed, amplitude, *x_in, b_in, *kb_in, *ka_in, a_in, *tables)
     return (*outs[:3], outs[3 : 3 + count], outs[3 + count : 3 + 2 * count], outs[3 + 2 * count :])
 
 
-def finish_kernel(chans, object_ref, g_core, b_in, *rest):
+def finish_kernel(chans, object_ref, g_core, *rest):
     count = len(chans)
-    x_in, kb_in, ka_in = rest[:count], rest[count : 2 * count], rest[2 * count : 3 * count]
-    a_in, out = rest[3 * count :]
+    x_in, b_in, rest = rest[:count], rest[count], rest[count + 1 :]
+    kb_in, ka_in = rest[:count], rest[count : 2 * count]
+    a_in, out = rest[2 * count :]
     size = object_ref.shape[1]
     lower = lower_partner()
     a_rows = pl.ds(pl.multiple_of(jnp.where(lower, size - MARGIN, 0), MARGIN), MARGIN)
@@ -494,7 +496,7 @@
         in_specs=[vmem] * (4 + 3 * len(chans)),
         out_specs=vmem,
         compiler_params=pltpu.CompilerParams(vmem_limit_bytes=6 * 1024 * 1024),
-    )(object_field, g_core, b_in, *x_in, *kb_in, *ka_in, a_in)
+    )(object_field, g_core, *x_in, b_in, *kb_in, *ka_in, a_in)
 
 
 def per_device(object_field, probe_field, intensity, view_offsets, view_counts):

time: 28.7 us -> 26.9 us (0.937)
  waiting for transfers between devices: 6.22 us -> 2.92 us
  starting transfers between devices: 10.8 us -> 12.3 us
    ppermute x2, starting transfers between devices: 1.07 us -> 3.61 us  [exchange(): lax.ppermute(block, 'col', channel[0])]
    ppermute x4, waiting for transfers between devices: 5.26 us -> 2.9 us  [across(): lax.ppermute(block, ('row', 'col'), route + (extra if mesh_cols == 2 else...]
    ppermute x2, waiting for transfers between devices: 0.95 us -> 0.01 us  [exchange(): lax.ppermute(block, 'col', channel[0])]
    ppermute x4, starting transfers between devices: 3.87 us -> 3.27 us  [over_rows(): return lax.ppermute(block, ('row', 'col'), route + extra)]
    ppermute x4, starting transfers between devices: 5.86 us -> 5.41 us  [across(): lax.ppermute(block, ('row', 'col'), route + (extra if mesh_cols == 2 else...]
  transfers between devices with their start and end apart: 10 -> 10, of which waited for: 2 -> 2; matrix products, arithmetic and copies ran while one was open for 0% -> 0% of each run, Pallas kernels for 11% -> 12%
where the time goes in v5:
time: 26.9 us; the launch traced here: 26.7 us
  starting transfers between devices  12.3 us (46%)
  Pallas kernels  9.69 us (36%)
  waiting for transfers between devices  2.92 us (11%)
  local copies, waits for them, and re-layouts  1.05 us (4%)
  between operations  0.75 us (3%)
    ppermute x4, starting transfers between devices, across(): lax.ppermute(block, ('row', 'col'), route + (extra if mesh_cols == 2 else...  5.41 us
    pallas_call x1, Pallas kernels, views_call(): pl.pallas_call(functools.partial(views_kernel, chans), out_shape=[jax.Sha...  5.3 us
    ppermute x2, starting transfers between devices, exchange(): lax.ppermute(block, 'col', channel[0])  3.61 us
    ppermute x4, starting transfers between devices, over_rows(): return lax.ppermute(block, ('row', 'col'), route + extra)  3.27 us
    pallas_call x1, Pallas kernels, prepare_call(): pl.pallas_call(prepare_kernel, out_shape=[jax.ShapeDtypeStruct((views, 2,...  3.25 us
    ppermute x4, waiting for transfers between devices, across(): lax.ppermute(block, ('row', 'col'), route + (extra if mesh_cols == 2 else...  2.9 us
    unnamed x8, local copies, waits for them, and re-layouts  1.05 us
    pallas_call x1, Pallas kernels, finish_call(): pl.pallas_call(functools.partial(finish_kernel, chans), out_shape=jax.Sha...  1 us
  transfers between devices with their start and end apart: 10, of which 2 were waited for; matrix products, arithmetic and copies ran while one was open for 0% of the time, Pallas kernels for 12%

profile of v5, /device:TPU:0, one launch (start us, length us, event | category | flops | bytes accessed | tf_op | source)
XLA Modules:
  0.0 26.7 jit_solution(17987206647664093390)
XLA Ops:
  0.0 0.0 copy-start
  0.0 1.0 %copy-done = f32[2,256,256]{2,1,0:T(8,128)S(1)} copy-done((f32[2,256,256]{2,1,0:T(8,128)S(1)}, f32[2,256,256]{2,1,0:T(8,128)}, u32[]{:S(2)}) %copy-start) | copy-done | bytes 524312
  1.0 0.0 copy-start.1
  1.0 0.0 copy-start.2
  1.0 0.0 copy-start.3
  1.0 0.1 shard_map.74
  1.2 3.0 %collective-permute-start = (f32[256,128]{1,0:T(8,128)S(1)}, f32[256,128]{1,0:T(8,128)S(1)}, u32[]{:S(2)}, u32[]{:S(2)}) collective-permute-start(f32[256,128]{1,0:T(8,128)S(1)} %get-tuple-element.20), channel_id=1, source_target_pairs={{0,1},{1,0},{2,3},{3,2},{4,5},{5,4},{6,7},{7,6},{8,9},{9,8},{10,11... | collective-permute-start | bytes 393224 | tf_op jit(solution)/shard_map/ppermute | solution.py:519
  4.2 0.1 collective-permute-start.1
  4.3 1.6 %collective-permute-start.4 = (f32[2,64,256]{2,1,0:T(8,128)S(1)}, f32[2,64,256]{2,1,0:T(8,128)S(1)}, u32[]{:S(2)}, u32[]{:S(2)}) collective-permute-start(f32[2,64,256]{2,1,0:T(8,128)S(1)} %get-tuple-element.24), channel_id=1, source_target_pairs={{0,2},{1,3},{4,6},{5,7},{8,10},{9,11},{12,14},{13,15},{16,18},{17,... | collective-permute-start | bytes 393224 | tf_op jit(solution)/shard_map/ppermute | solution.py:512
  5.8 0.5 %collective-permute-start.2 = (f32[64,128]{1,0:T(8,128)S(1)}, f32[64,128]{1,0:T(8,128)S(1)}, u32[]{:S(2)}, u32[]{:S(2)}) collective-permute-start(f32[64,128]{1,0:T(8,128)S(1)} %get-tuple-element.22), channel_id=1, source_target_pairs={{2,5},{3,4},{6,9},{7,8},{10,13},{11,12},{14,17},{15,16},{18,21},{1... | collective-permute-start | bytes 98312 | tf_op jit(solution)/shard_map/ppermute | solution.py:516
  6.4 2.2 %collective-permute-start.3 = (f32[64,128]{1,0:T(8,128)S(1)}, f32[64,128]{1,0:T(8,128)S(1)}, u32[]{:S(2)}, u32[]{:S(2)}) collective-permute-start(f32[64,128]{1,0:T(8,128)S(1)} %get-tuple-element.23), channel_id=1, source_target_pairs={{0,3},{1,2},{4,7},{5,6},{8,11},{9,10},{12,15},{13,14},{16,19},{17,... | collective-permute-start | bytes 98312 | tf_op jit(solution)/shard_map/ppermute | solution.py:516
  9.2 3.2 %shard_map.73 = (f32[4,2,256,256]{3,2,1,0:T(8,128)S(1)}, f32[4,2,256,128]{3,2,1,0:T(8,128)S(1)}) custom-call(s32[1,1,2,4]{3,2,1,0:T(2,128)} %bitcast.1, s32[1,1]{1,0:T(1,128)S(6)} %copy.8.counts, f32[2,256,256]{2,1,0:T(8,128)} %probe.1, f32[1,1,4,256,256]{4,3,2,1,0:T(8,128)} %intensity.1), custom_call_target="tpu_custom_call" | custom-call | flops 1000000000 | bytes 100000 | tf_op jit(solution)/shard_map/pallas_call | solution.py:200
  12.4 0.0 collective-permute-done.2.rest_2_
  12.4 0.0 collective-permute-done.3.rest_3_
  12.5 0.0 collective-permute-done.rest_0_
  12.5 0.0 collective-permute-done.1.rest_1_
  12.5 0.0 collective-permute-done.4.rest_4_
  12.5 0.0 copy-done.1
  12.5 0.0 copy-done.2
  12.5 0.0 copy-done.3
  12.5 5.3 %shard_map.75 = (f32[2,256,256]{2,1,0:T(8,128)S(1)}, f32[2,64,256]{2,1,0:T(8,128)S(1)}, f32[2,64,256]{2,1,0:T(8,128)S(1)}, f32[256,128]{1,0:T(8,128)S(1)}, f32[64,128]{1,0:T(8,128)S(1)}, /*index=5*/f32[64,128]{1,0:T(8,128)S(1)}) custom-call(s32[1,1,2,4]{3,2,1,0:T(2,128)} %bitcast.2, s32[1,1]{1,0:T(1,128)S(6)} %copy.8.counts, f32[2,256,256]{2,1,0:T(8,128)S(1)} %copy-done.1, ...), custom_call_target="tpu_custom_call" | custom-call | tf_op jit(solution)/shard_map/pallas_call | solution.py:430
  17.8 0.6 %collective-permute-start.5 = (f32[256,128]{1,0:T(8,128)S(1)}, f32[256,128]{1,0:T(8,128)S(1)}, u32[]{:S(2)}, u32[]{:S(2)}) collective-permute-start(f32[256,128]{1,0:T(8,128)S(1)} %get-tuple-element.26), channel_id=1, source_target_pairs={{0,1},{1,0},{2,3},{3,2},{4,5},{5,4},{6,7},{7,6},{8,9},{9,8},{10,11... | collective-permute-start | bytes 393224 | tf_op jit(solution)/shard_map/ppermute | solution.py:519
  18.4 1.5 %collective-permute-start.6 = (f32[2,64,256]{2,1,0:T(8,128)S(1)}, f32[2,64,256]{2,1,0:T(8,128)S(1)}, u32[]{:S(2)}, u32[]{:S(2)}) collective-permute-start(f32[2,64,256]{2,1,0:T(8,128)S(1)} %get-tuple-element.27), channel_id=1, source_target_pairs={{2,4},{3,5},{6,8},{7,9},{10,12},{11,13},{14,16},{15,17},{18,20},{1... | collective-permute-start | bytes 393224 | tf_op jit(solution)/shard_map/ppermute | solution.py:512
  19.9 0.1 collective-permute-start.9
  20.1 1.5 %collective-permute-start.7 = (f32[64,128]{1,0:T(8,128)S(1)}, f32[64,128]{1,0:T(8,128)S(1)}, u32[]{:S(2)}, u32[]{:S(2)}) collective-permute-start(f32[64,128]{1,0:T(8,128)S(1)} %get-tuple-element.28), channel_id=1, source_target_pairs={{2,5},{3,4},{6,9},{7,8},{10,13},{11,12},{14,17},{15,16},{18,21},{1... | collective-permute-start | bytes 98312 | tf_op jit(solution)/shard_map/ppermute | solution.py:516
  21.6 1.2 %collective-permute-start.8 = (f32[64,128]{1,0:T(8,128)S(1)}, f32[64,128]{1,0:T(8,128)S(1)}, u32[]{:S(2)}, u32[]{:S(2)}) collective-permute-start(f32[64,128]{1,0:T(8,128)S(1)} %get-tuple-element.29), channel_id=1, source_target_pairs={{0,3},{1,2},{4,7},{5,6},{8,11},{9,10},{12,15},{13,14},{16,19},{17,... | collective-permute-start | bytes 98312 | tf_op jit(solution)/shard_map/ppermute | solution.py:516
  22.8 2.4 %collective-permute-done.7.rest_2_ = f32[64,128]{1,0:T(8,128)S(1)} collective-permute-done((f32[64,128]{1,0:T(8,128)S(1)}, f32[64,128]{1,0:T(8,128)S(1)}, u32[]{:S(2)}, u32[]{:S(2)}) %collective-permute-start.7) | collective-permute-done | bytes 32800 | tf_op jit(solution)/shard_map/ppermute | solution.py:516
  25.2 0.5 %collective-permute-done.8.rest_3_ = f32[64,128]{1,0:T(8,128)S(1)} collective-permute-done((f32[64,128]{1,0:T(8,128)S(1)}, f32[64,128]{1,0:T(8,128)S(1)}, u32[]{:S(2)}, u32[]{:S(2)}) %collective-permute-start.8) | collective-permute-done | bytes 32800 | tf_op jit(solution)/shard_map/ppermute | solution.py:516
  25.7 0.0 collective-permute-done.5.rest_0_
  25.7 0.0 collective-permute-done.6.rest_1_
  25.7 0.0 collective-permute-done.9.rest_4_
  25.7 1.0 %shard_map.76 = f32[2,256,256]{2,1,0:T(8,128)} custom-call(f32[2,256,256]{2,1,0:T(8,128)S(1)} %copy-done.1, f32[2,256,256]{2,1,0:T(8,128)S(1)} %get-tuple-element.25.g_core, f32[256,128]{1,0:T(8,128)S(1)} %collective-permute-done.5.rest_0_, f32[2,64,256]{2,1,0:T(8,128)S(1)} %collective-permute-done.6.rest_1_, f32[64,128]{1,0:T(8,128)S(1)} %collective-permute-done.7.rest_2_, ...), custom_call_target="tpu_custom_call" | custom-call | tf_op jit(solution)/shard_map/pallas_call | solution.py:493
Async XLA Ops:
  0.0 1.0 %copy-start = (f32[2,256,256]{2,1,0:T(8,128)S(1)}, f32[2,256,256]{2,1,0:T(8,128)}, u32[]{:S(2)}) copy-start(f32[2,256,256]{2,1,0:T(8,128)} %object_ref.3) | copy-start | bytes 1572868
  1.0 11.4 %copy-start.1 = (f32[2,256,256]{2,1,0:T(8,128)S(1)}, f32[2,256,256]{2,1,0:T(8,128)}, u32[]{:S(2)}) copy-start(f32[2,256,256]{2,1,0:T(8,128)} %object_ref.3) | copy-start | bytes 1572868
  1.0 11.5 %copy-start.2 = (bf16[4,256,512]{2,1,0:T(8,128)(2,1)S(1)}, bf16[4,256,512]{2,1,0:T(8,128)(2,1)}, u32[]{:S(2)}) copy-start(bf16[4,256,512]{2,1,0:T(8,128)(2,1)} %constant.5.clone.rest_6_) | copy-start | bytes 3145732
  1.0 11.5 %copy-start.3 = (bf16[4,512,256]{2,1,0:T(8,128)(2,1)S(1)}, bf16[4,512,256]{2,1,0:T(8,128)(2,1)}, u32[]{:S(2)}) copy-start(bf16[4,512,256]{2,1,0:T(8,128)(2,1)} %constant.4.clone.rest_5_) | copy-start | bytes 3145732
  1.2 11.3 %collective-permute-start = (f32[256,128]{1,0:T(8,128)S(1)}, f32[256,128]{1,0:T(8,128)S(1)}, u32[]{:S(2)}, u32[]{:S(2)}) collective-permute-start(f32[256,128]{1,0:T(8,128)S(1)} %get-tuple-element.20), channel_id=1, source_target_pairs={{0,1},{1,0},{2,3},{3,2},{4,5},{5,4},{6,7},{7,6},{8,9},{9,8},{10,11... | collective-permute-start | bytes 393224 | tf_op jit(solution)/shard_map/ppermute | solution.py:519
  4.2 8.3 %collective-permute-start.1 = (f32[2,64,256]{2,1,0:T(8,128)S(1)}, f32[2,64,256]{2,1,0:T(8,128)S(1)}, u32[]{:S(2)}, u32[]{:S(2)}) collective-permute-start(f32[2,64,256]{2,1,0:T(8,128)S(1)} %get-tuple-element.21), channel_id=1, source_target_pairs={{2,4},{3,5},{6,8},{7,9},{10,12},{11,13},{14,16},{15,17},{18,20},{1... | collective-permute-start | bytes 393224 | tf_op jit(solution)/shard_map/ppermute | solution.py:512
  4.3 8.2 %collective-permute-start.4 = (f32[2,64,256]{2,1,0:T(8,128)S(1)}, f32[2,64,256]{2,1,0:T(8,128)S(1)}, u32[]{:S(2)}, u32[]{:S(2)}) collective-permute-start(f32[2,64,256]{2,1,0:T(8,128)S(1)} %get-tuple-element.24), channel_id=1, source_target_pairs={{0,2},{1,3},{4,6},{5,7},{8,10},{9,11},{12,14},{13,15},{16,18},{17,... | collective-permute-start | bytes 393224 | tf_op jit(solution)/shard_map/ppermute | solution.py:512
  5.8 6.6 %collective-permute-start.2 = (f32[64,128]{1,0:T(8,128)S(1)}, f32[64,128]{1,0:T(8,128)S(1)}, u32[]{:S(2)}, u32[]{:S(2)}) collective-permute-start(f32[64,128]{1,0:T(8,128)S(1)} %get-tuple-element.22), channel_id=1, source_target_pairs={{2,5},{3,4},{6,9},{7,8},{10,13},{11,12},{14,17},{15,16},{18,21},{1... | collective-permute-start | bytes 98312 | tf_op jit(solution)/shard_map/ppermute | solution.py:516
  6.4 6.1 %collective-permute-start.3 = (f32[64,128]{1,0:T(8,128)S(1)}, f32[64,128]{1,0:T(8,128)S(1)}, u32[]{:S(2)}, u32[]{:S(2)}) collective-permute-start(f32[64,128]{1,0:T(8,128)S(1)} %get-tuple-element.23), channel_id=1, source_target_pairs={{0,3},{1,2},{4,7},{5,6},{8,11},{9,10},{12,15},{13,14},{16,19},{17,... | collective-permute-start | bytes 98312 | tf_op jit(solution)/shard_map/ppermute | solution.py:516
  17.8 7.8 %collective-permute-start.5 = (f32[256,128]{1,0:T(8,128)S(1)}, f32[256,128]{1,0:T(8,128)S(1)}, u32[]{:S(2)}, u32[]{:S(2)}) collective-permute-start(f32[256,128]{1,0:T(8,128)S(1)} %get-tuple-element.26), channel_id=1, source_target_pairs={{0,1},{1,0},{2,3},{3,2},{4,5},{5,4},{6,7},{7,6},{8,9},{9,8},{10,11... | collective-permute-start | bytes 393224 | tf_op jit(solution)/shard_map/ppermute | solution.py:519
  18.4 7.2 %collective-permute-start.6 = (f32[2,64,256]{2,1,0:T(8,128)S(1)}, f32[2,64,256]{2,1,0:T(8,128)S(1)}, u32[]{:S(2)}, u32[]{:S(2)}) collective-permute-start(f32[2,64,256]{2,1,0:T(8,128)S(1)} %get-tuple-element.27), channel_id=1, source_target_pairs={{2,4},{3,5},{6,8},{7,9},{10,12},{11,13},{14,16},{15,17},{18,20},{1... | collective-permute-start | bytes 393224 | tf_op jit(solution)/shard_map/ppermute | solution.py:512
  19.9 5.8 %collective-permute-start.9 = (f32[2,64,256]{2,1,0:T(8,128)S(1)}, f32[2,64,256]{2,1,0:T(8,128)S(1)}, u32[]{:S(2)}, u32[]{:S(2)}) collective-permute-start(f32[2,64,256]{2,1,0:T(8,128)S(1)} %get-tuple-element.30), channel_id=1, source_target_pairs={{0,2},{1,3},{4,6},{5,7},{8,10},{9,11},{12,14},{13,15},{16,18},{17,... | collective-permute-start | bytes 393224 | tf_op jit(solution)/shard_map/ppermute | solution.py:512
  20.1 5.1 %collective-permute-start.7 = (f32[64,128]{1,0:T(8,128)S(1)}, f32[64,128]{1,0:T(8,128)S(1)}, u32[]{:S(2)}, u32[]{:S(2)}) collective-permute-start(f32[64,128]{1,0:T(8,128)S(1)} %get-tuple-element.28), channel_id=1, source_target_pairs={{2,5},{3,4},{6,9},{7,8},{10,13},{11,12},{14,17},{15,16},{18,21},{1... | collective-permute-start | bytes 98312 | tf_op jit(solution)/shard_map/ppermute | solution.py:516
  21.6 4.1 %collective-permute-start.8 = (f32[64,128]{1,0:T(8,128)S(1)}, f32[64,128]{1,0:T(8,128)S(1)}, u32[]{:S(2)}, u32[]{:S(2)}) collective-permute-start(f32[64,128]{1,0:T(8,128)S(1)} %get-tuple-element.29), channel_id=1, source_target_pairs={{0,3},{1,2},{4,7},{5,6},{8,11},{9,10},{12,15},{13,14},{16,19},{17,... | collective-permute-start | bytes 98312 | tf_op jit(solution)/shard_map/ppermute | solution.py:516

commit v6 on v5

--- a/solution.py
+++ b/solution.py
@@ -154,22 +154,13 @@
     )(object_field)
 
 
-def prepare_kernel(
-    offsets_in, counts, probe, intensity, placed, amplitude, offsets, doubled, measured, sems
-):
-    views, size = measured.shape[0], probe.shape[1]
-    half = size // 2
+def prepare_kernel(offsets_in, probe, placed, offsets, doubled, sems):
+    views, size = placed.shape[0], probe.shape[1]
     copies = fetch(
-        [(offsets_in, offsets)]
-        + [(probe, doubled.at[:, pl.ds(size * i, size)]) for i in range(2)]
-        + [(intensity.at[0, 0, view], measured.at[view]) for view in range(views)],
-        sems,
+        [(offsets_in, offsets)] + [(probe, doubled.at[:, pl.ds(size * i, size)]) for i in range(2)], sems
     )
-    source = lax.broadcasted_iota(jnp.int32, (size, size), 0)
-    target = lax.broadcasted_iota(jnp.int32, (size, size), 1)
-    order = (target == (source % 2) * half + source // 2).astype(F32).astype(BF16)
     sublane = lax.broadcasted_iota(jnp.int32, (1, 8, 1), 1)
-    for copy in copies[:3]:
+    for copy in copies:
         copy.wait()
     for view in range(views):
         shift_row = lax.rem(offsets[0, 0, 0, view] - MARGIN + size, size)
@@ -184,39 +175,27 @@
                 block = pltpu.roll(block, lax.rem(8 - rest, 8), 1)
                 block = jnp.where(sublane < 8 - rest, block[:-1], block[1:])
                 placed[view, part, row : row + CHUNK] = block.reshape(CHUNK, size)
-    for view in range(views):
-        copies[3 + view].wait()
-        valid = (view < counts[0, 0]).astype(F32)
-        power = measured[view] + smooth_eps
-        high, low = split(power * lax.rsqrt(power) * valid)
-        ordered = dot(high, order) + dot(low, order)
-        amplitude[view, 0] = ordered[:, :half]
-        amplitude[view, 1] = ordered[:, half:]
-
-
-def prepare_call(offsets, counts, probe, intensity):
-    views, size = intensity.shape[2], probe.shape[1]
+
+
+def prepare_call(offsets, probe):
+    views, size = offsets.shape[3], probe.shape[1]
     vmem, hbm = pl.BlockSpec(memory_space=pltpu.VMEM), pl.BlockSpec(memory_space=pltpu.HBM)
     return pl.pallas_call(
         prepare_kernel,
-        out_shape=[
-            jax.ShapeDtypeStruct((views, 2, size, size), F32),
-            jax.ShapeDtypeStruct((views, 2, size, size // 2), F32),
-        ],
-        in_specs=[hbm, pl.BlockSpec(memory_space=pltpu.SMEM), hbm, hbm],
-        out_specs=[vmem] * 2,
+        out_shape=jax.ShapeDtypeStruct((views, 2, size, size), F32),
+        in_specs=[hbm, hbm],
+        out_specs=vmem,
         scratch_shapes=[
             pltpu.SMEM(offsets.shape, jnp.int32),
             pltpu.VMEM((2, 2 * size, size), F32),
-            pltpu.VMEM((views, size, size), F32),
-            pltpu.SemaphoreType.DMA((3 + views,)),
+            pltpu.SemaphoreType.DMA((3,)),
         ],
         compiler_params=pltpu.CompilerParams(vmem_limit_bytes=16 * 1024 * 1024),
         cost_estimate=pl.CostEstimate(flops=10**9, bytes_accessed=10**5, transcendentals=0),
-    )(offsets, counts, probe, intensity)
-
-
-def views_kernel(chans, offsets_in, counts, core, placed, amplitude, *rest):
+    )(offsets, probe)
+
+
+def views_kernel(chans, offsets_in, counts, core, placed, intensity, *rest):
     count = len(chans)
     x_in, b_in, rest = rest[:count], rest[count], rest[count + 1 :]
     kb_in, ka_in = rest[:count], rest[count : 2 * count]
@@ -224,7 +203,7 @@
     g_core, g_a, g_b = rest[:3]
     g_x, g_ka = rest[3 : 3 + count], rest[3 + count : 3 + 2 * count]
     g_kb = rest[3 + 2 * count : 3 + 3 * count]
-    offsets, sem, cols_m, rows_m, corner_m, s1, y, s2, z, s3, u, s4, g = rest[3 + 3 * count :]
+    offsets, sem, amplitude, cols_m, rows_m, corner_m, s1, y, s2, z, s3, u, s4, g = rest[3 + 3 * count :]
     (offsets_copy,) = fetch([(offsets_in, offsets)], sem)
     views, size = placed.shape[0], core.shape[1]
     half, m = size // 2, MARGIN
@@ -327,10 +306,22 @@
                     put_below(s2.at[view, 0], part * half + row, odd * half, above + below)
                     put_below(s2.at[view, 1], part * half + row, odd * half, above - below)
                 yield
+        valid = (view < counts[0, 0]).astype(F32)
+        for row in range(0, size, CHUNK):
+            rows = slice(row, row + CHUNK)
+            lanes = lax.broadcasted_iota(jnp.int32, (CHUNK, LANES), 1)
+            wanted = []
+            for block in range(2):
+                power = intensity[0, 0, view, rows, block * LANES : (block + 1) * LANES] + smooth_eps
+                wanted.append(power * lax.rsqrt(power) * valid)
+            for odd in range(2):
+                taken = lax.rem(2 * lanes + odd, LANES)
+                ordered = [jnp.take_along_axis(block, taken, axis=1) for block in wanted]
+                amplitude[view, odd, rows] = jnp.where(lanes < LANES // 2, *ordered)
+        yield
         for odd in range(2):
             z[view, odd] = by_left(odd, s2.at[view, odd])
             yield
-        valid = (view < counts[0, 0]).astype(F32)
         for odd in range(2):
             for row in range(0, half, CHUNK):
                 re, im = z[view, odd, row : row + CHUNK], z[view, odd, half + row : half + row + CHUNK]
@@ -418,7 +409,7 @@
         g_kb[number][...] = jnp.where(lower, above, below)
 
 
-def views_call(chans, offsets, counts, core, placed, amplitude, tables, a_in, b_in, x_in, ka_in, kb_in):
+def views_call(chans, offsets, counts, core, placed, intensity, tables, a_in, b_in, x_in, ka_in, kb_in):
     views, size = placed.shape[0], core.shape[1]
     count = len(chans)
     vmem = pl.BlockSpec(memory_space=pltpu.VMEM)
@@ -439,13 +430,14 @@
         scratch_shapes=[
             pltpu.SMEM(offsets.shape, jnp.int32),
             pltpu.SemaphoreType.DMA((1,)),
+            pltpu.VMEM((views, 2, size, size // 2), F32),
             pltpu.VMEM((2, size, LANES), F32),
             pltpu.VMEM((2, 2 * MARGIN, size), F32),
             pltpu.VMEM((2, 2 * MARGIN, LANES), F32),
             wide, full, tall, full, tall, full, wide, full,
         ],
         compiler_params=pltpu.CompilerParams(vmem_limit_bytes=40 * 1024 * 1024),
-    )(offsets, counts, core, placed, amplitude, *x_in, b_in, *kb_in, *ka_in, a_in, *tables)
+    )(offsets, counts, core, placed, intensity, *x_in, b_in, *kb_in, *ka_in, a_in, *tables)
     return (*outs[:3], outs[3 : 3 + count], outs[3 + count : 3 + 2 * count], outs[3 + 2 * count :])
 
 
@@ -524,14 +516,14 @@
         return a_in, b_in, x_in, ka_in, kb_in
 
     packs = pack_call(object_field, chans)
-    offsets, probe, measured = (
+    offsets, probe = (
         pltpu.with_memory_space_constraint(array, pltpu.HBM)
-        for array in (jnp.swapaxes(view_offsets, 2, 3), probe_field, intensity)
+        for array in (jnp.swapaxes(view_offsets, 2, 3), probe_field)
     )
     margins = exchange(packs[0], packs[1], packs[2::3], packs[3::3], packs[4::3])
-    placed, amplitude = prepare_call(offsets, view_counts, probe, measured)
+    placed = prepare_call(offsets, probe)
     g_core, *sends = views_call(
-        chans, offsets, view_counts, object_field, placed, amplitude, tables, *margins
+        chans, offsets, view_counts, object_field, placed, intensity, tables, *margins
     )
     return finish_call(chans, object_field, g_core, *exchange(*sends))
 

time: 26.9 us -> 25.6 us (0.952)
  Pallas kernels: 9.69 us -> 8.45 us
  waiting for transfers between devices: 2.92 us -> 2.33 us
  starting transfers between devices: 12.3 us -> 12.6 us
    pallas_call x1, Pallas kernels: 3.25 us -> 1.9 us  [prepare_call(): pl.pallas_call(prepare_kernel, out_shape=jax.ShapeDtypeStruct((views, 2,...]
    ppermute x4, waiting for transfers between devices: 2.9 us -> 2.32 us  [across(): lax.ppermute(block, ('row', 'col'), route + (extra if mesh_cols == 2 else...]
    ppermute x2, starting transfers between devices: 3.61 us -> 4.19 us  [exchange(): lax.ppermute(block, 'col', channel[0])]
    ppermute x4, starting transfers between devices: 3.27 us -> 2.69 us  [over_rows(): return lax.ppermute(block, ('row', 'col'), route + extra)]
    ppermute x4, starting transfers between devices: 5.41 us -> 5.73 us  [across(): lax.ppermute(block, ('row', 'col'), route + (extra if mesh_cols == 2 else...]
    unnamed x8 -> x10, local copies, waits for them, and re-layouts: 1.05 us -> 1.06 us
  transfers between devices with their start and end apart: 10 -> 10, of which waited for: 2 -> 2; matrix products, arithmetic and copies ran while one was open for 0% -> 0% of each run, Pallas kernels for 12% -> 8%
where the time goes in v6:
time: 25.6 us; the launch traced here: 25.2 us
  starting transfers between devices  12.6 us (49%)
  Pallas kernels  8.45 us (33%)
  waiting for transfers between devices  2.33 us (9%)
  local copies, waits for them, and re-layouts  1.06 us (4%)
  between operations  0.76 us (3%)
    ppermute x4, starting transfers between devices, across(): lax.ppermute(block, ('row', 'col'), route + (extra if mesh_cols == 2 else...  5.73 us
    pallas_call x1, Pallas kernels, views_call(): pl.pallas_call(functools.partial(views_kernel, chans), out_shape=[jax.Sha...  5.41 us
    ppermute x2, starting transfers between devices, exchange(): lax.ppermute(block, 'col', channel[0])  4.19 us
    ppermute x4, starting transfers between devices, over_rows(): return lax.ppermute(block, ('row', 'col'), route + extra)  2.69 us
    ppermute x4, waiting for transfers between devices, across(): lax.ppermute(block, ('row', 'col'), route + (extra if mesh_cols == 2 else...  2.32 us
    pallas_call x1, Pallas kernels, prepare_call(): pl.pallas_call(prepare_kernel, out_shape=jax.ShapeDtypeStruct((views, 2,...  1.9 us
    unnamed x10, local copies, waits for them, and re-layouts  1.06 us
    pallas_call x1, Pallas kernels, finish_call(): pl.pallas_call(functools.partial(finish_kernel, chans), out_shape=jax.Sha...  1 us
  transfers between devices with their start and end apart: 10, of which 2 were waited for; matrix products, arithmetic and copies ran while one was open for 0% of the time, Pallas kernels for 8%

profile of v6, /device:TPU:0, one launch (start us, length us, event | category | flops | bytes accessed | tf_op | source)
XLA Modules:
  0.0 25.2 jit_solution(11587150033186024935)
XLA Ops:
  0.0 0.0 copy-start
  0.0 1.0 %copy-done = f32[2,256,256]{2,1,0:T(8,128)S(1)} copy-done((f32[2,256,256]{2,1,0:T(8,128)S(1)}, f32[2,256,256]{2,1,0:T(8,128)}, u32[]{:S(2)}) %copy-start) | copy-done | bytes 524312
  1.0 0.0 copy-start.1
  1.0 0.0 copy-start.2
  1.0 0.0 copy-start.3
  1.0 0.0 copy-start.4
  1.1 0.1 shard_map.74
  1.2 3.0 %collective-permute-start = (f32[256,128]{1,0:T(8,128)S(1)}, f32[256,128]{1,0:T(8,128)S(1)}, u32[]{:S(2)}, u32[]{:S(2)}) collective-permute-start(f32[256,128]{1,0:T(8,128)S(1)} %get-tuple-element.16), channel_id=1, source_target_pairs={{0,1},{1,0},{2,3},{3,2},{4,5},{5,4},{6,7},{7,6},{8,9},{9,8},{10,11... | collective-permute-start | bytes 393224 | tf_op jit(solution)/shard_map/ppermute | solution.py:511
  4.2 0.1 collective-permute-start.1
  4.3 1.6 %collective-permute-start.4 = (f32[2,64,256]{2,1,0:T(8,128)S(1)}, f32[2,64,256]{2,1,0:T(8,128)S(1)}, u32[]{:S(2)}, u32[]{:S(2)}) collective-permute-start(f32[2,64,256]{2,1,0:T(8,128)S(1)} %get-tuple-element.20), channel_id=1, source_target_pairs={{0,2},{1,3},{4,6},{5,7},{8,10},{9,11},{12,14},{13,15},{16,18},{17,... | collective-permute-start | bytes 393224 | tf_op jit(solution)/shard_map/ppermute | solution.py:504
  5.8 0.5 %collective-permute-start.2 = (f32[64,128]{1,0:T(8,128)S(1)}, f32[64,128]{1,0:T(8,128)S(1)}, u32[]{:S(2)}, u32[]{:S(2)}) collective-permute-start(f32[64,128]{1,0:T(8,128)S(1)} %get-tuple-element.18), channel_id=1, source_target_pairs={{2,5},{3,4},{6,9},{7,8},{10,13},{11,12},{14,17},{15,16},{18,21},{1... | collective-permute-start | bytes 98312 | tf_op jit(solution)/shard_map/ppermute | solution.py:508
  6.4 2.2 %collective-permute-start.3 = (f32[64,128]{1,0:T(8,128)S(1)}, f32[64,128]{1,0:T(8,128)S(1)}, u32[]{:S(2)}, u32[]{:S(2)}) collective-permute-start(f32[64,128]{1,0:T(8,128)S(1)} %get-tuple-element.19), channel_id=1, source_target_pairs={{0,3},{1,2},{4,7},{5,6},{8,11},{9,10},{12,15},{13,14},{16,19},{17,... | collective-permute-start | bytes 98312 | tf_op jit(solution)/shard_map/ppermute | solution.py:508
  8.5 1.9 %shard_map.73.placed = f32[4,2,256,256]{3,2,1,0:T(8,128)S(1)} custom-call(s32[1,1,2,4]{3,2,1,0:T(2,128)} %bitcast.1, f32[2,256,256]{2,1,0:T(8,128)} %probe.1), custom_call_target="tpu_custom_call" | custom-call | flops 1000000000 | bytes 100000 | tf_op jit(solution)/shard_map/pallas_call | solution.py:183
  11.1 0.0 collective-permute-done.2.rest_2_
  11.1 0.0 collective-permute-done.3.rest_3_
  11.1 0.0 collective-permute-done.rest_0_
  11.1 0.0 collective-permute-done.1.rest_1_
  11.1 0.0 collective-permute-done.4.rest_4_
  11.1 0.0 copy-done.1
  11.2 0.0 copy-done.2
  11.2 0.0 copy-done.3
  11.2 0.0 copy-done.4
  11.2 5.4 %shard_map.75 = (f32[2,256,256]{2,1,0:T(8,128)S(1)}, f32[2,64,256]{2,1,0:T(8,128)S(1)}, f32[2,64,256]{2,1,0:T(8,128)S(1)}, f32[256,128]{1,0:T(8,128)S(1)}, f32[64,128]{1,0:T(8,128)S(1)}, /*index=5*/f32[64,128]{1,0:T(8,128)S(1)}) custom-call(s32[1,1,2,4]{3,2,1,0:T(2,128)} %bitcast.2, s32[1,1]{1,0:T(1,128)S(6)} %copy.8.counts, f32[2,256,256]{2,1,0:T(8,128)S(1)} %copy-done.1, ...), custom_call_target="tpu_custom_call" | custom-call | tf_op jit(solution)/shard_map/pallas_call | solution.py:421
  16.6 1.2 %collective-permute-start.5 = (f32[256,128]{1,0:T(8,128)S(1)}, f32[256,128]{1,0:T(8,128)S(1)}, u32[]{:S(2)}, u32[]{:S(2)}) collective-permute-start(f32[256,128]{1,0:T(8,128)S(1)} %get-tuple-element.22), channel_id=1, source_target_pairs={{0,1},{1,0},{2,3},{3,2},{4,5},{5,4},{6,7},{7,6},{8,9},{9,8},{10,11... | collective-permute-start | bytes 393224 | tf_op jit(solution)/shard_map/ppermute | solution.py:511
  17.8 0.9 %collective-permute-start.6 = (f32[2,64,256]{2,1,0:T(8,128)S(1)}, f32[2,64,256]{2,1,0:T(8,128)S(1)}, u32[]{:S(2)}, u32[]{:S(2)}) collective-permute-start(f32[2,64,256]{2,1,0:T(8,128)S(1)} %get-tuple-element.23), channel_id=1, source_target_pairs={{2,4},{3,5},{6,8},{7,9},{10,12},{11,13},{14,16},{15,17},{18,20},{1... | collective-permute-start | bytes 393224 | tf_op jit(solution)/shard_map/ppermute | solution.py:504
  18.7 0.1 collective-permute-start.9
  18.8 1.5 %collective-permute-start.7 = (f32[64,128]{1,0:T(8,128)S(1)}, f32[64,128]{1,0:T(8,128)S(1)}, u32[]{:S(2)}, u32[]{:S(2)}) collective-permute-start(f32[64,128]{1,0:T(8,128)S(1)} %get-tuple-element.24), channel_id=1, source_target_pairs={{2,5},{3,4},{6,9},{7,8},{10,13},{11,12},{14,17},{15,16},{18,21},{1... | collective-permute-start | bytes 98312 | tf_op jit(solution)/shard_map/ppermute | solution.py:508
  20.3 1.5 %collective-permute-start.8 = (f32[64,128]{1,0:T(8,128)S(1)}, f32[64,128]{1,0:T(8,128)S(1)}, u32[]{:S(2)}, u32[]{:S(2)}) collective-permute-start(f32[64,128]{1,0:T(8,128)S(1)} %get-tuple-element.25), channel_id=1, source_target_pairs={{0,3},{1,2},{4,7},{5,6},{8,11},{9,10},{12,15},{13,14},{16,19},{17,... | collective-permute-start | bytes 98312 | tf_op jit(solution)/shard_map/ppermute | solution.py:508
  21.9 1.9 %collective-permute-done.7.rest_2_ = f32[64,128]{1,0:T(8,128)S(1)} collective-permute-done((f32[64,128]{1,0:T(8,128)S(1)}, f32[64,128]{1,0:T(8,128)S(1)}, u32[]{:S(2)}, u32[]{:S(2)}) %collective-permute-start.7) | collective-permute-done | bytes 32800 | tf_op jit(solution)/shard_map/ppermute | solution.py:508
  23.8 0.4 %collective-permute-done.8.rest_3_ = f32[64,128]{1,0:T(8,128)S(1)} collective-permute-done((f32[64,128]{1,0:T(8,128)S(1)}, f32[64,128]{1,0:T(8,128)S(1)}, u32[]{:S(2)}, u32[]{:S(2)}) %collective-permute-start.8) | collective-permute-done | bytes 32800 | tf_op jit(solution)/shard_map/ppermute | solution.py:508
  24.2 0.0 collective-permute-done.5.rest_0_
  24.2 0.0 collective-permute-done.6.rest_1_
  24.2 0.0 collective-permute-done.9.rest_4_
  24.2 1.0 %shard_map.76 = f32[2,256,256]{2,1,0:T(8,128)} custom-call(f32[2,256,256]{2,1,0:T(8,128)S(1)} %copy-done.1, f32[2,256,256]{2,1,0:T(8,128)S(1)} %get-tuple-element.21.g_core, f32[256,128]{1,0:T(8,128)S(1)} %collective-permute-done.5.rest_0_, f32[2,64,256]{2,1,0:T(8,128)S(1)} %collective-permute-done.6.rest_1_, f32[64,128]{1,0:T(8,128)S(1)} %collective-permute-done.7.rest_2_, ...), custom_call_target="tpu_custom_call" | custom-call | tf_op jit(solution)/shard_map/pallas_call | solution.py:485
Async XLA Ops:
  0.0 1.0 %copy-start = (f32[2,256,256]{2,1,0:T(8,128)S(1)}, f32[2,256,256]{2,1,0:T(8,128)}, u32[]{:S(2)}) copy-start(f32[2,256,256]{2,1,0:T(8,128)} %object_ref.3) | copy-start | bytes 1572868
  1.0 10.1 %copy-start.1 = (f32[2,256,256]{2,1,0:T(8,128)S(1)}, f32[2,256,256]{2,1,0:T(8,128)}, u32[]{:S(2)}) copy-start(f32[2,256,256]{2,1,0:T(8,128)} %object_ref.3) | copy-start | bytes 1572868
  1.0 10.1 %copy-start.2 = (f32[1,1,4,256,256]{4,3,2,1,0:T(8,128)S(1)}, f32[1,1,4,256,256]{4,3,2,1,0:T(8,128)}, u32[]{:S(2)}) copy-start(f32[1,1,4,256,256]{4,3,2,1,0:T(8,128)} %intensity.1) | copy-start | bytes 3145732
  1.0 10.1 %copy-start.3 = (bf16[4,256,512]{2,1,0:T(8,128)(2,1)S(1)}, bf16[4,256,512]{2,1,0:T(8,128)(2,1)}, u32[]{:S(2)}) copy-start(bf16[4,256,512]{2,1,0:T(8,128)(2,1)} %constant.5.clone.rest_6_) | copy-start | bytes 3145732
  1.0 10.1 %copy-start.4 = (bf16[4,512,256]{2,1,0:T(8,128)(2,1)S(1)}, bf16[4,512,256]{2,1,0:T(8,128)(2,1)}, u32[]{:S(2)}) copy-start(bf16[4,512,256]{2,1,0:T(8,128)(2,1)} %constant.4.clone.rest_5_) | copy-start | bytes 3145732
  1.2 9.9 %collective-permute-start = (f32[256,128]{1,0:T(8,128)S(1)}, f32[256,128]{1,0:T(8,128)S(1)}, u32[]{:S(2)}, u32[]{:S(2)}) collective-permute-start(f32[256,128]{1,0:T(8,128)S(1)} %get-tuple-element.16), channel_id=1, source_target_pairs={{0,1},{1,0},{2,3},{3,2},{4,5},{5,4},{6,7},{7,6},{8,9},{9,8},{10,11... | collective-permute-start | bytes 393224 | tf_op jit(solution)/shard_map/ppermute | solution.py:511
  4.2 6.9 %collective-permute-start.1 = (f32[2,64,256]{2,1,0:T(8,128)S(1)}, f32[2,64,256]{2,1,0:T(8,128)S(1)}, u32[]{:S(2)}, u32[]{:S(2)}) collective-permute-start(f32[2,64,256]{2,1,0:T(8,128)S(1)} %get-tuple-element.17), channel_id=1, source_target_pairs={{2,4},{3,5},{6,8},{7,9},{10,12},{11,13},{14,16},{15,17},{18,20},{1... | collective-permute-start | bytes 393224 | tf_op jit(solution)/shard_map/ppermute | solution.py:504
  4.3 6.9 %collective-permute-start.4 = (f32[2,64,256]{2,1,0:T(8,128)S(1)}, f32[2,64,256]{2,1,0:T(8,128)S(1)}, u32[]{:S(2)}, u32[]{:S(2)}) collective-permute-start(f32[2,64,256]{2,1,0:T(8,128)S(1)} %get-tuple-element.20), channel_id=1, source_target_pairs={{0,2},{1,3},{4,6},{5,7},{8,10},{9,11},{12,14},{13,15},{16,18},{17,... | collective-permute-start | bytes 393224 | tf_op jit(solution)/shard_map/ppermute | solution.py:504
  5.8 5.3 %collective-permute-start.2 = (f32[64,128]{1,0:T(8,128)S(1)}, f32[64,128]{1,0:T(8,128)S(1)}, u32[]{:S(2)}, u32[]{:S(2)}) collective-permute-start(f32[64,128]{1,0:T(8,128)S(1)} %get-tuple-element.18), channel_id=1, source_target_pairs={{2,5},{3,4},{6,9},{7,8},{10,13},{11,12},{14,17},{15,16},{18,21},{1... | collective-permute-start | bytes 98312 | tf_op jit(solution)/shard_map/ppermute | solution.py:508
  6.4 4.7 %collective-permute-start.3 = (f32[64,128]{1,0:T(8,128)S(1)}, f32[64,128]{1,0:T(8,128)S(1)}, u32[]{:S(2)}, u32[]{:S(2)}) collective-permute-start(f32[64,128]{1,0:T(8,128)S(1)} %get-tuple-element.19), channel_id=1, source_target_pairs={{0,3},{1,2},{4,7},{5,6},{8,11},{9,10},{12,15},{13,14},{16,19},{17,... | collective-permute-start | bytes 98312 | tf_op jit(solution)/shard_map/ppermute | solution.py:508
  16.6 7.6 %collective-permute-start.5 = (f32[256,128]{1,0:T(8,128)S(1)}, f32[256,128]{1,0:T(8,128)S(1)}, u32[]{:S(2)}, u32[]{:S(2)}) collective-permute-start(f32[256,128]{1,0:T(8,128)S(1)} %get-tuple-element.22), channel_id=1, source_target_pairs={{0,1},{1,0},{2,3},{3,2},{4,5},{5,4},{6,7},{7,6},{8,9},{9,8},{10,11... | collective-permute-start | bytes 393224 | tf_op jit(solution)/shard_map/ppermute | solution.py:511
  17.8 6.4 %collective-permute-start.6 = (f32[2,64,256]{2,1,0:T(8,128)S(1)}, f32[2,64,256]{2,1,0:T(8,128)S(1)}, u32[]{:S(2)}, u32[]{:S(2)}) collective-permute-start(f32[2,64,256]{2,1,0:T(8,128)S(1)} %get-tuple-element.23), channel_id=1, source_target_pairs={{2,4},{3,5},{6,8},{7,9},{10,12},{11,13},{14,16},{15,17},{18,20},{1... | collective-permute-start | bytes 393224 | tf_op jit(solution)/shard_map/ppermute | solution.py:504
  18.7 5.5 %collective-permute-start.9 = (f32[2,64,256]{2,1,0:T(8,128)S(1)}, f32[2,64,256]{2,1,0:T(8,128)S(1)}, u32[]{:S(2)}, u32[]{:S(2)}) collective-permute-start(f32[2,64,256]{2,1,0:T(8,128)S(1)} %get-tuple-element.26), channel_id=1, source_target_pairs={{0,2},{1,3},{4,6},{5,7},{8,10},{9,11},{12,14},{13,15},{16,18},{17,... | collective-permute-start | bytes 393224 | tf_op jit(solution)/shard_map/ppermute | solution.py:504
  18.8 4.9 %collective-permute-start.7 = (f32[64,128]{1,0:T(8,128)S(1)}, f32[64,128]{1,0:T(8,128)S(1)}, u32[]{:S(2)}, u32[]{:S(2)}) collective-permute-start(f32[64,128]{1,0:T(8,128)S(1)} %get-tuple-element.24), channel_id=1, source_target_pairs={{2,5},{3,4},{6,9},{7,8},{10,13},{11,12},{14,17},{15,16},{18,21},{1... | collective-permute-start | bytes 98312 | tf_op jit(solution)/shard_map/ppermute | solution.py:508
  20.3 3.9 %collective-permute-start.8 = (f32[64,128]{1,0:T(8,128)S(1)}, f32[64,128]{1,0:T(8,128)S(1)}, u32[]{:S(2)}, u32[]{:S(2)}) collective-permute-start(f32[64,128]{1,0:T(8,128)S(1)} %get-tuple-element.25), channel_id=1, source_target_pairs={{0,3},{1,2},{4,7},{5,6},{8,11},{9,10},{12,15},{13,14},{16,19},{17,... | collective-permute-start | bytes 98312 | tf_op jit(solution)/shard_map/ppermute | solution.py:508

commit v7 on v6

--- a/solution.py
+++ b/solution.py
@@ -114,7 +114,7 @@
     return copies
 
 
-def pack_kernel(chans, object_ref, a_ref, b_ref, *edge_refs):
+def pack_kernel(chans, counts, object_ref, a_ref, b_ref, *edge_refs):
     size = object_ref.shape[1]
     top, bottom = pl.ds(0, MARGIN), pl.ds(size - MARGIN, MARGIN)
     lower = lower_partner()
@@ -141,17 +141,17 @@
         kb_ref[...] = jnp.where(lower, x_ref[:MARGIN], x_ref[size - MARGIN :])
 
 
-def pack_call(object_field, chans):
+def pack_call(counts, object_field, chans):
     size = object_field.shape[1]
     shapes = [(2, MARGIN, size)] * 2 + [(size, LANES), (MARGIN, LANES), (MARGIN, LANES)] * len(chans)
     vmem = pl.BlockSpec(memory_space=pltpu.VMEM)
     return pl.pallas_call(
         functools.partial(pack_kernel, chans),
         out_shape=[jax.ShapeDtypeStruct(shape, F32) for shape in shapes],
-        in_specs=[vmem],
+        in_specs=[pl.BlockSpec(memory_space=pltpu.SMEM), vmem],
         out_specs=[vmem] * len(shapes),
         compiler_params=pltpu.CompilerParams(vmem_limit_bytes=4 * 1024 * 1024),
-    )(object_field)
+    )(counts, object_field)
 
 
 def prepare_kernel(offsets_in, probe, placed, offsets, doubled, sems):
@@ -195,15 +195,18 @@
     )(offsets, probe)
 
 
+def a_corner(size, number):
+    return slice(2 * size + number * LANES, 2 * size + (number + 1) * LANES)
+
+
 def views_kernel(chans, offsets_in, counts, core, placed, intensity, *rest):
     count = len(chans)
     x_in, b_in, rest = rest[:count], rest[count], rest[count + 1 :]
     kb_in, ka_in = rest[:count], rest[count : 2 * count]
     a_in, right, left, *rest = rest[2 * count :]
-    g_core, g_a, g_b = rest[:3]
-    g_x, g_ka = rest[3 : 3 + count], rest[3 + count : 3 + 2 * count]
-    g_kb = rest[3 + 2 * count : 3 + 3 * count]
-    offsets, sem, amplitude, cols_m, rows_m, corner_m, s1, y, s2, z, s3, u, s4, g = rest[3 + 3 * count :]
+    base, g_a, g_b = rest[:3]
+    g_x, g_kb = rest[3 : 3 + count], rest[3 + count : 3 + 2 * count]
+    offsets, sem, amplitude, cols_m, rows_m, corner_m, s1, y, s2, z, s3, u, s4, g = rest[3 + 2 * count :]
     (offsets_copy,) = fetch([(offsets_in, offsets)], sem)
     views, size = placed.shape[0], core.shape[1]
     half, m = size // 2, MARGIN
@@ -385,7 +388,7 @@
                 corner_m[part, place : place + CHUNK] = sums["corner", part]
             for block in range(2):
                 cols = slice(block * LANES, (block + 1) * LANES)
-                g_core[part, rows, cols] = sums["core", part, block]
+                base[part, rows, cols] = core[part, rows, cols] - step_size * sums["core", part, block]
                 if place is not None:
                     rows_m[part, place : place + CHUNK, cols] = sums["row", part, block]
 
@@ -396,7 +399,7 @@
 
     for part in range(2):
         bottom, top = rows_m[part, :m], rows_m[part, m:]
-        g_a[part] = jnp.where(lower, bottom, top)
+        g_a[:, part * size : (part + 1) * size] = jnp.where(lower, bottom, top)
         g_b[part] = jnp.where(lower, top, bottom)
     bottom = (corner_m[0, :m], corner_m[1, :m])
     top = (corner_m[0, m:], corner_m[1, m:])
@@ -405,7 +408,7 @@
             rows = slice(row, row + CHUNK)
             g_x[number][rows] = packed(channel, cols_m[0, rows], cols_m[1, rows])
         below, above = packed(channel, *bottom), packed(channel, *top)
-        g_ka[number][...] = jnp.where(lower, below, above)
+        g_a[:, a_corner(size, number)] = jnp.where(lower, below, above)
         g_kb[number][...] = jnp.where(lower, above, below)
 
 
@@ -413,8 +416,8 @@
     views, size = placed.shape[0], core.shape[1]
     count = len(chans)
     vmem = pl.BlockSpec(memory_space=pltpu.VMEM)
-    shapes = [(2, size, size), (2, MARGIN, size), (2, MARGIN, size)]
-    shapes += [(size, LANES)] * count + [(MARGIN, LANES)] * (2 * count)
+    shapes = [(2, size, size), (MARGIN, 2 * size + count * LANES), (2, MARGIN, size)]
+    shapes += [(size, LANES)] * count + [(MARGIN, LANES)] * count
     full = pltpu.VMEM((views, 2, size, size), F32)
     tall = pltpu.VMEM((views, 2, 2 * size, size), BF16)
     wide = pltpu.VMEM((views, 2, size, 2 * size), BF16)
@@ -438,57 +441,89 @@
         ],
         compiler_params=pltpu.CompilerParams(vmem_limit_bytes=40 * 1024 * 1024),
     )(offsets, counts, core, placed, intensity, *x_in, b_in, *kb_in, *ka_in, a_in, *tables)
-    return (*outs[:3], outs[3 : 3 + count], outs[3 + count : 3 + 2 * count], outs[3 + 2 * count :])
-
-
-def finish_kernel(chans, object_ref, g_core, *rest):
+    return (*outs[:3], outs[3 : 3 + count], outs[3 + count :])
+
+
+def merge_kernel(number, a_in, block, out):
+    size = block.shape[0]
+    lower = lower_partner()
+    corner = a_in[:, a_corner(size, number)]
+    out[...] = block[...]
+    rows = pl.ds(pl.multiple_of(jnp.where(lower, size - MARGIN, 0), MARGIN), MARGIN)
+    out[rows] += corner
+
+
+def merge_call(number, a_in, block):
+    vmem = pl.BlockSpec(memory_space=pltpu.VMEM)
+    return pl.pallas_call(
+        functools.partial(merge_kernel, number),
+        out_shape=jax.ShapeDtypeStruct(block.shape, F32),
+        in_specs=[vmem] * 2,
+        out_specs=vmem,
+        compiler_params=pltpu.CompilerParams(vmem_limit_bytes=2 * 1024 * 1024),
+    )(a_in, block)
+
+
+def finish_kernel(chans, base, *rest):
     count = len(chans)
-    x_in, b_in, rest = rest[:count], rest[count], rest[count + 1 :]
-    kb_in, ka_in = rest[:count], rest[count : 2 * count]
-    a_in, out = rest[2 * count :]
-    size = object_ref.shape[1]
-    lower = lower_partner()
-    a_rows = pl.ds(pl.multiple_of(jnp.where(lower, size - MARGIN, 0), MARGIN), MARGIN)
-    b_rows = pl.ds(pl.multiple_of(jnp.where(lower, 0, size - MARGIN), MARGIN), MARGIN)
+    x_in, b_in, kb_in = rest[:count], rest[count], rest[count + 1 : 2 * count + 1]
+    a_in, out, whole, sems = rest[2 * count + 1 :]
+    size = base.shape[1]
+    lower, partner = lower_partner(), b_partner()
     columns = []
     for channel in chans:
         right = takes_right(channel)
         mine = lane_ids() // (LANES // 2) == jnp.where(right, 1, 0)
-        block = pl.multiple_of(jnp.where(right, size - LANES, 0), LANES)
-        columns.append((mine, pl.ds(block, LANES)))
-
-    def take(place, value):
-        out[place] -= step_size * value
-
-    def take_packed(rows, column, block):
+        columns.append((mine, pl.ds(pl.multiple_of(jnp.where(right, size - LANES, 0), LANES), LANES)))
+
+    def take_packed(part, rows, column, block):
         mine, lanes = column
-        take((0, rows, lanes), jnp.where(mine, block, 0.0))
-        take((1, rows, lanes), jnp.where(mine, swap_halves(block), 0.0))
-
-    for part in range(2):
-        out[part] = object_ref[part] - step_size * g_core[part]
-        take((part, a_rows), a_in[part])
-    for number, column in enumerate(columns):
-        take_packed(slice(None), column, x_in[number][...])
-        take_packed(a_rows, column, ka_in[number][...])
-
-    @pl.when(b_partner())
-    def _():
+        block = block if part == 0 else swap_halves(block)
+        whole[part, rows, lanes] -= step_size * jnp.where(mine, block, 0.0)
+
+    copies = []
+    middle = range(MARGIN, size - MARGIN, MARGIN)
+    for start in (*middle, 0, size - MARGIN):
+        rows = slice(start, start + MARGIN)
         for part in range(2):
-            take((part, b_rows), b_in[part])
-        for number, column in enumerate(columns):
-            take_packed(b_rows, column, kb_in[number][...])
-
-
-def finish_call(chans, object_field, g_core, a_in, b_in, x_in, ka_in, kb_in):
+            whole[part, rows] = base[part, rows]
+            for number, column in enumerate(columns):
+                take_packed(part, rows, column, x_in[number][rows])
+            if start not in middle:
+                by_a = ~lower if start == 0 else lower
+
+                @pl.when(by_a)
+                def _():
+                    whole[part, rows] -= step_size * a_in[:, part * size : (part + 1) * size]
+
+                @pl.when(~by_a & partner)
+                def _():
+                    whole[part, rows] -= step_size * b_in[part]
+                    for number, column in enumerate(columns):
+                        take_packed(part, rows, column, kb_in[number][...])
+
+            copy = pltpu.make_async_copy(
+                whole.at[part, rows], out.at[part, rows], sems.at[part, start // MARGIN]
+            )
+            copy.start()
+            copies.append(copy)
+    for copy in copies:
+        copy.wait()
+
+
+def finish_call(chans, base, a_in, b_in, x_in, kb_in):
     vmem = pl.BlockSpec(memory_space=pltpu.VMEM)
     return pl.pallas_call(
         functools.partial(finish_kernel, chans),
-        out_shape=jax.ShapeDtypeStruct(object_field.shape, F32),
-        in_specs=[vmem] * (4 + 3 * len(chans)),
-        out_specs=vmem,
+        out_shape=jax.ShapeDtypeStruct(base.shape, F32),
+        in_specs=[vmem] * (3 + 2 * len(chans)),
+        out_specs=pl.BlockSpec(memory_space=pltpu.HBM),
+        scratch_shapes=[
+            pltpu.VMEM(base.shape, F32),
+            pltpu.SemaphoreType.DMA((2, base.shape[1] // MARGIN)),
+        ],
         compiler_params=pltpu.CompilerParams(vmem_limit_bytes=6 * 1024 * 1024),
-    )(object_field, g_core, *x_in, b_in, *kb_in, *ka_in, a_in)
+    )(base, *x_in, b_in, *kb_in, a_in)
 
 
 def per_device(object_field, probe_field, intensity, view_offsets, view_counts):
@@ -507,25 +542,30 @@
         route = [(i * mesh_cols + k, j * mesh_cols + l) for i, j in pairs for k, l in channel[0]]
         return lax.ppermute(block, ("row", "col"), route + (extra if mesh_cols == 2 else []))
 
-    def exchange(a_send, b_send, x_send, ka_send, kb_send):
-        x_in = [lax.ppermute(block, "col", channel[0]) for block, channel in zip(x_send, chans)]
-        b_in = over_rows(b_send, b_pairs, spare)
-        kb_in = [across(block, b_pairs, spare, channel) for block, channel in zip(kb_send, chans)]
-        ka_in = [across(block, a_pairs, [], channel) for block, channel in zip(ka_send, chans)]
-        a_in = over_rows(a_send, a_pairs, [])
-        return a_in, b_in, x_in, ka_in, kb_in
-
-    packs = pack_call(object_field, chans)
+    def swap_x(block, channel):
+        return lax.ppermute(block, "col", channel[0])
+
+    packs = pack_call(view_counts, object_field, chans)
+    x_in = [swap_x(block, channel) for block, channel in zip(packs[2::3], chans)]
+    b_in = over_rows(packs[1], b_pairs, spare)
+    kb_in = [across(block, b_pairs, spare, channel) for block, channel in zip(packs[4::3], chans)]
+    ka_in = [across(block, a_pairs, [], channel) for block, channel in zip(packs[3::3], chans)]
+    a_in = over_rows(packs[0], a_pairs, [])
     offsets, probe = (
         pltpu.with_memory_space_constraint(array, pltpu.HBM)
         for array in (jnp.swapaxes(view_offsets, 2, 3), probe_field)
     )
-    margins = exchange(packs[0], packs[1], packs[2::3], packs[3::3], packs[4::3])
     placed = prepare_call(offsets, probe)
-    g_core, *sends = views_call(
-        chans, offsets, view_counts, object_field, placed, intensity, tables, *margins
+    base, g_a, g_b, g_x, g_kb = views_call(
+        chans, offsets, view_counts, object_field, placed, intensity, tables,
+        a_in, b_in, x_in, ka_in, kb_in,
     )
-    return finish_call(chans, object_field, g_core, *exchange(*sends))
+    a_in = over_rows(g_a, a_pairs, [])
+    b_in = over_rows(g_b, b_pairs, spare)
+    g_x = [merge_call(number, a_in, block) for number, block in enumerate(g_x)]
+    x_in = [swap_x(block, channel) for block, channel in zip(g_x, chans)]
+    kb_in = [across(block, b_pairs, spare, channel) for block, channel in zip(g_kb, chans)]
+    return finish_call(chans, base, a_in, b_in, x_in, kb_in)
 
 
 def solution(mesh):

time: 25.6 us -> 27.1 us (1.059)
  waiting for transfers between devices: 2.33 us -> 5.13 us
  starting transfers between devices: 12.6 us -> 11.4 us
    ppermute x4 -> x3, waiting for transfers between devices: 2.32 us -> 5.11 us  [across(): lax.ppermute(block, ('row', 'col'), route + (extra if mesh_cols == 2 else...]
    ppermute x4 -> x3, starting transfers between devices: 5.73 us -> 3.5 us  [across(): lax.ppermute(block, ('row', 'col'), route + (extra if mesh_cols == 2 else...]
    ppermute x4, starting transfers between devices: 2.69 us -> 3.63 us  [over_rows(): return lax.ppermute(block, ('row', 'col'), route + extra)]
  transfers between devices with their start and end apart: 10 -> 9, of which waited for: 2 -> 1; matrix products, arithmetic and copies ran while one was open for 0% -> 0% of each run, Pallas kernels for 8% -> 7%
where the time goes in v7:
time: 27.1 us; the launch traced here: 26.9 us
  starting transfers between devices  11.4 us (42%)
  Pallas kernels  8.49 us (31%)
  waiting for transfers between devices  5.13 us (19%)
  local copies, waits for them, and re-layouts  1.05 us (4%)
  between operations  0.75 us (3%)
    pallas_call x1, Pallas kernels, views_call(): pl.pallas_call(functools.partial(views_kernel, chans), out_shape=[jax.Sha...  5.44 us
    ppermute x3, waiting for transfers between devices, across(): lax.ppermute(block, ('row', 'col'), route + (extra if mesh_cols == 2 else...  5.11 us
    ppermute x2, starting transfers between devices, swap_x(): return lax.ppermute(block, 'col', channel[0])  4.3 us
    ppermute x4, starting transfers between devices, over_rows(): return lax.ppermute(block, ('row', 'col'), route + extra)  3.63 us
    ppermute x3, starting transfers between devices, across(): lax.ppermute(block, ('row', 'col'), route + (extra if mesh_cols == 2 else...  3.5 us
    pallas_call x1, Pallas kernels, prepare_call(): pl.pallas_call(prepare_kernel, out_shape=jax.ShapeDtypeStruct((views, 2,...  1.9 us
    unnamed x10, local copies, waits for them, and re-layouts  1.05 us
    pallas_call x1, Pallas kernels, finish_call(): pl.pallas_call(functools.partial(finish_kernel, chans), out_shape=jax.Sha...  1 us
  transfers between devices with their start and end apart: 9, of which 1 were waited for; matrix products, arithmetic and copies ran while one was open for 0% of the time, Pallas kernels for 7%

profile of v7, /device:TPU:0, one launch (start us, length us, event | category | flops | bytes accessed | tf_op | source)
XLA Modules:
  0.0 26.9 jit_solution(16356483904328482826)
XLA Ops:
  0.7 0.0 copy-start
  0.7 1.0 %copy-done = f32[2,256,256]{2,1,0:T(8,128)S(1)} copy-done((f32[2,256,256]{2,1,0:T(8,128)S(1)}, f32[2,256,256]{2,1,0:T(8,128)}, u32[]{:S(2)}) %copy-start) | copy-done | bytes 524312
  1.7 0.0 copy-start.1
  1.7 0.0 copy-start.2
  1.7 0.0 copy-start.3
  1.7 0.0 copy-start.4
  1.7 0.1 shard_map.74
  1.8 3.0 %collective-permute-start = (f32[256,128]{1,0:T(8,128)S(1)}, f32[256,128]{1,0:T(8,128)S(1)}, u32[]{:S(2)}, u32[]{:S(2)}) collective-permute-start(f32[256,128]{1,0:T(8,128)S(1)} %get-tuple-element.15), channel_id=1, source_target_pairs={{0,1},{1,0},{2,3},{3,2},{4,5},{5,4},{6,7},{7,6},{8,9},{9,8},{10,11... | collective-permute-start | bytes 393224 | tf_op jit(solution)/shard_map/ppermute | solution.py:546
  4.9 0.1 collective-permute-start.1
  4.9 1.6 %collective-permute-start.4 = (f32[2,64,256]{2,1,0:T(8,128)S(1)}, f32[2,64,256]{2,1,0:T(8,128)S(1)}, u32[]{:S(2)}, u32[]{:S(2)}) collective-permute-start(f32[2,64,256]{2,1,0:T(8,128)S(1)} %get-tuple-element.19), channel_id=1, source_target_pairs={{0,2},{1,3},{4,6},{5,7},{8,10},{9,11},{12,14},{13,15},{16,18},{17,... | collective-permute-start | bytes 393224 | tf_op jit(solution)/shard_map/ppermute | solution.py:539
  6.5 0.5 %collective-permute-start.2 = (f32[64,128]{1,0:T(8,128)S(1)}, f32[64,128]{1,0:T(8,128)S(1)}, u32[]{:S(2)}, u32[]{:S(2)}) collective-permute-start(f32[64,128]{1,0:T(8,128)S(1)} %get-tuple-element.17), channel_id=1, source_target_pairs={{2,5},{3,4},{6,9},{7,8},{10,13},{11,12},{14,17},{15,16},{18,21},{1... | collective-permute-start | bytes 98312 | tf_op jit(solution)/shard_map/ppermute | solution.py:543
  7.0 2.2 %collective-permute-start.3 = (f32[64,128]{1,0:T(8,128)S(1)}, f32[64,128]{1,0:T(8,128)S(1)}, u32[]{:S(2)}, u32[]{:S(2)}) collective-permute-start(f32[64,128]{1,0:T(8,128)S(1)} %get-tuple-element.18), channel_id=1, source_target_pairs={{0,3},{1,2},{4,7},{5,6},{8,11},{9,10},{12,15},{13,14},{16,19},{17,... | collective-permute-start | bytes 98312 | tf_op jit(solution)/shard_map/ppermute | solution.py:543
  9.2 1.9 %shard_map.73.placed = f32[4,2,256,256]{3,2,1,0:T(8,128)S(1)} custom-call(s32[1,1,2,4]{3,2,1,0:T(2,128)} %bitcast.1, f32[2,256,256]{2,1,0:T(8,128)} %probe.1), custom_call_target="tpu_custom_call" | custom-call | flops 1000000000 | bytes 100000 | tf_op jit(solution)/shard_map/pallas_call | solution.py:183
  11.1 0.0 collective-permute-done.2.rest_2_
  11.1 0.0 collective-permute-done.3.rest_3_
  11.1 0.0 collective-permute-done.rest_0_
  11.1 0.0 collective-permute-done.1.rest_1_
  11.1 0.0 collective-permute-done.4.rest_4_
  11.2 0.0 copy-done.1
  11.2 0.0 copy-done.2
  11.2 0.0 copy-done.3
  11.2 0.0 copy-done.4
  11.2 5.4 %shard_map.75 = (f32[2,256,256]{2,1,0:T(8,128)S(1)}, f32[64,640]{1,0:T(8,128)S(1)}, f32[2,64,256]{2,1,0:T(8,128)S(1)}, f32[256,128]{1,0:T(8,128)S(1)}, f32[64,128]{1,0:T(8,128)S(1)}) custom-call(s32[1,1,2,4]{3,2,1,0:T(2,128)} %bitcast.2, s32[1,1]{1,0:T(1,128)S(6)} %copy.8.counts, f32[2,256,256]{2,1,0:T(8,128)S(1)} %copy-done.1, ...), custom_call_target="tpu_custom_call" | custom-call | tf_op jit(solution)/shard_map/pallas_call | solution.py:424
  16.6 0.4 %collective-permute-start.5 = (f32[64,640]{1,0:T(8,128)S(1)}, f32[64,640]{1,0:T(8,128)S(1)}, u32[]{:S(2)}, u32[]{:S(2)}) collective-permute-start(f32[64,640]{1,0:T(8,128)S(1)} %get-tuple-element.21), channel_id=1, source_target_pairs={{0,2},{1,3},{4,6},{5,7},{8,10},{9,11},{12,14},{13,15},{16,18},{17,... | collective-permute-start | bytes 491528 | tf_op jit(solution)/shard_map/ppermute | solution.py:539
  17.0 1.6 %collective-permute-start.7 = (f32[2,64,256]{2,1,0:T(8,128)S(1)}, f32[2,64,256]{2,1,0:T(8,128)S(1)}, u32[]{:S(2)}, u32[]{:S(2)}) collective-permute-start(f32[2,64,256]{2,1,0:T(8,128)S(1)} %get-tuple-element.23), channel_id=1, source_target_pairs={{2,4},{3,5},{6,8},{7,9},{10,12},{11,13},{14,16},{15,17},{18,20},{1... | collective-permute-start | bytes 393224 | tf_op jit(solution)/shard_map/ppermute | solution.py:539
  18.6 0.0 collective-permute-done.5.a_in.rest_3_
  18.7 1.3 %collective-permute-start.6 = (f32[256,128]{1,0:T(8,128)S(1)}, f32[256,128]{1,0:T(8,128)S(1)}, u32[]{:S(2)}, u32[]{:S(2)}) collective-permute-start(f32[256,128]{1,0:T(8,128)S(1)} %shard_map.76), channel_id=1, source_target_pairs={{0,1},{1,0},{2,3},{3,2},{4,5},{5,4},{6,7},{7,6},{8,9},{9,8},{10,11... | collective-permute-start | bytes 393224 | tf_op jit(solution)/shard_map/ppermute | solution.py:546
  20.0 0.8 %collective-permute-start.8 = (f32[64,128]{1,0:T(8,128)S(1)}, f32[64,128]{1,0:T(8,128)S(1)}, u32[]{:S(2)}, u32[]{:S(2)}) collective-permute-start(f32[64,128]{1,0:T(8,128)S(1)} %get-tuple-element.24), channel_id=1, source_target_pairs={{2,5},{3,4},{6,9},{7,8},{10,13},{11,12},{14,17},{15,16},{18,21},{1... | collective-permute-start | bytes 98312 | tf_op jit(solution)/shard_map/ppermute | solution.py:543
  20.8 5.1 %collective-permute-done.8.rest_2_ = f32[64,128]{1,0:T(8,128)S(1)} collective-permute-done((f32[64,128]{1,0:T(8,128)S(1)}, f32[64,128]{1,0:T(8,128)S(1)}, u32[]{:S(2)}, u32[]{:S(2)}) %collective-permute-start.8) | collective-permute-done | bytes 32800 | tf_op jit(solution)/shard_map/ppermute | solution.py:543
  25.8 0.0 collective-permute-done.7.rest_1_
  25.8 0.0 collective-permute-done.6.rest_0_
  25.9 1.0 %shard_map.77 = f32[2,256,256]{2,1,0:T(8,128)} custom-call(f32[2,256,256]{2,1,0:T(8,128)S(1)} %get-tuple-element.20.base, f32[256,128]{1,0:T(8,128)S(1)} %collective-permute-done.6.rest_0_, f32[2,64,256]{2,1,0:T(8,128)S(1)} %collective-permute-done.7.rest_1_, f32[64,128]{1,0:T(8,128)S(1)} %collective-permute-done.8.rest_2_, ...), custom_call_target="tpu_custom_call" | custom-call | tf_op jit(solution)/shard_map/pallas_call | solution.py:516
  (1 shorter events, 0.0 us)
Async XLA Ops:
  0.7 1.0 %copy-start = (f32[2,256,256]{2,1,0:T(8,128)S(1)}, f32[2,256,256]{2,1,0:T(8,128)}, u32[]{:S(2)}) copy-start(f32[2,256,256]{2,1,0:T(8,128)} %core.1) | copy-start | bytes 1572868
  1.7 9.5 %copy-start.1 = (f32[2,256,256]{2,1,0:T(8,128)S(1)}, f32[2,256,256]{2,1,0:T(8,128)}, u32[]{:S(2)}) copy-start(f32[2,256,256]{2,1,0:T(8,128)} %core.1) | copy-start | bytes 1572868
  1.7 9.5 %copy-start.2 = (f32[1,1,4,256,256]{4,3,2,1,0:T(8,128)S(1)}, f32[1,1,4,256,256]{4,3,2,1,0:T(8,128)}, u32[]{:S(2)}) copy-start(f32[1,1,4,256,256]{4,3,2,1,0:T(8,128)} %intensity.1) | copy-start | bytes 3145732
  1.7 9.5 %copy-start.3 = (bf16[4,256,512]{2,1,0:T(8,128)(2,1)S(1)}, bf16[4,256,512]{2,1,0:T(8,128)(2,1)}, u32[]{:S(2)}) copy-start(bf16[4,256,512]{2,1,0:T(8,128)(2,1)} %constant.5.clone.rest_6_) | copy-start | bytes 3145732
  1.7 9.5 %copy-start.4 = (bf16[4,512,256]{2,1,0:T(8,128)(2,1)S(1)}, bf16[4,512,256]{2,1,0:T(8,128)(2,1)}, u32[]{:S(2)}) copy-start(bf16[4,512,256]{2,1,0:T(8,128)(2,1)} %constant.4.clone.rest_5_) | copy-start | bytes 3145732
  1.8 9.3 %collective-permute-start = (f32[256,128]{1,0:T(8,128)S(1)}, f32[256,128]{1,0:T(8,128)S(1)}, u32[]{:S(2)}, u32[]{:S(2)}) collective-permute-start(f32[256,128]{1,0:T(8,128)S(1)} %get-tuple-element.15), channel_id=1, source_target_pairs={{0,1},{1,0},{2,3},{3,2},{4,5},{5,4},{6,7},{7,6},{8,9},{9,8},{10,11... | collective-permute-start | bytes 393224 | tf_op jit(solution)/shard_map/ppermute | solution.py:546
  4.9 6.3 %collective-permute-start.1 = (f32[2,64,256]{2,1,0:T(8,128)S(1)}, f32[2,64,256]{2,1,0:T(8,128)S(1)}, u32[]{:S(2)}, u32[]{:S(2)}) collective-permute-start(f32[2,64,256]{2,1,0:T(8,128)S(1)} %get-tuple-element.16), channel_id=1, source_target_pairs={{2,4},{3,5},{6,8},{7,9},{10,12},{11,13},{14,16},{15,17},{18,20},{1... | collective-permute-start | bytes 393224 | tf_op jit(solution)/shard_map/ppermute | solution.py:539
  4.9 6.2 %collective-permute-start.4 = (f32[2,64,256]{2,1,0:T(8,128)S(1)}, f32[2,64,256]{2,1,0:T(8,128)S(1)}, u32[]{:S(2)}, u32[]{:S(2)}) collective-permute-start(f32[2,64,256]{2,1,0:T(8,128)S(1)} %get-tuple-element.19), channel_id=1, source_target_pairs={{0,2},{1,3},{4,6},{5,7},{8,10},{9,11},{12,14},{13,15},{16,18},{17,... | collective-permute-start | bytes 393224 | tf_op jit(solution)/shard_map/ppermute | solution.py:539
  6.5 4.6 %collective-permute-start.2 = (f32[64,128]{1,0:T(8,128)S(1)}, f32[64,128]{1,0:T(8,128)S(1)}, u32[]{:S(2)}, u32[]{:S(2)}) collective-permute-start(f32[64,128]{1,0:T(8,128)S(1)} %get-tuple-element.17), channel_id=1, source_target_pairs={{2,5},{3,4},{6,9},{7,8},{10,13},{11,12},{14,17},{15,16},{18,21},{1... | collective-permute-start | bytes 98312 | tf_op jit(solution)/shard_map/ppermute | solution.py:543
  7.0 4.1 %collective-permute-start.3 = (f32[64,128]{1,0:T(8,128)S(1)}, f32[64,128]{1,0:T(8,128)S(1)}, u32[]{:S(2)}, u32[]{:S(2)}) collective-permute-start(f32[64,128]{1,0:T(8,128)S(1)} %get-tuple-element.18), channel_id=1, source_target_pairs={{0,3},{1,2},{4,7},{5,6},{8,11},{9,10},{12,15},{13,14},{16,19},{17,... | collective-permute-start | bytes 98312 | tf_op jit(solution)/shard_map/ppermute | solution.py:543
  16.6 2.0 %collective-permute-start.5 = (f32[64,640]{1,0:T(8,128)S(1)}, f32[64,640]{1,0:T(8,128)S(1)}, u32[]{:S(2)}, u32[]{:S(2)}) collective-permute-start(f32[64,640]{1,0:T(8,128)S(1)} %get-tuple-element.21), channel_id=1, source_target_pairs={{0,2},{1,3},{4,6},{5,7},{8,10},{9,11},{12,14},{13,15},{16,18},{17,... | collective-permute-start | bytes 491528 | tf_op jit(solution)/shard_map/ppermute | solution.py:539
  17.0 8.8 %collective-permute-start.7 = (f32[2,64,256]{2,1,0:T(8,128)S(1)}, f32[2,64,256]{2,1,0:T(8,128)S(1)}, u32[]{:S(2)}, u32[]{:S(2)}) collective-permute-start(f32[2,64,256]{2,1,0:T(8,128)S(1)} %get-tuple-element.23), channel_id=1, source_target_pairs={{2,4},{3,5},{6,8},{7,9},{10,12},{11,13},{14,16},{15,17},{18,20},{1... | collective-permute-start | bytes 393224 | tf_op jit(solution)/shard_map/ppermute | solution.py:539
  18.7 7.2 %collective-permute-start.6 = (f32[256,128]{1,0:T(8,128)S(1)}, f32[256,128]{1,0:T(8,128)S(1)}, u32[]{:S(2)}, u32[]{:S(2)}) collective-permute-start(f32[256,128]{1,0:T(8,128)S(1)} %shard_map.76), channel_id=1, source_target_pairs={{0,1},{1,0},{2,3},{3,2},{4,5},{5,4},{6,7},{7,6},{8,9},{9,8},{10,11... | collective-permute-start | bytes 393224 | tf_op jit(solution)/shard_map/ppermute | solution.py:546
  20.0 5.9 %collective-permute-start.8 = (f32[64,128]{1,0:T(8,128)S(1)}, f32[64,128]{1,0:T(8,128)S(1)}, u32[]{:S(2)}, u32[]{:S(2)}) collective-permute-start(f32[64,128]{1,0:T(8,128)S(1)} %get-tuple-element.24), channel_id=1, source_target_pairs={{2,5},{3,4},{6,9},{7,8},{10,13},{11,12},{14,17},{15,16},{18,21},{1... | collective-permute-start | bytes 98312 | tf_op jit(solution)/shard_map/ppermute | solution.py:543

commit v8 on v7

--- a/solution.py
+++ b/solution.py
@@ -114,7 +114,7 @@
     return copies
 
 
-def pack_kernel(chans, counts, object_ref, a_ref, b_ref, *edge_refs):
+def pack_kernel(chans, object_ref, a_ref, b_ref, *edge_refs):
     size = object_ref.shape[1]
     top, bottom = pl.ds(0, MARGIN), pl.ds(size - MARGIN, MARGIN)
     lower = lower_partner()
@@ -141,17 +141,17 @@
         kb_ref[...] = jnp.where(lower, x_ref[:MARGIN], x_ref[size - MARGIN :])
 
 
-def pack_call(counts, object_field, chans):
+def pack_call(object_field, chans):
     size = object_field.shape[1]
     shapes = [(2, MARGIN, size)] * 2 + [(size, LANES), (MARGIN, LANES), (MARGIN, LANES)] * len(chans)
     vmem = pl.BlockSpec(memory_space=pltpu.VMEM)
     return pl.pallas_call(
         functools.partial(pack_kernel, chans),
         out_shape=[jax.ShapeDtypeStruct(shape, F32) for shape in shapes],
-        in_specs=[pl.BlockSpec(memory_space=pltpu.SMEM), vmem],
+        in_specs=[vmem],
         out_specs=[vmem] * len(shapes),
         compiler_params=pltpu.CompilerParams(vmem_limit_bytes=4 * 1024 * 1024),
-    )(counts, object_field)
+    )(object_field)
 
 
 def prepare_kernel(offsets_in, probe, placed, offsets, doubled, sems):
@@ -193,10 +193,6 @@
         compiler_params=pltpu.CompilerParams(vmem_limit_bytes=16 * 1024 * 1024),
         cost_estimate=pl.CostEstimate(flops=10**9, bytes_accessed=10**5, transcendentals=0),
     )(offsets, probe)
-
-
-def a_corner(size, number):
-    return slice(2 * size + number * LANES, 2 * size + (number + 1) * LANES)
 
 
 def views_kernel(chans, offsets_in, counts, core, placed, intensity, *rest):
@@ -399,7 +395,7 @@
 
     for part in range(2):
         bottom, top = rows_m[part, :m], rows_m[part, m:]
-        g_a[:, part * size : (part + 1) * size] = jnp.where(lower, bottom, top)
+        g_a[part] = jnp.where(lower, bottom, top)
         g_b[part] = jnp.where(lower, top, bottom)
     bottom = (corner_m[0, :m], corner_m[1, :m])
     top = (corner_m[0, m:], corner_m[1, m:])
@@ -408,7 +404,7 @@
             rows = slice(row, row + CHUNK)
             g_x[number][rows] = packed(channel, cols_m[0, rows], cols_m[1, rows])
         below, above = packed(channel, *bottom), packed(channel, *top)
-        g_a[:, a_corner(size, number)] = jnp.where(lower, below, above)
+        g_x[number][size:] = jnp.where(lower, below, above)
         g_kb[number][...] = jnp.where(lower, above, below)
 
 
@@ -416,8 +412,8 @@
     views, size = placed.shape[0], core.shape[1]
     count = len(chans)
     vmem = pl.BlockSpec(memory_space=pltpu.VMEM)
-    shapes = [(2, size, size), (MARGIN, 2 * size + count * LANES), (2, MARGIN, size)]
-    shapes += [(size, LANES)] * count + [(MARGIN, LANES)] * count
+    shapes = [(2, size, size), (2, MARGIN, size), (2, MARGIN, size)]
+    shapes += [(size + MARGIN, LANES)] * count + [(MARGIN, LANES)] * count
     full = pltpu.VMEM((views, 2, size, size), F32)
     tall = pltpu.VMEM((views, 2, 2 * size, size), BF16)
     wide = pltpu.VMEM((views, 2, size, 2 * size), BF16)
@@ -444,30 +440,11 @@
     return (*outs[:3], outs[3 : 3 + count], outs[3 + count :])
 
 
-def merge_kernel(number, a_in, block, out):
-    size = block.shape[0]
-    lower = lower_partner()
-    corner = a_in[:, a_corner(size, number)]
-    out[...] = block[...]
-    rows = pl.ds(pl.multiple_of(jnp.where(lower, size - MARGIN, 0), MARGIN), MARGIN)
-    out[rows] += corner
-
-
-def merge_call(number, a_in, block):
-    vmem = pl.BlockSpec(memory_space=pltpu.VMEM)
-    return pl.pallas_call(
-        functools.partial(merge_kernel, number),
-        out_shape=jax.ShapeDtypeStruct(block.shape, F32),
-        in_specs=[vmem] * 2,
-        out_specs=vmem,
-        compiler_params=pltpu.CompilerParams(vmem_limit_bytes=2 * 1024 * 1024),
-    )(a_in, block)
-
-
 def finish_kernel(chans, base, *rest):
     count = len(chans)
-    x_in, b_in, kb_in = rest[:count], rest[count], rest[count + 1 : 2 * count + 1]
-    a_in, out, whole, sems = rest[2 * count + 1 :]
+    x_in, b_in, rest = rest[:count], rest[count], rest[count + 1 :]
+    kb_in, ka_in = rest[:count], rest[count : 2 * count]
+    a_in, out, whole, sems = rest[2 * count :]
     size = base.shape[1]
     lower, partner = lower_partner(), b_partner()
     columns = []
@@ -494,7 +471,9 @@
 
                 @pl.when(by_a)
                 def _():
-                    whole[part, rows] -= step_size * a_in[:, part * size : (part + 1) * size]
+                    whole[part, rows] -= step_size * a_in[part]
+                    for number, column in enumerate(columns):
+                        take_packed(part, rows, column, ka_in[number][...])
 
                 @pl.when(~by_a & partner)
                 def _():
@@ -511,19 +490,19 @@
         copy.wait()
 
 
-def finish_call(chans, base, a_in, b_in, x_in, kb_in):
+def finish_call(chans, base, a_in, b_in, x_in, ka_in, kb_in):
     vmem = pl.BlockSpec(memory_space=pltpu.VMEM)
     return pl.pallas_call(
         functools.partial(finish_kernel, chans),
         out_shape=jax.ShapeDtypeStruct(base.shape, F32),
-        in_specs=[vmem] * (3 + 2 * len(chans)),
+        in_specs=[vmem] * (3 + 3 * len(chans)),
         out_specs=pl.BlockSpec(memory_space=pltpu.HBM),
         scratch_shapes=[
             pltpu.VMEM(base.shape, F32),
             pltpu.SemaphoreType.DMA((2, base.shape[1] // MARGIN)),
         ],
         compiler_params=pltpu.CompilerParams(vmem_limit_bytes=6 * 1024 * 1024),
-    )(base, *x_in, b_in, *kb_in, a_in)
+    )(base, *x_in, b_in, *kb_in, *ka_in, a_in)
 
 
 def per_device(object_field, probe_field, intensity, view_offsets, view_counts):
@@ -545,7 +524,7 @@
     def swap_x(block, channel):
         return lax.ppermute(block, "col", channel[0])
 
-    packs = pack_call(view_counts, object_field, chans)
+    packs = pack_call(object_field, chans)
     x_in = [swap_x(block, channel) for block, channel in zip(packs[2::3], chans)]
     b_in = over_rows(packs[1], b_pairs, spare)
     kb_in = [across(block, b_pairs, spare, channel) for block, channel in zip(packs[4::3], chans)]
@@ -560,12 +539,12 @@
         chans, offsets, view_counts, object_field, placed, intensity, tables,
         a_in, b_in, x_in, ka_in, kb_in,
     )
+    x_in = [swap_x(block, channel) for block, channel in zip(g_x, chans)]
+    b_in = over_rows(g_b, b_pairs, spare)
+    kb_in = [across(block, b_pairs, spare, channel) for block, channel in zip(g_kb, chans)]
+    ka_in = [over_rows(block[size:], a_pairs, []) for block in x_in]
     a_in = over_rows(g_a, a_pairs, [])
-    b_in = over_rows(g_b, b_pairs, spare)
-    g_x = [merge_call(number, a_in, block) for number, block in enumerate(g_x)]
-    x_in = [swap_x(block, channel) for block, channel in zip(g_x, chans)]
-    kb_in = [across(block, b_pairs, spare, channel) for block, channel in zip(g_kb, chans)]
-    return finish_call(chans, base, a_in, b_in, x_in, kb_in)
+    return finish_call(chans, base, a_in, b_in, x_in, ka_in, kb_in)
 
 
 def solution(mesh):

time: 27.1 us -> 26.2 us (0.967)
  waiting for transfers between devices: 5.13 us -> 4.57 us
  starting transfers between devices: 11.4 us -> 11.1 us
    ppermute x3, waiting for transfers between devices: 5.11 us -> 2.46 us  [across(): lax.ppermute(block, ('row', 'col'), route + (extra if mesh_cols == 2 else...]
    ppermute x2, waiting for transfers between devices: 0.01 us -> 2.11 us  [swap_x(): return lax.ppermute(block, 'col', channel[0])]
    ppermute x4 -> x5, starting transfers between devices: 3.63 us -> 2.69 us  [over_rows(): return lax.ppermute(block, ('row', 'col'), route + extra)]
    ppermute x3, starting transfers between devices: 3.5 us -> 4.19 us  [across(): lax.ppermute(block, ('row', 'col'), route + (extra if mesh_cols == 2 else...]
  transfers between devices with their start and end apart: 9 -> 10, of which waited for: 1 -> 2; matrix products, arithmetic and copies ran while one was open for 0% -> 0% of each run, Pallas kernels for 7% -> 7%
where the time goes in v8:
time: 26.2 us; the launch traced here: 26 us
  starting transfers between devices  11.1 us (42%)
  Pallas kernels  8.54 us (33%)
  waiting for transfers between devices  4.57 us (17%)
  local copies, waits for them, and re-layouts  1.06 us (4%)
  between operations  0.76 us (3%)
    pallas_call x1, Pallas kernels, views_call(): pl.pallas_call(functools.partial(views_kernel, chans), out_shape=[jax.Sha...  5.44 us
    ppermute x3, starting transfers between devices, across(): lax.ppermute(block, ('row', 'col'), route + (extra if mesh_cols == 2 else...  4.19 us
    ppermute x2, starting transfers between devices, swap_x(): return lax.ppermute(block, 'col', channel[0])  4.19 us
    ppermute x5, starting transfers between devices, over_rows(): return lax.ppermute(block, ('row', 'col'), route + extra)  2.69 us
    ppermute x3, waiting for transfers between devices, across(): lax.ppermute(block, ('row', 'col'), route + (extra if mesh_cols == 2 else...  2.46 us
    ppermute x2, waiting for transfers between devices, swap_x(): return lax.ppermute(block, 'col', channel[0])  2.11 us
    pallas_call x1, Pallas kernels, prepare_call(): pl.pallas_call(prepare_kernel, out_shape=jax.ShapeDtypeStruct((views, 2,...  1.9 us
    pallas_call x1, Pallas kernels, finish_call(): pl.pallas_call(functools.partial(finish_kernel, chans), out_shape=jax.Sha...  1.06 us
  transfers between devices with their start and end apart: 10, of which 2 were waited for; matrix products, arithmetic and copies ran while one was open for 0% of the time, Pallas kernels for 7%

profile of v8, /device:TPU:0, one launch (start us, length us, event | category | flops | bytes accessed | tf_op | source)
XLA Modules:
  0.0 26.0 jit_solution(1465101333772839731)
XLA Ops:
  0.0 0.0 copy-start
  0.0 1.0 %copy-done = f32[2,256,256]{2,1,0:T(8,128)S(1)} copy-done((f32[2,256,256]{2,1,0:T(8,128)S(1)}, f32[2,256,256]{2,1,0:T(8,128)}, u32[]{:S(2)}) %copy-start) | copy-done | bytes 524312
  1.0 0.0 copy-start.1
  1.0 0.0 copy-start.2
  1.0 0.0 copy-start.3
  1.0 0.0 copy-start.4
  1.1 0.1 shard_map.74
  1.2 3.0 %collective-permute-start = (f32[256,128]{1,0:T(8,128)S(1)}, f32[256,128]{1,0:T(8,128)S(1)}, u32[]{:S(2)}, u32[]{:S(2)}) collective-permute-start(f32[256,128]{1,0:T(8,128)S(1)} %get-tuple-element.15), channel_id=1, source_target_pairs={{0,1},{1,0},{2,3},{3,2},{4,5},{5,4},{6,7},{7,6},{8,9},{9,8},{10,11... | collective-permute-start | bytes 393224 | tf_op jit(solution)/shard_map/ppermute | solution.py:525
  4.2 0.1 collective-permute-start.1
  4.3 1.6 %collective-permute-start.4 = (f32[2,64,256]{2,1,0:T(8,128)S(1)}, f32[2,64,256]{2,1,0:T(8,128)S(1)}, u32[]{:S(2)}, u32[]{:S(2)}) collective-permute-start(f32[2,64,256]{2,1,0:T(8,128)S(1)} %get-tuple-element.19), channel_id=1, source_target_pairs={{0,2},{1,3},{4,6},{5,7},{8,10},{9,11},{12,14},{13,15},{16,18},{17,... | collective-permute-start | bytes 393224 | tf_op jit(solution)/shard_map/ppermute | solution.py:518
  5.8 0.5 %collective-permute-start.2 = (f32[64,128]{1,0:T(8,128)S(1)}, f32[64,128]{1,0:T(8,128)S(1)}, u32[]{:S(2)}, u32[]{:S(2)}) collective-permute-start(f32[64,128]{1,0:T(8,128)S(1)} %get-tuple-element.17), channel_id=1, source_target_pairs={{2,5},{3,4},{6,9},{7,8},{10,13},{11,12},{14,17},{15,16},{18,21},{1... | collective-permute-start | bytes 98312 | tf_op jit(solution)/shard_map/ppermute | solution.py:522
  6.4 2.2 %collective-permute-start.3 = (f32[64,128]{1,0:T(8,128)S(1)}, f32[64,128]{1,0:T(8,128)S(1)}, u32[]{:S(2)}, u32[]{:S(2)}) collective-permute-start(f32[64,128]{1,0:T(8,128)S(1)} %get-tuple-element.18), channel_id=1, source_target_pairs={{0,3},{1,2},{4,7},{5,6},{8,11},{9,10},{12,15},{13,14},{16,19},{17,... | collective-permute-start | bytes 98312 | tf_op jit(solution)/shard_map/ppermute | solution.py:522
  8.5 1.9 %shard_map.73.placed = f32[4,2,256,256]{3,2,1,0:T(8,128)S(1)} custom-call(s32[1,1,2,4]{3,2,1,0:T(2,128)} %bitcast.1, f32[2,256,256]{2,1,0:T(8,128)} %probe.1), custom_call_target="tpu_custom_call" | custom-call | flops 1000000000 | bytes 100000 | tf_op jit(solution)/shard_map/pallas_call | solution.py:183
  11.1 0.0 collective-permute-done.2.rest_2_
  11.1 0.0 collective-permute-done.3.rest_3_
  11.1 0.0 collective-permute-done.rest_0_
  11.1 0.0 collective-permute-done.1.rest_1_
  11.1 0.0 collective-permute-done.4.rest_4_
  11.1 0.0 copy-done.1
  11.2 0.0 copy-done.2
  11.2 0.0 copy-done.3
  11.2 0.0 copy-done.4
  11.2 5.4 %shard_map.75 = (f32[2,256,256]{2,1,0:T(8,128)S(1)}, f32[2,64,256]{2,1,0:T(8,128)S(1)}, f32[2,64,256]{2,1,0:T(8,128)S(1)}, f32[320,128]{1,0:T(8,128)S(1)}, f32[64,128]{1,0:T(8,128)S(1)}) custom-call(s32[1,1,2,4]{3,2,1,0:T(2,128)} %bitcast.2, s32[1,1]{1,0:T(1,128)S(6)} %copy.8.counts, f32[2,256,256]{2,1,0:T(8,128)S(1)} %copy-done.1, ...), custom_call_target="tpu_custom_call" | custom-call | tf_op jit(solution)/shard_map/pallas_call | solution.py:420
  16.6 1.2 %collective-permute-start.5 = (f32[320,128]{1,0:T(8,128)S(1)}, f32[320,128]{1,0:T(8,128)S(1)}, u32[]{:S(2)}, u32[]{:S(2)}) collective-permute-start(f32[320,128]{1,0:T(8,128)S(1)} %get-tuple-element.21), channel_id=1, source_target_pairs={{0,1},{1,0},{2,3},{3,2},{4,5},{5,4},{6,7},{7,6},{8,9},{9,8},{10,11... | collective-permute-start | bytes 491528 | tf_op jit(solution)/shard_map/ppermute | solution.py:525
  17.8 0.9 %collective-permute-start.6 = (f32[2,64,256]{2,1,0:T(8,128)S(1)}, f32[2,64,256]{2,1,0:T(8,128)S(1)}, u32[]{:S(2)}, u32[]{:S(2)}) collective-permute-start(f32[2,64,256]{2,1,0:T(8,128)S(1)} %get-tuple-element.22), channel_id=1, source_target_pairs={{2,4},{3,5},{6,8},{7,9},{10,12},{11,13},{14,16},{15,17},{18,20},{1... | collective-permute-start | bytes 393224 | tf_op jit(solution)/shard_map/ppermute | solution.py:518
  18.7 0.1 collective-permute-start.9
  18.9 1.5 %collective-permute-start.7 = (f32[64,128]{1,0:T(8,128)S(1)}, f32[64,128]{1,0:T(8,128)S(1)}, u32[]{:S(2)}, u32[]{:S(2)}) collective-permute-start(f32[64,128]{1,0:T(8,128)S(1)} %get-tuple-element.23), channel_id=1, source_target_pairs={{2,5},{3,4},{6,9},{7,8},{10,13},{11,12},{14,17},{15,16},{18,21},{1... | collective-permute-start | bytes 98312 | tf_op jit(solution)/shard_map/ppermute | solution.py:522
  20.4 2.1 %collective-permute-done.5.rest_0_ = f32[320,128]{1,0:T(8,128)S(1)} collective-permute-done((f32[320,128]{1,0:T(8,128)S(1)}, f32[320,128]{1,0:T(8,128)S(1)}, u32[]{:S(2)}, u32[]{:S(2)}) %collective-permute-start.5) | collective-permute-done | bytes 163872 | tf_op jit(solution)/shard_map/ppermute | solution.py:525
  22.5 0.0 collective-permute-start.8
  22.5 2.5 %collective-permute-done.7.rest_2_ = f32[64,128]{1,0:T(8,128)S(1)} collective-permute-done((f32[64,128]{1,0:T(8,128)S(1)}, f32[64,128]{1,0:T(8,128)S(1)}, u32[]{:S(2)}, u32[]{:S(2)}) %collective-permute-start.7) | collective-permute-done | bytes 32800 | tf_op jit(solution)/shard_map/ppermute | solution.py:522
  24.9 0.0 collective-permute-done.6.rest_1_
  24.9 0.0 collective-permute-done.9.rest_4_
  24.9 0.0 collective-permute-done.8.rest_3_
  24.9 1.1 %shard_map.76 = f32[2,256,256]{2,1,0:T(8,128)} custom-call(f32[2,256,256]{2,1,0:T(8,128)S(1)} %get-tuple-element.20.base, f32[320,128]{1,0:T(8,128)S(1)} %collective-permute-done.5.rest_0_, f32[2,64,256]{2,1,0:T(8,128)S(1)} %collective-permute-done.6.rest_1_, f32[64,128]{1,0:T(8,128)S(1)} %collective-permute-done.7.rest_2_, ...), custom_call_target="tpu_custom_call" | custom-call | tf_op jit(solution)/shard_map/pallas_call | solution.py:495
  (1 shorter events, 0.0 us)
Async XLA Ops:
  0.0 1.0 %copy-start = (f32[2,256,256]{2,1,0:T(8,128)S(1)}, f32[2,256,256]{2,1,0:T(8,128)}, u32[]{:S(2)}) copy-start(f32[2,256,256]{2,1,0:T(8,128)} %core.1) | copy-start | bytes 1572868
  1.0 10.1 %copy-start.1 = (f32[2,256,256]{2,1,0:T(8,128)S(1)}, f32[2,256,256]{2,1,0:T(8,128)}, u32[]{:S(2)}) copy-start(f32[2,256,256]{2,1,0:T(8,128)} %core.1) | copy-start | bytes 1572868
  1.0 10.1 %copy-start.2 = (f32[1,1,4,256,256]{4,3,2,1,0:T(8,128)S(1)}, f32[1,1,4,256,256]{4,3,2,1,0:T(8,128)}, u32[]{:S(2)}) copy-start(f32[1,1,4,256,256]{4,3,2,1,0:T(8,128)} %intensity.1) | copy-start | bytes 3145732
  1.0 10.1 %copy-start.3 = (bf16[4,256,512]{2,1,0:T(8,128)(2,1)S(1)}, bf16[4,256,512]{2,1,0:T(8,128)(2,1)}, u32[]{:S(2)}) copy-start(bf16[4,256,512]{2,1,0:T(8,128)(2,1)} %constant.5.clone.rest_6_) | copy-start | bytes 3145732
  1.0 10.1 %copy-start.4 = (bf16[4,512,256]{2,1,0:T(8,128)(2,1)S(1)}, bf16[4,512,256]{2,1,0:T(8,128)(2,1)}, u32[]{:S(2)}) copy-start(bf16[4,512,256]{2,1,0:T(8,128)(2,1)} %constant.4.clone.rest_5_) | copy-start | bytes 3145732
  1.2 9.9 %collective-permute-start = (f32[256,128]{1,0:T(8,128)S(1)}, f32[256,128]{1,0:T(8,128)S(1)}, u32[]{:S(2)}, u32[]{:S(2)}) collective-permute-start(f32[256,128]{1,0:T(8,128)S(1)} %get-tuple-element.15), channel_id=1, source_target_pairs={{0,1},{1,0},{2,3},{3,2},{4,5},{5,4},{6,7},{7,6},{8,9},{9,8},{10,11... | collective-permute-start | bytes 393224 | tf_op jit(solution)/shard_map/ppermute | solution.py:525
  4.2 6.9 %collective-permute-start.1 = (f32[2,64,256]{2,1,0:T(8,128)S(1)}, f32[2,64,256]{2,1,0:T(8,128)S(1)}, u32[]{:S(2)}, u32[]{:S(2)}) collective-permute-start(f32[2,64,256]{2,1,0:T(8,128)S(1)} %get-tuple-element.16), channel_id=1, source_target_pairs={{2,4},{3,5},{6,8},{7,9},{10,12},{11,13},{14,16},{15,17},{18,20},{1... | collective-permute-start | bytes 393224 | tf_op jit(solution)/shard_map/ppermute | solution.py:518
  4.3 6.9 %collective-permute-start.4 = (f32[2,64,256]{2,1,0:T(8,128)S(1)}, f32[2,64,256]{2,1,0:T(8,128)S(1)}, u32[]{:S(2)}, u32[]{:S(2)}) collective-permute-start(f32[2,64,256]{2,1,0:T(8,128)S(1)} %get-tuple-element.19), channel_id=1, source_target_pairs={{0,2},{1,3},{4,6},{5,7},{8,10},{9,11},{12,14},{13,15},{16,18},{17,... | collective-permute-start | bytes 393224 | tf_op jit(solution)/shard_map/ppermute | solution.py:518
  5.8 5.3 %collective-permute-start.2 = (f32[64,128]{1,0:T(8,128)S(1)}, f32[64,128]{1,0:T(8,128)S(1)}, u32[]{:S(2)}, u32[]{:S(2)}) collective-permute-start(f32[64,128]{1,0:T(8,128)S(1)} %get-tuple-element.17), channel_id=1, source_target_pairs={{2,5},{3,4},{6,9},{7,8},{10,13},{11,12},{14,17},{15,16},{18,21},{1... | collective-permute-start | bytes 98312 | tf_op jit(solution)/shard_map/ppermute | solution.py:522
  6.4 4.7 %collective-permute-start.3 = (f32[64,128]{1,0:T(8,128)S(1)}, f32[64,128]{1,0:T(8,128)S(1)}, u32[]{:S(2)}, u32[]{:S(2)}) collective-permute-start(f32[64,128]{1,0:T(8,128)S(1)} %get-tuple-element.18), channel_id=1, source_target_pairs={{0,3},{1,2},{4,7},{5,6},{8,11},{9,10},{12,15},{13,14},{16,19},{17,... | collective-permute-start | bytes 98312 | tf_op jit(solution)/shard_map/ppermute | solution.py:522
  16.6 5.8 %collective-permute-start.5 = (f32[320,128]{1,0:T(8,128)S(1)}, f32[320,128]{1,0:T(8,128)S(1)}, u32[]{:S(2)}, u32[]{:S(2)}) collective-permute-start(f32[320,128]{1,0:T(8,128)S(1)} %get-tuple-element.21), channel_id=1, source_target_pairs={{0,1},{1,0},{2,3},{3,2},{4,5},{5,4},{6,7},{7,6},{8,9},{9,8},{10,11... | collective-permute-start | bytes 491528 | tf_op jit(solution)/shard_map/ppermute | solution.py:525
  17.8 7.1 %collective-permute-start.6 = (f32[2,64,256]{2,1,0:T(8,128)S(1)}, f32[2,64,256]{2,1,0:T(8,128)S(1)}, u32[]{:S(2)}, u32[]{:S(2)}) collective-permute-start(f32[2,64,256]{2,1,0:T(8,128)S(1)} %get-tuple-element.22), channel_id=1, source_target_pairs={{2,4},{3,5},{6,8},{7,9},{10,12},{11,13},{14,16},{15,17},{18,20},{1... | collective-permute-start | bytes 393224 | tf_op jit(solution)/shard_map/ppermute | solution.py:518
  18.7 6.2 %collective-permute-start.9 = (f32[2,64,256]{2,1,0:T(8,128)S(1)}, f32[2,64,256]{2,1,0:T(8,128)S(1)}, u32[]{:S(2)}, u32[]{:S(2)}) collective-permute-start(f32[2,64,256]{2,1,0:T(8,128)S(1)} %get-tuple-element.24), channel_id=1, source_target_pairs={{0,2},{1,3},{4,6},{5,7},{8,10},{9,11},{12,14},{13,15},{16,18},{17,... | collective-permute-start | bytes 393224 | tf_op jit(solution)/shard_map/ppermute | solution.py:518
  18.9 6.0 %collective-permute-start.7 = (f32[64,128]{1,0:T(8,128)S(1)}, f32[64,128]{1,0:T(8,128)S(1)}, u32[]{:S(2)}, u32[]{:S(2)}) collective-permute-start(f32[64,128]{1,0:T(8,128)S(1)} %get-tuple-element.23), channel_id=1, source_target_pairs={{2,5},{3,4},{6,9},{7,8},{10,13},{11,12},{14,17},{15,16},{18,21},{1... | collective-permute-start | bytes 98312 | tf_op jit(solution)/shard_map/ppermute | solution.py:522
  22.5 2.5 %collective-permute-start.8 = (f32[64,128]{1,0:T(8,128)S(1)}, f32[64,128]{1,0:T(8,128)S(1)}, u32[]{:S(2)}, u32[]{:S(2)}) collective-permute-start(f32[64,128]{1,0:T(8,128)S(1)} %slice.4), channel_id=1, source_target_pairs={{0,2},{1,3},{4,6},{5,7},{8,10},{9,11},{12,14},{13,15},{16,18},{17,... | collective-permute-start | bytes 98312 | tf_op jit(solution)/shard_map/ppermute | solution.py:518

commit v9 on v6

--- a/solution.py
+++ b/solution.py
@@ -114,47 +114,66 @@
     return copies
 
 
-def pack_kernel(chans, object_ref, a_ref, b_ref, *edge_refs):
+def pack_kernel(chans, object_ref, *rest):
+    count = len(chans)
+    a_ref, b_ref, *edge_refs = rest[: 2 + 3 * count]
+    head, tail, sides, sems = rest[2 + 3 * count :]
     size = object_ref.shape[1]
-    top, bottom = pl.ds(0, MARGIN), pl.ds(size - MARGIN, MARGIN)
+    inner = size - 2 * MARGIN
+    low = lane_ids() < LANES // 2
     lower = lower_partner()
+    pairs = [(object_ref.at[:, pl.ds(0, MARGIN)], head), (object_ref.at[:, pl.ds(size - MARGIN, MARGIN)], tail)]
+    starts = []
+    for number, channel in enumerate(chans):
+        starts.append(pl.multiple_of(jnp.where(sends_right(channel), size - LANES, 0), LANES))
+        block = object_ref.at[:, pl.ds(MARGIN, inner), pl.ds(starts[-1], LANES)]
+        pairs.append((block, sides.at[number]))
+    copies = fetch(pairs, sems)
+    copies[0].wait()
+    copies[1].wait()
     for part in range(2):
-        head, tail = object_ref[part, top, :], object_ref[part, bottom, :]
-        a_ref[part] = jnp.where(lower, tail, head)
-        b_ref[part] = jnp.where(lower, head, tail)
+        a_ref[part] = jnp.where(lower, tail[part], head[part])
+        b_ref[part] = jnp.where(lower, head[part], tail[part])
     for number, channel in enumerate(chans):
         right = sends_right(channel)
         x_ref, ka_ref, kb_ref = edge_refs[3 * number : 3 * number + 3]
-        low = lane_ids() < LANES // 2
-        for start in range(0, size, CHUNK):
-            rows = slice(start, start + CHUNK)
-            left_edge = jnp.where(
-                low, object_ref[0, rows, :LANES], swap_halves(object_ref[1, rows, :LANES])
+
+        def packed(re, im):
+            return jnp.where(
+                right, jnp.where(low, swap_halves(im), re), jnp.where(low, re, swap_halves(im))
             )
-            right_edge = jnp.where(
-                low,
-                swap_halves(object_ref[1, rows, size - LANES :]),
-                object_ref[0, rows, size - LANES :],
-            )
-            x_ref[rows] = jnp.where(right, right_edge, left_edge)
-        ka_ref[...] = jnp.where(lower, x_ref[size - MARGIN :], x_ref[:MARGIN])
-        kb_ref[...] = jnp.where(lower, x_ref[:MARGIN], x_ref[size - MARGIN :])
+
+        lanes = pl.ds(starts[number], LANES)
+        upper = packed(head[0, :, lanes], head[1, :, lanes])
+        under = packed(tail[0, :, lanes], tail[1, :, lanes])
+        x_ref[:MARGIN], x_ref[size - MARGIN :] = upper, under
+        ka_ref[...] = jnp.where(lower, under, upper)
+        kb_ref[...] = jnp.where(lower, upper, under)
+        copies[2 + number].wait()
+        x_ref[MARGIN : size - MARGIN] = packed(sides[number, 0], sides[number, 1])
 
 
 def pack_call(object_field, chans):
     size = object_field.shape[1]
-    shapes = [(2, MARGIN, size)] * 2 + [(size, LANES), (MARGIN, LANES), (MARGIN, LANES)] * len(chans)
+    count = len(chans)
+    shapes = [(2, MARGIN, size)] * 2 + [(size, LANES), (MARGIN, LANES), (MARGIN, LANES)] * count
     vmem = pl.BlockSpec(memory_space=pltpu.VMEM)
     return pl.pallas_call(
         functools.partial(pack_kernel, chans),
         out_shape=[jax.ShapeDtypeStruct(shape, F32) for shape in shapes],
-        in_specs=[vmem],
+        in_specs=[pl.BlockSpec(memory_space=pltpu.HBM)],
         out_specs=[vmem] * len(shapes),
+        scratch_shapes=[
+            pltpu.VMEM((2, MARGIN, size), F32),
+            pltpu.VMEM((2, MARGIN, size), F32),
+            pltpu.VMEM((max(count, 1), 2, size - 2 * MARGIN, LANES), F32),
+            pltpu.SemaphoreType.DMA((2 + count,)),
+        ],
         compiler_params=pltpu.CompilerParams(vmem_limit_bytes=4 * 1024 * 1024),
-    )(object_field)
-
-
-def prepare_kernel(offsets_in, probe, placed, offsets, doubled, sems):
+    )(pltpu.with_memory_space_constraint(object_field, pltpu.HBM))
+
+
+def prepare_kernel(offsets_in, probe, placed, spots, offsets, doubled, sems):
     views, size = placed.shape[0], probe.shape[1]
     copies = fetch(
         [(offsets_in, offsets)] + [(probe, doubled.at[:, pl.ds(size * i, size)]) for i in range(2)], sems
@@ -163,6 +182,8 @@
     for copy in copies:
         copy.wait()
     for view in range(views):
+        for axis in range(2):
+            spots[view, axis] = jnp.full(spots.shape[2:], offsets[0, 0, axis, view], jnp.int32)
         shift_row = lax.rem(offsets[0, 0, 0, view] - MARGIN + size, size)
         shift_col = lax.rem(offsets[0, 0, 1, view] - MARGIN + size, size)
         start = lax.rem(size - shift_row, size)
@@ -182,9 +203,12 @@
     vmem, hbm = pl.BlockSpec(memory_space=pltpu.VMEM), pl.BlockSpec(memory_space=pltpu.HBM)
     return pl.pallas_call(
         prepare_kernel,
-        out_shape=jax.ShapeDtypeStruct((views, 2, size, size), F32),
+        out_shape=[
+            jax.ShapeDtypeStruct((views, 2, size, size), F32),
+            jax.ShapeDtypeStruct((views, 2, 8, LANES), jnp.int32),
+        ],
         in_specs=[hbm, hbm],
-        out_specs=vmem,
+        out_specs=[vmem, vmem],
         scratch_shapes=[
             pltpu.SMEM(offsets.shape, jnp.int32),
             pltpu.VMEM((2, 2 * size, size), F32),
@@ -195,7 +219,7 @@
     )(offsets, probe)
 
 
-def views_kernel(chans, offsets_in, counts, core, placed, intensity, *rest):
+def views_kernel(chans, spots, counts, core, placed, intensity, *rest):
     count = len(chans)
     x_in, b_in, rest = rest[:count], rest[count], rest[count + 1 :]
     kb_in, ka_in = rest[:count], rest[count : 2 * count]
@@ -203,8 +227,7 @@
     g_core, g_a, g_b = rest[:3]
     g_x, g_ka = rest[3 : 3 + count], rest[3 + count : 3 + 2 * count]
     g_kb = rest[3 + 2 * count : 3 + 3 * count]
-    offsets, sem, amplitude, cols_m, rows_m, corner_m, s1, y, s2, z, s3, u, s4, g = rest[3 + 3 * count :]
-    (offsets_copy,) = fetch([(offsets_in, offsets)], sem)
+    amplitude, cols_m, rows_m, corner_m, s1, y, s2, z, s3, u, s4, g = rest[3 + 3 * count :]
     views, size = placed.shape[0], core.shape[1]
     half, m = size // 2, MARGIN
     lower, partner = lower_partner(), b_partner()
@@ -231,8 +254,6 @@
         corner_m[part, :m] = jnp.where(lower, corner_a[part], corner_b[part])
         corner_m[part, m:] = jnp.where(lower, corner_b[part], corner_a[part])
 
-    offsets_copy.wait()
-
     def by_right(lhs, t):
         out = dot(lhs[:, :size], right[t, :size]) + dot(lhs[:, size:], right[t, :size])
         return out + dot(lhs[:, :size], right[t, size:])
@@ -256,15 +277,15 @@
     def row_mask(view, row):
         ids = row + lax.broadcasted_iota(jnp.int32, (CHUNK, LANES), 0)
         if row < m:
-            return ids < offsets[0, 0, 0, view] - m, row
+            return ids < spots[view, 0, :1] - m, row
         if row >= size - m:
-            return ids >= size - m + offsets[0, 0, 0, view], row - size + 2 * m
+            return ids >= size - m + spots[view, 0, :1], row - size + 2 * m
         return None, None
 
     def col_mask(view, block):
         if block == 0:
-            return lane_ids() < offsets[0, 0, 1, view] - m
-        return lane_ids() >= m + offsets[0, 0, 1, view]
+            return lane_ids() < spots[view, 1, :1] - m
+        return lane_ids() >= m + spots[view, 1, :1]
 
     def patch(view, row, block):
         cols = slice(block * LANES, (block + 1) * LANES)
@@ -409,7 +430,7 @@
         g_kb[number][...] = jnp.where(lower, above, below)
 
 
-def views_call(chans, offsets, counts, core, placed, intensity, tables, a_in, b_in, x_in, ka_in, kb_in):
+def views_call(chans, spots, counts, core, placed, intensity, tables, a_in, b_in, x_in, ka_in, kb_in):
     views, size = placed.shape[0], core.shape[1]
     count = len(chans)
     vmem = pl.BlockSpec(memory_space=pltpu.VMEM)
@@ -422,14 +443,12 @@
         functools.partial(views_kernel, chans),
         out_shape=[jax.ShapeDtypeStruct(shape, F32) for shape in shapes],
         in_specs=[
-            pl.BlockSpec(memory_space=pltpu.HBM),
+            vmem,
             pl.BlockSpec(memory_space=pltpu.SMEM),
             *[vmem] * (7 + 3 * count),
         ],
         out_specs=[vmem] * len(shapes),
         scratch_shapes=[
-            pltpu.SMEM(offsets.shape, jnp.int32),
-            pltpu.SemaphoreType.DMA((1,)),
             pltpu.VMEM((views, 2, size, size // 2), F32),
             pltpu.VMEM((2, size, LANES), F32),
             pltpu.VMEM((2, 2 * MARGIN, size), F32),
@@ -437,7 +456,7 @@
             wide, full, tall, full, tall, full, wide, full,
         ],
         compiler_params=pltpu.CompilerParams(vmem_limit_bytes=40 * 1024 * 1024),
-    )(offsets, counts, core, placed, intensity, *x_in, b_in, *kb_in, *ka_in, a_in, *tables)
+    )(spots, counts, core, placed, intensity, *x_in, b_in, *kb_in, *ka_in, a_in, *tables)
     return (*outs[:3], outs[3 : 3 + count], outs[3 + count : 3 + 2 * count], outs[3 + 2 * count :])
 
 
@@ -521,9 +540,9 @@
         for array in (jnp.swapaxes(view_offsets, 2, 3), probe_field)
     )
     margins = exchange(packs[0], packs[1], packs[2::3], packs[3::3], packs[4::3])
-    placed = prepare_call(offsets, probe)
+    placed, spots = prepare_call(offsets, probe)
     g_core, *sends = views_call(
-        chans, offsets, view_counts, object_field, placed, intensity, tables, *margins
+        chans, spots, view_counts, object_field, placed, intensity, tables, *margins
     )
     return finish_call(chans, object_field, g_core, *exchange(*sends))
 

time: 25.6 us -> 25.8 us (level)
  local copies, waits for them, and re-layouts: 1.06 us -> 0.01 us
  waiting for transfers between devices: 2.33 us -> 3.08 us
  Pallas kernels: 8.45 us -> 9.15 us
    pallas_call x1, Pallas kernels: 0.13 us -> 1.32 us  [pack_call(): pl.pallas_call(functools.partial(pack_kernel, chans), out_shape=[jax.Shap...]
    unnamed x10 -> x8, local copies, waits for them, and re-layouts: 1.06 us -> 0.01 us
    ppermute x4, waiting for transfers between devices: 2.32 us -> 3.07 us  [across(): lax.ppermute(block, ('row', 'col'), route + (extra if mesh_cols == 2 else...]
    pallas_call x1, Pallas kernels: 5.41 us -> 4.92 us  [views_call(): pl.pallas_call(functools.partial(views_kernel, chans), out_shape=[jax.Sha...]
  transfers between devices with their start and end apart: 10 -> 10, of which waited for: 2 -> 2; matrix products, arithmetic and copies ran while one was open for 0% -> 0% of each run, Pallas kernels for 8% -> 7%
where the time goes in v9:
time: 25.8 us; the launch traced here: 25.6 us
  starting transfers between devices  12.6 us (49%)
  Pallas kernels  9.15 us (35%)
  waiting for transfers between devices  3.08 us (12%)
  between operations  0.76 us (3%)
    ppermute x4, starting transfers between devices, across(): lax.ppermute(block, ('row', 'col'), route + (extra if mesh_cols == 2 else...  5.73 us
    pallas_call x1, Pallas kernels, views_call(): pl.pallas_call(functools.partial(views_kernel, chans), out_shape=[jax.Sha...  4.92 us
    ppermute x2, starting transfers between devices, exchange(): lax.ppermute(block, 'col', channel[0])  4.2 us
    ppermute x4, waiting for transfers between devices, across(): lax.ppermute(block, ('row', 'col'), route + (extra if mesh_cols == 2 else...  3.07 us
    ppermute x4, starting transfers between devices, over_rows(): return lax.ppermute(block, ('row', 'col'), route + extra)  2.68 us
    pallas_call x1, Pallas kernels, prepare_call(): pl.pallas_call(prepare_kernel, out_shape=[jax.ShapeDtypeStruct((views, 2,...  1.91 us
    pallas_call x1, Pallas kernels, pack_call(): pl.pallas_call(functools.partial(pack_kernel, chans), out_shape=[jax.Shap...  1.32 us
    pallas_call x1, Pallas kernels, finish_call(): pl.pallas_call(functools.partial(finish_kernel, chans), out_shape=jax.Sha...  1 us
  transfers between devices with their start and end apart: 10, of which 2 were waited for; matrix products, arithmetic and copies ran while one was open for 0% of the time, Pallas kernels for 7%

profile of v9, /device:TPU:0, one launch (start us, length us, event | category | flops | bytes accessed | tf_op | source)
XLA Modules:
  0.0 25.6 jit_solution(7883747716598925144)
XLA Ops:
  0.0 0.0 copy-start.2
  0.0 0.0 copy-start.3
  0.0 0.0 copy-start
  0.0 0.0 copy-start.1
  0.0 1.3 %shard_map.74 = (f32[2,64,256]{2,1,0:T(8,128)S(1)}, f32[2,64,256]{2,1,0:T(8,128)S(1)}, f32[256,128]{1,0:T(8,128)S(1)}, f32[64,128]{1,0:T(8,128)S(1)}, f32[64,128]{1,0:T(8,128)S(1)}) custom-call(f32[2,256,256]{2,1,0:T(8,128)} %object_ref.3), custom_call_target="tpu_custom_call" | custom-call | tf_op jit(solution)/shard_map/pallas_call | solution.py:161
  1.3 3.0 %collective-permute-start = (f32[256,128]{1,0:T(8,128)S(1)}, f32[256,128]{1,0:T(8,128)S(1)}, u32[]{:S(2)}, u32[]{:S(2)}) collective-permute-start(f32[256,128]{1,0:T(8,128)S(1)} %get-tuple-element.20), channel_id=1, source_target_pairs={{0,1},{1,0},{2,3},{3,2},{4,5},{5,4},{6,7},{7,6},{8,9},{9,8},{10,11... | collective-permute-start | bytes 393224 | tf_op jit(solution)/shard_map/ppermute | solution.py:530
  4.3 0.1 collective-permute-start.1
  4.4 1.6 %collective-permute-start.4 = (f32[2,64,256]{2,1,0:T(8,128)S(1)}, f32[2,64,256]{2,1,0:T(8,128)S(1)}, u32[]{:S(2)}, u32[]{:S(2)}) collective-permute-start(f32[2,64,256]{2,1,0:T(8,128)S(1)} %get-tuple-element.24), channel_id=1, source_target_pairs={{0,2},{1,3},{4,6},{5,7},{8,10},{9,11},{12,14},{13,15},{16,18},{17,... | collective-permute-start | bytes 393224 | tf_op jit(solution)/shard_map/ppermute | solution.py:523
  6.0 0.5 %collective-permute-start.2 = (f32[64,128]{1,0:T(8,128)S(1)}, f32[64,128]{1,0:T(8,128)S(1)}, u32[]{:S(2)}, u32[]{:S(2)}) collective-permute-start(f32[64,128]{1,0:T(8,128)S(1)} %get-tuple-element.22), channel_id=1, source_target_pairs={{2,5},{3,4},{6,9},{7,8},{10,13},{11,12},{14,17},{15,16},{18,21},{1... | collective-permute-start | bytes 98312 | tf_op jit(solution)/shard_map/ppermute | solution.py:527
  6.5 2.2 %collective-permute-start.3 = (f32[64,128]{1,0:T(8,128)S(1)}, f32[64,128]{1,0:T(8,128)S(1)}, u32[]{:S(2)}, u32[]{:S(2)}) collective-permute-start(f32[64,128]{1,0:T(8,128)S(1)} %get-tuple-element.23), channel_id=1, source_target_pairs={{0,3},{1,2},{4,7},{5,6},{8,11},{9,10},{12,15},{13,14},{16,19},{17,... | collective-permute-start | bytes 98312 | tf_op jit(solution)/shard_map/ppermute | solution.py:527
  8.7 1.9 %shard_map.73 = (f32[4,2,256,256]{3,2,1,0:T(8,128)S(1)}, s32[4,2,8,128]{3,2,1,0:T(8,128)S(1)}) custom-call(s32[1,1,2,4]{3,2,1,0:T(2,128)} %bitcast.1, f32[2,256,256]{2,1,0:T(8,128)} %probe.1), custom_call_target="tpu_custom_call" | custom-call | flops 1000000000 | bytes 100000 | tf_op jit(solution)/shard_map/pallas_call | solution.py:204
  11.2 0.0 collective-permute-done.2.rest_2_
  11.3 0.0 collective-permute-done.3.rest_3_
  11.3 0.0 collective-permute-done.rest_0_
  11.3 0.0 collective-permute-done.1.rest_1_
  11.3 0.0 collective-permute-done.4.rest_4_
  11.3 0.0 copy-done.2
  11.3 0.0 copy-done.3
  11.3 0.0 copy-done
  11.3 0.0 copy-done.1
  11.3 4.9 %shard_map.75 = (f32[2,256,256]{2,1,0:T(8,128)S(1)}, f32[2,64,256]{2,1,0:T(8,128)S(1)}, f32[2,64,256]{2,1,0:T(8,128)S(1)}, f32[256,128]{1,0:T(8,128)S(1)}, f32[64,128]{1,0:T(8,128)S(1)}, /*index=5*/f32[64,128]{1,0:T(8,128)S(1)}) custom-call(s32[4,2,8,128]{3,2,1,0:T(8,128)S(1)} %get-tuple-element.18.spots, s32[1,1]{1,0:T(1,128)S(6)} %copy.8.counts, ...), custom_call_target="tpu_custom_call" | custom-call | tf_op jit(solution)/shard_map/pallas_call | solution.py:442
  16.3 1.2 %collective-permute-start.5 = (f32[256,128]{1,0:T(8,128)S(1)}, f32[256,128]{1,0:T(8,128)S(1)}, u32[]{:S(2)}, u32[]{:S(2)}) collective-permute-start(f32[256,128]{1,0:T(8,128)S(1)} %get-tuple-element.26), channel_id=1, source_target_pairs={{0,1},{1,0},{2,3},{3,2},{4,5},{5,4},{6,7},{7,6},{8,9},{9,8},{10,11... | collective-permute-start | bytes 393224 | tf_op jit(solution)/shard_map/ppermute | solution.py:530
  17.5 0.9 %collective-permute-start.6 = (f32[2,64,256]{2,1,0:T(8,128)S(1)}, f32[2,64,256]{2,1,0:T(8,128)S(1)}, u32[]{:S(2)}, u32[]{:S(2)}) collective-permute-start(f32[2,64,256]{2,1,0:T(8,128)S(1)} %get-tuple-element.27), channel_id=1, source_target_pairs={{2,4},{3,5},{6,8},{7,9},{10,12},{11,13},{14,16},{15,17},{18,20},{1... | collective-permute-start | bytes 393224 | tf_op jit(solution)/shard_map/ppermute | solution.py:523
  18.4 0.1 collective-permute-start.9
  18.5 1.5 %collective-permute-start.7 = (f32[64,128]{1,0:T(8,128)S(1)}, f32[64,128]{1,0:T(8,128)S(1)}, u32[]{:S(2)}, u32[]{:S(2)}) collective-permute-start(f32[64,128]{1,0:T(8,128)S(1)} %get-tuple-element.28), channel_id=1, source_target_pairs={{2,5},{3,4},{6,9},{7,8},{10,13},{11,12},{14,17},{15,16},{18,21},{1... | collective-permute-start | bytes 98312 | tf_op jit(solution)/shard_map/ppermute | solution.py:527
  20.0 1.5 %collective-permute-start.8 = (f32[64,128]{1,0:T(8,128)S(1)}, f32[64,128]{1,0:T(8,128)S(1)}, u32[]{:S(2)}, u32[]{:S(2)}) collective-permute-start(f32[64,128]{1,0:T(8,128)S(1)} %get-tuple-element.29), channel_id=1, source_target_pairs={{0,3},{1,2},{4,7},{5,6},{8,11},{9,10},{12,15},{13,14},{16,19},{17,... | collective-permute-start | bytes 98312 | tf_op jit(solution)/shard_map/ppermute | solution.py:527
  21.5 2.9 %collective-permute-done.7.rest_2_ = f32[64,128]{1,0:T(8,128)S(1)} collective-permute-done((f32[64,128]{1,0:T(8,128)S(1)}, f32[64,128]{1,0:T(8,128)S(1)}, u32[]{:S(2)}, u32[]{:S(2)}) %collective-permute-start.7) | collective-permute-done | bytes 32800 | tf_op jit(solution)/shard_map/ppermute | solution.py:527
  24.5 0.1 collective-permute-done.8.rest_3_
  24.6 0.0 collective-permute-done.5.rest_0_
  24.6 0.0 collective-permute-done.6.rest_1_
  24.6 0.0 collective-permute-done.9.rest_4_
  24.6 1.0 %shard_map.76 = f32[2,256,256]{2,1,0:T(8,128)} custom-call(f32[2,256,256]{2,1,0:T(8,128)S(1)} %copy-done, f32[2,256,256]{2,1,0:T(8,128)S(1)} %get-tuple-element.25.g_core, f32[256,128]{1,0:T(8,128)S(1)} %collective-permute-done.5.rest_0_, f32[2,64,256]{2,1,0:T(8,128)S(1)} %collective-permute-done.6.rest_1_, f32[64,128]{1,0:T(8,128)S(1)} %collective-permute-done.7.rest_2_, ...), custom_call_target="tpu_custom_call" | custom-call | tf_op jit(solution)/shard_map/pallas_call | solution.py:504
Async XLA Ops:
  0.0 11.3 %copy-start.2 = (bf16[4,256,512]{2,1,0:T(8,128)(2,1)S(1)}, bf16[4,256,512]{2,1,0:T(8,128)(2,1)}, u32[]{:S(2)}) copy-start(bf16[4,256,512]{2,1,0:T(8,128)(2,1)} %constant.5.clone.rest_6_) | copy-start | bytes 3145732
  0.0 11.3 %copy-start.3 = (bf16[4,512,256]{2,1,0:T(8,128)(2,1)S(1)}, bf16[4,512,256]{2,1,0:T(8,128)(2,1)}, u32[]{:S(2)}) copy-start(bf16[4,512,256]{2,1,0:T(8,128)(2,1)} %constant.4.clone.rest_5_) | copy-start | bytes 3145732
  0.0 11.3 %copy-start = (f32[2,256,256]{2,1,0:T(8,128)S(1)}, f32[2,256,256]{2,1,0:T(8,128)}, u32[]{:S(2)}) copy-start(f32[2,256,256]{2,1,0:T(8,128)} %object_ref.3) | copy-start | bytes 1572868
  0.0 11.3 %copy-start.1 = (f32[1,1,4,256,256]{4,3,2,1,0:T(8,128)S(1)}, f32[1,1,4,256,256]{4,3,2,1,0:T(8,128)}, u32[]{:S(2)}) copy-start(f32[1,1,4,256,256]{4,3,2,1,0:T(8,128)} %intensity.1) | copy-start | bytes 3145732
  1.3 9.9 %collective-permute-start = (f32[256,128]{1,0:T(8,128)S(1)}, f32[256,128]{1,0:T(8,128)S(1)}, u32[]{:S(2)}, u32[]{:S(2)}) collective-permute-start(f32[256,128]{1,0:T(8,128)S(1)} %get-tuple-element.20), channel_id=1, source_target_pairs={{0,1},{1,0},{2,3},{3,2},{4,5},{5,4},{6,7},{7,6},{8,9},{9,8},{10,11... | collective-permute-start | bytes 393224 | tf_op jit(solution)/shard_map/ppermute | solution.py:530
  4.3 6.9 %collective-permute-start.1 = (f32[2,64,256]{2,1,0:T(8,128)S(1)}, f32[2,64,256]{2,1,0:T(8,128)S(1)}, u32[]{:S(2)}, u32[]{:S(2)}) collective-permute-start(f32[2,64,256]{2,1,0:T(8,128)S(1)} %get-tuple-element.21), channel_id=1, source_target_pairs={{2,4},{3,5},{6,8},{7,9},{10,12},{11,13},{14,16},{15,17},{18,20},{1... | collective-permute-start | bytes 393224 | tf_op jit(solution)/shard_map/ppermute | solution.py:523
  4.4 6.9 %collective-permute-start.4 = (f32[2,64,256]{2,1,0:T(8,128)S(1)}, f32[2,64,256]{2,1,0:T(8,128)S(1)}, u32[]{:S(2)}, u32[]{:S(2)}) collective-permute-start(f32[2,64,256]{2,1,0:T(8,128)S(1)} %get-tuple-element.24), channel_id=1, source_target_pairs={{0,2},{1,3},{4,6},{5,7},{8,10},{9,11},{12,14},{13,15},{16,18},{17,... | collective-permute-start | bytes 393224 | tf_op jit(solution)/shard_map/ppermute | solution.py:523
  6.0 5.3 %collective-permute-start.2 = (f32[64,128]{1,0:T(8,128)S(1)}, f32[64,128]{1,0:T(8,128)S(1)}, u32[]{:S(2)}, u32[]{:S(2)}) collective-permute-start(f32[64,128]{1,0:T(8,128)S(1)} %get-tuple-element.22), channel_id=1, source_target_pairs={{2,5},{3,4},{6,9},{7,8},{10,13},{11,12},{14,17},{15,16},{18,21},{1... | collective-permute-start | bytes 98312 | tf_op jit(solution)/shard_map/ppermute | solution.py:527
  6.5 4.7 %collective-permute-start.3 = (f32[64,128]{1,0:T(8,128)S(1)}, f32[64,128]{1,0:T(8,128)S(1)}, u32[]{:S(2)}, u32[]{:S(2)}) collective-permute-start(f32[64,128]{1,0:T(8,128)S(1)} %get-tuple-element.23), channel_id=1, source_target_pairs={{0,3},{1,2},{4,7},{5,6},{8,11},{9,10},{12,15},{13,14},{16,19},{17,... | collective-permute-start | bytes 98312 | tf_op jit(solution)/shard_map/ppermute | solution.py:527
  16.3 8.3 %collective-permute-start.5 = (f32[256,128]{1,0:T(8,128)S(1)}, f32[256,128]{1,0:T(8,128)S(1)}, u32[]{:S(2)}, u32[]{:S(2)}) collective-permute-start(f32[256,128]{1,0:T(8,128)S(1)} %get-tuple-element.26), channel_id=1, source_target_pairs={{0,1},{1,0},{2,3},{3,2},{4,5},{5,4},{6,7},{7,6},{8,9},{9,8},{10,11... | collective-permute-start | bytes 393224 | tf_op jit(solution)/shard_map/ppermute | solution.py:530
  17.5 7.1 %collective-permute-start.6 = (f32[2,64,256]{2,1,0:T(8,128)S(1)}, f32[2,64,256]{2,1,0:T(8,128)S(1)}, u32[]{:S(2)}, u32[]{:S(2)}) collective-permute-start(f32[2,64,256]{2,1,0:T(8,128)S(1)} %get-tuple-element.27), channel_id=1, source_target_pairs={{2,4},{3,5},{6,8},{7,9},{10,12},{11,13},{14,16},{15,17},{18,20},{1... | collective-permute-start | bytes 393224 | tf_op jit(solution)/shard_map/ppermute | solution.py:523
  18.4 6.3 %collective-permute-start.9 = (f32[2,64,256]{2,1,0:T(8,128)S(1)}, f32[2,64,256]{2,1,0:T(8,128)S(1)}, u32[]{:S(2)}, u32[]{:S(2)}) collective-permute-start(f32[2,64,256]{2,1,0:T(8,128)S(1)} %get-tuple-element.30), channel_id=1, source_target_pairs={{0,2},{1,3},{4,6},{5,7},{8,10},{9,11},{12,14},{13,15},{16,18},{17,... | collective-permute-start | bytes 393224 | tf_op jit(solution)/shard_map/ppermute | solution.py:523
  18.5 6.0 %collective-permute-start.7 = (f32[64,128]{1,0:T(8,128)S(1)}, f32[64,128]{1,0:T(8,128)S(1)}, u32[]{:S(2)}, u32[]{:S(2)}) collective-permute-start(f32[64,128]{1,0:T(8,128)S(1)} %get-tuple-element.28), channel_id=1, source_target_pairs={{2,5},{3,4},{6,9},{7,8},{10,13},{11,12},{14,17},{15,16},{18,21},{1... | collective-permute-start | bytes 98312 | tf_op jit(solution)/shard_map/ppermute | solution.py:527
  20.0 4.6 %collective-permute-start.8 = (f32[64,128]{1,0:T(8,128)S(1)}, f32[64,128]{1,0:T(8,128)S(1)}, u32[]{:S(2)}, u32[]{:S(2)}) collective-permute-start(f32[64,128]{1,0:T(8,128)S(1)} %get-tuple-element.29), channel_id=1, source_target_pairs={{0,3},{1,2},{4,7},{5,6},{8,11},{9,10},{12,15},{13,14},{16,19},{17,... | collective-permute-start | bytes 98312 | tf_op jit(solution)/shard_map/ppermute | solution.py:527

commit v10 on v6

--- a/solution.py
+++ b/solution.py
@@ -14,7 +14,7 @@
 MARGIN = 64
 LANES = 128
 CHUNK = 64
-STAGGER = 4
+STAGGER = 2
 
 smooth_eps = 0.1
 step_size = 0.2
@@ -41,7 +41,7 @@
 
     even, odd = as_real(even), as_real(odd)
     by_right = [np.concatenate(parts(t), 0) for t in (even, odd, even.T, odd.T)]
-    by_left = [np.concatenate(parts(t), 1) for t in (even.T, odd.T, even, odd)]
+    by_left = [np.concatenate(parts(t), 0) for t in (even.T, odd.T, even, odd)]
     return np.stack(by_right), np.stack(by_left)
 
 
@@ -154,7 +154,7 @@
     )(object_field)
 
 
-def prepare_kernel(offsets_in, probe, placed, offsets, doubled, sems):
+def prepare_kernel(offsets_in, probe, placed, spots, offsets, doubled, sems):
     views, size = placed.shape[0], probe.shape[1]
     copies = fetch(
         [(offsets_in, offsets)] + [(probe, doubled.at[:, pl.ds(size * i, size)]) for i in range(2)], sems
@@ -163,6 +163,8 @@
     for copy in copies:
         copy.wait()
     for view in range(views):
+        for axis in range(2):
+            spots[view, axis] = jnp.full(spots.shape[2:], offsets[0, 0, axis, view], jnp.int32)
         shift_row = lax.rem(offsets[0, 0, 0, view] - MARGIN + size, size)
         shift_col = lax.rem(offsets[0, 0, 1, view] - MARGIN + size, size)
         start = lax.rem(size - shift_row, size)
@@ -182,9 +184,12 @@
     vmem, hbm = pl.BlockSpec(memory_space=pltpu.VMEM), pl.BlockSpec(memory_space=pltpu.HBM)
     return pl.pallas_call(
         prepare_kernel,
-        out_shape=jax.ShapeDtypeStruct((views, 2, size, size), F32),
+        out_shape=[
+            jax.ShapeDtypeStruct((views, 2, size, size), F32),
+            jax.ShapeDtypeStruct((views, 2, 8, LANES), jnp.int32),
+        ],
         in_specs=[hbm, hbm],
-        out_specs=vmem,
+        out_specs=[vmem, vmem],
         scratch_shapes=[
             pltpu.SMEM(offsets.shape, jnp.int32),
             pltpu.VMEM((2, 2 * size, size), F32),
@@ -195,7 +200,7 @@
     )(offsets, probe)
 
 
-def views_kernel(chans, offsets_in, counts, core, placed, intensity, *rest):
+def views_kernel(chans, spots, counts, core, placed, intensity, *rest):
     count = len(chans)
     x_in, b_in, rest = rest[:count], rest[count], rest[count + 1 :]
     kb_in, ka_in = rest[:count], rest[count : 2 * count]
@@ -203,8 +208,7 @@
     g_core, g_a, g_b = rest[:3]
     g_x, g_ka = rest[3 : 3 + count], rest[3 + count : 3 + 2 * count]
     g_kb = rest[3 + 2 * count : 3 + 3 * count]
-    offsets, sem, amplitude, cols_m, rows_m, corner_m, s1, y, s2, z, s3, u, s4, g = rest[3 + 3 * count :]
-    (offsets_copy,) = fetch([(offsets_in, offsets)], sem)
+    amplitude, cols_m, rows_m, corner_m, s1, y, s2, z, s3, u, s4, g = rest[3 + 3 * count :]
     views, size = placed.shape[0], core.shape[1]
     half, m = size // 2, MARGIN
     lower, partner = lower_partner(), b_partner()
@@ -231,40 +235,32 @@
         corner_m[part, :m] = jnp.where(lower, corner_a[part], corner_b[part])
         corner_m[part, m:] = jnp.where(lower, corner_b[part], corner_a[part])
 
-    offsets_copy.wait()
-
     def by_right(lhs, t):
-        out = dot(lhs[:, :size], right[t, :size]) + dot(lhs[:, size:], right[t, :size])
-        return out + dot(lhs[:, :size], right[t, size:])
+        both = dot(lhs[...], right[t, :size])
+        return both[:size] + both[size:] + dot(lhs[:size], right[t, size:])
 
     def by_left(t, rhs):
-        out = dot(left[t, :, :size], rhs[:size]) + dot(left[t, :, :size], rhs[size:])
-        return out + dot(left[t, :, size:], rhs[:size])
-
-    def put_below(ref, row, col, value):
+        both = dot(left[t], rhs[:size])
+        return both[:size] + both[size:] + dot(left[t, :size], rhs[size:])
+
+    def put(ref, row, col, value):
         high, low = split(value)
         rows, cols = value.shape
         ref[row : row + rows, col : col + cols] = high
         ref[size + row : size + row + rows, col : col + cols] = low
 
-    def put_beside(ref, row, col, value):
-        high, low = split(value)
-        rows, cols = value.shape
-        ref[row : row + rows, col : col + cols] = high
-        ref[row : row + rows, size + col : size + col + cols] = low
-
     def row_mask(view, row):
         ids = row + lax.broadcasted_iota(jnp.int32, (CHUNK, LANES), 0)
         if row < m:
-            return ids < offsets[0, 0, 0, view] - m, row
+            return ids < spots[view, 0, :1] - m, row
         if row >= size - m:
-            return ids >= size - m + offsets[0, 0, 0, view], row - size + 2 * m
+            return ids >= size - m + spots[view, 0, :1], row - size + 2 * m
         return None, None
 
     def col_mask(view, block):
         if block == 0:
-            return lane_ids() < offsets[0, 0, 1, view] - m
-        return lane_ids() >= m + offsets[0, 0, 1, view]
+            return lane_ids() < spots[view, 1, :1] - m
+        return lane_ids() >= m + spots[view, 1, :1]
 
     def patch(view, row, block):
         cols = slice(block * LANES, (block + 1) * LANES)
@@ -291,8 +287,8 @@
                 p_re, p_im = placed[view, 0, rows, cols], placed[view, 1, rows, cols]
                 waves.append((p_re * o_re - p_im * o_im, p_re * o_im + p_im * o_re))
             for part in range(2):
-                put_beside(s1.at[view, 0], row, part * half, waves[0][part] + waves[1][part])
-                put_beside(s1.at[view, 1], row, part * half, waves[0][part] - waves[1][part])
+                put(s1.at[view, 0], row, part * half, waves[0][part] + waves[1][part])
+                put(s1.at[view, 1], row, part * half, waves[0][part] - waves[1][part])
             yield
         for odd in range(2):
             y[view, odd] = by_right(s1.at[view, odd], odd)
@@ -303,8 +299,8 @@
                     cols = slice(part * half, (part + 1) * half)
                     above = y[view, odd, row : row + CHUNK, cols]
                     below = y[view, odd, half + row : half + row + CHUNK, cols]
-                    put_below(s2.at[view, 0], part * half + row, odd * half, above + below)
-                    put_below(s2.at[view, 1], part * half + row, odd * half, above - below)
+                    put(s2.at[view, 0], part * half + row, odd * half, above + below)
+                    put(s2.at[view, 1], part * half + row, odd * half, above - below)
                 yield
         valid = (view < counts[0, 0]).astype(F32)
         for row in range(0, size, CHUNK):
@@ -328,8 +324,8 @@
                 taken = pl.ds(2 * row + odd, CHUNK, stride=2)
                 wanted = jnp.concatenate([amplitude[view, 0, taken], amplitude[view, 1, taken]], 1)
                 scaling = valid - wanted * lax.rsqrt(re * re + im * im + smooth_eps)
-                put_below(s3.at[view, odd], row, 0, re * scaling)
-                put_below(s3.at[view, odd], half + row, 0, im * scaling)
+                put(s3.at[view, odd], row, 0, re * scaling)
+                put(s3.at[view, odd], half + row, 0, im * scaling)
                 yield
         for odd in range(2):
             u[view, odd] = by_left(2 + odd, s3.at[view, odd])
@@ -339,8 +335,8 @@
                 rows = slice(part * half + row, part * half + row + CHUNK)
                 even_rows, odd_rows = u[view, 0, rows], u[view, 1, rows]
                 for value, place in ((even_rows + odd_rows, row), (even_rows - odd_rows, half + row)):
-                    put_beside(s4.at[view, 0], place, part * half, value[:, :half])
-                    put_beside(s4.at[view, 1], place, part * half, value[:, half:])
+                    put(s4.at[view, 0], place, part * half, value[:, :half])
+                    put(s4.at[view, 1], place, part * half, value[:, half:])
                 yield
         for odd in range(2):
             g[view, odd] = by_right(s4.at[view, odd], 2 + odd)
@@ -409,7 +405,7 @@
         g_kb[number][...] = jnp.where(lower, above, below)
 
 
-def views_call(chans, offsets, counts, core, placed, intensity, tables, a_in, b_in, x_in, ka_in, kb_in):
+def views_call(chans, spots, counts, core, placed, intensity, tables, a_in, b_in, x_in, ka_in, kb_in):
     views, size = placed.shape[0], core.shape[1]
     count = len(chans)
     vmem = pl.BlockSpec(memory_space=pltpu.VMEM)
@@ -417,27 +413,24 @@
     shapes += [(size, LANES)] * count + [(MARGIN, LANES)] * (2 * count)
     full = pltpu.VMEM((views, 2, size, size), F32)
     tall = pltpu.VMEM((views, 2, 2 * size, size), BF16)
-    wide = pltpu.VMEM((views, 2, size, 2 * size), BF16)
     outs = pl.pallas_call(
         functools.partial(views_kernel, chans),
         out_shape=[jax.ShapeDtypeStruct(shape, F32) for shape in shapes],
         in_specs=[
-            pl.BlockSpec(memory_space=pltpu.HBM),
+            vmem,
             pl.BlockSpec(memory_space=pltpu.SMEM),
             *[vmem] * (7 + 3 * count),
         ],
         out_specs=[vmem] * len(shapes),
         scratch_shapes=[
-            pltpu.SMEM(offsets.shape, jnp.int32),
-            pltpu.SemaphoreType.DMA((1,)),
             pltpu.VMEM((views, 2, size, size // 2), F32),
             pltpu.VMEM((2, size, LANES), F32),
             pltpu.VMEM((2, 2 * MARGIN, size), F32),
             pltpu.VMEM((2, 2 * MARGIN, LANES), F32),
-            wide, full, tall, full, tall, full, wide, full,
+            *[tall, full] * 4,
         ],
         compiler_params=pltpu.CompilerParams(vmem_limit_bytes=40 * 1024 * 1024),
-    )(offsets, counts, core, placed, intensity, *x_in, b_in, *kb_in, *ka_in, a_in, *tables)
+    )(spots, counts, core, placed, intensity, *x_in, b_in, *kb_in, *ka_in, a_in, *tables)
     return (*outs[:3], outs[3 : 3 + count], outs[3 + count : 3 + 2 * count], outs[3 + 2 * count :])
 
 
@@ -521,9 +514,9 @@
         for array in (jnp.swapaxes(view_offsets, 2, 3), probe_field)
     )
     margins = exchange(packs[0], packs[1], packs[2::3], packs[3::3], packs[4::3])
-    placed = prepare_call(offsets, probe)
+    placed, spots = prepare_call(offsets, probe)
     g_core, *sends = views_call(
-        chans, offsets, view_counts, object_field, placed, intensity, tables, *margins
+        chans, spots, view_counts, object_field, placed, intensity, tables, *margins
     )
     return finish_call(chans, object_field, g_core, *exchange(*sends))
 

time: 25.6 us -> 25.1 us (0.980)
  Pallas kernels: 8.45 us -> 7.97 us
    pallas_call x1, Pallas kernels: 5.41 us -> 4.93 us  [views_call(): pl.pallas_call(functools.partial(views_kernel, chans), out_shape=[jax.Sha...]
where the time goes in v10:
time: 25.1 us; the launch traced here: 24.7 us
  starting transfers between devices  12.6 us (50%)
  Pallas kernels  7.97 us (32%)
  waiting for transfers between devices  2.33 us (9%)
  local copies, waits for them, and re-layouts  1.06 us (4%)
  between operations  0.76 us (3%)
    ppermute x4, starting transfers between devices, across(): lax.ppermute(block, ('row', 'col'), route + (extra if mesh_cols == 2 else...  5.73 us
    pallas_call x1, Pallas kernels, views_call(): pl.pallas_call(functools.partial(views_kernel, chans), out_shape=[jax.Sha...  4.93 us
    ppermute x2, starting transfers between devices, exchange(): lax.ppermute(block, 'col', channel[0])  4.18 us
    ppermute x4, starting transfers between devices, over_rows(): return lax.ppermute(block, ('row', 'col'), route + extra)  2.69 us
    ppermute x4, waiting for transfers between devices, across(): lax.ppermute(block, ('row', 'col'), route + (extra if mesh_cols == 2 else...  2.32 us
    pallas_call x1, Pallas kernels, prepare_call(): pl.pallas_call(prepare_kernel, out_shape=[jax.ShapeDtypeStruct((views, 2,...  1.91 us
    unnamed x10, local copies, waits for them, and re-layouts  1.06 us
    pallas_call x1, Pallas kernels, finish_call(): pl.pallas_call(functools.partial(finish_kernel, chans), out_shape=jax.Sha...  1 us
  transfers between devices with their start and end apart: 10, of which 2 were waited for; matrix products, arithmetic and copies ran while one was open for 0% of the time, Pallas kernels for 8%

profile of v10, /device:TPU:0, one launch (start us, length us, event | category | flops | bytes accessed | tf_op | source)
XLA Modules:
  0.0 24.7 jit_solution(2343502204187657739)
XLA Ops:
  0.0 0.0 copy-start
  0.0 1.0 %copy-done = f32[2,256,256]{2,1,0:T(8,128)S(1)} copy-done((f32[2,256,256]{2,1,0:T(8,128)S(1)}, f32[2,256,256]{2,1,0:T(8,128)}, u32[]{:S(2)}) %copy-start) | copy-done | bytes 524312
  1.0 0.0 copy-start.1
  1.0 0.0 copy-start.2
  1.0 0.0 copy-start.3
  1.0 0.0 copy-start.4
  1.1 0.1 shard_map.74
  1.2 3.0 %collective-permute-start = (f32[256,128]{1,0:T(8,128)S(1)}, f32[256,128]{1,0:T(8,128)S(1)}, u32[]{:S(2)}, u32[]{:S(2)}) collective-permute-start(f32[256,128]{1,0:T(8,128)S(1)} %get-tuple-element.20), channel_id=1, source_target_pairs={{0,1},{1,0},{2,3},{3,2},{4,5},{5,4},{6,7},{7,6},{8,9},{9,8},{10,11... | collective-permute-start | bytes 393224 | tf_op jit(solution)/shard_map/ppermute | solution.py:504
  4.2 0.1 collective-permute-start.1
  4.3 1.6 %collective-permute-start.4 = (f32[2,64,256]{2,1,0:T(8,128)S(1)}, f32[2,64,256]{2,1,0:T(8,128)S(1)}, u32[]{:S(2)}, u32[]{:S(2)}) collective-permute-start(f32[2,64,256]{2,1,0:T(8,128)S(1)} %get-tuple-element.24), channel_id=1, source_target_pairs={{0,2},{1,3},{4,6},{5,7},{8,10},{9,11},{12,14},{13,15},{16,18},{17,... | collective-permute-start | bytes 393224 | tf_op jit(solution)/shard_map/ppermute | solution.py:497
  5.8 0.5 %collective-permute-start.2 = (f32[64,128]{1,0:T(8,128)S(1)}, f32[64,128]{1,0:T(8,128)S(1)}, u32[]{:S(2)}, u32[]{:S(2)}) collective-permute-start(f32[64,128]{1,0:T(8,128)S(1)} %get-tuple-element.22), channel_id=1, source_target_pairs={{2,5},{3,4},{6,9},{7,8},{10,13},{11,12},{14,17},{15,16},{18,21},{1... | collective-permute-start | bytes 98312 | tf_op jit(solution)/shard_map/ppermute | solution.py:501
  6.4 2.2 %collective-permute-start.3 = (f32[64,128]{1,0:T(8,128)S(1)}, f32[64,128]{1,0:T(8,128)S(1)}, u32[]{:S(2)}, u32[]{:S(2)}) collective-permute-start(f32[64,128]{1,0:T(8,128)S(1)} %get-tuple-element.23), channel_id=1, source_target_pairs={{0,3},{1,2},{4,7},{5,6},{8,11},{9,10},{12,15},{13,14},{16,19},{17,... | collective-permute-start | bytes 98312 | tf_op jit(solution)/shard_map/ppermute | solution.py:501
  8.5 1.9 %shard_map.73 = (f32[4,2,256,256]{3,2,1,0:T(8,128)S(1)}, s32[4,2,8,128]{3,2,1,0:T(8,128)S(1)}) custom-call(s32[1,1,2,4]{3,2,1,0:T(2,128)} %bitcast.1, f32[2,256,256]{2,1,0:T(8,128)} %probe.1), custom_call_target="tpu_custom_call" | custom-call | flops 1000000000 | bytes 100000 | tf_op jit(solution)/shard_map/pallas_call | solution.py:185
  11.1 0.0 collective-permute-done.2.rest_2_
  11.1 0.0 collective-permute-done.3.rest_3_
  11.1 0.0 collective-permute-done.rest_0_
  11.1 0.0 collective-permute-done.1.rest_1_
  11.1 0.0 collective-permute-done.4.rest_4_
  11.2 0.0 copy-done.1
  11.2 0.0 copy-done.2
  11.2 0.0 copy-done.3
  11.2 0.0 copy-done.4
  11.2 4.9 %shard_map.75 = (f32[2,256,256]{2,1,0:T(8,128)S(1)}, f32[2,64,256]{2,1,0:T(8,128)S(1)}, f32[2,64,256]{2,1,0:T(8,128)S(1)}, f32[256,128]{1,0:T(8,128)S(1)}, f32[64,128]{1,0:T(8,128)S(1)}, /*index=5*/f32[64,128]{1,0:T(8,128)S(1)}) custom-call(s32[4,2,8,128]{3,2,1,0:T(8,128)S(1)} %get-tuple-element.18.spots, s32[1,1]{1,0:T(1,128)S(6)} %copy.8.counts, ...), custom_call_target="tpu_custom_call" | custom-call | tf_op jit(solution)/shard_map/pallas_call | solution.py:416
  16.1 1.2 %collective-permute-start.5 = (f32[256,128]{1,0:T(8,128)S(1)}, f32[256,128]{1,0:T(8,128)S(1)}, u32[]{:S(2)}, u32[]{:S(2)}) collective-permute-start(f32[256,128]{1,0:T(8,128)S(1)} %get-tuple-element.26), channel_id=1, source_target_pairs={{0,1},{1,0},{2,3},{3,2},{4,5},{5,4},{6,7},{7,6},{8,9},{9,8},{10,11... | collective-permute-start | bytes 393224 | tf_op jit(solution)/shard_map/ppermute | solution.py:504
  17.3 0.9 %collective-permute-start.6 = (f32[2,64,256]{2,1,0:T(8,128)S(1)}, f32[2,64,256]{2,1,0:T(8,128)S(1)}, u32[]{:S(2)}, u32[]{:S(2)}) collective-permute-start(f32[2,64,256]{2,1,0:T(8,128)S(1)} %get-tuple-element.27), channel_id=1, source_target_pairs={{2,4},{3,5},{6,8},{7,9},{10,12},{11,13},{14,16},{15,17},{18,20},{1... | collective-permute-start | bytes 393224 | tf_op jit(solution)/shard_map/ppermute | solution.py:497
  18.2 0.1 collective-permute-start.9
  18.4 1.5 %collective-permute-start.7 = (f32[64,128]{1,0:T(8,128)S(1)}, f32[64,128]{1,0:T(8,128)S(1)}, u32[]{:S(2)}, u32[]{:S(2)}) collective-permute-start(f32[64,128]{1,0:T(8,128)S(1)} %get-tuple-element.28), channel_id=1, source_target_pairs={{2,5},{3,4},{6,9},{7,8},{10,13},{11,12},{14,17},{15,16},{18,21},{1... | collective-permute-start | bytes 98312 | tf_op jit(solution)/shard_map/ppermute | solution.py:501
  19.9 1.5 %collective-permute-start.8 = (f32[64,128]{1,0:T(8,128)S(1)}, f32[64,128]{1,0:T(8,128)S(1)}, u32[]{:S(2)}, u32[]{:S(2)}) collective-permute-start(f32[64,128]{1,0:T(8,128)S(1)} %get-tuple-element.29), channel_id=1, source_target_pairs={{0,3},{1,2},{4,7},{5,6},{8,11},{9,10},{12,15},{13,14},{16,19},{17,... | collective-permute-start | bytes 98312 | tf_op jit(solution)/shard_map/ppermute | solution.py:501
  21.4 1.9 %collective-permute-done.7.rest_2_ = f32[64,128]{1,0:T(8,128)S(1)} collective-permute-done((f32[64,128]{1,0:T(8,128)S(1)}, f32[64,128]{1,0:T(8,128)S(1)}, u32[]{:S(2)}, u32[]{:S(2)}) %collective-permute-start.7) | collective-permute-done | bytes 32800 | tf_op jit(solution)/shard_map/ppermute | solution.py:501
  23.3 0.4 %collective-permute-done.8.rest_3_ = f32[64,128]{1,0:T(8,128)S(1)} collective-permute-done((f32[64,128]{1,0:T(8,128)S(1)}, f32[64,128]{1,0:T(8,128)S(1)}, u32[]{:S(2)}, u32[]{:S(2)}) %collective-permute-start.8) | collective-permute-done | bytes 32800 | tf_op jit(solution)/shard_map/ppermute | solution.py:501
  23.7 0.0 collective-permute-done.5.rest_0_
  23.7 0.0 collective-permute-done.6.rest_1_
  23.7 0.0 collective-permute-done.9.rest_4_
  23.7 1.0 %shard_map.76 = f32[2,256,256]{2,1,0:T(8,128)} custom-call(f32[2,256,256]{2,1,0:T(8,128)S(1)} %copy-done.1, f32[2,256,256]{2,1,0:T(8,128)S(1)} %get-tuple-element.25.g_core, f32[256,128]{1,0:T(8,128)S(1)} %collective-permute-done.5.rest_0_, f32[2,64,256]{2,1,0:T(8,128)S(1)} %collective-permute-done.6.rest_1_, f32[64,128]{1,0:T(8,128)S(1)} %collective-permute-done.7.rest_2_, ...), custom_call_target="tpu_custom_call" | custom-call | tf_op jit(solution)/shard_map/pallas_call | solution.py:478
Async XLA Ops:
  0.0 1.0 %copy-start = (f32[2,256,256]{2,1,0:T(8,128)S(1)}, f32[2,256,256]{2,1,0:T(8,128)}, u32[]{:S(2)}) copy-start(f32[2,256,256]{2,1,0:T(8,128)} %object_ref.3) | copy-start | bytes 1572868
  1.0 10.1 %copy-start.1 = (f32[2,256,256]{2,1,0:T(8,128)S(1)}, f32[2,256,256]{2,1,0:T(8,128)}, u32[]{:S(2)}) copy-start(f32[2,256,256]{2,1,0:T(8,128)} %object_ref.3) | copy-start | bytes 1572868
  1.0 10.1 %copy-start.2 = (f32[1,1,4,256,256]{4,3,2,1,0:T(8,128)S(1)}, f32[1,1,4,256,256]{4,3,2,1,0:T(8,128)}, u32[]{:S(2)}) copy-start(f32[1,1,4,256,256]{4,3,2,1,0:T(8,128)} %intensity.1) | copy-start | bytes 3145732
  1.0 10.1 %copy-start.3 = (bf16[4,512,256]{2,1,0:T(8,128)(2,1)S(1)}, bf16[4,512,256]{2,1,0:T(8,128)(2,1)}, u32[]{:S(2)}) copy-start(bf16[4,512,256]{2,1,0:T(8,128)(2,1)} %constant.5.clone.rest_6_) | copy-start | bytes 3145732
  1.0 10.1 %copy-start.4 = (bf16[4,512,256]{2,1,0:T(8,128)(2,1)S(1)}, bf16[4,512,256]{2,1,0:T(8,128)(2,1)}, u32[]{:S(2)}) copy-start(bf16[4,512,256]{2,1,0:T(8,128)(2,1)} %constant.4.clone.rest_5_) | copy-start | bytes 3145732
  1.2 9.9 %collective-permute-start = (f32[256,128]{1,0:T(8,128)S(1)}, f32[256,128]{1,0:T(8,128)S(1)}, u32[]{:S(2)}, u32[]{:S(2)}) collective-permute-start(f32[256,128]{1,0:T(8,128)S(1)} %get-tuple-element.20), channel_id=1, source_target_pairs={{0,1},{1,0},{2,3},{3,2},{4,5},{5,4},{6,7},{7,6},{8,9},{9,8},{10,11... | collective-permute-start | bytes 393224 | tf_op jit(solution)/shard_map/ppermute | solution.py:504
  4.2 6.9 %collective-permute-start.1 = (f32[2,64,256]{2,1,0:T(8,128)S(1)}, f32[2,64,256]{2,1,0:T(8,128)S(1)}, u32[]{:S(2)}, u32[]{:S(2)}) collective-permute-start(f32[2,64,256]{2,1,0:T(8,128)S(1)} %get-tuple-element.21), channel_id=1, source_target_pairs={{2,4},{3,5},{6,8},{7,9},{10,12},{11,13},{14,16},{15,17},{18,20},{1... | collective-permute-start | bytes 393224 | tf_op jit(solution)/shard_map/ppermute | solution.py:497
  4.3 6.9 %collective-permute-start.4 = (f32[2,64,256]{2,1,0:T(8,128)S(1)}, f32[2,64,256]{2,1,0:T(8,128)S(1)}, u32[]{:S(2)}, u32[]{:S(2)}) collective-permute-start(f32[2,64,256]{2,1,0:T(8,128)S(1)} %get-tuple-element.24), channel_id=1, source_target_pairs={{0,2},{1,3},{4,6},{5,7},{8,10},{9,11},{12,14},{13,15},{16,18},{17,... | collective-permute-start | bytes 393224 | tf_op jit(solution)/shard_map/ppermute | solution.py:497
  5.8 5.3 %collective-permute-start.2 = (f32[64,128]{1,0:T(8,128)S(1)}, f32[64,128]{1,0:T(8,128)S(1)}, u32[]{:S(2)}, u32[]{:S(2)}) collective-permute-start(f32[64,128]{1,0:T(8,128)S(1)} %get-tuple-element.22), channel_id=1, source_target_pairs={{2,5},{3,4},{6,9},{7,8},{10,13},{11,12},{14,17},{15,16},{18,21},{1... | collective-permute-start | bytes 98312 | tf_op jit(solution)/shard_map/ppermute | solution.py:501
  6.4 4.7 %collective-permute-start.3 = (f32[64,128]{1,0:T(8,128)S(1)}, f32[64,128]{1,0:T(8,128)S(1)}, u32[]{:S(2)}, u32[]{:S(2)}) collective-permute-start(f32[64,128]{1,0:T(8,128)S(1)} %get-tuple-element.23), channel_id=1, source_target_pairs={{0,3},{1,2},{4,7},{5,6},{8,11},{9,10},{12,15},{13,14},{16,19},{17,... | collective-permute-start | bytes 98312 | tf_op jit(solution)/shard_map/ppermute | solution.py:501
  16.1 7.6 %collective-permute-start.5 = (f32[256,128]{1,0:T(8,128)S(1)}, f32[256,128]{1,0:T(8,128)S(1)}, u32[]{:S(2)}, u32[]{:S(2)}) collective-permute-start(f32[256,128]{1,0:T(8,128)S(1)} %get-tuple-element.26), channel_id=1, source_target_pairs={{0,1},{1,0},{2,3},{3,2},{4,5},{5,4},{6,7},{7,6},{8,9},{9,8},{10,11... | collective-permute-start | bytes 393224 | tf_op jit(solution)/shard_map/ppermute | solution.py:504
  17.3 6.4 %collective-permute-start.6 = (f32[2,64,256]{2,1,0:T(8,128)S(1)}, f32[2,64,256]{2,1,0:T(8,128)S(1)}, u32[]{:S(2)}, u32[]{:S(2)}) collective-permute-start(f32[2,64,256]{2,1,0:T(8,128)S(1)} %get-tuple-element.27), channel_id=1, source_target_pairs={{2,4},{3,5},{6,8},{7,9},{10,12},{11,13},{14,16},{15,17},{18,20},{1... | collective-permute-start | bytes 393224 | tf_op jit(solution)/shard_map/ppermute | solution.py:497
  18.2 5.5 %collective-permute-start.9 = (f32[2,64,256]{2,1,0:T(8,128)S(1)}, f32[2,64,256]{2,1,0:T(8,128)S(1)}, u32[]{:S(2)}, u32[]{:S(2)}) collective-permute-start(f32[2,64,256]{2,1,0:T(8,128)S(1)} %get-tuple-element.30), channel_id=1, source_target_pairs={{0,2},{1,3},{4,6},{5,7},{8,10},{9,11},{12,14},{13,15},{16,18},{17,... | collective-permute-start | bytes 393224 | tf_op jit(solution)/shard_map/ppermute | solution.py:497
  18.4 4.9 %collective-permute-start.7 = (f32[64,128]{1,0:T(8,128)S(1)}, f32[64,128]{1,0:T(8,128)S(1)}, u32[]{:S(2)}, u32[]{:S(2)}) collective-permute-start(f32[64,128]{1,0:T(8,128)S(1)} %get-tuple-element.28), channel_id=1, source_target_pairs={{2,5},{3,4},{6,9},{7,8},{10,13},{11,12},{14,17},{15,16},{18,21},{1... | collective-permute-start | bytes 98312 | tf_op jit(solution)/shard_map/ppermute | solution.py:501
  19.9 3.8 %collective-permute-start.8 = (f32[64,128]{1,0:T(8,128)S(1)}, f32[64,128]{1,0:T(8,128)S(1)}, u32[]{:S(2)}, u32[]{:S(2)}) collective-permute-start(f32[64,128]{1,0:T(8,128)S(1)} %get-tuple-element.29), channel_id=1, source_target_pairs={{0,3},{1,2},{4,7},{5,6},{8,11},{9,10},{12,15},{13,14},{16,19},{17,... | collective-permute-start | bytes 98312 | tf_op jit(solution)/shard_map/ppermute | solution.py:501

commit v11 on v10

--- a/solution.py
+++ b/solution.py
@@ -202,9 +202,10 @@
 
 def views_kernel(chans, spots, counts, core, placed, intensity, *rest):
     count = len(chans)
+    a_in, *rest = rest
     x_in, b_in, rest = rest[:count], rest[count], rest[count + 1 :]
     kb_in, ka_in = rest[:count], rest[count : 2 * count]
-    a_in, right, left, *rest = rest[2 * count :]
+    right, left, *rest = rest[2 * count :]
     g_core, g_a, g_b = rest[:3]
     g_x, g_ka = rest[3 : 3 + count], rest[3 + count : 3 + 2 * count]
     g_kb = rest[3 + 2 * count : 3 + 3 * count]
@@ -430,15 +431,15 @@
             *[tall, full] * 4,
         ],
         compiler_params=pltpu.CompilerParams(vmem_limit_bytes=40 * 1024 * 1024),
-    )(spots, counts, core, placed, intensity, *x_in, b_in, *kb_in, *ka_in, a_in, *tables)
+    )(spots, counts, core, placed, intensity, a_in, *x_in, b_in, *kb_in, *ka_in, *tables)
     return (*outs[:3], outs[3 : 3 + count], outs[3 + count : 3 + 2 * count], outs[3 + 2 * count :])
 
 
 def finish_kernel(chans, object_ref, g_core, *rest):
     count = len(chans)
+    a_in, *rest = rest
     x_in, b_in, rest = rest[:count], rest[count], rest[count + 1 :]
-    kb_in, ka_in = rest[:count], rest[count : 2 * count]
-    a_in, out = rest[2 * count :]
+    kb_in, ka_in, out = rest[:count], rest[count : 2 * count], rest[-1]
     size = object_ref.shape[1]
     lower = lower_partner()
     a_rows = pl.ds(pl.multiple_of(jnp.where(lower, size - MARGIN, 0), MARGIN), MARGIN)
@@ -481,7 +482,7 @@
         in_specs=[vmem] * (4 + 3 * len(chans)),
         out_specs=vmem,
         compiler_params=pltpu.CompilerParams(vmem_limit_bytes=6 * 1024 * 1024),
-    )(object_field, g_core, *x_in, b_in, *kb_in, *ka_in, a_in)
+    )(object_field, g_core, a_in, *x_in, b_in, *kb_in, *ka_in)
 
 
 def per_device(object_field, probe_field, intensity, view_offsets, view_counts):

time: 25.1 us -> 26.2 us (1.044)
  waiting for transfers between devices: 2.33 us -> 4.96 us
  starting transfers between devices: 12.6 us -> 11.3 us
    ppermute x4, waiting for transfers between devices: 2.32 us -> 4.94 us  [across(): lax.ppermute(block, ('row', 'col'), route + (extra if mesh_cols == 2 else...]
    ppermute x4, starting transfers between devices: 2.69 us -> 1.44 us  [over_rows(): return lax.ppermute(block, ('row', 'col'), route + extra)]
  transfers between devices with their start and end apart: 10 -> 10, of which waited for: 2 -> 2; matrix products, arithmetic and copies ran while one was open for 0% -> 0% of each run, Pallas kernels for 8% -> 7%
where the time goes in v11:
time: 26.2 us; the launch traced here: 26 us
  starting transfers between devices  11.3 us (43%)
  Pallas kernels  7.97 us (30%)
  waiting for transfers between devices  4.96 us (19%)
  local copies, waits for them, and re-layouts  1.06 us (4%)
  between operations  0.74 us (3%)
    ppermute x4, starting transfers between devices, across(): lax.ppermute(block, ('row', 'col'), route + (extra if mesh_cols == 2 else...  5.52 us
    ppermute x4, waiting for transfers between devices, across(): lax.ppermute(block, ('row', 'col'), route + (extra if mesh_cols == 2 else...  4.94 us
    pallas_call x1, Pallas kernels, views_call(): pl.pallas_call(functools.partial(views_kernel, chans), out_shape=[jax.Sha...  4.92 us
    ppermute x2, starting transfers between devices, exchange(): lax.ppermute(block, 'col', channel[0])  4.32 us
    pallas_call x1, Pallas kernels, prepare_call(): pl.pallas_call(prepare_kernel, out_shape=[jax.ShapeDtypeStruct((views, 2,...  1.91 us
    ppermute x4, starting transfers between devices, over_rows(): return lax.ppermute(block, ('row', 'col'), route + extra)  1.44 us
    unnamed x10, local copies, waits for them, and re-layouts  1.06 us
    pallas_call x1, Pallas kernels, finish_call(): pl.pallas_call(functools.partial(finish_kernel, chans), out_shape=jax.Sha...  1 us
  transfers between devices with their start and end apart: 10, of which 2 were waited for; matrix products, arithmetic and copies ran while one was open for 0% of the time, Pallas kernels for 7%

profile of v11, /device:TPU:0, one launch (start us, length us, event | category | flops | bytes accessed | tf_op | source)
XLA Modules:
  0.0 26.0 jit_solution(5123433349430039825)
XLA Ops:
  0.0 0.0 copy-start
  0.0 1.0 %copy-done = f32[2,256,256]{2,1,0:T(8,128)S(1)} copy-done((f32[2,256,256]{2,1,0:T(8,128)S(1)}, f32[2,256,256]{2,1,0:T(8,128)}, u32[]{:S(2)}) %copy-start) | copy-done | bytes 524312
  1.0 0.0 copy-start.1
  1.0 0.0 copy-start.2
  1.0 0.0 copy-start.3
  1.0 0.0 copy-start.4
  1.1 0.1 shard_map.74
  1.2 0.5 %collective-permute-start = (f32[2,64,256]{2,1,0:T(8,128)S(1)}, f32[2,64,256]{2,1,0:T(8,128)S(1)}, u32[]{:S(2)}, u32[]{:S(2)}) collective-permute-start(f32[2,64,256]{2,1,0:T(8,128)S(1)} %get-tuple-element.20), channel_id=1, source_target_pairs={{0,2},{1,3},{4,6},{5,7},{8,10},{9,11},{12,14},{13,15},{16,18},{17,... | collective-permute-start | bytes 393224 | tf_op jit(solution)/shard_map/ppermute | solution.py:498
  1.7 2.6 %collective-permute-start.1 = (f32[256,128]{1,0:T(8,128)S(1)}, f32[256,128]{1,0:T(8,128)S(1)}, u32[]{:S(2)}, u32[]{:S(2)}) collective-permute-start(f32[256,128]{1,0:T(8,128)S(1)} %get-tuple-element.21), channel_id=1, source_target_pairs={{0,1},{1,0},{2,3},{3,2},{4,5},{5,4},{6,7},{7,6},{8,9},{9,8},{10,11... | collective-permute-start | bytes 393224 | tf_op jit(solution)/shard_map/ppermute | solution.py:505
  4.3 0.1 collective-permute-start.2
  4.4 1.9 %collective-permute-start.3 = (f32[64,128]{1,0:T(8,128)S(1)}, f32[64,128]{1,0:T(8,128)S(1)}, u32[]{:S(2)}, u32[]{:S(2)}) collective-permute-start(f32[64,128]{1,0:T(8,128)S(1)} %get-tuple-element.23), channel_id=1, source_target_pairs={{2,5},{3,4},{6,9},{7,8},{10,13},{11,12},{14,17},{15,16},{18,21},{1... | collective-permute-start | bytes 98312 | tf_op jit(solution)/shard_map/ppermute | solution.py:502
  6.3 1.0 %collective-permute-start.4 = (f32[64,128]{1,0:T(8,128)S(1)}, f32[64,128]{1,0:T(8,128)S(1)}, u32[]{:S(2)}, u32[]{:S(2)}) collective-permute-start(f32[64,128]{1,0:T(8,128)S(1)} %get-tuple-element.24), channel_id=1, source_target_pairs={{0,3},{1,2},{4,7},{5,6},{8,11},{9,10},{12,15},{13,14},{16,19},{17,... | collective-permute-start | bytes 98312 | tf_op jit(solution)/shard_map/ppermute | solution.py:502
  7.3 1.9 %shard_map.73 = (f32[4,2,256,256]{3,2,1,0:T(8,128)S(1)}, s32[4,2,8,128]{3,2,1,0:T(8,128)S(1)}) custom-call(s32[1,1,2,4]{3,2,1,0:T(2,128)} %bitcast.1, f32[2,256,256]{2,1,0:T(8,128)} %probe.1), custom_call_target="tpu_custom_call" | custom-call | flops 1000000000 | bytes 100000 | tf_op jit(solution)/shard_map/pallas_call | solution.py:185
  9.8 1.0 %collective-permute-done.3.rest_3_ = f32[64,128]{1,0:T(8,128)S(1)} collective-permute-done((f32[64,128]{1,0:T(8,128)S(1)}, f32[64,128]{1,0:T(8,128)S(1)}, u32[]{:S(2)}, u32[]{:S(2)}) %collective-permute-start.3) | collective-permute-done | bytes 32800 | tf_op jit(solution)/shard_map/ppermute | solution.py:502
  10.8 0.0 collective-permute-done.4.rest_4_
  10.8 0.0 collective-permute-done.rest_0_
  10.8 0.0 collective-permute-done.1.rest_1_
  10.8 0.0 collective-permute-done.2.rest_2_
  10.8 0.0 copy-done.1
  10.9 0.0 copy-done.2
  10.9 0.0 copy-done.3
  10.9 0.0 copy-done.4
  10.9 4.9 %shard_map.75 = (f32[2,256,256]{2,1,0:T(8,128)S(1)}, f32[2,64,256]{2,1,0:T(8,128)S(1)}, f32[2,64,256]{2,1,0:T(8,128)S(1)}, f32[256,128]{1,0:T(8,128)S(1)}, f32[64,128]{1,0:T(8,128)S(1)}, /*index=5*/f32[64,128]{1,0:T(8,128)S(1)}) custom-call(s32[4,2,8,128]{3,2,1,0:T(8,128)S(1)} %get-tuple-element.18.spots, s32[1,1]{1,0:T(1,128)S(6)} %copy.8.counts, ...), custom_call_target="tpu_custom_call" | custom-call | tf_op jit(solution)/shard_map/pallas_call | solution.py:417
  15.8 0.6 %collective-permute-start.5 = (f32[2,64,256]{2,1,0:T(8,128)S(1)}, f32[2,64,256]{2,1,0:T(8,128)S(1)}, u32[]{:S(2)}, u32[]{:S(2)}) collective-permute-start(f32[2,64,256]{2,1,0:T(8,128)S(1)} %get-tuple-element.26), channel_id=1, source_target_pairs={{0,2},{1,3},{4,6},{5,7},{8,10},{9,11},{12,14},{13,15},{16,18},{17,... | collective-permute-start | bytes 393224 | tf_op jit(solution)/shard_map/ppermute | solution.py:498
  16.4 1.8 %collective-permute-start.6 = (f32[256,128]{1,0:T(8,128)S(1)}, f32[256,128]{1,0:T(8,128)S(1)}, u32[]{:S(2)}, u32[]{:S(2)}) collective-permute-start(f32[256,128]{1,0:T(8,128)S(1)} %get-tuple-element.27), channel_id=1, source_target_pairs={{0,1},{1,0},{2,3},{3,2},{4,5},{5,4},{6,7},{7,6},{8,9},{9,8},{10,11... | collective-permute-start | bytes 393224 | tf_op jit(solution)/shard_map/ppermute | solution.py:505
  18.2 0.3 %collective-permute-start.7 = (f32[2,64,256]{2,1,0:T(8,128)S(1)}, f32[2,64,256]{2,1,0:T(8,128)S(1)}, u32[]{:S(2)}, u32[]{:S(2)}) collective-permute-start(f32[2,64,256]{2,1,0:T(8,128)S(1)} %get-tuple-element.28), channel_id=1, source_target_pairs={{2,4},{3,5},{6,8},{7,9},{10,12},{11,13},{14,16},{15,17},{18,20},{1... | collective-permute-start | bytes 393224 | tf_op jit(solution)/shard_map/ppermute | solution.py:498
  18.4 1.8 %collective-permute-start.8 = (f32[64,128]{1,0:T(8,128)S(1)}, f32[64,128]{1,0:T(8,128)S(1)}, u32[]{:S(2)}, u32[]{:S(2)}) collective-permute-start(f32[64,128]{1,0:T(8,128)S(1)} %get-tuple-element.29), channel_id=1, source_target_pairs={{2,5},{3,4},{6,9},{7,8},{10,13},{11,12},{14,17},{15,16},{18,21},{1... | collective-permute-start | bytes 98312 | tf_op jit(solution)/shard_map/ppermute | solution.py:502
  20.2 0.9 %collective-permute-start.9 = (f32[64,128]{1,0:T(8,128)S(1)}, f32[64,128]{1,0:T(8,128)S(1)}, u32[]{:S(2)}, u32[]{:S(2)}) collective-permute-start(f32[64,128]{1,0:T(8,128)S(1)} %get-tuple-element.30), channel_id=1, source_target_pairs={{0,3},{1,2},{4,7},{5,6},{8,11},{9,10},{12,15},{13,14},{16,19},{17,... | collective-permute-start | bytes 98312 | tf_op jit(solution)/shard_map/ppermute | solution.py:502
  21.0 3.9 %collective-permute-done.8.rest_3_ = f32[64,128]{1,0:T(8,128)S(1)} collective-permute-done((f32[64,128]{1,0:T(8,128)S(1)}, f32[64,128]{1,0:T(8,128)S(1)}, u32[]{:S(2)}, u32[]{:S(2)}) %collective-permute-start.8) | collective-permute-done | bytes 32800 | tf_op jit(solution)/shard_map/ppermute | solution.py:502
  25.0 0.0 collective-permute-done.9.rest_4_
  25.0 0.0 collective-permute-done.5.rest_0_
  25.0 0.0 collective-permute-done.6.rest_1_
  25.0 0.0 collective-permute-done.7.rest_2_
  25.0 1.0 %shard_map.76 = f32[2,256,256]{2,1,0:T(8,128)} custom-call(f32[2,256,256]{2,1,0:T(8,128)S(1)} %copy-done.1, f32[2,256,256]{2,1,0:T(8,128)S(1)} %get-tuple-element.25.g_core, f32[2,64,256]{2,1,0:T(8,128)S(1)} %collective-permute-done.5.rest_0_, f32[256,128]{1,0:T(8,128)S(1)} %collective-permute-done.6.rest_1_, ...), custom_call_target="tpu_custom_call" | custom-call | tf_op jit(solution)/shard_map/pallas_call | solution.py:479
Async XLA Ops:
  0.0 1.0 %copy-start = (f32[2,256,256]{2,1,0:T(8,128)S(1)}, f32[2,256,256]{2,1,0:T(8,128)}, u32[]{:S(2)}) copy-start(f32[2,256,256]{2,1,0:T(8,128)} %object_ref.3) | copy-start | bytes 1572868
  1.0 9.8 %copy-start.1 = (f32[2,256,256]{2,1,0:T(8,128)S(1)}, f32[2,256,256]{2,1,0:T(8,128)}, u32[]{:S(2)}) copy-start(f32[2,256,256]{2,1,0:T(8,128)} %object_ref.3) | copy-start | bytes 1572868
  1.0 9.8 %copy-start.2 = (f32[1,1,4,256,256]{4,3,2,1,0:T(8,128)S(1)}, f32[1,1,4,256,256]{4,3,2,1,0:T(8,128)}, u32[]{:S(2)}) copy-start(f32[1,1,4,256,256]{4,3,2,1,0:T(8,128)} %intensity.1) | copy-start | bytes 3145732
  1.0 9.8 %copy-start.3 = (bf16[4,512,256]{2,1,0:T(8,128)(2,1)S(1)}, bf16[4,512,256]{2,1,0:T(8,128)(2,1)}, u32[]{:S(2)}) copy-start(bf16[4,512,256]{2,1,0:T(8,128)(2,1)} %constant.5.clone.rest_6_) | copy-start | bytes 3145732
  1.0 9.8 %copy-start.4 = (bf16[4,512,256]{2,1,0:T(8,128)(2,1)S(1)}, bf16[4,512,256]{2,1,0:T(8,128)(2,1)}, u32[]{:S(2)}) copy-start(bf16[4,512,256]{2,1,0:T(8,128)(2,1)} %constant.4.clone.rest_5_) | copy-start | bytes 3145732
  1.2 9.6 %collective-permute-start = (f32[2,64,256]{2,1,0:T(8,128)S(1)}, f32[2,64,256]{2,1,0:T(8,128)S(1)}, u32[]{:S(2)}, u32[]{:S(2)}) collective-permute-start(f32[2,64,256]{2,1,0:T(8,128)S(1)} %get-tuple-element.20), channel_id=1, source_target_pairs={{0,2},{1,3},{4,6},{5,7},{8,10},{9,11},{12,14},{13,15},{16,18},{17,... | collective-permute-start | bytes 393224 | tf_op jit(solution)/shard_map/ppermute | solution.py:498
  1.7 9.1 %collective-permute-start.1 = (f32[256,128]{1,0:T(8,128)S(1)}, f32[256,128]{1,0:T(8,128)S(1)}, u32[]{:S(2)}, u32[]{:S(2)}) collective-permute-start(f32[256,128]{1,0:T(8,128)S(1)} %get-tuple-element.21), channel_id=1, source_target_pairs={{0,1},{1,0},{2,3},{3,2},{4,5},{5,4},{6,7},{7,6},{8,9},{9,8},{10,11... | collective-permute-start | bytes 393224 | tf_op jit(solution)/shard_map/ppermute | solution.py:505
  4.3 6.6 %collective-permute-start.2 = (f32[2,64,256]{2,1,0:T(8,128)S(1)}, f32[2,64,256]{2,1,0:T(8,128)S(1)}, u32[]{:S(2)}, u32[]{:S(2)}) collective-permute-start(f32[2,64,256]{2,1,0:T(8,128)S(1)} %get-tuple-element.22), channel_id=1, source_target_pairs={{2,4},{3,5},{6,8},{7,9},{10,12},{11,13},{14,16},{15,17},{18,20},{1... | collective-permute-start | bytes 393224 | tf_op jit(solution)/shard_map/ppermute | solution.py:498
  4.4 6.5 %collective-permute-start.3 = (f32[64,128]{1,0:T(8,128)S(1)}, f32[64,128]{1,0:T(8,128)S(1)}, u32[]{:S(2)}, u32[]{:S(2)}) collective-permute-start(f32[64,128]{1,0:T(8,128)S(1)} %get-tuple-element.23), channel_id=1, source_target_pairs={{2,5},{3,4},{6,9},{7,8},{10,13},{11,12},{14,17},{15,16},{18,21},{1... | collective-permute-start | bytes 98312 | tf_op jit(solution)/shard_map/ppermute | solution.py:502
  6.3 4.5 %collective-permute-start.4 = (f32[64,128]{1,0:T(8,128)S(1)}, f32[64,128]{1,0:T(8,128)S(1)}, u32[]{:S(2)}, u32[]{:S(2)}) collective-permute-start(f32[64,128]{1,0:T(8,128)S(1)} %get-tuple-element.24), channel_id=1, source_target_pairs={{0,3},{1,2},{4,7},{5,6},{8,11},{9,10},{12,15},{13,14},{16,19},{17,... | collective-permute-start | bytes 98312 | tf_op jit(solution)/shard_map/ppermute | solution.py:502
  15.8 9.2 %collective-permute-start.5 = (f32[2,64,256]{2,1,0:T(8,128)S(1)}, f32[2,64,256]{2,1,0:T(8,128)S(1)}, u32[]{:S(2)}, u32[]{:S(2)}) collective-permute-start(f32[2,64,256]{2,1,0:T(8,128)S(1)} %get-tuple-element.26), channel_id=1, source_target_pairs={{0,2},{1,3},{4,6},{5,7},{8,10},{9,11},{12,14},{13,15},{16,18},{17,... | collective-permute-start | bytes 393224 | tf_op jit(solution)/shard_map/ppermute | solution.py:498
  16.4 8.6 %collective-permute-start.6 = (f32[256,128]{1,0:T(8,128)S(1)}, f32[256,128]{1,0:T(8,128)S(1)}, u32[]{:S(2)}, u32[]{:S(2)}) collective-permute-start(f32[256,128]{1,0:T(8,128)S(1)} %get-tuple-element.27), channel_id=1, source_target_pairs={{0,1},{1,0},{2,3},{3,2},{4,5},{5,4},{6,7},{7,6},{8,9},{9,8},{10,11... | collective-permute-start | bytes 393224 | tf_op jit(solution)/shard_map/ppermute | solution.py:505
  18.2 6.8 %collective-permute-start.7 = (f32[2,64,256]{2,1,0:T(8,128)S(1)}, f32[2,64,256]{2,1,0:T(8,128)S(1)}, u32[]{:S(2)}, u32[]{:S(2)}) collective-permute-start(f32[2,64,256]{2,1,0:T(8,128)S(1)} %get-tuple-element.28), channel_id=1, source_target_pairs={{2,4},{3,5},{6,8},{7,9},{10,12},{11,13},{14,16},{15,17},{18,20},{1... | collective-permute-start | bytes 393224 | tf_op jit(solution)/shard_map/ppermute | solution.py:498
  18.4 6.6 %collective-permute-start.8 = (f32[64,128]{1,0:T(8,128)S(1)}, f32[64,128]{1,0:T(8,128)S(1)}, u32[]{:S(2)}, u32[]{:S(2)}) collective-permute-start(f32[64,128]{1,0:T(8,128)S(1)} %get-tuple-element.29), channel_id=1, source_target_pairs={{2,5},{3,4},{6,9},{7,8},{10,13},{11,12},{14,17},{15,16},{18,21},{1... | collective-permute-start | bytes 98312 | tf_op jit(solution)/shard_map/ppermute | solution.py:502
  20.2 4.8 %collective-permute-start.9 = (f32[64,128]{1,0:T(8,128)S(1)}, f32[64,128]{1,0:T(8,128)S(1)}, u32[]{:S(2)}, u32[]{:S(2)}) collective-permute-start(f32[64,128]{1,0:T(8,128)S(1)} %get-tuple-element.30), channel_id=1, source_target_pairs={{0,3},{1,2},{4,7},{5,6},{8,11},{9,10},{12,15},{13,14},{16,19},{17,... | collective-permute-start | bytes 98312 | tf_op jit(solution)/shard_map/ppermute | solution.py:502

commit v12 on v11

--- a/solution.py
+++ b/solution.py
@@ -492,6 +492,8 @@
     tables = dft_tables(size)
     a_pairs, b_pairs = row_pairs(mesh_rows, 0), row_pairs(mesh_rows, 1)
     spare = spare_route(b_pairs, mesh_rows, mesh_cols)
+    alone = [i for i in range(mesh_rows) if i not in dict(b_pairs)]
+    ends = list(zip(alone, alone[::-1])) if len(alone) == 2 else []
 
     def over_rows(block, pairs, extra):
         route = [(i * mesh_cols + k, j * mesh_cols + k) for i, j in pairs for k in range(mesh_cols)]
@@ -503,7 +505,7 @@
 
     def exchange(a_send, b_send, x_send, ka_send, kb_send):
         x_in = [lax.ppermute(block, "col", channel[0]) for block, channel in zip(x_send, chans)]
-        b_in = over_rows(b_send, b_pairs, spare)
+        b_in = over_rows(b_send, b_pairs + ends, [])
         kb_in = [across(block, b_pairs, spare, channel) for block, channel in zip(kb_send, chans)]
         ka_in = [across(block, a_pairs, [], channel) for block, channel in zip(ka_send, chans)]
         a_in = over_rows(a_send, a_pairs, [])

time: 26.2 us -> 27.4 us (1.046)
  starting transfers between devices: 11.3 us -> 12.7 us
    ppermute x4, starting transfers between devices: 1.44 us -> 7.36 us  [over_rows(): return lax.ppermute(block, ('row', 'col'), route + extra)]
    ppermute x4, starting transfers between devices: 5.52 us -> 2.03 us  [across(): lax.ppermute(block, ('row', 'col'), route + (extra if mesh_cols == 2 else...]
    ppermute x2, starting transfers between devices: 4.32 us -> 3.27 us  [exchange(): lax.ppermute(block, 'col', channel[0])]
    ppermute x4, waiting for transfers between devices: 4.94 us -> 4.47 us  [across(): lax.ppermute(block, ('row', 'col'), route + (extra if mesh_cols == 2 else...]
    ppermute x4, waiting for transfers between devices: 0.01 us -> 0.32 us  [over_rows(): return lax.ppermute(block, ('row', 'col'), route + extra)]
  transfers between devices with their start and end apart: 10 -> 10, of which waited for: 2 -> 4; matrix products, arithmetic and copies ran while one was open for 0% -> 0% of each run, Pallas kernels for 7% -> 7%
where the time goes in v12:
time: 27.4 us; the launch traced here: 27.2 us
  starting transfers between devices  12.7 us (46%)
  Pallas kernels  7.96 us (29%)
  waiting for transfers between devices  4.79 us (17%)
  local copies, waits for them, and re-layouts  1.06 us (4%)
  between operations  0.73 us (3%)
    ppermute x4, starting transfers between devices, over_rows(): return lax.ppermute(block, ('row', 'col'), route + extra)  7.36 us
    pallas_call x1, Pallas kernels, views_call(): pl.pallas_call(functools.partial(views_kernel, chans), out_shape=[jax.Sha...  4.92 us
    ppermute x4, waiting for transfers between devices, across(): lax.ppermute(block, ('row', 'col'), route + (extra if mesh_cols == 2 else...  4.47 us
    ppermute x2, starting transfers between devices, exchange(): lax.ppermute(block, 'col', channel[0])  3.27 us
    ppermute x4, starting transfers between devices, across(): lax.ppermute(block, ('row', 'col'), route + (extra if mesh_cols == 2 else...  2.03 us
    pallas_call x1, Pallas kernels, prepare_call(): pl.pallas_call(prepare_kernel, out_shape=[jax.ShapeDtypeStruct((views, 2,...  1.91 us
    unnamed x10, local copies, waits for them, and re-layouts  1.06 us
    pallas_call x1, Pallas kernels, finish_call(): pl.pallas_call(functools.partial(finish_kernel, chans), out_shape=jax.Sha...  1 us
  transfers between devices with their start and end apart: 10, of which 4 were waited for; matrix products, arithmetic and copies ran while one was open for 0% of the time, Pallas kernels for 7%

profile of v12, /device:TPU:0, one launch (start us, length us, event | category | flops | bytes accessed | tf_op | source)
XLA Modules:
  0.0 27.2 jit_solution(7744950086859880497)
XLA Ops:
  0.0 0.0 copy-start
  0.0 1.0 %copy-done = f32[2,256,256]{2,1,0:T(8,128)S(1)} copy-done((f32[2,256,256]{2,1,0:T(8,128)S(1)}, f32[2,256,256]{2,1,0:T(8,128)}, u32[]{:S(2)}) %copy-start) | copy-done | bytes 524312
  1.0 0.0 copy-start.1
  1.0 0.0 copy-start.2
  1.0 0.0 copy-start.3
  1.0 0.0 copy-start.4
  1.1 0.1 shard_map.74
  1.2 0.5 %collective-permute-start = (f32[2,64,256]{2,1,0:T(8,128)S(1)}, f32[2,64,256]{2,1,0:T(8,128)S(1)}, u32[]{:S(2)}, u32[]{:S(2)}) collective-permute-start(f32[2,64,256]{2,1,0:T(8,128)S(1)} %get-tuple-element.20), channel_id=1, source_target_pairs={{0,2},{1,3},{4,6},{5,7},{8,10},{9,11},{12,14},{13,15},{16,18},{17,... | collective-permute-start | bytes 393224 | tf_op jit(solution)/shard_map/ppermute | solution.py:500
  1.7 2.6 %collective-permute-start.1 = (f32[256,128]{1,0:T(8,128)S(1)}, f32[256,128]{1,0:T(8,128)S(1)}, u32[]{:S(2)}, u32[]{:S(2)}) collective-permute-start(f32[256,128]{1,0:T(8,128)S(1)} %get-tuple-element.21), channel_id=1, source_target_pairs={{0,1},{1,0},{2,3},{3,2},{4,5},{5,4},{6,7},{7,6},{8,9},{9,8},{10,11... | collective-permute-start | bytes 393224 | tf_op jit(solution)/shard_map/ppermute | solution.py:507
  4.3 4.3 %collective-permute-start.2 = (f32[2,64,256]{2,1,0:T(8,128)S(1)}, f32[2,64,256]{2,1,0:T(8,128)S(1)}, u32[]{:S(2)}, u32[]{:S(2)}) collective-permute-start(f32[2,64,256]{2,1,0:T(8,128)S(1)} %get-tuple-element.22), channel_id=1, source_target_pairs={{2,4},{3,5},{6,8},{7,9},{10,12},{11,13},{14,16},{15,17},{18,20},{1... | collective-permute-start | bytes 393224 | tf_op jit(solution)/shard_map/ppermute | solution.py:500
  8.6 0.5 %collective-permute-start.3 = (f32[64,128]{1,0:T(8,128)S(1)}, f32[64,128]{1,0:T(8,128)S(1)}, u32[]{:S(2)}, u32[]{:S(2)}) collective-permute-start(f32[64,128]{1,0:T(8,128)S(1)} %get-tuple-element.23), channel_id=1, source_target_pairs={{2,5},{3,4},{6,9},{7,8},{10,13},{11,12},{14,17},{15,16},{18,21},{1... | collective-permute-start | bytes 98312 | tf_op jit(solution)/shard_map/ppermute | solution.py:504
  9.1 0.0 collective-permute-start.4
  9.1 1.9 %shard_map.73 = (f32[4,2,256,256]{3,2,1,0:T(8,128)S(1)}, s32[4,2,8,128]{3,2,1,0:T(8,128)S(1)}) custom-call(s32[1,1,2,4]{3,2,1,0:T(2,128)} %bitcast.1, f32[2,256,256]{2,1,0:T(8,128)} %probe.1), custom_call_target="tpu_custom_call" | custom-call | flops 1000000000 | bytes 100000 | tf_op jit(solution)/shard_map/pallas_call | solution.py:185
  11.7 1.1 %collective-permute-done.3.rest_3_ = f32[64,128]{1,0:T(8,128)S(1)} collective-permute-done((f32[64,128]{1,0:T(8,128)S(1)}, f32[64,128]{1,0:T(8,128)S(1)}, u32[]{:S(2)}, u32[]{:S(2)}) %collective-permute-start.3) | collective-permute-done | bytes 32800 | tf_op jit(solution)/shard_map/ppermute | solution.py:504
  12.8 0.0 collective-permute-done.4.rest_4_
  12.8 0.0 collective-permute-done.rest_0_
  12.8 0.0 collective-permute-done.1.rest_1_
  12.8 0.0 collective-permute-done.2.rest_2_
  12.9 0.0 copy-done.1
  12.9 0.0 copy-done.2
  12.9 0.0 copy-done.3
  12.9 0.0 copy-done.4
  12.9 4.9 %shard_map.75 = (f32[2,256,256]{2,1,0:T(8,128)S(1)}, f32[2,64,256]{2,1,0:T(8,128)S(1)}, f32[2,64,256]{2,1,0:T(8,128)S(1)}, f32[256,128]{1,0:T(8,128)S(1)}, f32[64,128]{1,0:T(8,128)S(1)}, /*index=5*/f32[64,128]{1,0:T(8,128)S(1)}) custom-call(s32[4,2,8,128]{3,2,1,0:T(8,128)S(1)} %get-tuple-element.18.spots, s32[1,1]{1,0:T(1,128)S(6)} %copy.8.counts, ...), custom_call_target="tpu_custom_call" | custom-call | tf_op jit(solution)/shard_map/pallas_call | solution.py:417
  17.8 0.6 %collective-permute-start.5 = (f32[2,64,256]{2,1,0:T(8,128)S(1)}, f32[2,64,256]{2,1,0:T(8,128)S(1)}, u32[]{:S(2)}, u32[]{:S(2)}) collective-permute-start(f32[2,64,256]{2,1,0:T(8,128)S(1)} %get-tuple-element.26), channel_id=1, source_target_pairs={{0,2},{1,3},{4,6},{5,7},{8,10},{9,11},{12,14},{13,15},{16,18},{17,... | collective-permute-start | bytes 393224 | tf_op jit(solution)/shard_map/ppermute | solution.py:500
  18.4 0.7 %collective-permute-start.6 = (f32[256,128]{1,0:T(8,128)S(1)}, f32[256,128]{1,0:T(8,128)S(1)}, u32[]{:S(2)}, u32[]{:S(2)}) collective-permute-start(f32[256,128]{1,0:T(8,128)S(1)} %get-tuple-element.27), channel_id=1, source_target_pairs={{0,1},{1,0},{2,3},{3,2},{4,5},{5,4},{6,7},{7,6},{8,9},{9,8},{10,11... | collective-permute-start | bytes 393224 | tf_op jit(solution)/shard_map/ppermute | solution.py:507
  19.1 1.9 %collective-permute-start.7 = (f32[2,64,256]{2,1,0:T(8,128)S(1)}, f32[2,64,256]{2,1,0:T(8,128)S(1)}, u32[]{:S(2)}, u32[]{:S(2)}) collective-permute-start(f32[2,64,256]{2,1,0:T(8,128)S(1)} %get-tuple-element.28), channel_id=1, source_target_pairs={{2,4},{3,5},{6,8},{7,9},{10,12},{11,13},{14,16},{15,17},{18,20},{1... | collective-permute-start | bytes 393224 | tf_op jit(solution)/shard_map/ppermute | solution.py:500
  21.0 1.5 %collective-permute-start.8 = (f32[64,128]{1,0:T(8,128)S(1)}, f32[64,128]{1,0:T(8,128)S(1)}, u32[]{:S(2)}, u32[]{:S(2)}) collective-permute-start(f32[64,128]{1,0:T(8,128)S(1)} %get-tuple-element.29), channel_id=1, source_target_pairs={{2,5},{3,4},{6,9},{7,8},{10,13},{11,12},{14,17},{15,16},{18,21},{1... | collective-permute-start | bytes 98312 | tf_op jit(solution)/shard_map/ppermute | solution.py:504
  22.5 0.0 collective-permute-start.9
  22.5 2.4 %collective-permute-done.8.rest_3_ = f32[64,128]{1,0:T(8,128)S(1)} collective-permute-done((f32[64,128]{1,0:T(8,128)S(1)}, f32[64,128]{1,0:T(8,128)S(1)}, u32[]{:S(2)}, u32[]{:S(2)}) %collective-permute-start.8) | collective-permute-done | bytes 32800 | tf_op jit(solution)/shard_map/ppermute | solution.py:504
  25.0 0.9 %collective-permute-done.9.rest_4_ = f32[64,128]{1,0:T(8,128)S(1)} collective-permute-done((f32[64,128]{1,0:T(8,128)S(1)}, f32[64,128]{1,0:T(8,128)S(1)}, u32[]{:S(2)}, u32[]{:S(2)}) %collective-permute-start.9) | collective-permute-done | bytes 32800 | tf_op jit(solution)/shard_map/ppermute | solution.py:504
  25.9 0.0 collective-permute-done.5.rest_0_
  25.9 0.0 collective-permute-done.6.rest_1_
  25.9 0.3 %collective-permute-done.7.rest_2_ = f32[2,64,256]{2,1,0:T(8,128)S(1)} collective-permute-done((f32[2,64,256]{2,1,0:T(8,128)S(1)}, f32[2,64,256]{2,1,0:T(8,128)S(1)}, u32[]{:S(2)}, u32[]{:S(2)}) %collective-permute-start.7) | collective-permute-done | bytes 131104 | tf_op jit(solution)/shard_map/ppermute | solution.py:500
  26.2 1.0 %shard_map.76 = f32[2,256,256]{2,1,0:T(8,128)} custom-call(f32[2,256,256]{2,1,0:T(8,128)S(1)} %copy-done.1, f32[2,256,256]{2,1,0:T(8,128)S(1)} %get-tuple-element.25.g_core, f32[2,64,256]{2,1,0:T(8,128)S(1)} %collective-permute-done.5.rest_0_, f32[256,128]{1,0:T(8,128)S(1)} %collective-permute-done.6.rest_1_, ...), custom_call_target="tpu_custom_call" | custom-call | tf_op jit(solution)/shard_map/pallas_call | solution.py:479
Async XLA Ops:
  0.0 1.0 %copy-start = (f32[2,256,256]{2,1,0:T(8,128)S(1)}, f32[2,256,256]{2,1,0:T(8,128)}, u32[]{:S(2)}) copy-start(f32[2,256,256]{2,1,0:T(8,128)} %object_ref.3) | copy-start | bytes 1572868
  1.0 11.8 %copy-start.1 = (f32[2,256,256]{2,1,0:T(8,128)S(1)}, f32[2,256,256]{2,1,0:T(8,128)}, u32[]{:S(2)}) copy-start(f32[2,256,256]{2,1,0:T(8,128)} %object_ref.3) | copy-start | bytes 1572868
  1.0 11.8 %copy-start.2 = (f32[1,1,4,256,256]{4,3,2,1,0:T(8,128)S(1)}, f32[1,1,4,256,256]{4,3,2,1,0:T(8,128)}, u32[]{:S(2)}) copy-start(f32[1,1,4,256,256]{4,3,2,1,0:T(8,128)} %intensity.1) | copy-start | bytes 3145732
  1.0 11.8 %copy-start.3 = (bf16[4,512,256]{2,1,0:T(8,128)(2,1)S(1)}, bf16[4,512,256]{2,1,0:T(8,128)(2,1)}, u32[]{:S(2)}) copy-start(bf16[4,512,256]{2,1,0:T(8,128)(2,1)} %constant.5.clone.rest_6_) | copy-start | bytes 3145732
  1.0 11.8 %copy-start.4 = (bf16[4,512,256]{2,1,0:T(8,128)(2,1)S(1)}, bf16[4,512,256]{2,1,0:T(8,128)(2,1)}, u32[]{:S(2)}) copy-start(bf16[4,512,256]{2,1,0:T(8,128)(2,1)} %constant.4.clone.rest_5_) | copy-start | bytes 3145732
  1.2 11.6 %collective-permute-start = (f32[2,64,256]{2,1,0:T(8,128)S(1)}, f32[2,64,256]{2,1,0:T(8,128)S(1)}, u32[]{:S(2)}, u32[]{:S(2)}) collective-permute-start(f32[2,64,256]{2,1,0:T(8,128)S(1)} %get-tuple-element.20), channel_id=1, source_target_pairs={{0,2},{1,3},{4,6},{5,7},{8,10},{9,11},{12,14},{13,15},{16,18},{17,... | collective-permute-start | bytes 393224 | tf_op jit(solution)/shard_map/ppermute | solution.py:500
  1.7 11.1 %collective-permute-start.1 = (f32[256,128]{1,0:T(8,128)S(1)}, f32[256,128]{1,0:T(8,128)S(1)}, u32[]{:S(2)}, u32[]{:S(2)}) collective-permute-start(f32[256,128]{1,0:T(8,128)S(1)} %get-tuple-element.21), channel_id=1, source_target_pairs={{0,1},{1,0},{2,3},{3,2},{4,5},{5,4},{6,7},{7,6},{8,9},{9,8},{10,11... | collective-permute-start | bytes 393224 | tf_op jit(solution)/shard_map/ppermute | solution.py:507
  4.3 8.6 %collective-permute-start.2 = (f32[2,64,256]{2,1,0:T(8,128)S(1)}, f32[2,64,256]{2,1,0:T(8,128)S(1)}, u32[]{:S(2)}, u32[]{:S(2)}) collective-permute-start(f32[2,64,256]{2,1,0:T(8,128)S(1)} %get-tuple-element.22), channel_id=1, source_target_pairs={{2,4},{3,5},{6,8},{7,9},{10,12},{11,13},{14,16},{15,17},{18,20},{1... | collective-permute-start | bytes 393224 | tf_op jit(solution)/shard_map/ppermute | solution.py:500
  8.6 4.2 %collective-permute-start.3 = (f32[64,128]{1,0:T(8,128)S(1)}, f32[64,128]{1,0:T(8,128)S(1)}, u32[]{:S(2)}, u32[]{:S(2)}) collective-permute-start(f32[64,128]{1,0:T(8,128)S(1)} %get-tuple-element.23), channel_id=1, source_target_pairs={{2,5},{3,4},{6,9},{7,8},{10,13},{11,12},{14,17},{15,16},{18,21},{1... | collective-permute-start | bytes 98312 | tf_op jit(solution)/shard_map/ppermute | solution.py:504
  9.1 3.7 %collective-permute-start.4 = (f32[64,128]{1,0:T(8,128)S(1)}, f32[64,128]{1,0:T(8,128)S(1)}, u32[]{:S(2)}, u32[]{:S(2)}) collective-permute-start(f32[64,128]{1,0:T(8,128)S(1)} %get-tuple-element.24), channel_id=1, source_target_pairs={{0,3},{1,2},{4,7},{5,6},{8,11},{9,10},{12,15},{13,14},{16,19},{17,... | collective-permute-start | bytes 98312 | tf_op jit(solution)/shard_map/ppermute | solution.py:504
  17.8 8.1 %collective-permute-start.5 = (f32[2,64,256]{2,1,0:T(8,128)S(1)}, f32[2,64,256]{2,1,0:T(8,128)S(1)}, u32[]{:S(2)}, u32[]{:S(2)}) collective-permute-start(f32[2,64,256]{2,1,0:T(8,128)S(1)} %get-tuple-element.26), channel_id=1, source_target_pairs={{0,2},{1,3},{4,6},{5,7},{8,10},{9,11},{12,14},{13,15},{16,18},{17,... | collective-permute-start | bytes 393224 | tf_op jit(solution)/shard_map/ppermute | solution.py:500
  18.4 7.5 %collective-permute-start.6 = (f32[256,128]{1,0:T(8,128)S(1)}, f32[256,128]{1,0:T(8,128)S(1)}, u32[]{:S(2)}, u32[]{:S(2)}) collective-permute-start(f32[256,128]{1,0:T(8,128)S(1)} %get-tuple-element.27), channel_id=1, source_target_pairs={{0,1},{1,0},{2,3},{3,2},{4,5},{5,4},{6,7},{7,6},{8,9},{9,8},{10,11... | collective-permute-start | bytes 393224 | tf_op jit(solution)/shard_map/ppermute | solution.py:507
  19.1 7.1 %collective-permute-start.7 = (f32[2,64,256]{2,1,0:T(8,128)S(1)}, f32[2,64,256]{2,1,0:T(8,128)S(1)}, u32[]{:S(2)}, u32[]{:S(2)}) collective-permute-start(f32[2,64,256]{2,1,0:T(8,128)S(1)} %get-tuple-element.28), channel_id=1, source_target_pairs={{2,4},{3,5},{6,8},{7,9},{10,12},{11,13},{14,16},{15,17},{18,20},{1... | collective-permute-start | bytes 393224 | tf_op jit(solution)/shard_map/ppermute | solution.py:500
  21.0 3.9 %collective-permute-start.8 = (f32[64,128]{1,0:T(8,128)S(1)}, f32[64,128]{1,0:T(8,128)S(1)}, u32[]{:S(2)}, u32[]{:S(2)}) collective-permute-start(f32[64,128]{1,0:T(8,128)S(1)} %get-tuple-element.29), channel_id=1, source_target_pairs={{2,5},{3,4},{6,9},{7,8},{10,13},{11,12},{14,17},{15,16},{18,21},{1... | collective-permute-start | bytes 98312 | tf_op jit(solution)/shard_map/ppermute | solution.py:504
  22.5 3.3 %collective-permute-start.9 = (f32[64,128]{1,0:T(8,128)S(1)}, f32[64,128]{1,0:T(8,128)S(1)}, u32[]{:S(2)}, u32[]{:S(2)}) collective-permute-start(f32[64,128]{1,0:T(8,128)S(1)} %get-tuple-element.30), channel_id=1, source_target_pairs={{0,3},{1,2},{4,7},{5,6},{8,11},{9,10},{12,15},{13,14},{16,19},{17,... | collective-permute-start | bytes 98312 | tf_op jit(solution)/shard_map/ppermute | solution.py:504

commit v13 on v11

--- a/solution.py
+++ b/solution.py
@@ -202,8 +202,7 @@
 
 def views_kernel(chans, spots, counts, core, placed, intensity, *rest):
     count = len(chans)
-    a_in, *rest = rest
-    x_in, b_in, rest = rest[:count], rest[count], rest[count + 1 :]
+    x_in, (a_in, b_in), rest = rest[:count], rest[count : count + 2], rest[count + 2 :]
     kb_in, ka_in = rest[:count], rest[count : 2 * count]
     right, left, *rest = rest[2 * count :]
     g_core, g_a, g_b = rest[:3]
@@ -431,14 +430,13 @@
             *[tall, full] * 4,
         ],
         compiler_params=pltpu.CompilerParams(vmem_limit_bytes=40 * 1024 * 1024),
-    )(spots, counts, core, placed, intensity, a_in, *x_in, b_in, *kb_in, *ka_in, *tables)
+    )(spots, counts, core, placed, intensity, *x_in, a_in, b_in, *kb_in, *ka_in, *tables)
     return (*outs[:3], outs[3 : 3 + count], outs[3 + count : 3 + 2 * count], outs[3 + 2 * count :])
 
 
 def finish_kernel(chans, object_ref, g_core, *rest):
     count = len(chans)
-    a_in, *rest = rest
-    x_in, b_in, rest = rest[:count], rest[count], rest[count + 1 :]
+    x_in, (a_in, b_in), rest = rest[:count], rest[count : count + 2], rest[count + 2 :]
     kb_in, ka_in, out = rest[:count], rest[count : 2 * count], rest[-1]
     size = object_ref.shape[1]
     lower = lower_partner()
@@ -482,7 +480,7 @@
         in_specs=[vmem] * (4 + 3 * len(chans)),
         out_specs=vmem,
         compiler_params=pltpu.CompilerParams(vmem_limit_bytes=6 * 1024 * 1024),
-    )(object_field, g_core, a_in, *x_in, b_in, *kb_in, *ka_in)
+    )(object_field, g_core, *x_in, a_in, b_in, *kb_in, *ka_in)
 
 
 def per_device(object_field, probe_field, intensity, view_offsets, view_counts):

time: 26.2 us -> 24.9 us (0.950)
  waiting for transfers between devices: 4.96 us -> 3.46 us
    ppermute x4, waiting for transfers between devices: 4.94 us -> 3.44 us  [across(): lax.ppermute(block, ('row', 'col'), route + (extra if mesh_cols == 2 else...]
    ppermute x4, starting transfers between devices: 1.44 us -> 0.74 us  [over_rows(): return lax.ppermute(block, ('row', 'col'), route + extra)]
    ppermute x2, starting transfers between devices: 4.32 us -> 4.75 us  [exchange(): lax.ppermute(block, 'col', channel[0])]
    ppermute x4, starting transfers between devices: 5.52 us -> 5.91 us  [across(): lax.ppermute(block, ('row', 'col'), route + (extra if mesh_cols == 2 else...]
  transfers between devices with their start and end apart: 10 -> 10, of which waited for: 2 -> 2; matrix products, arithmetic and copies ran while one was open for 0% -> 0% of each run, Pallas kernels for 7% -> 8%
where the time goes in v13:
time: 24.9 us; the launch traced here: 24.6 us
  starting transfers between devices  11.4 us (46%)
  Pallas kernels  7.96 us (32%)
  waiting for transfers between devices  3.46 us (14%)
  local copies, waits for them, and re-layouts  1.06 us (4%)
  between operations  0.74 us (3%)
    ppermute x4, starting transfers between devices, across(): lax.ppermute(block, ('row', 'col'), route + (extra if mesh_cols == 2 else...  5.91 us
    pallas_call x1, Pallas kernels, views_call(): pl.pallas_call(functools.partial(views_kernel, chans), out_shape=[jax.Sha...  4.92 us
    ppermute x2, starting transfers between devices, exchange(): lax.ppermute(block, 'col', channel[0])  4.75 us
    ppermute x4, waiting for transfers between devices, across(): lax.ppermute(block, ('row', 'col'), route + (extra if mesh_cols == 2 else...  3.44 us
    pallas_call x1, Pallas kernels, prepare_call(): pl.pallas_call(prepare_kernel, out_shape=[jax.ShapeDtypeStruct((views, 2,...  1.91 us
    unnamed x10, local copies, waits for them, and re-layouts  1.06 us
    pallas_call x1, Pallas kernels, finish_call(): pl.pallas_call(functools.partial(finish_kernel, chans), out_shape=jax.Sha...  1 us
    ppermute x4, starting transfers between devices, over_rows(): return lax.ppermute(block, ('row', 'col'), route + extra)  0.74 us
  transfers between devices with their start and end apart: 10, of which 2 were waited for; matrix products, arithmetic and copies ran while one was open for 0% of the time, Pallas kernels for 8%

profile of v13, /device:TPU:0, one launch (start us, length us, event | category | flops | bytes accessed | tf_op | source)
XLA Modules:
  0.0 24.6 jit_solution(10917534714929414666)
XLA Ops:
  0.0 0.0 copy-start
  0.0 1.0 %copy-done = f32[2,256,256]{2,1,0:T(8,128)S(1)} copy-done((f32[2,256,256]{2,1,0:T(8,128)S(1)}, f32[2,256,256]{2,1,0:T(8,128)}, u32[]{:S(2)}) %copy-start) | copy-done | bytes 524312
  1.0 0.0 copy-start.1
  1.0 0.0 copy-start.2
  1.0 0.0 copy-start.3
  1.0 0.0 copy-start.4
  1.1 0.1 shard_map.74
  1.2 3.0 %collective-permute-start = (f32[256,128]{1,0:T(8,128)S(1)}, f32[256,128]{1,0:T(8,128)S(1)}, u32[]{:S(2)}, u32[]{:S(2)}) collective-permute-start(f32[256,128]{1,0:T(8,128)S(1)} %get-tuple-element.20), channel_id=1, source_target_pairs={{0,1},{1,0},{2,3},{3,2},{4,5},{5,4},{6,7},{7,6},{8,9},{9,8},{10,11... | collective-permute-start | bytes 393224 | tf_op jit(solution)/shard_map/ppermute | solution.py:503
  4.2 0.0 collective-permute-start.1
  4.2 0.2 collective-permute-start.2
  4.4 1.9 %collective-permute-start.3 = (f32[64,128]{1,0:T(8,128)S(1)}, f32[64,128]{1,0:T(8,128)S(1)}, u32[]{:S(2)}, u32[]{:S(2)}) collective-permute-start(f32[64,128]{1,0:T(8,128)S(1)} %get-tuple-element.23), channel_id=1, source_target_pairs={{2,5},{3,4},{6,9},{7,8},{10,13},{11,12},{14,17},{15,16},{18,21},{1... | collective-permute-start | bytes 98312 | tf_op jit(solution)/shard_map/ppermute | solution.py:500
  6.2 1.3 %collective-permute-start.4 = (f32[64,128]{1,0:T(8,128)S(1)}, f32[64,128]{1,0:T(8,128)S(1)}, u32[]{:S(2)}, u32[]{:S(2)}) collective-permute-start(f32[64,128]{1,0:T(8,128)S(1)} %get-tuple-element.24), channel_id=1, source_target_pairs={{0,3},{1,2},{4,7},{5,6},{8,11},{9,10},{12,15},{13,14},{16,19},{17,... | collective-permute-start | bytes 98312 | tf_op jit(solution)/shard_map/ppermute | solution.py:500
  7.5 1.9 %shard_map.73 = (f32[4,2,256,256]{3,2,1,0:T(8,128)S(1)}, s32[4,2,8,128]{3,2,1,0:T(8,128)S(1)}) custom-call(s32[1,1,2,4]{3,2,1,0:T(2,128)} %bitcast.1, f32[2,256,256]{2,1,0:T(8,128)} %probe.1), custom_call_target="tpu_custom_call" | custom-call | flops 1000000000 | bytes 100000 | tf_op jit(solution)/shard_map/pallas_call | solution.py:185
  10.1 0.1 collective-permute-done.3.rest_3_
  10.2 0.0 collective-permute-done.4.rest_4_
  10.2 0.0 collective-permute-done.rest_0_
  10.2 0.0 collective-permute-done.1.rest_1_
  10.2 0.0 collective-permute-done.2.rest_2_
  10.2 0.0 copy-done.1
  10.3 0.0 copy-done.2
  10.3 0.0 copy-done.3
  10.3 0.0 copy-done.4
  10.3 4.9 %shard_map.75 = (f32[2,256,256]{2,1,0:T(8,128)S(1)}, f32[2,64,256]{2,1,0:T(8,128)S(1)}, f32[2,64,256]{2,1,0:T(8,128)S(1)}, f32[256,128]{1,0:T(8,128)S(1)}, f32[64,128]{1,0:T(8,128)S(1)}, /*index=5*/f32[64,128]{1,0:T(8,128)S(1)}) custom-call(s32[4,2,8,128]{3,2,1,0:T(8,128)S(1)} %get-tuple-element.18.spots, s32[1,1]{1,0:T(1,128)S(6)} %copy.8.counts, ...), custom_call_target="tpu_custom_call" | custom-call | tf_op jit(solution)/shard_map/pallas_call | solution.py:416
  15.2 1.7 %collective-permute-start.5 = (f32[256,128]{1,0:T(8,128)S(1)}, f32[256,128]{1,0:T(8,128)S(1)}, u32[]{:S(2)}, u32[]{:S(2)}) collective-permute-start(f32[256,128]{1,0:T(8,128)S(1)} %get-tuple-element.26), channel_id=1, source_target_pairs={{0,1},{1,0},{2,3},{3,2},{4,5},{5,4},{6,7},{7,6},{8,9},{9,8},{10,11... | collective-permute-start | bytes 393224 | tf_op jit(solution)/shard_map/ppermute | solution.py:503
  17.0 0.2 collective-permute-start.6
  17.2 0.4 %collective-permute-start.7 = (f32[2,64,256]{2,1,0:T(8,128)S(1)}, f32[2,64,256]{2,1,0:T(8,128)S(1)}, u32[]{:S(2)}, u32[]{:S(2)}) collective-permute-start(f32[2,64,256]{2,1,0:T(8,128)S(1)} %get-tuple-element.28), channel_id=1, source_target_pairs={{2,4},{3,5},{6,8},{7,9},{10,12},{11,13},{14,16},{15,17},{18,20},{1... | collective-permute-start | bytes 393224 | tf_op jit(solution)/shard_map/ppermute | solution.py:496
  17.5 1.7 %collective-permute-start.8 = (f32[64,128]{1,0:T(8,128)S(1)}, f32[64,128]{1,0:T(8,128)S(1)}, u32[]{:S(2)}, u32[]{:S(2)}) collective-permute-start(f32[64,128]{1,0:T(8,128)S(1)} %get-tuple-element.29), channel_id=1, source_target_pairs={{2,5},{3,4},{6,9},{7,8},{10,13},{11,12},{14,17},{15,16},{18,21},{1... | collective-permute-start | bytes 98312 | tf_op jit(solution)/shard_map/ppermute | solution.py:500
  19.2 1.1 %collective-permute-start.9 = (f32[64,128]{1,0:T(8,128)S(1)}, f32[64,128]{1,0:T(8,128)S(1)}, u32[]{:S(2)}, u32[]{:S(2)}) collective-permute-start(f32[64,128]{1,0:T(8,128)S(1)} %get-tuple-element.30), channel_id=1, source_target_pairs={{0,3},{1,2},{4,7},{5,6},{8,11},{9,10},{12,15},{13,14},{16,19},{17,... | collective-permute-start | bytes 98312 | tf_op jit(solution)/shard_map/ppermute | solution.py:500
  20.3 3.3 %collective-permute-done.8.rest_3_ = f32[64,128]{1,0:T(8,128)S(1)} collective-permute-done((f32[64,128]{1,0:T(8,128)S(1)}, f32[64,128]{1,0:T(8,128)S(1)}, u32[]{:S(2)}, u32[]{:S(2)}) %collective-permute-start.8) | collective-permute-done | bytes 32800 | tf_op jit(solution)/shard_map/ppermute | solution.py:500
  23.6 0.0 collective-permute-done.9.rest_4_
  23.6 0.0 collective-permute-done.5.rest_0_
  23.6 0.0 collective-permute-done.6.rest_1_
  23.6 0.0 collective-permute-done.7.rest_2_
  23.6 1.0 %shard_map.76 = f32[2,256,256]{2,1,0:T(8,128)} custom-call(f32[2,256,256]{2,1,0:T(8,128)S(1)} %copy-done.1, f32[2,256,256]{2,1,0:T(8,128)S(1)} %get-tuple-element.25.g_core, f32[256,128]{1,0:T(8,128)S(1)} %collective-permute-done.5.rest_0_, f32[2,64,256]{2,1,0:T(8,128)S(1)} %collective-permute-done.6.rest_1_, ...), custom_call_target="tpu_custom_call" | custom-call | tf_op jit(solution)/shard_map/pallas_call | solution.py:477
Async XLA Ops:
  0.0 1.0 %copy-start = (f32[2,256,256]{2,1,0:T(8,128)S(1)}, f32[2,256,256]{2,1,0:T(8,128)}, u32[]{:S(2)}) copy-start(f32[2,256,256]{2,1,0:T(8,128)} %object_ref.3) | copy-start | bytes 1572868
  1.0 9.2 %copy-start.1 = (f32[2,256,256]{2,1,0:T(8,128)S(1)}, f32[2,256,256]{2,1,0:T(8,128)}, u32[]{:S(2)}) copy-start(f32[2,256,256]{2,1,0:T(8,128)} %object_ref.3) | copy-start | bytes 1572868
  1.0 9.2 %copy-start.2 = (f32[1,1,4,256,256]{4,3,2,1,0:T(8,128)S(1)}, f32[1,1,4,256,256]{4,3,2,1,0:T(8,128)}, u32[]{:S(2)}) copy-start(f32[1,1,4,256,256]{4,3,2,1,0:T(8,128)} %intensity.1) | copy-start | bytes 3145732
  1.0 9.2 %copy-start.3 = (bf16[4,512,256]{2,1,0:T(8,128)(2,1)S(1)}, bf16[4,512,256]{2,1,0:T(8,128)(2,1)}, u32[]{:S(2)}) copy-start(bf16[4,512,256]{2,1,0:T(8,128)(2,1)} %constant.5.clone.rest_6_) | copy-start | bytes 3145732
  1.0 9.2 %copy-start.4 = (bf16[4,512,256]{2,1,0:T(8,128)(2,1)S(1)}, bf16[4,512,256]{2,1,0:T(8,128)(2,1)}, u32[]{:S(2)}) copy-start(bf16[4,512,256]{2,1,0:T(8,128)(2,1)} %constant.4.clone.rest_5_) | copy-start | bytes 3145732
  1.2 9.0 %collective-permute-start = (f32[256,128]{1,0:T(8,128)S(1)}, f32[256,128]{1,0:T(8,128)S(1)}, u32[]{:S(2)}, u32[]{:S(2)}) collective-permute-start(f32[256,128]{1,0:T(8,128)S(1)} %get-tuple-element.20), channel_id=1, source_target_pairs={{0,1},{1,0},{2,3},{3,2},{4,5},{5,4},{6,7},{7,6},{8,9},{9,8},{10,11... | collective-permute-start | bytes 393224 | tf_op jit(solution)/shard_map/ppermute | solution.py:503
  4.2 6.0 %collective-permute-start.1 = (f32[2,64,256]{2,1,0:T(8,128)S(1)}, f32[2,64,256]{2,1,0:T(8,128)S(1)}, u32[]{:S(2)}, u32[]{:S(2)}) collective-permute-start(f32[2,64,256]{2,1,0:T(8,128)S(1)} %get-tuple-element.21), channel_id=1, source_target_pairs={{0,2},{1,3},{4,6},{5,7},{8,10},{9,11},{12,14},{13,15},{16,18},{17,... | collective-permute-start | bytes 393224 | tf_op jit(solution)/shard_map/ppermute | solution.py:496
  4.2 6.0 %collective-permute-start.2 = (f32[2,64,256]{2,1,0:T(8,128)S(1)}, f32[2,64,256]{2,1,0:T(8,128)S(1)}, u32[]{:S(2)}, u32[]{:S(2)}) collective-permute-start(f32[2,64,256]{2,1,0:T(8,128)S(1)} %get-tuple-element.22), channel_id=1, source_target_pairs={{2,4},{3,5},{6,8},{7,9},{10,12},{11,13},{14,16},{15,17},{18,20},{1... | collective-permute-start | bytes 393224 | tf_op jit(solution)/shard_map/ppermute | solution.py:496
  4.4 5.9 %collective-permute-start.3 = (f32[64,128]{1,0:T(8,128)S(1)}, f32[64,128]{1,0:T(8,128)S(1)}, u32[]{:S(2)}, u32[]{:S(2)}) collective-permute-start(f32[64,128]{1,0:T(8,128)S(1)} %get-tuple-element.23), channel_id=1, source_target_pairs={{2,5},{3,4},{6,9},{7,8},{10,13},{11,12},{14,17},{15,16},{18,21},{1... | collective-permute-start | bytes 98312 | tf_op jit(solution)/shard_map/ppermute | solution.py:500
  6.2 4.0 %collective-permute-start.4 = (f32[64,128]{1,0:T(8,128)S(1)}, f32[64,128]{1,0:T(8,128)S(1)}, u32[]{:S(2)}, u32[]{:S(2)}) collective-permute-start(f32[64,128]{1,0:T(8,128)S(1)} %get-tuple-element.24), channel_id=1, source_target_pairs={{0,3},{1,2},{4,7},{5,6},{8,11},{9,10},{12,15},{13,14},{16,19},{17,... | collective-permute-start | bytes 98312 | tf_op jit(solution)/shard_map/ppermute | solution.py:500
  15.2 8.4 %collective-permute-start.5 = (f32[256,128]{1,0:T(8,128)S(1)}, f32[256,128]{1,0:T(8,128)S(1)}, u32[]{:S(2)}, u32[]{:S(2)}) collective-permute-start(f32[256,128]{1,0:T(8,128)S(1)} %get-tuple-element.26), channel_id=1, source_target_pairs={{0,1},{1,0},{2,3},{3,2},{4,5},{5,4},{6,7},{7,6},{8,9},{9,8},{10,11... | collective-permute-start | bytes 393224 | tf_op jit(solution)/shard_map/ppermute | solution.py:503
  17.0 6.6 %collective-permute-start.6 = (f32[2,64,256]{2,1,0:T(8,128)S(1)}, f32[2,64,256]{2,1,0:T(8,128)S(1)}, u32[]{:S(2)}, u32[]{:S(2)}) collective-permute-start(f32[2,64,256]{2,1,0:T(8,128)S(1)} %get-tuple-element.27), channel_id=1, source_target_pairs={{0,2},{1,3},{4,6},{5,7},{8,10},{9,11},{12,14},{13,15},{16,18},{17,... | collective-permute-start | bytes 393224 | tf_op jit(solution)/shard_map/ppermute | solution.py:496
  17.2 6.4 %collective-permute-start.7 = (f32[2,64,256]{2,1,0:T(8,128)S(1)}, f32[2,64,256]{2,1,0:T(8,128)S(1)}, u32[]{:S(2)}, u32[]{:S(2)}) collective-permute-start(f32[2,64,256]{2,1,0:T(8,128)S(1)} %get-tuple-element.28), channel_id=1, source_target_pairs={{2,4},{3,5},{6,8},{7,9},{10,12},{11,13},{14,16},{15,17},{18,20},{1... | collective-permute-start | bytes 393224 | tf_op jit(solution)/shard_map/ppermute | solution.py:496
  17.5 6.0 %collective-permute-start.8 = (f32[64,128]{1,0:T(8,128)S(1)}, f32[64,128]{1,0:T(8,128)S(1)}, u32[]{:S(2)}, u32[]{:S(2)}) collective-permute-start(f32[64,128]{1,0:T(8,128)S(1)} %get-tuple-element.29), channel_id=1, source_target_pairs={{2,5},{3,4},{6,9},{7,8},{10,13},{11,12},{14,17},{15,16},{18,21},{1... | collective-permute-start | bytes 98312 | tf_op jit(solution)/shard_map/ppermute | solution.py:500
  19.2 4.4 %collective-permute-start.9 = (f32[64,128]{1,0:T(8,128)S(1)}, f32[64,128]{1,0:T(8,128)S(1)}, u32[]{:S(2)}, u32[]{:S(2)}) collective-permute-start(f32[64,128]{1,0:T(8,128)S(1)} %get-tuple-element.30), channel_id=1, source_target_pairs={{0,3},{1,2},{4,7},{5,6},{8,11},{9,10},{12,15},{13,14},{16,19},{17,... | collective-permute-start | bytes 98312 | tf_op jit(solution)/shard_map/ppermute | solution.py:500

commit v14 on v13

--- a/solution.py
+++ b/solution.py
@@ -124,7 +124,7 @@
         b_ref[part] = jnp.where(lower, head, tail)
     for number, channel in enumerate(chans):
         right = sends_right(channel)
-        x_ref, ka_ref, kb_ref = edge_refs[3 * number : 3 * number + 3]
+        x_ref, kb_ref = edge_refs[2 * number : 2 * number + 2]
         low = lane_ids() < LANES // 2
         for start in range(0, size, CHUNK):
             rows = slice(start, start + CHUNK)
@@ -137,13 +137,12 @@
                 object_ref[0, rows, size - LANES :],
             )
             x_ref[rows] = jnp.where(right, right_edge, left_edge)
-        ka_ref[...] = jnp.where(lower, x_ref[size - MARGIN :], x_ref[:MARGIN])
         kb_ref[...] = jnp.where(lower, x_ref[:MARGIN], x_ref[size - MARGIN :])
 
 
 def pack_call(object_field, chans):
     size = object_field.shape[1]
-    shapes = [(2, MARGIN, size)] * 2 + [(size, LANES), (MARGIN, LANES), (MARGIN, LANES)] * len(chans)
+    shapes = [(2, MARGIN, size)] * 2 + [(size, LANES), (MARGIN, LANES)] * len(chans)
     vmem = pl.BlockSpec(memory_space=pltpu.VMEM)
     return pl.pallas_call(
         functools.partial(pack_kernel, chans),
@@ -157,26 +156,30 @@
 def prepare_kernel(offsets_in, probe, placed, spots, offsets, doubled, sems):
     views, size = placed.shape[0], probe.shape[1]
     copies = fetch(
-        [(offsets_in, offsets)] + [(probe, doubled.at[:, pl.ds(size * i, size)]) for i in range(2)], sems
+        [(offsets_in, offsets)]
+        + [(probe.at[part], doubled.at[part, pl.ds(0, size)]) for part in range(2)],
+        sems,
     )
     sublane = lax.broadcasted_iota(jnp.int32, (1, 8, 1), 1)
-    for copy in copies:
-        copy.wait()
-    for view in range(views):
-        for axis in range(2):
-            spots[view, axis] = jnp.full(spots.shape[2:], offsets[0, 0, axis, view], jnp.int32)
-        shift_row = lax.rem(offsets[0, 0, 0, view] - MARGIN + size, size)
-        shift_col = lax.rem(offsets[0, 0, 1, view] - MARGIN + size, size)
-        start = lax.rem(size - shift_row, size)
-        whole = pl.multiple_of((start // 8) * 8, 8)
-        rest = start - whole
-        for part in range(2):
+    copies[0].wait()
+    for part in range(2):
+        copies[1 + part].wait()
+        doubled[part, size:] = doubled[part, :size]
+        for view in range(views):
+            shift_row = lax.rem(offsets[0, 0, 0, view] - MARGIN + size, size)
+            shift_col = lax.rem(offsets[0, 0, 1, view] - MARGIN + size, size)
+            start = lax.rem(size - shift_row, size)
+            whole = pl.multiple_of((start // 8) * 8, 8)
+            rest = start - whole
             for row in range(0, size, CHUNK):
                 block = doubled[part, pl.ds(whole + row, CHUNK + 8), :]
                 block = pltpu.roll(block, shift_col, 1).reshape(CHUNK // 8 + 1, 8, size)
                 block = pltpu.roll(block, lax.rem(8 - rest, 8), 1)
                 block = jnp.where(sublane < 8 - rest, block[:-1], block[1:])
                 placed[view, part, row : row + CHUNK] = block.reshape(CHUNK, size)
+    for view in range(views):
+        for axis in range(2):
+            spots[view, axis] = jnp.full(spots.shape[2:], offsets[0, 0, axis, view], jnp.int32)
 
 
 def prepare_call(offsets, probe):
@@ -198,6 +201,21 @@
         compiler_params=pltpu.CompilerParams(vmem_limit_bytes=16 * 1024 * 1024),
         cost_estimate=pl.CostEstimate(flops=10**9, bytes_accessed=10**5, transcendentals=0),
     )(offsets, probe)
+
+
+def edge_kernel(block, spots, out):
+    out[...] = jnp.where(lower_partner(), block[block.shape[0] - MARGIN :], block[:MARGIN])
+
+
+def edge_call(block, spots):
+    vmem = pl.BlockSpec(memory_space=pltpu.VMEM)
+    return pl.pallas_call(
+        edge_kernel,
+        out_shape=jax.ShapeDtypeStruct((MARGIN, LANES), F32),
+        in_specs=[vmem, vmem],
+        out_specs=vmem,
+        compiler_params=pltpu.CompilerParams(vmem_limit_bytes=2 * 1024 * 1024),
+    )(block, spots)
 
 
 def views_kernel(chans, spots, counts, core, placed, intensity, *rest):
@@ -499,25 +517,28 @@
         route = [(i * mesh_cols + k, j * mesh_cols + l) for i, j in pairs for k, l in channel[0]]
         return lax.ppermute(block, ("row", "col"), route + (extra if mesh_cols == 2 else []))
 
-    def exchange(a_send, b_send, x_send, ka_send, kb_send):
+    def exchange(a_send, b_send, x_send, kb_send):
         x_in = [lax.ppermute(block, "col", channel[0]) for block, channel in zip(x_send, chans)]
+        a_in = over_rows(a_send, a_pairs, [])
         b_in = over_rows(b_send, b_pairs, spare)
         kb_in = [across(block, b_pairs, spare, channel) for block, channel in zip(kb_send, chans)]
-        ka_in = [across(block, a_pairs, [], channel) for block, channel in zip(ka_send, chans)]
-        a_in = over_rows(a_send, a_pairs, [])
-        return a_in, b_in, x_in, ka_in, kb_in
+        return a_in, b_in, x_in, kb_in
 
     packs = pack_call(object_field, chans)
+    a_in, b_in, x_in, kb_in = exchange(packs[0], packs[1], packs[2::2], packs[3::2])
     offsets, probe = (
         pltpu.with_memory_space_constraint(array, pltpu.HBM)
         for array in (jnp.swapaxes(view_offsets, 2, 3), probe_field)
     )
-    margins = exchange(packs[0], packs[1], packs[2::3], packs[3::3], packs[4::3])
     placed, spots = prepare_call(offsets, probe)
-    g_core, *sends = views_call(
-        chans, spots, view_counts, object_field, placed, intensity, tables, *margins
+    ka_in = [over_rows(edge_call(block, spots), a_pairs, []) for block in x_in]
+    g_core, g_a, g_b, g_x, g_ka, g_kb = views_call(
+        chans, spots, view_counts, object_field, placed, intensity, tables,
+        a_in, b_in, x_in, ka_in, kb_in,
     )
-    return finish_call(chans, object_field, g_core, *exchange(*sends))
+    a_in, b_in, x_in, kb_in = exchange(g_a, g_b, g_x, g_kb)
+    ka_in = [across(block, a_pairs, [], channel) for block, channel in zip(g_ka, chans)]
+    return finish_call(chans, object_field, g_core, a_in, b_in, x_in, ka_in, kb_in)
 
 
 def solution(mesh):

time: 24.9 us -> 24.3 us (0.976)
  starting transfers between devices: 11.4 us -> 10.2 us
  waiting for transfers between devices: 3.46 us -> 4.2 us
    ppermute x4 -> x3, starting transfers between devices: 5.91 us -> 4.84 us  [across(): lax.ppermute(block, ('row', 'col'), route + (extra if mesh_cols == 2 else...]
    ppermute x4 -> x3, waiting for transfers between devices: 3.44 us -> 4.18 us  [across(): lax.ppermute(block, ('row', 'col'), route + (extra if mesh_cols == 2 else...]
    ppermute x4 -> x5, starting transfers between devices: 0.74 us -> 0.58 us  [over_rows(): return lax.ppermute(block, ('row', 'col'), route + extra)]
  transfers between devices with their start and end apart: 10 -> 10, of which waited for: 2 -> 2; matrix products, arithmetic and copies ran while one was open for 0% -> 0% of each run, Pallas kernels for 8% -> 7%
where the time goes in v14:
time: 24.3 us; the launch traced here: 24 us
  starting transfers between devices  10.2 us (42%)
  Pallas kernels  7.84 us (32%)
  waiting for transfers between devices  4.2 us (17%)
  local copies, waits for them, and re-layouts  1.06 us (4%)
  between operations  0.76 us (3%)
    pallas_call x1, Pallas kernels, views_call(): pl.pallas_call(functools.partial(views_kernel, chans), out_shape=[jax.Sha...  4.92 us
    ppermute x3, starting transfers between devices, across(): lax.ppermute(block, ('row', 'col'), route + (extra if mesh_cols == 2 else...  4.84 us
    ppermute x2, starting transfers between devices, exchange(): lax.ppermute(block, 'col', channel[0])  4.74 us
    ppermute x3, waiting for transfers between devices, across(): lax.ppermute(block, ('row', 'col'), route + (extra if mesh_cols == 2 else...  4.18 us
    pallas_call x1, Pallas kernels, prepare_call(): pl.pallas_call(prepare_kernel, out_shape=[jax.ShapeDtypeStruct((views, 2,...  1.76 us
    unnamed x10, local copies, waits for them, and re-layouts  1.06 us
    pallas_call x1, Pallas kernels, finish_call(): pl.pallas_call(functools.partial(finish_kernel, chans), out_shape=jax.Sha...  1 us
    ppermute x5, starting transfers between devices, over_rows(): return lax.ppermute(block, ('row', 'col'), route + extra)  0.58 us
  transfers between devices with their start and end apart: 10, of which 2 were waited for; matrix products, arithmetic and copies ran while one was open for 0% of the time, Pallas kernels for 7%

profile of v14, /device:TPU:0, one launch (start us, length us, event | category | flops | bytes accessed | tf_op | source)
XLA Modules:
  0.0 24.0 jit_solution(14887591454625162899)
XLA Ops:
  0.0 0.0 copy-start
  0.0 1.0 %copy-done = f32[2,256,256]{2,1,0:T(8,128)S(1)} copy-done((f32[2,256,256]{2,1,0:T(8,128)S(1)}, f32[2,256,256]{2,1,0:T(8,128)}, u32[]{:S(2)}) %copy-start) | copy-done | bytes 524312
  1.0 0.0 copy-start.1
  1.0 0.0 copy-start.2
  1.0 0.0 copy-start.3
  1.0 0.0 copy-start.4
  1.1 0.1 shard_map.74
  1.2 3.0 %collective-permute-start = (f32[256,128]{1,0:T(8,128)S(1)}, f32[256,128]{1,0:T(8,128)S(1)}, u32[]{:S(2)}, u32[]{:S(2)}) collective-permute-start(f32[256,128]{1,0:T(8,128)S(1)} %get-tuple-element.19), channel_id=1, source_target_pairs={{0,1},{1,0},{2,3},{3,2},{4,5},{5,4},{6,7},{7,6},{8,9},{9,8},{10,11... | collective-permute-start | bytes 393224 | tf_op jit(solution)/shard_map/ppermute | solution.py:521
  4.2 0.0 collective-permute-start.1
  4.2 0.2 collective-permute-start.2
  4.4 1.9 %collective-permute-start.3 = (f32[64,128]{1,0:T(8,128)S(1)}, f32[64,128]{1,0:T(8,128)S(1)}, u32[]{:S(2)}, u32[]{:S(2)}) collective-permute-start(f32[64,128]{1,0:T(8,128)S(1)} %get-tuple-element.22), channel_id=1, source_target_pairs={{2,5},{3,4},{6,9},{7,8},{10,13},{11,12},{14,17},{15,16},{18,21},{1... | collective-permute-start | bytes 98312 | tf_op jit(solution)/shard_map/ppermute | solution.py:518
  6.2 1.8 %shard_map.73 = (f32[4,2,256,256]{3,2,1,0:T(8,128)S(1)}, s32[4,2,8,128]{3,2,1,0:T(8,128)S(1)}) custom-call(s32[1,1,2,4]{3,2,1,0:T(2,128)} %bitcast.1, f32[2,256,256]{2,1,0:T(8,128)} %probe.1), custom_call_target="tpu_custom_call" | custom-call | flops 1000000000 | bytes 100000 | tf_op jit(solution)/shard_map/pallas_call | solution.py:188
  8.0 0.0 collective-permute-done.block.rest_0_
  8.0 0.1 collective-permute-start.4
  8.8 1.1 %collective-permute-done.3.rest_3_ = f32[64,128]{1,0:T(8,128)S(1)} collective-permute-done((f32[64,128]{1,0:T(8,128)S(1)}, f32[64,128]{1,0:T(8,128)S(1)}, u32[]{:S(2)}, u32[]{:S(2)}) %collective-permute-start.3) | collective-permute-done | bytes 32800 | tf_op jit(solution)/shard_map/ppermute | solution.py:518
  9.9 0.0 collective-permute-done.1.rest_1_
  9.9 0.0 collective-permute-done.2.rest_2_
  9.9 0.0 collective-permute-done.4.rest_4_
  9.9 0.0 copy-done.1
  9.9 0.0 copy-done.2
  9.9 0.0 copy-done.3
  9.9 0.0 copy-done.4
  9.9 4.9 %shard_map.76 = (f32[2,256,256]{2,1,0:T(8,128)S(1)}, f32[2,64,256]{2,1,0:T(8,128)S(1)}, f32[2,64,256]{2,1,0:T(8,128)S(1)}, f32[256,128]{1,0:T(8,128)S(1)}, f32[64,128]{1,0:T(8,128)S(1)}, /*index=5*/f32[64,128]{1,0:T(8,128)S(1)}) custom-call(s32[4,2,8,128]{3,2,1,0:T(8,128)S(1)} %get-tuple-element.17.spots, s32[1,1]{1,0:T(1,128)S(6)} %copy.8.counts, ...), custom_call_target="tpu_custom_call" | custom-call | tf_op jit(solution)/shard_map/pallas_call | solution.py:434
  14.9 1.7 %collective-permute-start.5 = (f32[256,128]{1,0:T(8,128)S(1)}, f32[256,128]{1,0:T(8,128)S(1)}, u32[]{:S(2)}, u32[]{:S(2)}) collective-permute-start(f32[256,128]{1,0:T(8,128)S(1)} %get-tuple-element.24), channel_id=1, source_target_pairs={{0,1},{1,0},{2,3},{3,2},{4,5},{5,4},{6,7},{7,6},{8,9},{9,8},{10,11... | collective-permute-start | bytes 393224 | tf_op jit(solution)/shard_map/ppermute | solution.py:521
  16.6 0.0 collective-permute-start.6
  16.6 0.4 %collective-permute-start.7 = (f32[2,64,256]{2,1,0:T(8,128)S(1)}, f32[2,64,256]{2,1,0:T(8,128)S(1)}, u32[]{:S(2)}, u32[]{:S(2)}) collective-permute-start(f32[2,64,256]{2,1,0:T(8,128)S(1)} %get-tuple-element.26), channel_id=1, source_target_pairs={{2,4},{3,5},{6,8},{7,9},{10,12},{11,13},{14,16},{15,17},{18,20},{1... | collective-permute-start | bytes 393224 | tf_op jit(solution)/shard_map/ppermute | solution.py:514
  16.9 1.7 %collective-permute-start.8 = (f32[64,128]{1,0:T(8,128)S(1)}, f32[64,128]{1,0:T(8,128)S(1)}, u32[]{:S(2)}, u32[]{:S(2)}) collective-permute-start(f32[64,128]{1,0:T(8,128)S(1)} %get-tuple-element.27), channel_id=1, source_target_pairs={{2,5},{3,4},{6,9},{7,8},{10,13},{11,12},{14,17},{15,16},{18,21},{1... | collective-permute-start | bytes 98312 | tf_op jit(solution)/shard_map/ppermute | solution.py:518
  18.6 1.3 %collective-permute-start.9 = (f32[64,128]{1,0:T(8,128)S(1)}, f32[64,128]{1,0:T(8,128)S(1)}, u32[]{:S(2)}, u32[]{:S(2)}) collective-permute-start(f32[64,128]{1,0:T(8,128)S(1)} %get-tuple-element.28), channel_id=1, source_target_pairs={{0,3},{1,2},{4,7},{5,6},{8,11},{9,10},{12,15},{13,14},{16,19},{17,... | collective-permute-start | bytes 98312 | tf_op jit(solution)/shard_map/ppermute | solution.py:518
  19.9 3.1 %collective-permute-done.8.rest_3_ = f32[64,128]{1,0:T(8,128)S(1)} collective-permute-done((f32[64,128]{1,0:T(8,128)S(1)}, f32[64,128]{1,0:T(8,128)S(1)}, u32[]{:S(2)}, u32[]{:S(2)}) %collective-permute-start.8) | collective-permute-done | bytes 32800 | tf_op jit(solution)/shard_map/ppermute | solution.py:518
  23.0 0.0 collective-permute-done.9.rest_4_
  23.0 0.0 collective-permute-done.5.rest_0_
  23.0 0.0 collective-permute-done.6.rest_1_
  23.0 0.0 collective-permute-done.7.rest_2_
  23.0 1.0 %shard_map.77 = f32[2,256,256]{2,1,0:T(8,128)} custom-call(f32[2,256,256]{2,1,0:T(8,128)S(1)} %copy-done.1, f32[2,256,256]{2,1,0:T(8,128)S(1)} %get-tuple-element.23.g_core, f32[256,128]{1,0:T(8,128)S(1)} %collective-permute-done.5.rest_0_, f32[2,64,256]{2,1,0:T(8,128)S(1)} %collective-permute-done.6.rest_1_, ...), custom_call_target="tpu_custom_call" | custom-call | tf_op jit(solution)/shard_map/pallas_call | solution.py:495
  (1 shorter events, 0.0 us)
Async XLA Ops:
  0.0 1.0 %copy-start = (f32[2,256,256]{2,1,0:T(8,128)S(1)}, f32[2,256,256]{2,1,0:T(8,128)}, u32[]{:S(2)}) copy-start(f32[2,256,256]{2,1,0:T(8,128)} %object_ref.3) | copy-start | bytes 1572868
  1.0 8.8 %copy-start.1 = (f32[2,256,256]{2,1,0:T(8,128)S(1)}, f32[2,256,256]{2,1,0:T(8,128)}, u32[]{:S(2)}) copy-start(f32[2,256,256]{2,1,0:T(8,128)} %object_ref.3) | copy-start | bytes 1572868
  1.0 8.9 %copy-start.2 = (f32[1,1,4,256,256]{4,3,2,1,0:T(8,128)S(1)}, f32[1,1,4,256,256]{4,3,2,1,0:T(8,128)}, u32[]{:S(2)}) copy-start(f32[1,1,4,256,256]{4,3,2,1,0:T(8,128)} %intensity.1) | copy-start | bytes 3145732
  1.0 8.9 %copy-start.3 = (bf16[4,512,256]{2,1,0:T(8,128)(2,1)S(1)}, bf16[4,512,256]{2,1,0:T(8,128)(2,1)}, u32[]{:S(2)}) copy-start(bf16[4,512,256]{2,1,0:T(8,128)(2,1)} %constant.5.clone.rest_6_) | copy-start | bytes 3145732
  1.0 8.9 %copy-start.4 = (bf16[4,512,256]{2,1,0:T(8,128)(2,1)S(1)}, bf16[4,512,256]{2,1,0:T(8,128)(2,1)}, u32[]{:S(2)}) copy-start(bf16[4,512,256]{2,1,0:T(8,128)(2,1)} %constant.4.clone.rest_5_) | copy-start | bytes 3145732
  1.2 6.8 %collective-permute-start = (f32[256,128]{1,0:T(8,128)S(1)}, f32[256,128]{1,0:T(8,128)S(1)}, u32[]{:S(2)}, u32[]{:S(2)}) collective-permute-start(f32[256,128]{1,0:T(8,128)S(1)} %get-tuple-element.19), channel_id=1, source_target_pairs={{0,1},{1,0},{2,3},{3,2},{4,5},{5,4},{6,7},{7,6},{8,9},{9,8},{10,11... | collective-permute-start | bytes 393224 | tf_op jit(solution)/shard_map/ppermute | solution.py:521
  4.2 5.7 %collective-permute-start.1 = (f32[2,64,256]{2,1,0:T(8,128)S(1)}, f32[2,64,256]{2,1,0:T(8,128)S(1)}, u32[]{:S(2)}, u32[]{:S(2)}) collective-permute-start(f32[2,64,256]{2,1,0:T(8,128)S(1)} %get-tuple-element.20), channel_id=1, source_target_pairs={{0,2},{1,3},{4,6},{5,7},{8,10},{9,11},{12,14},{13,15},{16,18},{17,... | collective-permute-start | bytes 393224 | tf_op jit(solution)/shard_map/ppermute | solution.py:514
  4.2 5.7 %collective-permute-start.2 = (f32[2,64,256]{2,1,0:T(8,128)S(1)}, f32[2,64,256]{2,1,0:T(8,128)S(1)}, u32[]{:S(2)}, u32[]{:S(2)}) collective-permute-start(f32[2,64,256]{2,1,0:T(8,128)S(1)} %get-tuple-element.21), channel_id=1, source_target_pairs={{2,4},{3,5},{6,8},{7,9},{10,12},{11,13},{14,16},{15,17},{18,20},{1... | collective-permute-start | bytes 393224 | tf_op jit(solution)/shard_map/ppermute | solution.py:514
  4.4 5.5 %collective-permute-start.3 = (f32[64,128]{1,0:T(8,128)S(1)}, f32[64,128]{1,0:T(8,128)S(1)}, u32[]{:S(2)}, u32[]{:S(2)}) collective-permute-start(f32[64,128]{1,0:T(8,128)S(1)} %get-tuple-element.22), channel_id=1, source_target_pairs={{2,5},{3,4},{6,9},{7,8},{10,13},{11,12},{14,17},{15,16},{18,21},{1... | collective-permute-start | bytes 98312 | tf_op jit(solution)/shard_map/ppermute | solution.py:518
  8.0 1.8 %collective-permute-start.4 = (f32[64,128]{1,0:T(8,128)S(1)}, f32[64,128]{1,0:T(8,128)S(1)}, u32[]{:S(2)}, u32[]{:S(2)}) collective-permute-start(f32[64,128]{1,0:T(8,128)S(1)} %shard_map.75), channel_id=1, source_target_pairs={{0,2},{1,3},{4,6},{5,7},{8,10},{9,11},{12,14},{13,15},{16,18},{17,... | collective-permute-start | bytes 98312 | tf_op jit(solution)/shard_map/ppermute | solution.py:514
  14.9 8.1 %collective-permute-start.5 = (f32[256,128]{1,0:T(8,128)S(1)}, f32[256,128]{1,0:T(8,128)S(1)}, u32[]{:S(2)}, u32[]{:S(2)}) collective-permute-start(f32[256,128]{1,0:T(8,128)S(1)} %get-tuple-element.24), channel_id=1, source_target_pairs={{0,1},{1,0},{2,3},{3,2},{4,5},{5,4},{6,7},{7,6},{8,9},{9,8},{10,11... | collective-permute-start | bytes 393224 | tf_op jit(solution)/shard_map/ppermute | solution.py:521
  16.6 6.4 %collective-permute-start.6 = (f32[2,64,256]{2,1,0:T(8,128)S(1)}, f32[2,64,256]{2,1,0:T(8,128)S(1)}, u32[]{:S(2)}, u32[]{:S(2)}) collective-permute-start(f32[2,64,256]{2,1,0:T(8,128)S(1)} %get-tuple-element.25), channel_id=1, source_target_pairs={{0,2},{1,3},{4,6},{5,7},{8,10},{9,11},{12,14},{13,15},{16,18},{17,... | collective-permute-start | bytes 393224 | tf_op jit(solution)/shard_map/ppermute | solution.py:514
  16.6 6.4 %collective-permute-start.7 = (f32[2,64,256]{2,1,0:T(8,128)S(1)}, f32[2,64,256]{2,1,0:T(8,128)S(1)}, u32[]{:S(2)}, u32[]{:S(2)}) collective-permute-start(f32[2,64,256]{2,1,0:T(8,128)S(1)} %get-tuple-element.26), channel_id=1, source_target_pairs={{2,4},{3,5},{6,8},{7,9},{10,12},{11,13},{14,16},{15,17},{18,20},{1... | collective-permute-start | bytes 393224 | tf_op jit(solution)/shard_map/ppermute | solution.py:514
  16.9 6.0 %collective-permute-start.8 = (f32[64,128]{1,0:T(8,128)S(1)}, f32[64,128]{1,0:T(8,128)S(1)}, u32[]{:S(2)}, u32[]{:S(2)}) collective-permute-start(f32[64,128]{1,0:T(8,128)S(1)} %get-tuple-element.27), channel_id=1, source_target_pairs={{2,5},{3,4},{6,9},{7,8},{10,13},{11,12},{14,17},{15,16},{18,21},{1... | collective-permute-start | bytes 98312 | tf_op jit(solution)/shard_map/ppermute | solution.py:518
  18.6 4.4 %collective-permute-start.9 = (f32[64,128]{1,0:T(8,128)S(1)}, f32[64,128]{1,0:T(8,128)S(1)}, u32[]{:S(2)}, u32[]{:S(2)}) collective-permute-start(f32[64,128]{1,0:T(8,128)S(1)} %get-tuple-element.28), channel_id=1, source_target_pairs={{0,3},{1,2},{4,7},{5,6},{8,11},{9,10},{12,15},{13,14},{16,19},{17,... | collective-permute-start | bytes 98312 | tf_op jit(solution)/shard_map/ppermute | solution.py:518

commit v15 on v14

--- a/solution.py
+++ b/solution.py
@@ -13,7 +13,7 @@
 
 MARGIN = 64
 LANES = 128
-CHUNK = 64
+CHUNK = MARGIN
 STAGGER = 2
 
 smooth_eps = 0.1
@@ -218,7 +218,83 @@
     )(block, spots)
 
 
-def views_kernel(chans, spots, counts, core, placed, intensity, *rest):
+def unpack(chans, blocks):
+    re = im = jnp.zeros((MARGIN, LANES), F32)
+    for channel, block in zip(chans, blocks):
+        mine = half_lanes(takes_right(channel))
+        re, im = jnp.where(mine, block, re), jnp.where(mine, swap_halves(block), im)
+    return re, im
+
+
+def col_mask(spots, view, block):
+    if block == 0:
+        return lane_ids() < spots[view, 1, :1] - MARGIN
+    return lane_ids() >= MARGIN + spots[view, 1, :1]
+
+
+def put(ref, row, col, value):
+    high, low = split(value)
+    count, (rows, cols) = ref.shape[0] // 2, value.shape
+    ref[row : row + rows, col : col + cols] = high
+    ref[count + row : count + row + rows, col : col + cols] = low
+
+
+def by_right(lhs, right, t):
+    count, size = lhs.shape[0] // 2, lhs.shape[1]
+    both = dot(lhs[...], right[t, :size])
+    return both[:count] + both[count:] + dot(lhs[:count], right[t, size:])
+
+
+def put_waves(ref, placed, view, row, place, patch):
+    rows = slice(row, row + CHUNK)
+    waves = []
+    for block in range(2):
+        cols = slice(block * LANES, (block + 1) * LANES)
+        o_re, o_im = patch(view, row, block)
+        p_re, p_im = placed[view, 0, rows, cols], placed[view, 1, rows, cols]
+        waves.append((p_re * o_re - p_im * o_im, p_re * o_im + p_im * o_re))
+    for part in range(2):
+        put(ref.at[0], place, part * LANES, waves[0][part] + waves[1][part])
+        put(ref.at[1], place, part * LANES, waves[0][part] - waves[1][part])
+
+
+def early_kernel(chans, spots, core, placed, right, _, *rest):
+    x_in, out, cols_m, s1 = rest[: len(chans)], *rest[len(chans) :]
+    views, size = placed.shape[0], core.shape[1]
+
+    def patch(view, row, block):
+        cols, rows = slice(block * LANES, (block + 1) * LANES), slice(row, row + CHUNK)
+        beside = col_mask(spots, view, block)
+        return [jnp.where(beside, cols_m[p, rows], core[p, rows, cols]) for p in range(2)]
+
+    for row in range(CHUNK, size - CHUNK, CHUNK):
+        rows = slice(row, row + CHUNK)
+        cols_m[0, rows], cols_m[1, rows] = unpack(chans, [ref[rows] for ref in x_in])
+    for view in range(views):
+        for row in range(CHUNK, size - CHUNK, CHUNK):
+            put_waves(s1.at[view], placed, view, row, row - CHUNK, patch)
+        for odd in range(2):
+            out[view, odd] = by_right(s1.at[view, odd], right, odd)
+
+
+def early_call(chans, spots, core, placed, right, edge, x_in):
+    views, size = placed.shape[0], core.shape[1]
+    vmem = pl.BlockSpec(memory_space=pltpu.VMEM)
+    return pl.pallas_call(
+        functools.partial(early_kernel, chans),
+        out_shape=jax.ShapeDtypeStruct((views, 2, size - 2 * CHUNK, size), F32),
+        in_specs=[vmem] * (5 + len(chans)),
+        out_specs=vmem,
+        scratch_shapes=[
+            pltpu.VMEM((2, size, LANES), F32),
+            pltpu.VMEM((views, 2, 2 * (size - 2 * CHUNK), size), BF16),
+        ],
+        compiler_params=pltpu.CompilerParams(vmem_limit_bytes=8 * 1024 * 1024),
+        cost_estimate=pl.CostEstimate(flops=10**8, bytes_accessed=10**4, transcendentals=0),
+    )(spots, core, placed, right, edge, *x_in)
+
+
+def views_kernel(chans, spots, counts, core, placed, inner, intensity, *rest):
     count = len(chans)
     x_in, (a_in, b_in), rest = rest[:count], rest[count : count + 2], rest[count + 2 :]
     kb_in, ka_in = rest[:count], rest[count : 2 * count]
@@ -233,19 +309,11 @@
     low_lanes = lane_ids() < LANES // 2
     zero = jnp.zeros((CHUNK, LANES), F32)
 
-    def unpack(blocks):
-        re = im = None
-        for channel, block in zip(chans, blocks):
-            mine = half_lanes(takes_right(channel))
-            re = jnp.where(mine, block, 0.0 if re is None else re)
-            im = jnp.where(mine, swap_halves(block), 0.0 if im is None else im)
-        return (re, im) if blocks else (jnp.zeros((MARGIN, LANES), F32),) * 2
-
-    for row in range(0, size, CHUNK):
+    for row in (0, size - CHUNK):
         rows = slice(row, row + CHUNK)
-        cols_m[0, rows], cols_m[1, rows] = unpack([ref[rows] for ref in x_in]) if chans else (zero, zero)
-    corner_a = unpack([ref[...] for ref in ka_in])
-    corner_b = [jnp.where(partner, part, 0.0) for part in unpack([ref[...] for ref in kb_in])]
+        cols_m[0, rows], cols_m[1, rows] = unpack(chans, [ref[rows] for ref in x_in])
+    corner_a = unpack(chans, [ref[...] for ref in ka_in])
+    corner_b = [jnp.where(partner, part, 0.0) for part in unpack(chans, [ref[...] for ref in kb_in])]
     for part in range(2):
         a_rows, b_rows = a_in[part], jnp.where(partner, b_in[part], 0.0)
         rows_m[part, :m] = jnp.where(lower, a_rows, b_rows)
@@ -253,19 +321,9 @@
         corner_m[part, :m] = jnp.where(lower, corner_a[part], corner_b[part])
         corner_m[part, m:] = jnp.where(lower, corner_b[part], corner_a[part])
 
-    def by_right(lhs, t):
-        both = dot(lhs[...], right[t, :size])
-        return both[:size] + both[size:] + dot(lhs[:size], right[t, size:])
-
     def by_left(t, rhs):
         both = dot(left[t], rhs[:size])
         return both[:size] + both[size:] + dot(left[t, :size], rhs[size:])
-
-    def put(ref, row, col, value):
-        high, low = split(value)
-        rows, cols = value.shape
-        ref[row : row + rows, col : col + cols] = high
-        ref[size + row : size + row + rows, col : col + cols] = low
 
     def row_mask(view, row):
         ids = row + lax.broadcasted_iota(jnp.int32, (CHUNK, LANES), 0)
@@ -275,15 +333,10 @@
             return ids >= size - m + spots[view, 0, :1], row - size + 2 * m
         return None, None
 
-    def col_mask(view, block):
-        if block == 0:
-            return lane_ids() < spots[view, 1, :1] - m
-        return lane_ids() >= m + spots[view, 1, :1]
-
     def patch(view, row, block):
         cols = slice(block * LANES, (block + 1) * LANES)
         rows = slice(row, row + CHUNK)
-        beside = col_mask(view, block)
+        beside = col_mask(spots, view, block)
         beyond, place = row_mask(view, row)
         found = []
         for part in range(2):
@@ -295,28 +348,24 @@
             found.append(value)
         return found
 
+    def first(view, odd, row, cols):
+        if CHUNK <= row < size - CHUNK:
+            return inner[view, odd, row - CHUNK : row, cols]
+        place = 0 if row == 0 else CHUNK
+        return y[view, odd, place : place + CHUNK, cols]
+
     def steps(view):
-        for row in range(0, size, CHUNK):
-            rows = slice(row, row + CHUNK)
-            waves = []
-            for block in range(2):
-                cols = slice(block * LANES, (block + 1) * LANES)
-                o_re, o_im = patch(view, row, block)
-                p_re, p_im = placed[view, 0, rows, cols], placed[view, 1, rows, cols]
-                waves.append((p_re * o_re - p_im * o_im, p_re * o_im + p_im * o_re))
-            for part in range(2):
-                put(s1.at[view, 0], row, part * half, waves[0][part] + waves[1][part])
-                put(s1.at[view, 1], row, part * half, waves[0][part] - waves[1][part])
+        for row in (0, size - CHUNK):
+            put_waves(s1.at[view], placed, view, row, 0 if row == 0 else CHUNK, patch)
             yield
         for odd in range(2):
-            y[view, odd] = by_right(s1.at[view, odd], odd)
+            y[view, odd] = by_right(s1.at[view, odd], right, odd)
             yield
         for odd in range(2):
             for row in range(0, half, CHUNK):
                 for part in range(2):
                     cols = slice(part * half, (part + 1) * half)
-                    above = y[view, odd, row : row + CHUNK, cols]
-                    below = y[view, odd, half + row : half + row + CHUNK, cols]
+                    above, below = first(view, odd, row, cols), first(view, odd, half + row, cols)
                     put(s2.at[view, 0], part * half + row, odd * half, above + below)
                     put(s2.at[view, 1], part * half + row, odd * half, above - below)
                 yield
@@ -357,7 +406,7 @@
                     put(s4.at[view, 1], place, part * half, value[:, half:])
                 yield
         for odd in range(2):
-            g[view, odd] = by_right(s4.at[view, odd], 2 + odd)
+            g[view, odd] = by_right(s4.at[view, odd], right, 2 + odd)
             yield
 
     work = [steps(view) for view in range(views)]
@@ -383,7 +432,7 @@
                 halves.append((even_cols + odd_cols, even_cols - odd_cols))
             for block in range(2):
                 cols = slice(block * LANES, (block + 1) * LANES)
-                beside = col_mask(view, block)
+                beside = col_mask(spots, view, block)
                 b_re, b_im = halves[0][block], halves[1][block]
                 p_re, p_im = placed[view, 0, rows, cols], placed[view, 1, rows, cols]
                 for part, value in enumerate((p_re * b_re + p_im * b_im, p_re * b_im - p_im * b_re)):
@@ -423,7 +472,7 @@
         g_kb[number][...] = jnp.where(lower, above, below)
 
 
-def views_call(chans, spots, counts, core, placed, intensity, tables, a_in, b_in, x_in, ka_in, kb_in):
+def views_call(chans, spots, counts, core, placed, inner, intensity, tables, a_in, b_in, x_in, ka_in, kb_in):
     views, size = placed.shape[0], core.shape[1]
     count = len(chans)
     vmem = pl.BlockSpec(memory_space=pltpu.VMEM)
@@ -437,7 +486,7 @@
         in_specs=[
             vmem,
             pl.BlockSpec(memory_space=pltpu.SMEM),
-            *[vmem] * (7 + 3 * count),
+            *[vmem] * (8 + 3 * count),
         ],
         out_specs=[vmem] * len(shapes),
         scratch_shapes=[
@@ -445,10 +494,12 @@
             pltpu.VMEM((2, size, LANES), F32),
             pltpu.VMEM((2, 2 * MARGIN, size), F32),
             pltpu.VMEM((2, 2 * MARGIN, LANES), F32),
-            *[tall, full] * 4,
+            pltpu.VMEM((views, 2, 4 * CHUNK, size), BF16),
+            pltpu.VMEM((views, 2, 2 * CHUNK, size), F32),
+            *[tall, full] * 3,
         ],
         compiler_params=pltpu.CompilerParams(vmem_limit_bytes=40 * 1024 * 1024),
-    )(spots, counts, core, placed, intensity, *x_in, a_in, b_in, *kb_in, *ka_in, *tables)
+    )(spots, counts, core, placed, inner, intensity, *x_in, a_in, b_in, *kb_in, *ka_in, *tables)
     return (*outs[:3], outs[3 : 3 + count], outs[3 + count : 3 + 2 * count], outs[3 + 2 * count :])
 
 
@@ -531,9 +582,13 @@
         for array in (jnp.swapaxes(view_offsets, 2, 3), probe_field)
     )
     placed, spots = prepare_call(offsets, probe)
-    ka_in = [over_rows(edge_call(block, spots), a_pairs, []) for block in x_in]
+    edges = [edge_call(block, spots) for block in x_in]
+    ka_in = [over_rows(block, a_pairs, []) for block in edges]
+    inner = early_call(
+        chans, spots, object_field, placed, tables[0], edges[0] if edges else spots, x_in
+    )
     g_core, g_a, g_b, g_x, g_ka, g_kb = views_call(
-        chans, spots, view_counts, object_field, placed, intensity, tables,
+        chans, spots, view_counts, object_field, placed, inner, intensity, tables,
         a_in, b_in, x_in, ka_in, kb_in,
     )
     a_in, b_in, x_in, kb_in = exchange(g_a, g_b, g_x, g_kb)

time: 24.3 us -> 24.9 us (1.025)
  the two profiles are of different devices: /device:TPU:0 before, /device:TPU:30 now
where the time goes in v15:
time: 24.9 us; the launch traced here: 24.7 us
  Pallas kernels  8.06 us (32%)
  waiting for transfers between devices  7.22 us (29%)
  starting transfers between devices  7.01 us (28%)
  local copies, waits for them, and re-layouts  1.64 us (7%)
  between operations  0.77 us (3%)
    ppermute x3, waiting for transfers between devices, across(): lax.ppermute(block, ('row', 'col'), route + (extra if mesh_cols == 2 else...  5.46 us
    ppermute x3, starting transfers between devices, across(): lax.ppermute(block, ('row', 'col'), route + (extra if mesh_cols == 2 else...  5.08 us
    pallas_call x1, Pallas kernels, views_call(): pl.pallas_call(functools.partial(views_kernel, chans), out_shape=[jax.Sha...  4.19 us
    pallas_call x1, Pallas kernels, prepare_call(): pl.pallas_call(prepare_kernel, out_shape=[jax.ShapeDtypeStruct((views, 2,...  1.76 us
    ppermute x2, waiting for transfers between devices, exchange(): lax.ppermute(block, 'col', channel[0])  1.75 us
    unnamed x10, local copies, waits for them, and re-layouts  1.64 us
    ppermute x5, starting transfers between devices, over_rows(): return lax.ppermute(block, ('row', 'col'), route + extra)  1.26 us
    pallas_call x1, Pallas kernels, finish_call(): pl.pallas_call(functools.partial(finish_kernel, chans), out_shape=jax.Sha...  1.08 us
  transfers between devices with their start and end apart: 10, of which 3 were waited for; matrix products, arithmetic and copies ran while one was open for 0% of the time, Pallas kernels for 11%

profile of v15, /device:TPU:30, one launch (start us, length us, event | category | flops | bytes accessed | tf_op | source)
XLA Modules:
  0.0 24.7 jit_solution(10230547081051633176)
XLA Ops:
  0.0 0.0 copy-start
  0.0 1.0 %copy-done = f32[2,256,256]{2,1,0:T(8,128)S(1)} copy-done((f32[2,256,256]{2,1,0:T(8,128)S(1)}, f32[2,256,256]{2,1,0:T(8,128)}, u32[]{:S(2)}) %copy-start) | copy-done | bytes 524312
  1.0 0.0 copy-start.1
  1.0 0.0 copy-start.2
  1.0 0.1 shard_map.74
  1.2 0.6 %collective-permute-start = (f32[256,128]{1,0:T(8,128)S(1)}, f32[256,128]{1,0:T(8,128)S(1)}, u32[]{:S(2)}, u32[]{:S(2)}) collective-permute-start(f32[256,128]{1,0:T(8,128)S(1)} %get-tuple-element.19), channel_id=1, source_target_pairs={{0,1},{1,0},{2,3},{3,2},{4,5},{5,4},{6,7},{7,6},{8,9},{9,8},{10,11... | collective-permute-start | bytes 393224 | tf_op jit(solution)/shard_map/ppermute | solution.py:572
  1.8 0.0 collective-permute-start.1
  1.8 0.6 %collective-permute-start.2 = (f32[2,64,256]{2,1,0:T(8,128)S(1)}, f32[2,64,256]{2,1,0:T(8,128)S(1)}, u32[]{:S(2)}, u32[]{:S(2)}) collective-permute-start(f32[2,64,256]{2,1,0:T(8,128)S(1)} %get-tuple-element.21), channel_id=1, source_target_pairs={{2,4},{3,5},{6,8},{7,9},{10,12},{11,13},{14,16},{15,17},{18,20},{1... | collective-permute-start | bytes 393224 | tf_op jit(solution)/shard_map/ppermute | solution.py:565
  2.4 2.1 %collective-permute-start.3 = (f32[64,128]{1,0:T(8,128)S(1)}, f32[64,128]{1,0:T(8,128)S(1)}, u32[]{:S(2)}, u32[]{:S(2)}) collective-permute-start(f32[64,128]{1,0:T(8,128)S(1)} %get-tuple-element.22), channel_id=1, source_target_pairs={{2,5},{3,4},{6,9},{7,8},{10,13},{11,12},{14,17},{15,16},{18,21},{1... | collective-permute-start | bytes 98312 | tf_op jit(solution)/shard_map/ppermute | solution.py:569
  4.5 1.8 %shard_map.73 = (f32[4,2,256,256]{3,2,1,0:T(8,128)S(1)}, s32[4,2,8,128]{3,2,1,0:T(8,128)S(1)}) custom-call(s32[1,1,2,4]{3,2,1,0:T(2,128)} %bitcast.1, f32[2,256,256]{2,1,0:T(8,128)} %probe.1), custom_call_target="tpu_custom_call" | custom-call | flops 1000000000 | bytes 100000 | tf_op jit(solution)/shard_map/pallas_call | solution.py:188
  6.2 1.8 %collective-permute-done.block.rest_0_ = f32[256,128]{1,0:T(8,128)S(1)} collective-permute-done((f32[256,128]{1,0:T(8,128)S(1)}, f32[256,128]{1,0:T(8,128)S(1)}, u32[]{:S(2)}, u32[]{:S(2)}) %collective-permute-start) | collective-permute-done | bytes 131104 | tf_op jit(solution)/shard_map/ppermute | solution.py:572
  8.0 0.1 collective-permute-start.4
  8.7 0.0 copy-done.1
  8.7 0.0 copy-done.2
  8.7 0.0 copy-start.3
  8.8 0.0 copy-start.4
  8.8 0.9 %shard_map.76.inner = f32[4,2,128,256]{3,2,1,0:T(8,128)S(1)} custom-call(s32[4,2,8,128]{3,2,1,0:T(8,128)S(1)} %get-tuple-element.17.spots, f32[2,256,256]{2,1,0:T(8,128)S(1)} %copy-done.1, f32[4,2,256,256]{3,2,1,0:T(8,128)S(1)} %get-tuple-element.18.placed, bf16[4,512,256]{2,1,0:T(8,128)(2,1)S(1)} %copy-done.2, f32[64,128]{1,0:T(8,128)S(1)} %shard_map.75._, ...), custom_call_target="tpu_custom_call" | custom-call | flops 100000000 | bytes 10000 | tf_op jit(solution)/shard_map/pallas_call | solution.py:283
  9.7 0.0 collective-permute-done.3.rest_3_
  9.7 0.0 collective-permute-done.1.rest_1_
  9.7 0.0 collective-permute-done.2.rest_2_
  9.7 0.0 collective-permute-done.4.rest_4_
  9.7 0.3 %copy-done.3 = f32[1,1,4,256,256]{4,3,2,1,0:T(8,128)S(1)} copy-done((f32[1,1,4,256,256]{4,3,2,1,0:T(8,128)S(1)}, f32[1,1,4,256,256]{4,3,2,1,0:T(8,128)}, u32[]{:S(2)}) %copy-start.3) | copy-done | bytes 1048600
  10.0 0.3 %copy-done.4 = bf16[4,512,256]{2,1,0:T(8,128)(2,1)S(1)} copy-done((bf16[4,512,256]{2,1,0:T(8,128)(2,1)S(1)}, bf16[4,512,256]{2,1,0:T(8,128)(2,1)}, u32[]{:S(2)}) %copy-start.4) | copy-done | bytes 1048600
  10.3 4.2 %shard_map.77 = (f32[2,256,256]{2,1,0:T(8,128)S(1)}, f32[2,64,256]{2,1,0:T(8,128)S(1)}, f32[2,64,256]{2,1,0:T(8,128)S(1)}, f32[256,128]{1,0:T(8,128)S(1)}, f32[64,128]{1,0:T(8,128)S(1)}, /*index=5*/f32[64,128]{1,0:T(8,128)S(1)}) custom-call(s32[4,2,8,128]{3,2,1,0:T(8,128)S(1)} %get-tuple-element.17.spots, s32[1,1]{1,0:T(1,128)S(6)} %copy.8.counts, ...), custom_call_target="tpu_custom_call" | custom-call | tf_op jit(solution)/shard_map/pallas_call | solution.py:483
  14.5 0.1 collective-permute-start.5
  14.6 0.6 %collective-permute-start.6 = (f32[2,64,256]{2,1,0:T(8,128)S(1)}, f32[2,64,256]{2,1,0:T(8,128)S(1)}, u32[]{:S(2)}, u32[]{:S(2)}) collective-permute-start(f32[2,64,256]{2,1,0:T(8,128)S(1)} %get-tuple-element.25), channel_id=1, source_target_pairs={{0,2},{1,3},{4,6},{5,7},{8,10},{9,11},{12,14},{13,15},{16,18},{17,... | collective-permute-start | bytes 393224 | tf_op jit(solution)/shard_map/ppermute | solution.py:565
  15.1 0.0 collective-permute-start.7
  15.1 2.8 %collective-permute-start.8 = (f32[64,128]{1,0:T(8,128)S(1)}, f32[64,128]{1,0:T(8,128)S(1)}, u32[]{:S(2)}, u32[]{:S(2)}) collective-permute-start(f32[64,128]{1,0:T(8,128)S(1)} %get-tuple-element.27), channel_id=1, source_target_pairs={{2,5},{3,4},{6,9},{7,8},{10,13},{11,12},{14,17},{15,16},{18,21},{1... | collective-permute-start | bytes 98312 | tf_op jit(solution)/shard_map/ppermute | solution.py:569
  18.0 0.2 collective-permute-start.9
  18.2 1.9 %collective-permute-done.8.rest_3_ = f32[64,128]{1,0:T(8,128)S(1)} collective-permute-done((f32[64,128]{1,0:T(8,128)S(1)}, f32[64,128]{1,0:T(8,128)S(1)}, u32[]{:S(2)}, u32[]{:S(2)}) %collective-permute-start.8) | collective-permute-done | bytes 32800 | tf_op jit(solution)/shard_map/ppermute | solution.py:569
  20.0 3.6 %collective-permute-done.9.rest_4_ = f32[64,128]{1,0:T(8,128)S(1)} collective-permute-done((f32[64,128]{1,0:T(8,128)S(1)}, f32[64,128]{1,0:T(8,128)S(1)}, u32[]{:S(2)}, u32[]{:S(2)}) %collective-permute-start.9) | collective-permute-done | bytes 32800 | tf_op jit(solution)/shard_map/ppermute | solution.py:569
  23.6 0.0 collective-permute-done.5.rest_0_
  23.6 0.0 collective-permute-done.6.rest_1_
  23.6 0.0 collective-permute-done.7.rest_2_
  23.6 1.1 %shard_map.78 = f32[2,256,256]{2,1,0:T(8,128)} custom-call(f32[2,256,256]{2,1,0:T(8,128)S(1)} %copy-done.1, f32[2,256,256]{2,1,0:T(8,128)S(1)} %get-tuple-element.23.g_core, f32[256,128]{1,0:T(8,128)S(1)} %collective-permute-done.5.rest_0_, f32[2,64,256]{2,1,0:T(8,128)S(1)} %collective-permute-done.6.rest_1_, ...), custom_call_target="tpu_custom_call" | custom-call | tf_op jit(solution)/shard_map/pallas_call | solution.py:546
  (1 shorter events, 0.0 us)
Async XLA Ops:
  0.0 1.0 %copy-start = (f32[2,256,256]{2,1,0:T(8,128)S(1)}, f32[2,256,256]{2,1,0:T(8,128)}, u32[]{:S(2)}) copy-start(f32[2,256,256]{2,1,0:T(8,128)} %object_ref.3) | copy-start | bytes 1572868
  1.0 7.7 %copy-start.1 = (f32[2,256,256]{2,1,0:T(8,128)S(1)}, f32[2,256,256]{2,1,0:T(8,128)}, u32[]{:S(2)}) copy-start(f32[2,256,256]{2,1,0:T(8,128)} %object_ref.3) | copy-start | bytes 1572868
  1.0 7.7 %copy-start.2 = (bf16[4,512,256]{2,1,0:T(8,128)(2,1)S(1)}, bf16[4,512,256]{2,1,0:T(8,128)(2,1)}, u32[]{:S(2)}) copy-start(bf16[4,512,256]{2,1,0:T(8,128)(2,1)} %constant.4.clone.right.rest_5_) | copy-start | bytes 3145732
  1.2 6.8 %collective-permute-start = (f32[256,128]{1,0:T(8,128)S(1)}, f32[256,128]{1,0:T(8,128)S(1)}, u32[]{:S(2)}, u32[]{:S(2)}) collective-permute-start(f32[256,128]{1,0:T(8,128)S(1)} %get-tuple-element.19), channel_id=1, source_target_pairs={{0,1},{1,0},{2,3},{3,2},{4,5},{5,4},{6,7},{7,6},{8,9},{9,8},{10,11... | collective-permute-start | bytes 393224 | tf_op jit(solution)/shard_map/ppermute | solution.py:572
  1.8 7.9 %collective-permute-start.1 = (f32[2,64,256]{2,1,0:T(8,128)S(1)}, f32[2,64,256]{2,1,0:T(8,128)S(1)}, u32[]{:S(2)}, u32[]{:S(2)}) collective-permute-start(f32[2,64,256]{2,1,0:T(8,128)S(1)} %get-tuple-element.20), channel_id=1, source_target_pairs={{0,2},{1,3},{4,6},{5,7},{8,10},{9,11},{12,14},{13,15},{16,18},{17,... | collective-permute-start | bytes 393224 | tf_op jit(solution)/shard_map/ppermute | solution.py:565
  1.8 7.9 %collective-permute-start.2 = (f32[2,64,256]{2,1,0:T(8,128)S(1)}, f32[2,64,256]{2,1,0:T(8,128)S(1)}, u32[]{:S(2)}, u32[]{:S(2)}) collective-permute-start(f32[2,64,256]{2,1,0:T(8,128)S(1)} %get-tuple-element.21), channel_id=1, source_target_pairs={{2,4},{3,5},{6,8},{7,9},{10,12},{11,13},{14,16},{15,17},{18,20},{1... | collective-permute-start | bytes 393224 | tf_op jit(solution)/shard_map/ppermute | solution.py:565
  2.4 7.3 %collective-permute-start.3 = (f32[64,128]{1,0:T(8,128)S(1)}, f32[64,128]{1,0:T(8,128)S(1)}, u32[]{:S(2)}, u32[]{:S(2)}) collective-permute-start(f32[64,128]{1,0:T(8,128)S(1)} %get-tuple-element.22), channel_id=1, source_target_pairs={{2,5},{3,4},{6,9},{7,8},{10,13},{11,12},{14,17},{15,16},{18,21},{1... | collective-permute-start | bytes 98312 | tf_op jit(solution)/shard_map/ppermute | solution.py:569
  8.0 1.7 %collective-permute-start.4 = (f32[64,128]{1,0:T(8,128)S(1)}, f32[64,128]{1,0:T(8,128)S(1)}, u32[]{:S(2)}, u32[]{:S(2)}) collective-permute-start(f32[64,128]{1,0:T(8,128)S(1)} %shard_map.75._), channel_id=1, source_target_pairs={{0,2},{1,3},{4,6},{5,7},{8,10},{9,11},{12,14},{13,15},{16,18},{17,... | collective-permute-start | bytes 98312 | tf_op jit(solution)/shard_map/ppermute | solution.py:565
  8.7 1.2 %copy-start.3 = (f32[1,1,4,256,256]{4,3,2,1,0:T(8,128)S(1)}, f32[1,1,4,256,256]{4,3,2,1,0:T(8,128)}, u32[]{:S(2)}) copy-start(f32[1,1,4,256,256]{4,3,2,1,0:T(8,128)} %intensity.1) | copy-start | bytes 3145732
  8.8 1.5 %copy-start.4 = (bf16[4,512,256]{2,1,0:T(8,128)(2,1)S(1)}, bf16[4,512,256]{2,1,0:T(8,128)(2,1)}, u32[]{:S(2)}) copy-start(bf16[4,512,256]{2,1,0:T(8,128)(2,1)} %constant.5.clone.rest_6_) | copy-start | bytes 3145732
  14.5 9.1 %collective-permute-start.5 = (f32[256,128]{1,0:T(8,128)S(1)}, f32[256,128]{1,0:T(8,128)S(1)}, u32[]{:S(2)}, u32[]{:S(2)}) collective-permute-start(f32[256,128]{1,0:T(8,128)S(1)} %get-tuple-element.24), channel_id=1, source_target_pairs={{0,1},{1,0},{2,3},{3,2},{4,5},{5,4},{6,7},{7,6},{8,9},{9,8},{10,11... | collective-permute-start | bytes 393224 | tf_op jit(solution)/shard_map/ppermute | solution.py:572
  14.6 9.1 %collective-permute-start.6 = (f32[2,64,256]{2,1,0:T(8,128)S(1)}, f32[2,64,256]{2,1,0:T(8,128)S(1)}, u32[]{:S(2)}, u32[]{:S(2)}) collective-permute-start(f32[2,64,256]{2,1,0:T(8,128)S(1)} %get-tuple-element.25), channel_id=1, source_target_pairs={{0,2},{1,3},{4,6},{5,7},{8,10},{9,11},{12,14},{13,15},{16,18},{17,... | collective-permute-start | bytes 393224 | tf_op jit(solution)/shard_map/ppermute | solution.py:565
  15.1 8.5 %collective-permute-start.7 = (f32[2,64,256]{2,1,0:T(8,128)S(1)}, f32[2,64,256]{2,1,0:T(8,128)S(1)}, u32[]{:S(2)}, u32[]{:S(2)}) collective-permute-start(f32[2,64,256]{2,1,0:T(8,128)S(1)} %get-tuple-element.26), channel_id=1, source_target_pairs={{2,4},{3,5},{6,8},{7,9},{10,12},{11,13},{14,16},{15,17},{18,20},{1... | collective-permute-start | bytes 393224 | tf_op jit(solution)/shard_map/ppermute | solution.py:565
  15.1 4.9 %collective-permute-start.8 = (f32[64,128]{1,0:T(8,128)S(1)}, f32[64,128]{1,0:T(8,128)S(1)}, u32[]{:S(2)}, u32[]{:S(2)}) collective-permute-start(f32[64,128]{1,0:T(8,128)S(1)} %get-tuple-element.27), channel_id=1, source_target_pairs={{2,5},{3,4},{6,9},{7,8},{10,13},{11,12},{14,17},{15,16},{18,21},{1... | collective-permute-start | bytes 98312 | tf_op jit(solution)/shard_map/ppermute | solution.py:569
  18.0 5.6 %collective-permute-start.9 = (f32[64,128]{1,0:T(8,128)S(1)}, f32[64,128]{1,0:T(8,128)S(1)}, u32[]{:S(2)}, u32[]{:S(2)}) collective-permute-start(f32[64,128]{1,0:T(8,128)S(1)} %get-tuple-element.28), channel_id=1, source_target_pairs={{0,3},{1,2},{4,7},{5,6},{8,11},{9,10},{12,15},{13,14},{16,19},{17,... | collective-permute-start | bytes 98312 | tf_op jit(solution)/shard_map/ppermute | solution.py:569

commit v16 on v15

--- a/solution.py
+++ b/solution.py
@@ -258,7 +258,8 @@
         put(ref.at[1], place, part * LANES, waves[0][part] - waves[1][part])
 
 
-def early_kernel(chans, spots, core, placed, right, _, *rest):
+def early_kernel(chans, spots, core, placed, right, *rest):
+    rest = rest[3:]
     x_in, out, cols_m, s1 = rest[: len(chans)], *rest[len(chans) :]
     views, size = placed.shape[0], core.shape[1]
 
@@ -277,13 +278,13 @@
             out[view, odd] = by_right(s1.at[view, odd], right, odd)
 
 
-def early_call(chans, spots, core, placed, right, edge, x_in):
+def early_call(chans, spots, core, placed, right, unused, x_in):
     views, size = placed.shape[0], core.shape[1]
     vmem = pl.BlockSpec(memory_space=pltpu.VMEM)
     return pl.pallas_call(
         functools.partial(early_kernel, chans),
         out_shape=jax.ShapeDtypeStruct((views, 2, size - 2 * CHUNK, size), F32),
-        in_specs=[vmem] * (5 + len(chans)),
+        in_specs=[vmem] * (7 + len(chans)),
         out_specs=vmem,
         scratch_shapes=[
             pltpu.VMEM((2, size, LANES), F32),
@@ -291,7 +292,7 @@
         ],
         compiler_params=pltpu.CompilerParams(vmem_limit_bytes=8 * 1024 * 1024),
         cost_estimate=pl.CostEstimate(flops=10**8, bytes_accessed=10**4, transcendentals=0),
-    )(spots, core, placed, right, edge, *x_in)
+    )(spots, core, placed, right, *unused, *x_in)
 
 
 def views_kernel(chans, spots, counts, core, placed, inner, intensity, *rest):
@@ -584,9 +585,8 @@
     placed, spots = prepare_call(offsets, probe)
     edges = [edge_call(block, spots) for block in x_in]
     ka_in = [over_rows(block, a_pairs, []) for block in edges]
-    inner = early_call(
-        chans, spots, object_field, placed, tables[0], edges[0] if edges else spots, x_in
-    )
+    unused = (edges[0] if edges else spots, tables[1], intensity)
+    inner = early_call(chans, spots, object_field, placed, tables[0], unused, x_in)
     g_core, g_a, g_b, g_x, g_ka, g_kb = views_call(
         chans, spots, view_counts, object_field, placed, inner, intensity, tables,
         a_in, b_in, x_in, ka_in, kb_in,

time: 24.9 us -> 24.3 us (0.976)
  local copies, waits for them, and re-layouts: 1.64 us -> 1.06 us
    unnamed x10, local copies, waits for them, and re-layouts: 1.64 us -> 1.06 us
    ppermute x5, starting transfers between devices: 1.26 us -> 1.68 us  [over_rows(): return lax.ppermute(block, ('row', 'col'), route + extra)]
    ppermute x3, starting transfers between devices: 5.08 us -> 4.66 us  [across(): lax.ppermute(block, ('row', 'col'), route + (extra if mesh_cols == 2 else...]
where the time goes in v16:
time: 24.3 us; the launch traced here: 24.1 us
  Pallas kernels  8.08 us (33%)
  waiting for transfers between devices  7.22 us (30%)
  starting transfers between devices  7.01 us (29%)
  local copies, waits for them, and re-layouts  1.06 us (4%)
  between operations  0.78 us (3%)
    ppermute x3, waiting for transfers between devices, across(): lax.ppermute(block, ('row', 'col'), route + (extra if mesh_cols == 2 else...  5.46 us
    ppermute x3, starting transfers between devices, across(): lax.ppermute(block, ('row', 'col'), route + (extra if mesh_cols == 2 else...  4.66 us
    pallas_call x1, Pallas kernels, views_call(): pl.pallas_call(functools.partial(views_kernel, chans), out_shape=[jax.Sha...  4.2 us
    pallas_call x1, Pallas kernels, prepare_call(): pl.pallas_call(prepare_kernel, out_shape=[jax.ShapeDtypeStruct((views, 2,...  1.76 us
    ppermute x2, waiting for transfers between devices, exchange(): lax.ppermute(block, 'col', channel[0])  1.75 us
    ppermute x5, starting transfers between devices, over_rows(): return lax.ppermute(block, ('row', 'col'), route + extra)  1.68 us
    pallas_call x1, Pallas kernels, finish_call(): pl.pallas_call(functools.partial(finish_kernel, chans), out_shape=jax.Sha...  1.08 us
    unnamed x10, local copies, waits for them, and re-layouts  1.06 us
  transfers between devices with their start and end apart: 10, of which 3 were waited for; matrix products, arithmetic and copies ran while one was open for 0% of the time, Pallas kernels for 11%

profile of v16, /device:TPU:30, one launch (start us, length us, event | category | flops | bytes accessed | tf_op | source)
XLA Modules:
  0.0 24.1 jit_solution(16255390947728489551)
XLA Ops:
  0.0 0.0 copy-start
  0.0 1.0 %copy-done = f32[2,256,256]{2,1,0:T(8,128)S(1)} copy-done((f32[2,256,256]{2,1,0:T(8,128)S(1)}, f32[2,256,256]{2,1,0:T(8,128)}, u32[]{:S(2)}) %copy-start) | copy-done | bytes 524312
  1.0 0.0 copy-start.1
  1.0 0.0 copy-start.2
  1.0 0.0 copy-start.3
  1.0 0.0 copy-start.4
  1.1 0.1 shard_map.74
  1.2 0.6 %collective-permute-start = (f32[256,128]{1,0:T(8,128)S(1)}, f32[256,128]{1,0:T(8,128)S(1)}, u32[]{:S(2)}, u32[]{:S(2)}) collective-permute-start(f32[256,128]{1,0:T(8,128)S(1)} %get-tuple-element.19), channel_id=1, source_target_pairs={{0,1},{1,0},{2,3},{3,2},{4,5},{5,4},{6,7},{7,6},{8,9},{9,8},{10,11... | collective-permute-start | bytes 393224 | tf_op jit(solution)/shard_map/ppermute | solution.py:573
  1.8 0.0 collective-permute-start.1
  1.8 0.6 %collective-permute-start.2 = (f32[2,64,256]{2,1,0:T(8,128)S(1)}, f32[2,64,256]{2,1,0:T(8,128)S(1)}, u32[]{:S(2)}, u32[]{:S(2)}) collective-permute-start(f32[2,64,256]{2,1,0:T(8,128)S(1)} %get-tuple-element.21), channel_id=1, source_target_pairs={{2,4},{3,5},{6,8},{7,9},{10,12},{11,13},{14,16},{15,17},{18,20},{1... | collective-permute-start | bytes 393224 | tf_op jit(solution)/shard_map/ppermute | solution.py:566
  2.4 2.1 %collective-permute-start.3 = (f32[64,128]{1,0:T(8,128)S(1)}, f32[64,128]{1,0:T(8,128)S(1)}, u32[]{:S(2)}, u32[]{:S(2)}) collective-permute-start(f32[64,128]{1,0:T(8,128)S(1)} %get-tuple-element.22), channel_id=1, source_target_pairs={{2,5},{3,4},{6,9},{7,8},{10,13},{11,12},{14,17},{15,16},{18,21},{1... | collective-permute-start | bytes 98312 | tf_op jit(solution)/shard_map/ppermute | solution.py:570
  4.5 1.8 %shard_map.73 = (f32[4,2,256,256]{3,2,1,0:T(8,128)S(1)}, s32[4,2,8,128]{3,2,1,0:T(8,128)S(1)}) custom-call(s32[1,1,2,4]{3,2,1,0:T(2,128)} %bitcast.1, f32[2,256,256]{2,1,0:T(8,128)} %probe.1), custom_call_target="tpu_custom_call" | custom-call | flops 1000000000 | bytes 100000 | tf_op jit(solution)/shard_map/pallas_call | solution.py:188
  6.2 1.8 %collective-permute-done.block.rest_3_.rest_0_ = f32[256,128]{1,0:T(8,128)S(1)} collective-permute-done((f32[256,128]{1,0:T(8,128)S(1)}, f32[256,128]{1,0:T(8,128)S(1)}, u32[]{:S(2)}, u32[]{:S(2)}) %collective-permute-start) | collective-permute-done | bytes 131104 | tf_op jit(solution)/shard_map/ppermute | solution.py:573
  8.0 0.1 collective-permute-start.4
  8.7 0.0 copy-done.1
  8.7 0.0 copy-done.2
  8.8 0.0 copy-done.3
  8.8 0.0 copy-done.4
  8.8 0.9 %shard_map.76.inner = f32[4,2,128,256]{3,2,1,0:T(8,128)S(1)} custom-call(s32[4,2,8,128]{3,2,1,0:T(8,128)S(1)} %get-tuple-element.17.spots, f32[2,256,256]{2,1,0:T(8,128)S(1)} %copy-done.1, f32[4,2,256,256]{3,2,1,0:T(8,128)S(1)} %get-tuple-element.18.placed, bf16[4,512,256]{2,1,0:T(8,128)(2,1)S(1)} %copy-done.4, f32[64,128]{1,0:T(8,128)S(1)} %shard_map.75.rest_0_, ...), custom_call_target="tpu_custom_call" | custom-call | flops 100000000 | bytes 10000 | tf_op jit(solution)/shard_map/pallas_call | solution.py:284
  9.7 0.0 collective-permute-done.3.rest_3_
  9.7 0.0 collective-permute-done.1.rest_1_
  9.7 0.0 collective-permute-done.2.rest_2_
  9.7 0.0 collective-permute-done.4.rest_4_
  9.7 4.2 %shard_map.77 = (f32[2,256,256]{2,1,0:T(8,128)S(1)}, f32[2,64,256]{2,1,0:T(8,128)S(1)}, f32[2,64,256]{2,1,0:T(8,128)S(1)}, f32[256,128]{1,0:T(8,128)S(1)}, f32[64,128]{1,0:T(8,128)S(1)}, /*index=5*/f32[64,128]{1,0:T(8,128)S(1)}) custom-call(s32[4,2,8,128]{3,2,1,0:T(8,128)S(1)} %get-tuple-element.17.spots, s32[1,1]{1,0:T(1,128)S(6)} %copy.8.counts, ...), custom_call_target="tpu_custom_call" | custom-call | tf_op jit(solution)/shard_map/pallas_call | solution.py:484
  13.9 0.1 collective-permute-start.5
  14.0 0.6 %collective-permute-start.6 = (f32[2,64,256]{2,1,0:T(8,128)S(1)}, f32[2,64,256]{2,1,0:T(8,128)S(1)}, u32[]{:S(2)}, u32[]{:S(2)}) collective-permute-start(f32[2,64,256]{2,1,0:T(8,128)S(1)} %get-tuple-element.25), channel_id=1, source_target_pairs={{0,2},{1,3},{4,6},{5,7},{8,10},{9,11},{12,14},{13,15},{16,18},{17,... | collective-permute-start | bytes 393224 | tf_op jit(solution)/shard_map/ppermute | solution.py:566
  14.6 0.4 %collective-permute-start.7 = (f32[2,64,256]{2,1,0:T(8,128)S(1)}, f32[2,64,256]{2,1,0:T(8,128)S(1)}, u32[]{:S(2)}, u32[]{:S(2)}) collective-permute-start(f32[2,64,256]{2,1,0:T(8,128)S(1)} %get-tuple-element.26), channel_id=1, source_target_pairs={{2,4},{3,5},{6,8},{7,9},{10,12},{11,13},{14,16},{15,17},{18,20},{1... | collective-permute-start | bytes 393224 | tf_op jit(solution)/shard_map/ppermute | solution.py:566
  15.0 2.4 %collective-permute-start.8 = (f32[64,128]{1,0:T(8,128)S(1)}, f32[64,128]{1,0:T(8,128)S(1)}, u32[]{:S(2)}, u32[]{:S(2)}) collective-permute-start(f32[64,128]{1,0:T(8,128)S(1)} %get-tuple-element.27), channel_id=1, source_target_pairs={{2,5},{3,4},{6,9},{7,8},{10,13},{11,12},{14,17},{15,16},{18,21},{1... | collective-permute-start | bytes 98312 | tf_op jit(solution)/shard_map/ppermute | solution.py:570
  17.4 0.2 collective-permute-start.9
  17.6 1.9 %collective-permute-done.8.rest_3_ = f32[64,128]{1,0:T(8,128)S(1)} collective-permute-done((f32[64,128]{1,0:T(8,128)S(1)}, f32[64,128]{1,0:T(8,128)S(1)}, u32[]{:S(2)}, u32[]{:S(2)}) %collective-permute-start.8) | collective-permute-done | bytes 32800 | tf_op jit(solution)/shard_map/ppermute | solution.py:570
  19.5 3.6 %collective-permute-done.9.rest_4_ = f32[64,128]{1,0:T(8,128)S(1)} collective-permute-done((f32[64,128]{1,0:T(8,128)S(1)}, f32[64,128]{1,0:T(8,128)S(1)}, u32[]{:S(2)}, u32[]{:S(2)}) %collective-permute-start.9) | collective-permute-done | bytes 32800 | tf_op jit(solution)/shard_map/ppermute | solution.py:570
  23.1 0.0 collective-permute-done.5.rest_0_
  23.1 0.0 collective-permute-done.6.rest_1_
  23.1 0.0 collective-permute-done.7.rest_2_
  23.1 1.1 %shard_map.78 = f32[2,256,256]{2,1,0:T(8,128)} custom-call(f32[2,256,256]{2,1,0:T(8,128)S(1)} %copy-done.1, f32[2,256,256]{2,1,0:T(8,128)S(1)} %get-tuple-element.23.g_core, f32[256,128]{1,0:T(8,128)S(1)} %collective-permute-done.5.rest_0_, f32[2,64,256]{2,1,0:T(8,128)S(1)} %collective-permute-done.6.rest_1_, ...), custom_call_target="tpu_custom_call" | custom-call | tf_op jit(solution)/shard_map/pallas_call | solution.py:547
  (1 shorter events, 0.0 us)
Async XLA Ops:
  0.0 1.0 %copy-start = (f32[2,256,256]{2,1,0:T(8,128)S(1)}, f32[2,256,256]{2,1,0:T(8,128)}, u32[]{:S(2)}) copy-start(f32[2,256,256]{2,1,0:T(8,128)} %object_ref.3) | copy-start | bytes 1572868
  1.0 7.7 %copy-start.1 = (f32[2,256,256]{2,1,0:T(8,128)S(1)}, f32[2,256,256]{2,1,0:T(8,128)}, u32[]{:S(2)}) copy-start(f32[2,256,256]{2,1,0:T(8,128)} %object_ref.3) | copy-start | bytes 1572868
  1.0 7.7 %copy-start.2 = (f32[1,1,4,256,256]{4,3,2,1,0:T(8,128)S(1)}, f32[1,1,4,256,256]{4,3,2,1,0:T(8,128)}, u32[]{:S(2)}) copy-start(f32[1,1,4,256,256]{4,3,2,1,0:T(8,128)} %intensity.1) | copy-start | bytes 3145732
  1.0 7.7 %copy-start.3 = (bf16[4,512,256]{2,1,0:T(8,128)(2,1)S(1)}, bf16[4,512,256]{2,1,0:T(8,128)(2,1)}, u32[]{:S(2)}) copy-start(bf16[4,512,256]{2,1,0:T(8,128)(2,1)} %constant.5.clone.rest_1_.rest_6_) | copy-start | bytes 3145732
  1.0 7.7 %copy-start.4 = (bf16[4,512,256]{2,1,0:T(8,128)(2,1)S(1)}, bf16[4,512,256]{2,1,0:T(8,128)(2,1)}, u32[]{:S(2)}) copy-start(bf16[4,512,256]{2,1,0:T(8,128)(2,1)} %constant.4.clone.right.rest_5_) | copy-start | bytes 3145732
  1.2 6.8 %collective-permute-start = (f32[256,128]{1,0:T(8,128)S(1)}, f32[256,128]{1,0:T(8,128)S(1)}, u32[]{:S(2)}, u32[]{:S(2)}) collective-permute-start(f32[256,128]{1,0:T(8,128)S(1)} %get-tuple-element.19), channel_id=1, source_target_pairs={{0,1},{1,0},{2,3},{3,2},{4,5},{5,4},{6,7},{7,6},{8,9},{9,8},{10,11... | collective-permute-start | bytes 393224 | tf_op jit(solution)/shard_map/ppermute | solution.py:573
  1.8 7.9 %collective-permute-start.1 = (f32[2,64,256]{2,1,0:T(8,128)S(1)}, f32[2,64,256]{2,1,0:T(8,128)S(1)}, u32[]{:S(2)}, u32[]{:S(2)}) collective-permute-start(f32[2,64,256]{2,1,0:T(8,128)S(1)} %get-tuple-element.20), channel_id=1, source_target_pairs={{0,2},{1,3},{4,6},{5,7},{8,10},{9,11},{12,14},{13,15},{16,18},{17,... | collective-permute-start | bytes 393224 | tf_op jit(solution)/shard_map/ppermute | solution.py:566
  1.8 7.9 %collective-permute-start.2 = (f32[2,64,256]{2,1,0:T(8,128)S(1)}, f32[2,64,256]{2,1,0:T(8,128)S(1)}, u32[]{:S(2)}, u32[]{:S(2)}) collective-permute-start(f32[2,64,256]{2,1,0:T(8,128)S(1)} %get-tuple-element.21), channel_id=1, source_target_pairs={{2,4},{3,5},{6,8},{7,9},{10,12},{11,13},{14,16},{15,17},{18,20},{1... | collective-permute-start | bytes 393224 | tf_op jit(solution)/shard_map/ppermute | solution.py:566
  2.4 7.3 %collective-permute-start.3 = (f32[64,128]{1,0:T(8,128)S(1)}, f32[64,128]{1,0:T(8,128)S(1)}, u32[]{:S(2)}, u32[]{:S(2)}) collective-permute-start(f32[64,128]{1,0:T(8,128)S(1)} %get-tuple-element.22), channel_id=1, source_target_pairs={{2,5},{3,4},{6,9},{7,8},{10,13},{11,12},{14,17},{15,16},{18,21},{1... | collective-permute-start | bytes 98312 | tf_op jit(solution)/shard_map/ppermute | solution.py:570
  8.0 1.7 %collective-permute-start.4 = (f32[64,128]{1,0:T(8,128)S(1)}, f32[64,128]{1,0:T(8,128)S(1)}, u32[]{:S(2)}, u32[]{:S(2)}) collective-permute-start(f32[64,128]{1,0:T(8,128)S(1)} %shard_map.75.rest_0_), channel_id=1, source_target_pairs={{0,2},{1,3},{4,6},{5,7},{8,10},{9,11},{12,14},{13,15},{16,18},{17,... | collective-permute-start | bytes 98312 | tf_op jit(solution)/shard_map/ppermute | solution.py:566
  13.9 9.1 %collective-permute-start.5 = (f32[256,128]{1,0:T(8,128)S(1)}, f32[256,128]{1,0:T(8,128)S(1)}, u32[]{:S(2)}, u32[]{:S(2)}) collective-permute-start(f32[256,128]{1,0:T(8,128)S(1)} %get-tuple-element.24), channel_id=1, source_target_pairs={{0,1},{1,0},{2,3},{3,2},{4,5},{5,4},{6,7},{7,6},{8,9},{9,8},{10,11... | collective-permute-start | bytes 393224 | tf_op jit(solution)/shard_map/ppermute | solution.py:573
  14.0 9.1 %collective-permute-start.6 = (f32[2,64,256]{2,1,0:T(8,128)S(1)}, f32[2,64,256]{2,1,0:T(8,128)S(1)}, u32[]{:S(2)}, u32[]{:S(2)}) collective-permute-start(f32[2,64,256]{2,1,0:T(8,128)S(1)} %get-tuple-element.25), channel_id=1, source_target_pairs={{0,2},{1,3},{4,6},{5,7},{8,10},{9,11},{12,14},{13,15},{16,18},{17,... | collective-permute-start | bytes 393224 | tf_op jit(solution)/shard_map/ppermute | solution.py:566
  14.6 8.5 %collective-permute-start.7 = (f32[2,64,256]{2,1,0:T(8,128)S(1)}, f32[2,64,256]{2,1,0:T(8,128)S(1)}, u32[]{:S(2)}, u32[]{:S(2)}) collective-permute-start(f32[2,64,256]{2,1,0:T(8,128)S(1)} %get-tuple-element.26), channel_id=1, source_target_pairs={{2,4},{3,5},{6,8},{7,9},{10,12},{11,13},{14,16},{15,17},{18,20},{1... | collective-permute-start | bytes 393224 | tf_op jit(solution)/shard_map/ppermute | solution.py:566
  15.0 4.5 %collective-permute-start.8 = (f32[64,128]{1,0:T(8,128)S(1)}, f32[64,128]{1,0:T(8,128)S(1)}, u32[]{:S(2)}, u32[]{:S(2)}) collective-permute-start(f32[64,128]{1,0:T(8,128)S(1)} %get-tuple-element.27), channel_id=1, source_target_pairs={{2,5},{3,4},{6,9},{7,8},{10,13},{11,12},{14,17},{15,16},{18,21},{1... | collective-permute-start | bytes 98312 | tf_op jit(solution)/shard_map/ppermute | solution.py:570
  17.4 5.6 %collective-permute-start.9 = (f32[64,128]{1,0:T(8,128)S(1)}, f32[64,128]{1,0:T(8,128)S(1)}, u32[]{:S(2)}, u32[]{:S(2)}) collective-permute-start(f32[64,128]{1,0:T(8,128)S(1)} %get-tuple-element.28), channel_id=1, source_target_pairs={{0,3},{1,2},{4,7},{5,6},{8,11},{9,10},{12,15},{13,14},{16,19},{17,... | collective-permute-start | bytes 98312 | tf_op jit(solution)/shard_map/ppermute | solution.py:570

commit v17 on v16

--- a/solution.py
+++ b/solution.py
@@ -507,7 +507,7 @@
 def finish_kernel(chans, object_ref, g_core, *rest):
     count = len(chans)
     x_in, (a_in, b_in), rest = rest[:count], rest[count : count + 2], rest[count + 2 :]
-    kb_in, ka_in, out = rest[:count], rest[count : 2 * count], rest[-1]
+    ka_in, kb_in, out = rest[:count], rest[count : 2 * count], rest[-1]
     size = object_ref.shape[1]
     lower = lower_partner()
     a_rows = pl.ds(pl.multiple_of(jnp.where(lower, size - MARGIN, 0), MARGIN), MARGIN)
@@ -550,7 +550,7 @@
         in_specs=[vmem] * (4 + 3 * len(chans)),
         out_specs=vmem,
         compiler_params=pltpu.CompilerParams(vmem_limit_bytes=6 * 1024 * 1024),
-    )(object_field, g_core, *x_in, a_in, b_in, *kb_in, *ka_in)
+    )(object_field, g_core, *x_in, a_in, b_in, *ka_in, *kb_in)
 
 
 def per_device(object_field, probe_field, intensity, view_offsets, view_counts):

time: 24.3 us -> 24.2 us (level)
  the two profiles are of different devices: /device:TPU:30 before, /device:TPU:27 now
where the time goes in v17:
time: 24.2 us; the launch traced here: 24.1 us
  starting transfers between devices  10.2 us (42%)
  Pallas kernels  8.08 us (33%)
  waiting for transfers between devices  4.01 us (17%)
  local copies, waits for them, and re-layouts  1.06 us (4%)
  between operations  0.75 us (3%)
    ppermute x5, starting transfers between devices, over_rows(): return lax.ppermute(block, ('row', 'col'), route + extra)  4.97 us
    ppermute x3, starting transfers between devices, across(): lax.ppermute(block, ('row', 'col'), route + (extra if mesh_cols == 2 else...  4.29 us
    pallas_call x1, Pallas kernels, views_call(): pl.pallas_call(functools.partial(views_kernel, chans), out_shape=[jax.Sha...  4.2 us
    ppermute x3, waiting for transfers between devices, across(): lax.ppermute(block, ('row', 'col'), route + (extra if mesh_cols == 2 else...  3.99 us
    pallas_call x1, Pallas kernels, prepare_call(): pl.pallas_call(prepare_kernel, out_shape=[jax.ShapeDtypeStruct((views, 2,...  1.76 us
    pallas_call x1, Pallas kernels, finish_call(): pl.pallas_call(functools.partial(finish_kernel, chans), out_shape=jax.Sha...  1.07 us
    unnamed x10, local copies, waits for them, and re-layouts  1.06 us
    ppermute x2, starting transfers between devices, exchange(): lax.ppermute(block, 'col', channel[0])  0.91 us
  transfers between devices with their start and end apart: 10, of which 3 were waited for; matrix products, arithmetic and copies ran while one was open for 0% of the time, Pallas kernels for 11%

profile of v17, /device:TPU:27, one launch (start us, length us, event | category | flops | bytes accessed | tf_op | source)
XLA Modules:
  0.0 24.1 jit_solution(2185066355619676741)
XLA Ops:
  0.0 0.0 copy-start
  0.0 1.0 %copy-done = f32[2,256,256]{2,1,0:T(8,128)S(1)} copy-done((f32[2,256,256]{2,1,0:T(8,128)S(1)}, f32[2,256,256]{2,1,0:T(8,128)}, u32[]{:S(2)}) %copy-start) | copy-done | bytes 524312
  1.0 0.0 copy-start.1
  1.0 0.0 copy-start.2
  1.0 0.0 copy-start.3
  1.0 0.0 copy-start.4
  1.1 0.1 shard_map.74
  1.2 0.3 %collective-permute-start = (f32[256,128]{1,0:T(8,128)S(1)}, f32[256,128]{1,0:T(8,128)S(1)}, u32[]{:S(2)}, u32[]{:S(2)}) collective-permute-start(f32[256,128]{1,0:T(8,128)S(1)} %get-tuple-element.19), channel_id=1, source_target_pairs={{0,1},{1,0},{2,3},{3,2},{4,5},{5,4},{6,7},{7,6},{8,9},{9,8},{10,11... | collective-permute-start | bytes 393224 | tf_op jit(solution)/shard_map/ppermute | solution.py:573
  1.5 1.0 %collective-permute-start.1 = (f32[2,64,256]{2,1,0:T(8,128)S(1)}, f32[2,64,256]{2,1,0:T(8,128)S(1)}, u32[]{:S(2)}, u32[]{:S(2)}) collective-permute-start(f32[2,64,256]{2,1,0:T(8,128)S(1)} %get-tuple-element.20), channel_id=1, source_target_pairs={{0,2},{1,3},{4,6},{5,7},{8,10},{9,11},{12,14},{13,15},{16,18},{17,... | collective-permute-start | bytes 393224 | tf_op jit(solution)/shard_map/ppermute | solution.py:566
  2.5 1.1 %collective-permute-start.2 = (f32[2,64,256]{2,1,0:T(8,128)S(1)}, f32[2,64,256]{2,1,0:T(8,128)S(1)}, u32[]{:S(2)}, u32[]{:S(2)}) collective-permute-start(f32[2,64,256]{2,1,0:T(8,128)S(1)} %get-tuple-element.21), channel_id=1, source_target_pairs={{2,4},{3,5},{6,8},{7,9},{10,12},{11,13},{14,16},{15,17},{18,20},{1... | collective-permute-start | bytes 393224 | tf_op jit(solution)/shard_map/ppermute | solution.py:566
  3.6 1.5 %collective-permute-start.3 = (f32[64,128]{1,0:T(8,128)S(1)}, f32[64,128]{1,0:T(8,128)S(1)}, u32[]{:S(2)}, u32[]{:S(2)}) collective-permute-start(f32[64,128]{1,0:T(8,128)S(1)} %get-tuple-element.22), channel_id=1, source_target_pairs={{2,5},{3,4},{6,9},{7,8},{10,13},{11,12},{14,17},{15,16},{18,21},{1... | collective-permute-start | bytes 98312 | tf_op jit(solution)/shard_map/ppermute | solution.py:570
  5.1 1.8 %shard_map.73 = (f32[4,2,256,256]{3,2,1,0:T(8,128)S(1)}, s32[4,2,8,128]{3,2,1,0:T(8,128)S(1)}) custom-call(s32[1,1,2,4]{3,2,1,0:T(2,128)} %bitcast.1, f32[2,256,256]{2,1,0:T(8,128)} %probe.1), custom_call_target="tpu_custom_call" | custom-call | flops 1000000000 | bytes 100000 | tf_op jit(solution)/shard_map/pallas_call | solution.py:188
  6.9 0.0 collective-permute-done.block.rest_3_.rest_0_
  7.0 1.0 %collective-permute-start.4 = (f32[64,128]{1,0:T(8,128)S(1)}, f32[64,128]{1,0:T(8,128)S(1)}, u32[]{:S(2)}, u32[]{:S(2)}) collective-permute-start(f32[64,128]{1,0:T(8,128)S(1)} %shard_map.75.rest_0_), channel_id=1, source_target_pairs={{0,2},{1,3},{4,6},{5,7},{8,10},{9,11},{12,14},{13,15},{16,18},{17,... | collective-permute-start | bytes 98312 | tf_op jit(solution)/shard_map/ppermute | solution.py:566
  8.6 0.0 copy-done.1
  8.6 0.0 copy-done.2
  8.6 0.0 copy-done.3
  8.6 0.0 copy-done.4
  8.6 0.9 %shard_map.76.inner = f32[4,2,128,256]{3,2,1,0:T(8,128)S(1)} custom-call(s32[4,2,8,128]{3,2,1,0:T(8,128)S(1)} %get-tuple-element.17.spots, f32[2,256,256]{2,1,0:T(8,128)S(1)} %copy-done.1, f32[4,2,256,256]{3,2,1,0:T(8,128)S(1)} %get-tuple-element.18.placed, bf16[4,512,256]{2,1,0:T(8,128)(2,1)S(1)} %copy-done.4, f32[64,128]{1,0:T(8,128)S(1)} %shard_map.75.rest_0_, ...), custom_call_target="tpu_custom_call" | custom-call | flops 100000000 | bytes 10000 | tf_op jit(solution)/shard_map/pallas_call | solution.py:284
  9.5 0.1 collective-permute-done.3.rest_3_
  9.6 0.0 collective-permute-done.1.rest_1_
  9.6 0.0 collective-permute-done.2.rest_2_
  9.6 0.0 collective-permute-done.4.rest_4_
  9.7 4.2 %shard_map.77 = (f32[2,256,256]{2,1,0:T(8,128)S(1)}, f32[2,64,256]{2,1,0:T(8,128)S(1)}, f32[2,64,256]{2,1,0:T(8,128)S(1)}, f32[256,128]{1,0:T(8,128)S(1)}, f32[64,128]{1,0:T(8,128)S(1)}, /*index=5*/f32[64,128]{1,0:T(8,128)S(1)}) custom-call(s32[4,2,8,128]{3,2,1,0:T(8,128)S(1)} %get-tuple-element.17.spots, s32[1,1]{1,0:T(1,128)S(6)} %copy.8.counts, ...), custom_call_target="tpu_custom_call" | custom-call | tf_op jit(solution)/shard_map/pallas_call | solution.py:484
  13.9 0.6 %collective-permute-start.5 = (f32[256,128]{1,0:T(8,128)S(1)}, f32[256,128]{1,0:T(8,128)S(1)}, u32[]{:S(2)}, u32[]{:S(2)}) collective-permute-start(f32[256,128]{1,0:T(8,128)S(1)} %get-tuple-element.24), channel_id=1, source_target_pairs={{0,1},{1,0},{2,3},{3,2},{4,5},{5,4},{6,7},{7,6},{8,9},{9,8},{10,11... | collective-permute-start | bytes 393224 | tf_op jit(solution)/shard_map/ppermute | solution.py:573
  14.5 0.6 %collective-permute-start.6 = (f32[2,64,256]{2,1,0:T(8,128)S(1)}, f32[2,64,256]{2,1,0:T(8,128)S(1)}, u32[]{:S(2)}, u32[]{:S(2)}) collective-permute-start(f32[2,64,256]{2,1,0:T(8,128)S(1)} %get-tuple-element.25), channel_id=1, source_target_pairs={{0,2},{1,3},{4,6},{5,7},{8,10},{9,11},{12,14},{13,15},{16,18},{17,... | collective-permute-start | bytes 393224 | tf_op jit(solution)/shard_map/ppermute | solution.py:566
  15.0 1.3 %collective-permute-start.7 = (f32[2,64,256]{2,1,0:T(8,128)S(1)}, f32[2,64,256]{2,1,0:T(8,128)S(1)}, u32[]{:S(2)}, u32[]{:S(2)}) collective-permute-start(f32[2,64,256]{2,1,0:T(8,128)S(1)} %get-tuple-element.26), channel_id=1, source_target_pairs={{2,4},{3,5},{6,8},{7,9},{10,12},{11,13},{14,16},{15,17},{18,20},{1... | collective-permute-start | bytes 393224 | tf_op jit(solution)/shard_map/ppermute | solution.py:566
  16.4 1.1 %collective-permute-start.8 = (f32[64,128]{1,0:T(8,128)S(1)}, f32[64,128]{1,0:T(8,128)S(1)}, u32[]{:S(2)}, u32[]{:S(2)}) collective-permute-start(f32[64,128]{1,0:T(8,128)S(1)} %get-tuple-element.27), channel_id=1, source_target_pairs={{0,3},{1,2},{4,7},{5,6},{8,11},{9,10},{12,15},{13,14},{16,19},{17,... | collective-permute-start | bytes 98312 | tf_op jit(solution)/shard_map/ppermute | solution.py:570
  17.5 1.6 %collective-permute-start.9 = (f32[64,128]{1,0:T(8,128)S(1)}, f32[64,128]{1,0:T(8,128)S(1)}, u32[]{:S(2)}, u32[]{:S(2)}) collective-permute-start(f32[64,128]{1,0:T(8,128)S(1)} %get-tuple-element.28), channel_id=1, source_target_pairs={{2,5},{3,4},{6,9},{7,8},{10,13},{11,12},{14,17},{15,16},{18,21},{1... | collective-permute-start | bytes 98312 | tf_op jit(solution)/shard_map/ppermute | solution.py:570
  19.1 0.9 %collective-permute-done.8.rest_3_ = f32[64,128]{1,0:T(8,128)S(1)} collective-permute-done((f32[64,128]{1,0:T(8,128)S(1)}, f32[64,128]{1,0:T(8,128)S(1)}, u32[]{:S(2)}, u32[]{:S(2)}) %collective-permute-start.8) | collective-permute-done | bytes 32800 | tf_op jit(solution)/shard_map/ppermute | solution.py:570
  20.0 3.0 %collective-permute-done.9.rest_4_ = f32[64,128]{1,0:T(8,128)S(1)} collective-permute-done((f32[64,128]{1,0:T(8,128)S(1)}, f32[64,128]{1,0:T(8,128)S(1)}, u32[]{:S(2)}, u32[]{:S(2)}) %collective-permute-start.9) | collective-permute-done | bytes 32800 | tf_op jit(solution)/shard_map/ppermute | solution.py:570
  23.0 0.0 collective-permute-done.5.rest_0_
  23.0 0.0 collective-permute-done.6.rest_1_
  23.0 0.0 collective-permute-done.7.rest_2_
  23.0 1.1 %shard_map.78 = f32[2,256,256]{2,1,0:T(8,128)} custom-call(f32[2,256,256]{2,1,0:T(8,128)S(1)} %copy-done.1, f32[2,256,256]{2,1,0:T(8,128)S(1)} %get-tuple-element.23.g_core, f32[256,128]{1,0:T(8,128)S(1)} %collective-permute-done.5.rest_0_, f32[2,64,256]{2,1,0:T(8,128)S(1)} %collective-permute-done.6.rest_1_, ...), custom_call_target="tpu_custom_call" | custom-call | tf_op jit(solution)/shard_map/pallas_call | solution.py:547
  (1 shorter events, 0.0 us)
Async XLA Ops:
  0.0 1.0 %copy-start = (f32[2,256,256]{2,1,0:T(8,128)S(1)}, f32[2,256,256]{2,1,0:T(8,128)}, u32[]{:S(2)}) copy-start(f32[2,256,256]{2,1,0:T(8,128)} %object_ref.3) | copy-start | bytes 1572868
  1.0 7.5 %copy-start.1 = (f32[2,256,256]{2,1,0:T(8,128)S(1)}, f32[2,256,256]{2,1,0:T(8,128)}, u32[]{:S(2)}) copy-start(f32[2,256,256]{2,1,0:T(8,128)} %object_ref.3) | copy-start | bytes 1572868
  1.0 7.5 %copy-start.2 = (f32[1,1,4,256,256]{4,3,2,1,0:T(8,128)S(1)}, f32[1,1,4,256,256]{4,3,2,1,0:T(8,128)}, u32[]{:S(2)}) copy-start(f32[1,1,4,256,256]{4,3,2,1,0:T(8,128)} %intensity.1) | copy-start | bytes 3145732
  1.0 7.5 %copy-start.3 = (bf16[4,512,256]{2,1,0:T(8,128)(2,1)S(1)}, bf16[4,512,256]{2,1,0:T(8,128)(2,1)}, u32[]{:S(2)}) copy-start(bf16[4,512,256]{2,1,0:T(8,128)(2,1)} %constant.5.clone.rest_1_.rest_6_) | copy-start | bytes 3145732
  1.0 7.6 %copy-start.4 = (bf16[4,512,256]{2,1,0:T(8,128)(2,1)S(1)}, bf16[4,512,256]{2,1,0:T(8,128)(2,1)}, u32[]{:S(2)}) copy-start(bf16[4,512,256]{2,1,0:T(8,128)(2,1)} %constant.4.clone.right.rest_5_) | copy-start | bytes 3145732
  1.2 5.7 %collective-permute-start = (f32[256,128]{1,0:T(8,128)S(1)}, f32[256,128]{1,0:T(8,128)S(1)}, u32[]{:S(2)}, u32[]{:S(2)}) collective-permute-start(f32[256,128]{1,0:T(8,128)S(1)} %get-tuple-element.19), channel_id=1, source_target_pairs={{0,1},{1,0},{2,3},{3,2},{4,5},{5,4},{6,7},{7,6},{8,9},{9,8},{10,11... | collective-permute-start | bytes 393224 | tf_op jit(solution)/shard_map/ppermute | solution.py:573
  1.5 8.1 %collective-permute-start.1 = (f32[2,64,256]{2,1,0:T(8,128)S(1)}, f32[2,64,256]{2,1,0:T(8,128)S(1)}, u32[]{:S(2)}, u32[]{:S(2)}) collective-permute-start(f32[2,64,256]{2,1,0:T(8,128)S(1)} %get-tuple-element.20), channel_id=1, source_target_pairs={{0,2},{1,3},{4,6},{5,7},{8,10},{9,11},{12,14},{13,15},{16,18},{17,... | collective-permute-start | bytes 393224 | tf_op jit(solution)/shard_map/ppermute | solution.py:566
  2.5 7.2 %collective-permute-start.2 = (f32[2,64,256]{2,1,0:T(8,128)S(1)}, f32[2,64,256]{2,1,0:T(8,128)S(1)}, u32[]{:S(2)}, u32[]{:S(2)}) collective-permute-start(f32[2,64,256]{2,1,0:T(8,128)S(1)} %get-tuple-element.21), channel_id=1, source_target_pairs={{2,4},{3,5},{6,8},{7,9},{10,12},{11,13},{14,16},{15,17},{18,20},{1... | collective-permute-start | bytes 393224 | tf_op jit(solution)/shard_map/ppermute | solution.py:566
  3.6 6.0 %collective-permute-start.3 = (f32[64,128]{1,0:T(8,128)S(1)}, f32[64,128]{1,0:T(8,128)S(1)}, u32[]{:S(2)}, u32[]{:S(2)}) collective-permute-start(f32[64,128]{1,0:T(8,128)S(1)} %get-tuple-element.22), channel_id=1, source_target_pairs={{2,5},{3,4},{6,9},{7,8},{10,13},{11,12},{14,17},{15,16},{18,21},{1... | collective-permute-start | bytes 98312 | tf_op jit(solution)/shard_map/ppermute | solution.py:570
  7.0 2.7 %collective-permute-start.4 = (f32[64,128]{1,0:T(8,128)S(1)}, f32[64,128]{1,0:T(8,128)S(1)}, u32[]{:S(2)}, u32[]{:S(2)}) collective-permute-start(f32[64,128]{1,0:T(8,128)S(1)} %shard_map.75.rest_0_), channel_id=1, source_target_pairs={{0,2},{1,3},{4,6},{5,7},{8,10},{9,11},{12,14},{13,15},{16,18},{17,... | collective-permute-start | bytes 98312 | tf_op jit(solution)/shard_map/ppermute | solution.py:566
  13.9 9.1 %collective-permute-start.5 = (f32[256,128]{1,0:T(8,128)S(1)}, f32[256,128]{1,0:T(8,128)S(1)}, u32[]{:S(2)}, u32[]{:S(2)}) collective-permute-start(f32[256,128]{1,0:T(8,128)S(1)} %get-tuple-element.24), channel_id=1, source_target_pairs={{0,1},{1,0},{2,3},{3,2},{4,5},{5,4},{6,7},{7,6},{8,9},{9,8},{10,11... | collective-permute-start | bytes 393224 | tf_op jit(solution)/shard_map/ppermute | solution.py:573
  14.5 8.5 %collective-permute-start.6 = (f32[2,64,256]{2,1,0:T(8,128)S(1)}, f32[2,64,256]{2,1,0:T(8,128)S(1)}, u32[]{:S(2)}, u32[]{:S(2)}) collective-permute-start(f32[2,64,256]{2,1,0:T(8,128)S(1)} %get-tuple-element.25), channel_id=1, source_target_pairs={{0,2},{1,3},{4,6},{5,7},{8,10},{9,11},{12,14},{13,15},{16,18},{17,... | collective-permute-start | bytes 393224 | tf_op jit(solution)/shard_map/ppermute | solution.py:566
  15.0 7.9 %collective-permute-start.7 = (f32[2,64,256]{2,1,0:T(8,128)S(1)}, f32[2,64,256]{2,1,0:T(8,128)S(1)}, u32[]{:S(2)}, u32[]{:S(2)}) collective-permute-start(f32[2,64,256]{2,1,0:T(8,128)S(1)} %get-tuple-element.26), channel_id=1, source_target_pairs={{2,4},{3,5},{6,8},{7,9},{10,12},{11,13},{14,16},{15,17},{18,20},{1... | collective-permute-start | bytes 393224 | tf_op jit(solution)/shard_map/ppermute | solution.py:566
  16.4 3.6 %collective-permute-start.8 = (f32[64,128]{1,0:T(8,128)S(1)}, f32[64,128]{1,0:T(8,128)S(1)}, u32[]{:S(2)}, u32[]{:S(2)}) collective-permute-start(f32[64,128]{1,0:T(8,128)S(1)} %get-tuple-element.27), channel_id=1, source_target_pairs={{0,3},{1,2},{4,7},{5,6},{8,11},{9,10},{12,15},{13,14},{16,19},{17,... | collective-permute-start | bytes 98312 | tf_op jit(solution)/shard_map/ppermute | solution.py:570
  17.5 5.5 %collective-permute-start.9 = (f32[64,128]{1,0:T(8,128)S(1)}, f32[64,128]{1,0:T(8,128)S(1)}, u32[]{:S(2)}, u32[]{:S(2)}) collective-permute-start(f32[64,128]{1,0:T(8,128)S(1)} %get-tuple-element.28), channel_id=1, source_target_pairs={{2,5},{3,4},{6,9},{7,8},{10,13},{11,12},{14,17},{15,16},{18,21},{1... | collective-permute-start | bytes 98312 | tf_op jit(solution)/shard_map/ppermute | solution.py:570
